TPU v7x, 128 devices: a whole 4x4x4 slice. The times are simulated.
128 devices in a mesh: dp: 8 (over x, z_lo), tp: 16 (over z_hi, y, core).
Axes of the slice: x: 4, y: 4, z: 4 (z_hi: 2, z_lo: 2; z = z_hi * 2 + z_lo), core: 2. Of those that a mesh axis runs over, the one named last changes fastest.
Arguments:
- cache: bfloat16 [512, 256, 576], P(('dp', 'tp')), may hold values from -3 to 3, as said below
- cache_length: int32 [512], P(('dp', 'tp')), may hold values from 64 to 254, as said below
- move_slot: int32 [8, 16], P('dp'), may hold values from 0 to 3
- move_peer: int32 [8, 16], P('dp'), may hold values from 0 to 15, as said below
- queries: bfloat16 [2, 512, 128, 576], P(None, ('dp', 'tp')), may hold values from -16 to 16
- new_latent: bfloat16 [2, 512, 576], P(None, ('dp', 'tp')), may hold values from -3 to 3
- value_up: bfloat16 [128, 512, 128], P('tp'), may hold values from -0.25 to 0.25
- out_proj: bfloat16 [16384, 7168], P('tp', 'dp'), may hold values from -0.046875 to 0.046875
- residual: bfloat16 [2, 512, 7168], P(None, None, 'dp'), may hold values from -1.5 to 1.5
- norm_gain: bfloat16 [7168], P('dp'), may hold values from 0.5 to 1.5
- gate_weight: bfloat16 [7168, 18432], P('dp', 'tp'), may hold values from -0.0625 to 0.0625
- up_weight: bfloat16 [7168, 18432], P('dp', 'tp'), may hold values from -0.0625 to 0.0625
- down_weight: bfloat16 [18432, 7168], P('tp', 'dp'), may hold values from -0.046875 to 0.046875
Outputs:
- layer_out: bfloat16 [2, 512, 7168], P(None, 'tp', 'dp')
Inputs may be any that keep to these rules, and one draw needn't show every extreme that they name: Row g of cache holds the request of slot g before migration; its positions from cache_length onward (in the slot after migration) are never read. `cache_length`: at least two positions of every request stay free for the new tokens; some request is that long in every draw. `move_peer`: each row is a permutation of the tp indices 0 .. 15; a device whose entry is its own index keeps its requests.
All inputs are finite; a program needn't handle non-finite values.
Results may differ from a plain program's by a relative error of at most 0.01.
Values may be sent and summed in bfloat16 or wider, within the bound.
No kernel may reach another device: no remote copies, remote signals or barrier semaphores. Data moves between devices by JAX's collectives and lax.ppermute only.
A program may use at most 128 MiB of HBM per device.

v0:
```python
import jax
import jax.numpy as jnp
from jax import lax
from jax.sharding import PartitionSpec as P

D = 7168
QKD = 192
STEPS = 2


norm_eps = 1e-06


def activate(gate_sum, up_sum, square_sum):
    inverse = lax.rsqrt(square_sum / D + norm_eps)[:, None]
    return (jax.nn.silu(gate_sum * inverse) * (up_sum * inverse)).astype(jnp.bfloat16)


def local(
    cache,
    cache_length,
    move_slot,
    move_peer,
    queries,
    new_latent,
    value_up,
    out_proj,
    residual,
    norm_gain,
    gate_weight,
    up_weight,
    down_weight,
):
    group_size = lax.axis_size("tp")
    member = lax.axis_index("tp")
    lane_ids = jnp.arange(group_size, dtype=jnp.int32)
    peer_row = move_peer[0]
    slot_row = move_slot[0]
    own_slot = jnp.sum(jnp.where(lane_ids == member, slot_row, 0))
    outgoing = lax.dynamic_slice_in_dim(cache, own_slot, 1, 0)
    shard_rows = lax.all_gather(outgoing, "tp", axis=0, tiled=True)
    senders = jnp.arange(shard_rows.shape[0], dtype=jnp.int32)
    targets = jnp.sum(
        jnp.where(lane_ids[None, :] == senders[:, None], peer_row[None, :], 0), axis=1
    )
    matched = targets == member
    picked = jnp.sum(
        jnp.where(matched[:, None, None], shard_rows, jnp.zeros_like(shard_rows)), axis=0
    )
    arrived = jnp.where(jnp.any(matched), picked, jnp.zeros(outgoing.shape[1:], outgoing.dtype))
    latents = lax.dynamic_update_slice_in_dim(cache, arrived[None], own_slot, 0)
    positions = jnp.arange(latents.shape[1], dtype=jnp.int32)[None, :]
    latent_width = value_up.shape[1]
    rows_out = residual.shape[1] // group_size
    score_scale = QKD ** (-0.5)
    results = []
    for decode_step in range(STEPS):
        current = cache_length[:, None] + decode_step
        latents = jnp.where(
            (positions == current)[:, :, None], new_latent[decode_step][:, None, :], latents
        )
        scores = (
            jnp.einsum(
                "rhc,rlc->rhl", queries[decode_step], latents, preferred_element_type=jnp.float32
            )
            * score_scale
        )
        scores = jnp.where((positions <= current)[:, None, :], scores, -jnp.inf)
        largest = jnp.max(scores, axis=-1, keepdims=True)
        expo = jnp.exp(scores - largest)
        denominator = jnp.sum(expo, axis=-1, keepdims=True)
        attn_probs = (expo / denominator).astype(jnp.bfloat16)
        latent_out = jnp.einsum(
            "rhl,rlc->rhc",
            attn_probs,
            latents[:, :, :latent_width],
            preferred_element_type=jnp.float32,
        ).astype(jnp.bfloat16)
        by_head = lax.all_to_all(latent_out, "tp", split_axis=1, concat_axis=0, tiled=True)
        value_heads = jnp.einsum(
            "thl,hlv->thv", by_head, value_up, preferred_element_type=jnp.float32
        ).astype(jnp.bfloat16)
        project_shard_rows = lax.all_gather(value_heads, "dp", axis=0, tiled=True)
        partial_value = jnp.dot(
            project_shard_rows.reshape(project_shard_rows.shape[0], -1),
            out_proj,
            preferred_element_type=jnp.float32,
        )
        attended = lax.psum(partial_value, "tp")
        hidden = residual[decode_step].astype(jnp.float32) + attended
        squares = jnp.sum(hidden * hidden, axis=1)
        normed = (hidden * norm_gain.astype(jnp.float32)).astype(jnp.bfloat16)
        gate_part = jnp.dot(normed, gate_weight, preferred_element_type=jnp.float32)
        up_part = jnp.dot(normed, up_weight, preferred_element_type=jnp.float32)
        gate_sum, up_sum, square_sum = lax.psum((gate_part, up_part, squares), "dp")
        activated = activate(gate_sum, up_sum, square_sum)
        down_part = jnp.dot(activated, down_weight, preferred_element_type=jnp.float32)
        ffn_out = lax.psum_scatter(down_part, "tp", scatter_dimension=0, tiled=True)
        residue = lax.dynamic_slice_in_dim(hidden, member * rows_out, rows_out, 0)
        results.append((residue + ffn_out).astype(jnp.bfloat16))
    return jnp.stack(results)


def solution(mesh):
    in_specs = (
        P(("dp", "tp"), None, None),
        P(("dp", "tp")),
        P("dp", None),
        P("dp", None),
        P(None, ("dp", "tp"), None, None),
        P(None, ("dp", "tp"), None),
        P("tp", None, None),
        P("tp", "dp"),
        P(None, None, "dp"),
        P("dp"),
        P("dp", "tp"),
        P("dp", "tp"),
        P("tp", "dp"),
    )
    out_specs = P(None, "tp", "dp")
    return jax.shard_map(local, mesh=mesh, in_specs=in_specs, out_specs=out_specs, check_vma=False)
```

profile of v0, /device:TPU:1, one launch (start us, length us, event | category | flops | bytes accessed | tf_op | source)
XLA Modules:
  0.0 900.4 jit_solution(5526216506247910013)
XLA Ops:
  6.6 1.4 fusion.28
  10.0 1.7 constant_dynamic-slice_fusion
  11.7 1.7 copy.43
  13.5 0.6 fusion.33
  14.3 59.2 %all-gather.4.cloned.1.call-done = bf16[16,256,576]{1,2,0:T(8,128)(2,1)} async-done(((bf16[1,256,576]{1,2,0:T(8,128)(2,1)}), bf16[16,256,576]{1,2,0:T(8,128)(2,1)}) %all-gather.4.cloned.1.call-update) | async-done | bytes 4718608 | tf_op jit(solution)/shard_map/all_gather | solution.py:41
  73.5 4.1 select_reduce_fusion
  77.6 1.8 copy.42
  79.4 1.7 bitcast_dynamic-update-slice_fusion
  81.1 1.4 broadcast_select_fusion
  82.6 1.1 copy-done.5
  83.6 0.5 fusion.8
  84.3 1.6 convolution_convert_fusion.1
  85.9 0.4 copy.46
  86.3 15.3 %all_to_all.36 = bf16[4,128,512]{2,0,1:T(4,128)(2,1)S(1)} all-to-all(bf16[4,128,512]{2,0,1:T(4,128)(2,1)S(1)} %copy.46), channel_id=1, replica_groups=mesh['dp'=8,'tp'=16] {'tp'}, dimensions={1} | all-to-all | bytes 1048576 | tf_op jit(solution)/shard_map/all_to_all | solution.py:79
  101.6 1.0 copy.61
  102.6 2.0 all_to_all.29
  104.6 2.0 fusion.12
  106.7 2.0 fusion.9
  108.7 0.8 copy-done.6
  109.6 2.8 convolution_convert_fusion
  112.4 1.5 copy.51
  113.9 17.7 %all_to_all.37 = bf16[4,128,512]{2,0,1:T(4,128)(2,1)S(1)} all-to-all(bf16[4,128,512]{2,0,1:T(4,128)(2,1)S(1)} %copy.51), channel_id=1, replica_groups=mesh['dp'=8,'tp'=16] {'tp'}, dimensions={1} | all-to-all | bytes 1048576 | tf_op jit(solution)/shard_map/all_to_all | solution.py:79
  131.7 1.0 copy.60
  132.7 2.0 all_to_all.33
  134.6 2.0 fusion.13
  136.7 8.3 all-gather.6.cloned.1.call-done
  145.1 1.5 copy.48
  146.5 4.0 fusion.36
  150.6 35.0 %all-gather.8.cloned.1.call-done = bf16[512,8,128]{2,0,1:T(8,128)(2,1)} async-done(((bf16[64,8,128]{2,0,1:T(8,128)(2,1)}), bf16[512,8,128]{2,0,1:T(8,128)(2,1)}) %all-gather.8.cloned.1.call-update) | async-done | bytes 1048592 | tf_op jit(solution)/shard_map/all_gather | solution.py:83
  185.6 1.5 copy.53
  187.1 4.1 fusion.37
  191.1 0.2 all-reduce.8.cloned.1.call-start
  191.4 0.4 copy-done.8
  191.8 152.3 %all-reduce.6.cloned.1.call-done = (f32[512,896]{1,0:T(8,128)}, f32[512,896]{1,0:T(8,128)}) async-done(((f32[512,896]{1,0:T(8,128)}, f32[512,896]{1,0:T(8,128)}), (f32[512,896]{1,0:T(8,128)}, f32[512,896]{1,0:T(8,128)})) %all-reduce.6.cloned.1.call-update) | async-done | bytes 3670032 | tf_op jit(solution)/shard_map/psum | solution.py:89
  344.1 3.3 multiply_reduce_fusion.1
  347.4 2.9 fusion.20
  350.3 2.9 fusion.21
  353.2 3.0 fusion.23
  356.2 2.9 fusion.22
  359.2 15.4 %all-reduce.1 = (f32[512]{0:T(512)S(1)}, f32[512]{0:T(512)S(1)}) all-reduce(f32[512]{0:T(512)S(1)} %get-tuple-element.21, f32[512]{0:T(512)S(1)} %get-tuple-element.13), channel_id=1, replica_groups=mesh['dp'=8,'tp'=16] {'dp'}, use_global_device_ids=true, to_apply=%region_17.18 | all-reduce | flops 1024 | bytes 8192 | tf_op jit(solution)/shard_map/psum | solution.py:95
  374.7 367.2 %all-reduce.8.cloned.1.call-done = (f32[512,1152]{1,0:T(8,128)}, f32[512,1152]{1,0:T(8,128)}, f32[512,1152]{1,0:T(8,128)}, f32[512,1152]{1,0:T(8,128)}) async-done(((f32[512,1152]{1,0:T(8,128)}, f32[512,1152]{1,0:T(8,128)}, f32[512,1152]{1,0:T(8,128)}, f32[512,1152]{1,0:T(8,128)}), (f32[512,1152]{1,0:T(8,128)}, f32[512,1152]{1,0:T(8,128)}, f32[512,1152]{1,0:T(8,128)}, ...) | async-done | bytes 9437200 | tf_op jit(solution)/shard_map/psum | solution.py:95
  741.8 5.8 fusion.10
  747.7 6.0 fusion.11
  753.8 64.9 %reduce-scatter.3.cloned.1.call-done = f32[32,896]{1,0:T(8,128)} async-done(((f32[512,896]{1,0:T(8,128)}), f32[32,896]{1,0:T(8,128)}) %reduce-scatter.3.cloned.1.call-update) | async-done | bytes 114704 | tf_op jit(solution)/shard_map/reduce_scatter | solution.py:98
  818.7 1.0 fusion.26
  819.6 72.3 %reduce-scatter.5.cloned.1.call-done = f32[32,896]{1,0:T(8,128)} async-done(((f32[512,896]{1,0:T(8,128)}), f32[32,896]{1,0:T(8,128)}) %reduce-scatter.5.cloned.1.call-update) | async-done | bytes 114704 | tf_op jit(solution)/shard_map/reduce_scatter | solution.py:98
  891.9 1.0 fusion.27
  892.9 0.7 pad_maximum_fusion
  (45 shorter events, 0.9 us)
Async XLA Ops:
  6.5 343.8 %copy-start = (bf16[896,1152]{1,0:T(8,128)(2,1)S(1)}, bf16[896,1152]{1,0:T(8,128)(2,1)}, u32[]{:S(2)}) copy-start(bf16[896,1152]{1,0:T(8,128)(2,1)} %param.23) | copy-start | bytes 6193156
  6.5 6.9 copy-start.12
  6.5 7.7 copy-start.9
  6.5 7.7 copy-start.7
  6.5 66.9 %all-gather.4.cloned.1.call-start = ((), (), s32[]{:S(2)}) async-start(), calls=%async_computation.4 | async-start | bytes 5013504 | tf_op jit(solution)/shard_map/all_gather | solution.py:41
  11.7 133.4 %all-gather.6.cloned.1.call-start = ((), (), s32[]{:S(2)}) async-start(), calls=%async_computation.5 | async-start | bytes 1179648 | tf_op jit(solution)/shard_map/all_gather | solution.py:83
  81.1 2.5 copy-start.11
  82.6 1.1 copy-start.5
  86.3 18.3 %copy-start.2 = (bf16[8,512,128]{2,1,0:T(8,128)(2,1)S(1)}, bf16[8,512,128]{2,1,0:T(8,128)(2,1)}, u32[]{:S(2)}) copy-start(bf16[8,512,128]{2,1,0:T(8,128)(2,1)} %param.19) | copy-start | bytes 3145732
  106.7 78.9 %all-gather.8.cloned.1.call-start = ((), (), s32[]{:S(2)}) async-start(), calls=%async_computation.7 | async-start | bytes 1179648 | tf_op jit(solution)/shard_map/all_gather | solution.py:83
  108.7 0.8 copy-start.6
  136.7 207.4 %all-reduce.6.cloned.1.call-start = ((), (), s32[]{:S(2)}) async-start(), calls=%async_computation.9 | async-start | bytes 7340032 | tf_op jit(solution)/shard_map/psum | solution.py:89
  191.1 0.7 copy-start.8
  191.1 550.7 %all-reduce.8.cloned.1.call-start = ((), (), s32[]{:S(2)}) async-start(), calls=%async_computation.10 | async-start | bytes 18874368 | tf_op jit(solution)/shard_map/psum | solution.py:95
  344.1 3.3 copy-start.10
  347.4 2.9 copy-start.4
  347.4 8.8 copy-start.3
  359.2 459.5 %reduce-scatter.3.cloned.1.call-start = ((), (), s32[]{:S(2)}) async-start(), calls=%async_computation.6 | async-start | bytes 1949696 | tf_op jit(solution)/shard_map/reduce_scatter | solution.py:98
  747.7 144.3 %reduce-scatter.5.cloned.1.call-start = ((), (), s32[]{:S(2)}) async-start(), calls=%async_computation.8 | async-start | bytes 1949696 | tf_op jit(solution)/shard_map/reduce_scatter | solution.py:98
  747.7 145.8 %copy-start.1 = (bf16[896,1152]{1,0:T(8,128)(2,1)S(1)}, bf16[896,1152]{1,0:T(8,128)(2,1)}, u32[]{:S(2)}) copy-start(bf16[896,1152]{1,0:T(8,128)(2,1)} %param.23) | copy-start | bytes 6193156
Sparse Core Ops, SparseCore 0:
  11.8 61.6 all-gather.3
  106.8 38.2 all-gather.5
  146.7 38.8 all-gather.7
  191.3 152.7 all-reduce.5
  359.3 382.4 all-reduce.7
  747.8 70.8 reduce-scatter.2
  823.1 68.8 reduce-scatter.4
where the time goes:
time: 902 us; the launch traced here: 900 us
  waiting for transfers between devices  759 us (84%)
  blocking collectives  48.5 us (5%)
  matrix products  42.5 us (5%)
  local copies, waits for them, and re-layouts  18.4 us (2%)
  other arithmetic  15.7 us (2%)
  between operations  15.6 us (2%)
    psum x1, waiting for transfers between devices, local(): gate_sum, up_sum, square_sum = lax.psum((gate_part, up_part, squares), 'dp')  367 us
    psum x1, waiting for transfers between devices, local(): attended = lax.psum(partial_value, 'tp')  152 us
    reduce_scatter x2, waiting for transfers between devices, local(): ffn_out = lax.psum_scatter(down_part, 'tp', scatter_dimension=0, tiled=True)  137 us
    all_gather x1, waiting for transfers between devices, local(): shard_rows = lax.all_gather(outgoing, 'tp', axis=0, tiled=True)  59.2 us
    all_gather x2, waiting for transfers between devices, local(): project_shard_rows = lax.all_gather(value_heads, 'dp', axis=0, tiled=True)  43.3 us
    all_to_all x2, blocking collectives, local(): lax.all_to_all(latent_out, 'tp', split_axis=1, concat_axis=0, tiled=True)  33 us
  transfers between devices with their start and end apart: 7, of which 7 were waited for; matrix products, arithmetic and copies ran while one was open for 3% of the time, Pallas kernels for 0%

commit v1 on v0

v1 whole, which is shorter than its diff:
```python
import jax
import jax.numpy as jnp
from jax import lax
from jax.sharding import Mesh, PartitionSpec as P

D = 7168
QKD = 192
STEPS = 2
norm_eps = 1e-06

DP = ("x", "zl")
TP = ("zh", "y", "c")
ZY = ("zh", "y")
N_DP = 8
N_TP = 16
N_ZY = 8
SWAP = [(0, 1), (1, 0)]
bf16 = jnp.bfloat16
f32 = jnp.float32


def exchange(blocks, axes):
    return lax.all_to_all(blocks, axes, 0, 0, tiled=True)


def spread(block, axes, copies):
    return exchange(jnp.broadcast_to(block[None], (copies,) + block.shape), axes)


def migrate(cache, slot_row, peer_row, member, own_slot):
    lanes = jnp.arange(N_TP, dtype=jnp.int32)
    outgoing = lax.dynamic_slice_in_dim(cache, own_slot, 1, 0)[0]
    rows, width = outgoing.shape
    pieces = exchange(outgoing.reshape(N_TP, rows // N_TP, width), TP)
    route = (peer_row[None, :] == lanes[:, None]).astype(bf16)
    routed = jnp.einsum(
        "ji,ipc->jpc", route, pieces, preferred_element_type=f32
    ).astype(bf16)
    arrived = exchange(routed, TP).reshape(1, rows, width)
    return lax.dynamic_update_slice_in_dim(cache, arrived, own_slot, 0)


def attend(latents, cache_length, queries, new_latent, latent_width):
    positions = jnp.arange(latents.shape[1], dtype=jnp.int32)[None, :]
    for step in range(STEPS):
        latents = jnp.where(
            (positions == cache_length[:, None] + step)[:, :, None],
            new_latent[step][:, None, :],
            latents,
        )
    scores = jnp.einsum("srhc,rlc->rshl", queries, latents, preferred_element_type=f32)
    scores = scores * QKD ** (-0.5)
    limit = cache_length[:, None] + jnp.arange(STEPS, dtype=jnp.int32)[None, :]
    seen = positions[None] <= limit[:, :, None]
    scores = jnp.where(seen[:, :, None, :], scores, -jnp.inf)
    expo = jnp.exp(scores - jnp.max(scores, axis=-1, keepdims=True))
    probs = (expo / jnp.sum(expo, axis=-1, keepdims=True)).astype(bf16)
    out = jnp.einsum(
        "rshl,rlc->rshc", probs, latents[:, :, :latent_width], preferred_element_type=f32
    ).astype(bf16)
    return out


def local(
    cache,
    cache_length,
    move_slot,
    move_peer,
    queries,
    new_latent,
    value_up,
    out_proj,
    residual,
    norm_gain,
    gate_weight,
    up_weight,
    down_weight,
):
    member = lax.axis_index(TP)
    core = lax.axis_index("c")
    lanes = jnp.arange(N_TP, dtype=jnp.int32)
    own_slot = jnp.sum(jnp.where(lanes == member, move_slot[0], 0))
    latents = migrate(cache, move_slot[0], move_peer[0], member, own_slot)
    rows_dev = cache.shape[0]
    heads, latent_width, value_width = value_up.shape
    out = attend(latents, cache_length, queries, new_latent, latent_width)

    out = out.reshape(rows_dev, STEPS, N_TP, heads, latent_width)
    out = out.transpose(2, 0, 1, 3, 4)
    by_head = exchange(out, TP).reshape(-1, heads, latent_width)
    value_heads = jnp.einsum(
        "thl,hlv->thv", by_head, value_up, preferred_element_type=f32
    ).astype(bf16)
    value_heads = value_heads.reshape(value_heads.shape[0], heads * value_width)

    gathered = spread(value_heads, DP, N_DP)
    chunk = gathered.shape[1] // 2
    gathered = gathered.reshape(N_DP, 2, chunk, gathered.shape[2])
    first = core == 0
    own_rows = jnp.where(first, gathered[:, 0], gathered[:, 1]).reshape(N_DP * chunk, -1)
    other_rows = jnp.where(first, gathered[:, 1], gathered[:, 0]).reshape(N_DP * chunk, -1)

    def sum_tp(own, other, weight):
        away = jnp.dot(other, weight, preferred_element_type=f32).astype(bf16)
        near = lax.ppermute(away, "c", SWAP)
        total = jnp.dot(own, weight, preferred_element_type=f32) + near.astype(f32)
        parts = exchange(total.astype(bf16).reshape(N_ZY, chunk, -1), ZY)
        return jnp.sum(parts.astype(f32), axis=0)

    attended = sum_tp(own_rows, other_rows, out_proj)
    rows_out = residual.shape[1] // N_TP
    residue = lax.dynamic_slice_in_dim(residual, member * rows_out, rows_out, 1)
    residue = residue.transpose(1, 0, 2).reshape(chunk, -1)
    hidden = residue.astype(f32) + attended

    own_hidden = spread(hidden.astype(bf16), ZY, N_ZY).reshape(N_ZY * chunk, -1)
    other_hidden = lax.ppermute(own_hidden, "c", SWAP)

    def feed(part):
        wide = part.astype(f32)
        squares = jnp.sum(wide * wide, axis=1, keepdims=True)
        normed = (wide * norm_gain.astype(f32)).astype(bf16)
        gate = jnp.dot(normed, gate_weight, preferred_element_type=f32).astype(bf16)
        up = jnp.dot(normed, up_weight, preferred_element_type=f32).astype(bf16)
        high = squares.astype(bf16)
        low = (squares - high.astype(f32)).astype(bf16)
        lane = jnp.arange(128)[None, :]
        extra = jnp.where(lane == 0, high, jnp.where(lane == 1, low, jnp.zeros_like(low)))
        sent = jnp.concatenate([gate, up, extra], axis=1)
        units = gate.shape[1]
        parts = exchange(sent.reshape(N_DP, chunk, -1), DP)
        total = jnp.sum(parts.astype(f32), axis=0)
        square_sum = total[:, 2 * units] + total[:, 2 * units + 1]
        inverse = lax.rsqrt(square_sum / D + norm_eps)[:, None]
        active = jax.nn.silu(total[:, :units] * inverse) * (total[:, units : 2 * units] * inverse)
        return spread(active.astype(bf16), DP, N_DP).reshape(N_DP * chunk, units)

    own_active = feed(own_hidden)
    other_active = feed(other_hidden)
    ffn_out = sum_tp(own_active, other_active, down_weight)
    result = (hidden + ffn_out).astype(bf16)
    return result.reshape(rows_out, STEPS, -1).transpose(1, 0, 2)


def solution(mesh):
    split = Mesh(mesh.devices.reshape(4, 2, 2, 4, 2), ("x", "zl", "zh", "y", "c"))
    in_specs = (
        P(DP + TP, None, None),
        P(DP + TP),
        P(DP, None),
        P(DP, None),
        P(None, DP + TP, None, None),
        P(None, DP + TP, None),
        P(TP, None, None),
        P(TP, DP),
        P(None, None, DP),
        P(DP),
        P(DP, TP),
        P(DP, TP),
        P(TP, DP),
    )
    out_specs = P(None, TP, DP)
    return jax.shard_map(local, mesh=split, in_specs=in_specs, out_specs=out_specs, check_vma=False)
```

time: 902 us -> 320 us (0.35)
  waiting for transfers between devices: 759 us -> 169 us
  starting transfers between devices: 0.47 us -> 49.2 us
  matrix products: 42.5 us -> 26.4 us
  between operations: 15.6 us -> 2.26 us
  blocking collectives: 48.5 us -> 38.1 us
    psum x2 -> x0, waiting for transfers between devices: 519 us -> none  [the longest x1 367 us: local(): gate_sum, up_sum, square_sum = lax.psum((gate_part, up_part, squares), 'dp')]
    all_to_all x0 -> x9, waiting for transfers between devices: none -> 165 us  [exchange(): return lax.all_to_all(blocks, axes, 0, 0, tiled=True)]
    reduce_scatter x2 -> x0, waiting for transfers between devices: 137 us -> none  [local(): ffn_out = lax.psum_scatter(down_part, 'tp', scatter_dimension=0, tiled=True)]
    all_gather x3 -> x0, waiting for transfers between devices: 103 us -> none  [the longest x1 59.2 us: local(): shard_rows = lax.all_gather(outgoing, 'tp', axis=0, tiled=True)]
    all_to_all x0 -> x9, starting transfers between devices: none -> 43.7 us  [exchange(): return lax.all_to_all(blocks, axes, 0, 0, tiled=True)]
    dot_general x14 -> x12, matrix products: 42.5 us -> 26.4 us  [the longest x2 6.57 us: sum_tp(): total = jnp.dot(own, weight, preferred_element_type=f32) + near.astype(f32)]
    psum x1 -> x0, blocking collectives: 15.4 us -> none  [local(): gate_sum, up_sum, square_sum = lax.psum((gate_part, up_part, squares), 'dp')]
  transfers between devices with their start and end apart: 7 -> 12, of which waited for: 7 -> 11; matrix products, arithmetic and copies ran while one was open for 3% -> 5% of each run, Pallas kernels for 0% -> 0%
where the time goes in v1:
time: 320 us; the launch traced here: 319 us
  waiting for transfers between devices  169 us (53%)
  starting transfers between devices  49.2 us (15%)
  blocking collectives  38.1 us (12%)
  matrix products  26.4 us (8%)
  other arithmetic  19.2 us (6%)
  local copies, waits for them, and re-layouts  14.3 us (4%)
    all_to_all x9, waiting for transfers between devices, exchange(): return lax.all_to_all(blocks, axes, 0, 0, tiled=True)  165 us
    all_to_all x9, starting transfers between devices, exchange(): return lax.all_to_all(blocks, axes, 0, 0, tiled=True)  43.7 us
    all_to_all x2, blocking collectives, exchange(): return lax.all_to_all(blocks, axes, 0, 0, tiled=True)  38.1 us
    dot_general x2, matrix products, sum_tp(): total = jnp.dot(own, weight, preferred_element_type=f32) + near.astype(f32)  6.57 us
  transfers between devices with their start and end apart: 12, of which 11 were waited for; matrix products, arithmetic and copies ran while one was open for 5% of the time, Pallas kernels for 0%

profile of v1, /device:TPU:1, one launch (start us, length us, event | category | flops | bytes accessed | tf_op | source)
XLA Modules:
  0.0 319.0 jit_solution(2334518904492893129)
XLA Ops:
  0.0 1.4 fusion.31
  2.8 1.7 copy.67
  5.9 9.3 %all-to-all-start = ((bf16[16,16,576]{2,1,0:T(8,128)(2,1)}), bf16[16,16,576]{2,1,0:T(8,128)(2,1)}, u32[]{:S(2)}, u32[]{:S(2)}) async-start(bf16[16,16,576]{2,1,0:T(8,128)(2,1)} %bitcast.76), calls=%async_computation | async-start | bytes 655360 | tf_op jit(solution)/shard_map/all_to_all | solution.py:23
  15.4 9.1 %all-to-all-done = bf16[16,16,576]{2,1,0:T(8,128)(2,1)} async-done(((bf16[16,16,576]{2,1,0:T(8,128)(2,1)}), bf16[16,16,576]{2,1,0:T(8,128)(2,1)}, u32[]{:S(2)}, u32[]{:S(2)}) %all-to-all-start) | async-done | bytes 294944 | tf_op jit(solution)/shard_map/all_to_all | solution.py:23
  24.4 1.2 convolution_convert_fusion.7
  26.4 5.0 %all-to-all-start.1 = ((bf16[16,16,576]{2,1,0:T(8,128)(2,1)}), bf16[16,16,576]{2,1,0:T(8,128)(2,1)}, u32[]{:S(2)}, u32[]{:S(2)}) async-start(bf16[16,16,576]{2,1,0:T(8,128)(2,1)} %copy.66), calls=%async_computation.1 | async-start | bytes 655360 | tf_op jit(solution)/shard_map/all_to_all | solution.py:23
  31.5 9.2 %all-to-all-done.1 = bf16[16,16,576]{2,1,0:T(8,128)(2,1)} async-done(((bf16[16,16,576]{2,1,0:T(8,128)(2,1)}), bf16[16,16,576]{2,1,0:T(8,128)(2,1)}, u32[]{:S(2)}, u32[]{:S(2)}) %all-to-all-start.1) | async-done | bytes 294944 | tf_op jit(solution)/shard_map/all_to_all | solution.py:23
  43.7 2.8 fusion.5
  46.4 1.5 copy.95
  47.9 20.5 %all_to_all.55 = bf16[16,4,2,8,512]{4,3,2,1,0:T(8,128)(2,1)S(1)} all-to-all(bf16[16,4,2,8,512]{4,3,2,1,0:T(8,128)(2,1)S(1)} %bitcast.71), channel_id=1, replica_groups=mesh['x'=4,'zl'=2,'zh'=2,'y'=4,'c'=2] {'zh','y','c'}, dimensions={0} | all-to-all | bytes 2097152 | tf_op jit(solution)/shard_map/all_to_all | solution.py:23
  69.5 1.6 broadcast_in_dim.164
  71.1 4.5 %all-to-all-start.3 = ((bf16[8,128,1024]{2,1,0:T(8,128)(2,1)}), bf16[8,128,1024]{2,1,0:T(8,128)(2,1)}, u32[]{:S(2)}, u32[]{:S(2)}) async-start(bf16[8,128,1024]{2,1,0:T(8,128)(2,1)} %broadcast_in_dim.164), calls=%async_computation.3 | async-start | bytes 4194304 | tf_op jit(solution)/shard_map/all_to_all | solution.py:23
  75.5 30.1 %all-to-all-done.3 = bf16[8,128,1024]{2,1,0:T(8,128)(2,1)} async-done(((bf16[8,128,1024]{2,1,0:T(8,128)(2,1)}), bf16[8,128,1024]{2,1,0:T(8,128)(2,1)}, u32[]{:S(2)}, u32[]{:S(2)}) %all-to-all-start.3) | async-done | bytes 2097184 | tf_op jit(solution)/shard_map/all_to_all | solution.py:23
  105.6 1.8 broadcast_select_fusion
  107.7 1.3 convolution_convert_fusion.6
  109.0 1.9 collective-permute-start
  110.9 2.1 collective-permute-done
  113.0 2.2 add_convert_fusion.1
  115.2 4.0 %all-to-all-start.4 = ((bf16[8,64,896]{2,1,0:T(8,128)(2,1)}), bf16[8,64,896]{2,1,0:T(8,128)(2,1)S(1)}, u32[]{:S(2)}, u32[]{:S(2)}) async-start(bf16[8,64,896]{2,1,0:T(8,128)(2,1)} %bitcast.80), calls=%async_computation.4 | async-start | bytes 1835008 | tf_op jit(solution)/shard_map/all_to_all | solution.py:23
  121.2 14.0 %all-to-all-done.4 = bf16[8,64,896]{2,1,0:T(8,128)(2,1)S(1)} async-done(((bf16[8,64,896]{2,1,0:T(8,128)(2,1)}), bf16[8,64,896]{2,1,0:T(8,128)(2,1)S(1)}, u32[]{:S(2)}, u32[]{:S(2)}) %all-to-all-start.4) | async-done | bytes 917536 | tf_op jit(solution)/shard_map/all_to_all | solution.py:23
  136.4 17.6 %all_to_all.56 = bf16[8,64,896]{2,1,0:T(8,128)(2,1)S(1)} all-to-all(bf16[8,64,896]{2,1,0:T(8,128)(2,1)S(1)} %broadcast_in_dim.165), channel_id=1, replica_groups=mesh['x'=4,'zl'=2,'zh'=2,'y'=4,'c'=2] {'zh','y'}, dimensions={0} | all-to-all | bytes 1835008 | tf_op jit(solution)/shard_map/all_to_all | solution.py:23
  154.0 1.6 collective-permute-start.1
  155.9 1.9 collective-permute-done.1
  157.8 1.4 fusion.2
  160.2 2.8 convolution_convert_fusion
  163.1 2.7 convolution_convert_fusion.1
  165.8 1.6 pad_maximum_fusion.1
  167.4 4.6 %all-to-all-start.8 = ((bf16[8,64,2432]{2,1,0:T(8,128)(2,1)}), bf16[8,64,2432]{2,1,0:T(8,128)(2,1)}, u32[]{:S(2)}, u32[]{:S(2)}) async-start(bf16[8,64,2432]{2,1,0:T(8,128)(2,1)} %bitcast.70), calls=%async_computation.8 | async-start | bytes 4980736 | tf_op jit(solution)/shard_map/all_to_all | solution.py:23
  172.0 1.5 convolution_convert_fusion.2
  173.6 1.5 convolution_convert_fusion.3
  175.1 1.7 pad_maximum_fusion
  176.8 31.7 %all-to-all-done.8 = bf16[8,64,2432]{2,1,0:T(8,128)(2,1)} async-done(((bf16[8,64,2432]{2,1,0:T(8,128)(2,1)}), bf16[8,64,2432]{2,1,0:T(8,128)(2,1)}, u32[]{:S(2)}, u32[]{:S(2)}) %all-to-all-start.8) | async-done | bytes 2490400 | tf_op jit(solution)/shard_map/all_to_all | solution.py:23
  208.5 4.4 %all-to-all-start.6 = ((bf16[8,64,2432]{2,1,0:T(8,128)(2,1)}), bf16[8,64,2432]{2,1,0:T(8,128)(2,1)}, u32[]{:S(2)}, u32[]{:S(2)}) async-start(bf16[8,64,2432]{2,1,0:T(8,128)(2,1)} %bitcast.69), calls=%async_computation.6 | async-start | bytes 4980736 | tf_op jit(solution)/shard_map/all_to_all | solution.py:23
  212.8 2.1 convert_reduce_fusion
  215.3 33.3 %all-to-all-done.6 = bf16[8,64,2432]{2,1,0:T(8,128)(2,1)} async-done(((bf16[8,64,2432]{2,1,0:T(8,128)(2,1)}), bf16[8,64,2432]{2,1,0:T(8,128)(2,1)}, u32[]{:S(2)}, u32[]{:S(2)}) %all-to-all-start.6) | async-done | bytes 2490400 | tf_op jit(solution)/shard_map/all_to_all | solution.py:23
  248.6 1.2 broadcast_in_dim.174
  249.8 4.2 %all-to-all-start.9 = ((bf16[8,64,1152]{2,1,0:T(8,128)(2,1)}), bf16[8,64,1152]{2,1,0:T(8,128)(2,1)}, u32[]{:S(2)}, u32[]{:S(2)}) async-start(bf16[8,64,1152]{2,1,0:T(8,128)(2,1)} %broadcast_in_dim.174), calls=%async_computation.9 | async-start | bytes 2359296 | tf_op jit(solution)/shard_map/all_to_all | solution.py:23
  254.1 2.1 convert_reduce_fusion.1
  256.5 13.6 %all-to-all-done.9 = bf16[8,64,1152]{2,1,0:T(8,128)(2,1)} async-done(((bf16[8,64,1152]{2,1,0:T(8,128)(2,1)}), bf16[8,64,1152]{2,1,0:T(8,128)(2,1)}, u32[]{:S(2)}, u32[]{:S(2)}) %all-to-all-start.9) | async-done | bytes 1179680 | tf_op jit(solution)/shard_map/all_to_all | solution.py:23
  270.1 1.2 broadcast_in_dim.171
  271.3 4.2 %all-to-all-start.7 = ((bf16[8,64,1152]{2,1,0:T(8,128)(2,1)}), bf16[8,64,1152]{2,1,0:T(8,128)(2,1)}, u32[]{:S(2)}, u32[]{:S(2)}) async-start(bf16[8,64,1152]{2,1,0:T(8,128)(2,1)} %broadcast_in_dim.171), calls=%async_computation.7 | async-start | bytes 2359296 | tf_op jit(solution)/shard_map/all_to_all | solution.py:23
  275.6 4.3 %convolution_convert_fusion.5 = bf16[512,896]{1,0:T(8,128)(2,1)} fusion(bf16[512,1152]{1,0:T(8,128)(2,1)} %bitcast.25, bf16[1152,896]{1,0:T(8,128)(2,1)} %param.25), kind=kOutput, calls=%fused_computation.21 | convolution fusion | flops 1057423360 | bytes 4161536 | tf_op jit(solution)/shard_map/dot_general | solution.py:104
  279.9 2.0 collective-permute-start.2
  281.9 9.5 %all-to-all-done.7 = bf16[8,64,1152]{2,1,0:T(8,128)(2,1)} async-done(((bf16[8,64,1152]{2,1,0:T(8,128)(2,1)}), bf16[8,64,1152]{2,1,0:T(8,128)(2,1)}, u32[]{:S(2)}, u32[]{:S(2)}) %all-to-all-start.7) | async-done | bytes 1179680 | tf_op jit(solution)/shard_map/all_to_all | solution.py:23
  291.4 4.4 %add_convert_fusion = bf16[512,896]{1,0:T(8,128)(2,1)} fusion(bf16[512,896]{1,0:T(8,128)(2,1)S(1)} %collective-permute-done.2, bf16[512,1152]{1,0:T(8,128)(2,1)} %bitcast.23, bf16[1152,896]{1,0:T(8,128)(2,1)} %param.25), kind=kOutput, calls=%fused_computation.14 | convolution fusion | flops 1058340864 | bytes 5079040 | tf_op jit(solution)/shard_map/dot_general | solution.py:106
  295.8 3.6 %all-to-all-start.10 = ((bf16[8,64,896]{2,1,0:T(8,128)(2,1)}), bf16[8,64,896]{2,1,0:T(8,128)(2,1)S(1)}, u32[]{:S(2)}, u32[]{:S(2)}) async-start(bf16[8,64,896]{2,1,0:T(8,128)(2,1)} %bitcast.81), calls=%async_computation.10 | async-start | bytes 1835008 | tf_op jit(solution)/shard_map/all_to_all | solution.py:23
  300.2 15.0 %all-to-all-done.10 = bf16[8,64,896]{2,1,0:T(8,128)(2,1)S(1)} async-done(((bf16[8,64,896]{2,1,0:T(8,128)(2,1)}), bf16[8,64,896]{2,1,0:T(8,128)(2,1)S(1)}, u32[]{:S(2)}, u32[]{:S(2)}) %all-to-all-start.10) | async-done | bytes 917536 | tf_op jit(solution)/shard_map/all_to_all | solution.py:23
  317.1 1.2 fusion.19
  (59 shorter events, 14.7 us)
Async XLA Ops:
  0.0 160.2 %copy-start = (bf16[896,1152]{1,0:T(8,128)(2,1)S(1)}, bf16[896,1152]{1,0:T(8,128)(2,1)}, u32[]{:S(2)}) copy-start(bf16[896,1152]{1,0:T(8,128)(2,1)} %param.24) | copy-start | bytes 6193156
  2.7 12.5 %copy-start.6 = (s32[4]{0:T(128)S(1)}, s32[4]{0:T(128)}, u32[]{:S(2)}) copy-start(s32[4]{0:T(128)} %param.14) | copy-start | bytes 52
  2.8 21.7 %copy-start.7 = (s32[1,16]{1,0:T(1,128)S(1)}, s32[1,16]{1,0:T(1,128)}, u32[]{:S(2)}) copy-start(s32[1,16]{1,0:T(1,128)} %param.16) | copy-start | bytes 196
  4.5 27.0 %copy-start.4 = (bf16[2,4,576]{2,1,0:T(4,128)(2,1)S(1)}, bf16[2,4,576]{2,1,0:T(4,128)(2,1)}, u32[]{:S(2)}) copy-start(bf16[2,4,576]{2,1,0:T(4,128)(2,1)} %param.18) | copy-start | bytes 27652
  5.9 18.5 %all-to-all-start = ((bf16[16,16,576]{2,1,0:T(8,128)(2,1)}), bf16[16,16,576]{2,1,0:T(8,128)(2,1)}, u32[]{:S(2)}, u32[]{:S(2)}) async-start(bf16[16,16,576]{2,1,0:T(8,128)(2,1)} %bitcast.76), calls=%async_computation | async-start | bytes 655360 | tf_op jit(solution)/shard_map/all_to_all | solution.py:23
  26.4 14.3 %all-to-all-start.1 = ((bf16[16,16,576]{2,1,0:T(8,128)(2,1)}), bf16[16,16,576]{2,1,0:T(8,128)(2,1)}, u32[]{:S(2)}, u32[]{:S(2)}) async-start(bf16[16,16,576]{2,1,0:T(8,128)(2,1)} %copy.66), calls=%async_computation.1 | async-start | bytes 655360 | tf_op jit(solution)/shard_map/all_to_all | solution.py:23
  40.7 1.6 copy-start.11
  42.3 1.1 copy-start.1
  46.4 22.0 %copy-start.2 = (bf16[8,512,128]{2,1,0:T(8,128)(2,1)S(1)}, bf16[8,512,128]{2,1,0:T(8,128)(2,1)}, u32[]{:S(2)}) copy-start(bf16[8,512,128]{2,1,0:T(8,128)(2,1)} %param.19) | copy-start | bytes 3145732
  71.1 34.5 %all-to-all-start.3 = ((bf16[8,128,1024]{2,1,0:T(8,128)(2,1)}), bf16[8,128,1024]{2,1,0:T(8,128)(2,1)}, u32[]{:S(2)}, u32[]{:S(2)}) async-start(bf16[8,128,1024]{2,1,0:T(8,128)(2,1)} %broadcast_in_dim.164), calls=%async_computation.3 | async-start | bytes 4194304 | tf_op jit(solution)/shard_map/all_to_all | solution.py:23
  105.6 2.1 copy-start.10
  109.0 4.0 %collective-permute-start = (bf16[512,896]{1,0:T(8,128)(2,1)S(1)}, bf16[512,896]{1,0:T(8,128)(2,1)S(1)}, u32[]{:S(2)}, u32[]{:S(2)}) collective-permute-start(bf16[512,896]{1,0:T(8,128)(2,1)S(1)} %convolution_convert_fusion.6), channel_id=1, source_target_pairs={{0,1},{1,0},{2,3},{3,2},{4,5},{5,4},{6,7},{7,6},{8,9},{9,8},{10,11... | collective-permute-start | bytes 2752520 | tf_op jit(solution)/shard_map/ppermute | solution.py:105
  115.2 20.0 %all-to-all-start.4 = ((bf16[8,64,896]{2,1,0:T(8,128)(2,1)}), bf16[8,64,896]{2,1,0:T(8,128)(2,1)S(1)}, u32[]{:S(2)}, u32[]{:S(2)}) async-start(bf16[8,64,896]{2,1,0:T(8,128)(2,1)} %bitcast.80), calls=%async_computation.4 | async-start | bytes 1835008 | tf_op jit(solution)/shard_map/all_to_all | solution.py:23
  135.3 20.3 %copy-start.5 = (bf16[896]{0:T(1024)(128)(2,1)S(1)}, bf16[896]{0:T(1024)(128)(2,1)}, u32[]{:S(2)}) copy-start(bf16[896]{0:T(1024)(128)(2,1)} %param.22) | copy-start | bytes 5380
  154.0 3.8 %collective-permute-start.1 = (bf16[512,896]{1,0:T(8,128)(2,1)S(1)}, bf16[512,896]{1,0:T(8,128)(2,1)}, u32[]{:S(2)}, u32[]{:S(2)}) collective-permute-start(bf16[512,896]{1,0:T(8,128)(2,1)S(1)} %bitcast.73), channel_id=1, source_target_pairs={{0,1},{1,0},{2,3},{3,2},{4,5},{5,4},{6,7},{7,6},{8,9},{9,8},{10,11... | collective-permute-start | bytes 2752520 | tf_op jit(solution)/shard_map/ppermute | solution.py:117
  160.2 2.8 copy-start.8
  167.4 41.0 %all-to-all-start.8 = ((bf16[8,64,2432]{2,1,0:T(8,128)(2,1)}), bf16[8,64,2432]{2,1,0:T(8,128)(2,1)}, u32[]{:S(2)}, u32[]{:S(2)}) async-start(bf16[8,64,2432]{2,1,0:T(8,128)(2,1)} %bitcast.70), calls=%async_computation.8 | async-start | bytes 4980736 | tf_op jit(solution)/shard_map/all_to_all | solution.py:23
  172.0 1.6 copy-start.9
  173.6 1.5 copy-start.3
  208.5 40.2 %all-to-all-start.6 = ((bf16[8,64,2432]{2,1,0:T(8,128)(2,1)}), bf16[8,64,2432]{2,1,0:T(8,128)(2,1)}, u32[]{:S(2)}, u32[]{:S(2)}) async-start(bf16[8,64,2432]{2,1,0:T(8,128)(2,1)} %bitcast.69), calls=%async_computation.6 | async-start | bytes 4980736 | tf_op jit(solution)/shard_map/all_to_all | solution.py:23
  249.8 20.3 %all-to-all-start.9 = ((bf16[8,64,1152]{2,1,0:T(8,128)(2,1)}), bf16[8,64,1152]{2,1,0:T(8,128)(2,1)}, u32[]{:S(2)}, u32[]{:S(2)}) async-start(bf16[8,64,1152]{2,1,0:T(8,128)(2,1)} %broadcast_in_dim.174), calls=%async_computation.9 | async-start | bytes 2359296 | tf_op jit(solution)/shard_map/all_to_all | solution.py:23
  271.3 20.1 %all-to-all-start.7 = ((bf16[8,64,1152]{2,1,0:T(8,128)(2,1)}), bf16[8,64,1152]{2,1,0:T(8,128)(2,1)}, u32[]{:S(2)}, u32[]{:S(2)}) async-start(bf16[8,64,1152]{2,1,0:T(8,128)(2,1)} %broadcast_in_dim.171), calls=%async_computation.7 | async-start | bytes 2359296 | tf_op jit(solution)/shard_map/all_to_all | solution.py:23
  279.9 11.5 %collective-permute-start.2 = (bf16[512,896]{1,0:T(8,128)(2,1)}, bf16[512,896]{1,0:T(8,128)(2,1)S(1)}, u32[]{:S(2)}, u32[]{:S(2)}) collective-permute-start(bf16[512,896]{1,0:T(8,128)(2,1)} %convolution_convert_fusion.5), channel_id=1, source_target_pairs={{0,1},{1,0},{2,3},{3,2},{4,5},{5,4},{6,7},{7,6},{8,9},{9,8},{10,11... | collective-permute-start | bytes 2752520 | tf_op jit(solution)/shard_map/ppermute | solution.py:105
  295.8 19.4 %all-to-all-start.10 = ((bf16[8,64,896]{2,1,0:T(8,128)(2,1)}), bf16[8,64,896]{2,1,0:T(8,128)(2,1)S(1)}, u32[]{:S(2)}, u32[]{:S(2)}) async-start(bf16[8,64,896]{2,1,0:T(8,128)(2,1)} %bitcast.81), calls=%async_computation.10 | async-start | bytes 1835008 | tf_op jit(solution)/shard_map/all_to_all | solution.py:23

commit v2 on v1

v2 whole, which is shorter than its diff:
```python
import jax
import jax.numpy as jnp
from jax import lax
from jax.experimental import pallas as pl
from jax.experimental.pallas import tpu as pltpu
from jax.sharding import Mesh, PartitionSpec as P

D = 7168
QKD = 192
norm_eps = 1e-06

DP = ("xh", "xl", "zl")
TP = ("zh", "y", "c")
ZY = ("zh", "y")
FOUR = ("xh", "zl")
PAIR = ("xl",) + ZY
N_DP = 8
N_TP = 16
N_ZY = 8
N_FOUR = 4
SWAP = [(0, 1), (1, 0)]
FIRST_ROWS = 384
bf16 = jnp.bfloat16
f32 = jnp.float32
VMEM = 48 * 1024 * 1024


def exchange(blocks, axes):
    return lax.all_to_all(blocks, axes, 0, 0, tiled=True)


def spread(block, axes, copies):
    return exchange(jnp.broadcast_to(block[None], (copies,) + block.shape), axes)


def swap(block, axis):
    return lax.ppermute(block, axis, SWAP)


def params():
    return pltpu.CompilerParams(vmem_limit_bytes=VMEM)


def whole(shape):
    return pl.BlockSpec(shape, lambda *_: (0,) * len(shape))


def leave(ids, cache_t):
    _, entries, length = cache_t.shape
    piece = entries // N_TP

    def body(ids_ref, row_ref, out_ref):
        row = row_ref[0].astype(f32)
        for j in range(N_TP):
            out_ref[j] = row[j * piece : (j + 1) * piece].astype(bf16)

    return pl.pallas_call(
        body,
        grid_spec=pltpu.PrefetchScalarGridSpec(
            num_scalar_prefetch=1,
            grid=(1,),
            in_specs=[pl.BlockSpec((1, entries, length), lambda i, ids: (ids[0], 0, 0))],
            out_specs=whole((N_TP, piece, length)),
        ),
        out_shape=jax.ShapeDtypeStruct((N_TP, piece, length), bf16),
        compiler_params=params(),
        name="leave",
    )(ids, cache_t)


def route(peer, pieces):
    def body(peer_ref, in_ref, out_ref):
        for i in range(N_TP):
            out_ref[peer_ref[i]] = in_ref[i]

    return pl.pallas_call(
        body,
        grid_spec=pltpu.PrefetchScalarGridSpec(
            num_scalar_prefetch=1,
            grid=(1,),
            in_specs=[whole(pieces.shape)],
            out_specs=whole(pieces.shape),
        ),
        out_shape=jax.ShapeDtypeStruct(pieces.shape, bf16),
        compiler_params=params(),
        name="route",
    )(peer, pieces)


def attend(ids, lengths, cache_t, arrived, fresh_t, queries_t, heads, latent_width):
    rows, entries, length = cache_t.shape
    steps, _, _, all_heads = queries_t.shape
    parts = all_heads // heads

    def body(ids_ref, lengths_ref, cache_ref, arrived_ref, fresh_ref, q_ref, out_ref):
        r = pl.program_id(0)
        here = r == ids_ref[0]
        came = jnp.concatenate([arrived_ref[j].astype(f32) for j in range(N_TP)], axis=0)
        latents = jnp.where(here, came, cache_ref[0].astype(f32))
        current = lengths_ref[r]
        position = lax.broadcasted_iota(jnp.int32, (entries, length), 1)
        for s in range(steps):
            token = fresh_ref[0, :, s : s + 1].astype(f32)
            latents = jnp.where(position == current + s, token, latents)
        latents = latents.astype(bf16)
        place = lax.broadcasted_iota(jnp.int32, (all_heads, length), 1)
        outs = []
        for s in range(steps):
            scores = lax.dot_general(
                q_ref[s, 0], latents, (((0,), (0,)), ((), ())), preferred_element_type=f32
            )
            scores = jnp.where(place <= current + s, scores * QKD ** (-0.5), -jnp.inf)
            expo = jnp.exp(scores - jnp.max(scores, axis=-1, keepdims=True))
            probs = (expo / jnp.sum(expo, axis=-1, keepdims=True)).astype(bf16)
            out = lax.dot_general(
                probs, latents[:latent_width], (((1,), (1,)), ((), ())), preferred_element_type=f32
            )
            outs.append(out.reshape(parts, heads, latent_width))
        out_ref[:, 0] = jnp.concatenate(outs, axis=1).astype(bf16)

    return pl.pallas_call(
        body,
        grid_spec=pltpu.PrefetchScalarGridSpec(
            num_scalar_prefetch=2,
            grid=(rows,),
            in_specs=[
                pl.BlockSpec((1, entries, length), lambda r, *_: (r, 0, 0)),
                whole(arrived.shape),
                pl.BlockSpec((1, entries, steps), lambda r, *_: (r, 0, 0)),
                pl.BlockSpec((steps, 1, entries, all_heads), lambda r, *_: (0, r, 0, 0)),
            ],
            out_specs=pl.BlockSpec(
                (parts, 1, steps * heads, latent_width), lambda r, *_: (0, r, 0, 0)
            ),
        ),
        out_shape=jax.ShapeDtypeStruct((parts, rows, steps * heads, latent_width), bf16),
        compiler_params=params(),
        name="attend",
    )(ids, lengths, cache_t, arrived, fresh_t, queries_t)


def project(ids, half, rows, weights, near=None):
    groups, _, count, depth = rows.shape
    width = weights[0].shape[1]
    blocks = len(weights)
    per = groups // 2

    def body(ids_ref, rows_ref, *refs):
        out_ref = refs[-1]
        lhs = rows_ref[...].reshape(per * count, depth)
        for k in range(blocks):
            at = lax.rem(ids_ref[2] + k, blocks)
            total = jnp.dot(lhs, refs[k][...], preferred_element_type=f32)
            if near is not None:
                total = total + refs[blocks][at].astype(f32)
            out_ref[at] = total.astype(bf16)

    block = pl.BlockSpec((blocks, per * count, width), lambda i, ids: (0, i, 0))
    extra = [] if near is None else [near]
    return pl.pallas_call(
        body,
        grid_spec=pltpu.PrefetchScalarGridSpec(
            num_scalar_prefetch=1,
            grid=(2,),
            in_specs=[pl.BlockSpec((per, 1, count, depth), lambda i, ids: (i, half(ids), 0, 0))]
            + [whole(w.shape) for w in weights]
            + [block for _ in extra],
            out_specs=block,
        ),
        out_shape=jax.ShapeDtypeStruct((blocks, groups * count, width), bf16),
        compiler_params=params(),
        name="project",
    )(ids, rows, *weights, *extra)


def widen(ids, own, other, kept, came):
    _, _, chunk, features = own.shape
    columns = kept.shape[1]
    per = 2 * chunk

    def body(ids_ref, own_ref, other_ref, kept_ref, first_ref, second_ref, out_ref):
        pair = ids_ref[2]

        def pick(at):
            return jnp.concatenate(
                [ref[at].reshape(per, features) for ref in (own_ref, other_ref)], axis=0
            )

        mine, near = pick(pair), pick(1 - pair)
        total = jnp.dot(mine, kept_ref[...], preferred_element_type=f32)
        total += jnp.dot(near[:, :FIRST_ROWS], first_ref[...], preferred_element_type=f32)
        total += jnp.dot(near[:, FIRST_ROWS:], second_ref[...], preferred_element_type=f32)
        out_ref[0, :, :columns] = total.astype(bf16)
        squares = jnp.zeros((2 * per, 1), f32)
        for rows in (mine, near):
            wide = rows.astype(f32)
            squares += jnp.sum(wide * wide, axis=1, keepdims=True)
        high = squares.astype(bf16).astype(f32)
        lane = lax.broadcasted_iota(jnp.int32, (2 * per, 128), 1)
        extra = jnp.where(lane == 0, high, jnp.where(lane == 1, squares - high, 0.0))
        out_ref[0, :, columns:] = extra.astype(bf16)

    rows = pl.BlockSpec((2, 2, chunk, features), lambda q, ids: (0, q, 0, 0))
    return pl.pallas_call(
        body,
        grid_spec=pltpu.PrefetchScalarGridSpec(
            num_scalar_prefetch=1,
            grid=(N_FOUR,),
            in_specs=[rows, rows] + [whole(w.shape) for w in (kept,) + came],
            out_specs=pl.BlockSpec((1, 2 * per, columns + 128), lambda q, ids: (q, 0, 0)),
        ),
        out_shape=jax.ShapeDtypeStruct((N_FOUR, 2 * per, columns + 128), bf16),
        compiler_params=params(),
        name="widen",
    )(ids, own, other, kept, *came)


def local(
    cache,
    cache_length,
    move_slot,
    move_peer,
    queries,
    new_latent,
    value_up,
    out_proj,
    residual,
    norm_gain,
    gate_weight,
    up_weight,
    down_weight,
):
    member = lax.axis_index(TP)
    core = lax.axis_index("c")
    pair = lax.axis_index("xl")
    rows_dev = cache.shape[0]
    steps = new_latent.shape[0]
    heads, latent_width, value_width = value_up.shape
    rows_out = residual.shape[1] // N_TP
    chunk = rows_out * steps
    features, units = gate_weight.shape
    part = units // 2

    lanes = jnp.arange(N_TP, dtype=jnp.int32)
    own_slot = jnp.sum(jnp.where(lanes == member, move_slot[0], 0))
    ids = jnp.stack([own_slot, core, pair]).astype(jnp.int32)
    cache_t = cache.transpose(0, 2, 1)
    pieces = exchange(leave(ids, cache_t), TP)

    gain = norm_gain.astype(f32)[:, None]

    def columns(index, low, high):
        return jnp.concatenate(
            [
                lax.dynamic_slice(w, (low, index * part), (high - low, part)).astype(f32)
                * gain[low:high]
                for w in (gate_weight, up_weight)
            ],
            axis=1,
        ).astype(bf16)

    came = (
        swap(columns(1 - pair, 0, FIRST_ROWS), "xl"),
        swap(columns(1 - pair, FIRST_ROWS, features), "xl"),
    )
    kept = columns(pair, 0, features)

    arrived = exchange(route(move_peer[0], pieces), TP)
    out = attend(
        ids,
        cache_length,
        cache_t,
        arrived,
        new_latent.transpose(1, 2, 0),
        queries.transpose(0, 1, 3, 2),
        heads,
        latent_width,
    )
    by_head = exchange(out, TP).reshape(-1, heads, latent_width)
    by_head, kept, came = lax.optimization_barrier((by_head, kept, came))
    value_heads = jnp.einsum(
        "thl,hlv->thv", by_head, value_up, preferred_element_type=f32
    ).astype(bf16)
    value_heads = value_heads.reshape(-1, heads * value_width)

    gathered = spread(value_heads, DP, N_DP).reshape(N_DP, 2, chunk, -1)
    gathered, down_weight = lax.optimization_barrier((gathered, down_weight))
    down_kept = lax.dynamic_slice_in_dim(down_weight, pair * part, part, 0)
    down_came = swap(lax.dynamic_slice_in_dim(down_weight, (1 - pair) * part, part, 0), "xl")
    away = swap(project(ids, lambda i: 1 - i[1], gathered, [out_proj]), "c")
    total = project(ids, lambda i: i[1], gathered, [out_proj], away)
    parts = exchange(total.reshape(N_ZY, chunk, -1), ZY)
    residue = lax.dynamic_slice_in_dim(residual, member * rows_out, rows_out, 1)
    residue = residue.transpose(1, 0, 2).reshape(chunk, -1)
    hidden = residue.astype(f32) + jnp.sum(parts.astype(f32), axis=0)

    own = spread(hidden.astype(bf16), PAIR, 2 * N_ZY).reshape(2, N_ZY, chunk, features)
    other = swap(own, "c")
    sums = exchange(widen(ids, own, other, kept, came), FOUR)
    sums = jnp.sum(sums.astype(f32), axis=0)
    squares = sums[:, units] + sums[:, units + 1]
    inverse = lax.rsqrt(squares / D + norm_eps)[:, None]
    active = jax.nn.silu(sums[:, :part] * inverse) * (sums[:, part:units] * inverse)
    active = spread(active.astype(bf16), FOUR, N_FOUR).reshape(N_FOUR, 2, 2 * chunk, part)

    weights = [down_kept, down_came]
    away = swap(project(ids, lambda i: 1, active, weights), "c")
    total = project(ids, lambda i: 0, active, weights, away)
    parts = exchange(total.reshape(2 * N_ZY, chunk, -1), PAIR)
    result = (hidden + jnp.sum(parts.astype(f32), axis=0)).astype(bf16)
    return result.reshape(rows_out, steps, -1).transpose(1, 0, 2)


def solution(mesh):
    split = Mesh(
        mesh.devices.reshape(2, 2, 2, 2, 4, 2), ("xh", "xl", "zl", "zh", "y", "c")
    )
    in_specs = (
        P(DP + TP, None, None),
        P(DP + TP),
        P(DP, None),
        P(DP, None),
        P(None, DP + TP, None, None),
        P(None, DP + TP, None),
        P(TP, None, None),
        P(TP, DP),
        P(None, None, DP),
        P(DP),
        P(DP, TP),
        P(DP, TP),
        P(TP, DP),
    )
    out_specs = P(None, TP, DP)
    return jax.shard_map(local, mesh=split, in_specs=in_specs, out_specs=out_specs, check_vma=False)
```

time: 320 us -> 309 us (0.966)
  waiting for transfers between devices: 169 us -> 109 us
  blocking collectives: 38.1 us -> 89.7 us
  Pallas kernels: 0 us -> 29.9 us
  matrix products: 26.4 us -> 0.96 us
  starting transfers between devices: 49.2 us -> 42.6 us
    all_to_all x9 -> x6, waiting for transfers between devices: 165 us -> 79.8 us  [exchange(): return lax.all_to_all(blocks, axes, 0, 0, tiled=True)]
    all_to_all x2 -> x3, blocking collectives: 38.1 us -> 89.7 us  [exchange(): return lax.all_to_all(blocks, axes, 0, 0, tiled=True)]
    pallas_call x0 -> x8, Pallas kernels: none -> 29.9 us  [the longest x4 13.1 us: project(): pl.pallas_call(body, grid_spec=pltpu.PrefetchScalarGridSpec(num_scalar_pr...]
    dot_general x11 -> x0, matrix products: 25.5 us -> none  [the longest x2 6.57 us: sum_tp(): total = jnp.dot(own, weight, preferred_element_type=f32) + near.astype(f32)]
    ppermute x3 -> x6, waiting for transfers between devices: 3.98 us -> 29.3 us  [swap(): return lax.ppermute(block, axis, SWAP)]
    all_to_all x9 -> x6, starting transfers between devices: 43.7 us -> 33.8 us  [exchange(): return lax.all_to_all(blocks, axes, 0, 0, tiled=True)]
    another operation x0 -> x4, other arithmetic: none -> 8.88 us
    unnamed x26 -> x38, local copies, waits for them, and re-layouts: 2.54 us -> 7.01 us
  transfers between devices with their start and end apart: 12 -> 12, of which waited for: 11 -> 9; matrix products, arithmetic and copies ran while one was open for 5% -> 7% of each run, Pallas kernels for 0% -> 2%
where the time goes in v2:
time: 309 us; the launch traced here: 307 us
  waiting for transfers between devices  109 us (35%)
  blocking collectives  89.7 us (29%)
  starting transfers between devices  42.6 us (14%)
  Pallas kernels  29.9 us (10%)
  other arithmetic  20 us (6%)
  local copies, waits for them, and re-layouts  15 us (5%)
    all_to_all x3, blocking collectives, exchange(): return lax.all_to_all(blocks, axes, 0, 0, tiled=True)  89.7 us
    all_to_all x6, waiting for transfers between devices, exchange(): return lax.all_to_all(blocks, axes, 0, 0, tiled=True)  79.8 us
    all_to_all x6, starting transfers between devices, exchange(): return lax.all_to_all(blocks, axes, 0, 0, tiled=True)  33.8 us
    ppermute x6, waiting for transfers between devices, swap(): return lax.ppermute(block, axis, SWAP)  29.3 us
    pallas_call x4, Pallas kernels, project(): pl.pallas_call(body, grid_spec=pltpu.PrefetchScalarGridSpec(num_scalar_pr...  13.1 us
    pallas_call x1, Pallas kernels, widen(): pl.pallas_call(body, grid_spec=pltpu.PrefetchScalarGridSpec(num_scalar_pr...  9.59 us
    ppermute x6, starting transfers between devices, swap(): return lax.ppermute(block, axis, SWAP)  8.74 us
    another operation x3, other arithmetic  8.24 us
  transfers between devices with their start and end apart: 12, of which 9 were waited for; matrix products, arithmetic and copies ran while one was open for 7% of the time, Pallas kernels for 2%

profile of v2, /device:TPU:1, one launch (start us, length us, event | category | flops | bytes accessed | tf_op | source)
XLA Modules:
  0.0 307.5 jit_solution(13126154733460687119)
XLA Ops:
  0.0 1.4 fusion.8
  2.0 1.3 copy-done.3
  3.3 1.3 leave.1
  4.6 9.4 %all-to-all-start = ((bf16[16,36,256]{2,1,0:T(8,128)(2,1)}), bf16[16,36,256]{2,1,0:T(8,128)(2,1)S(1)}, u32[]{:S(2)}, u32[]{:S(2)}) async-start(bf16[16,36,256]{2,1,0:T(8,128)(2,1)} %leave.1), calls=%async_computation | async-start | bytes 655360 | tf_op jit(solution)/shard_map/all_to_all | solution.py:29
  14.1 2.1 multiply_convert_fusion.3
  16.2 7.0 %all-to-all-done.in_ref = bf16[16,36,256]{2,1,0:T(8,128)(2,1)S(1)} async-done(((bf16[16,36,256]{2,1,0:T(8,128)(2,1)}), bf16[16,36,256]{2,1,0:T(8,128)(2,1)S(1)}, u32[]{:S(2)}, u32[]{:S(2)}) %all-to-all-start) | async-done | bytes 294944 | tf_op jit(solution)/shard_map/all_to_all | solution.py:29
  23.2 1.3 route.1
  24.5 4.3 %all-to-all-start.1 = ((bf16[16,36,256]{2,1,0:T(8,128)(2,1)}), bf16[16,36,256]{2,1,0:T(8,128)(2,1)S(1)}, u32[]{:S(2)}, u32[]{:S(2)}) async-start(bf16[16,36,256]{2,1,0:T(8,128)(2,1)} %route.1), calls=%async_computation.1 | async-start | bytes 655360 | tf_op jit(solution)/shard_map/all_to_all | solution.py:29
  28.8 1.4 pad_maximum_fusion.1
  30.2 1.2 collective-permute-start.1
  31.4 2.8 multiply_convert_fusion.5
  34.6 3.4 %all-to-all-done.1.arrived_ref = bf16[16,36,256]{2,1,0:T(8,128)(2,1)S(1)} async-done(((bf16[16,36,256]{2,1,0:T(8,128)(2,1)}), bf16[16,36,256]{2,1,0:T(8,128)(2,1)S(1)}, u32[]{:S(2)}, u32[]{:S(2)}) %all-to-all-start.1) | async-done | bytes 294944 | tf_op jit(solution)/shard_map/all_to_all | solution.py:29
  38.0 1.3 copy-done.5
  39.3 4.7 %attend.1 = bf16[16,4,16,512]{3,2,1,0:T(8,128)(2,1)} custom-call(s32[3]{0:T(128)S(1)} %pad_add_fusion.ids_ref, s32[4]{0:T(128)S(1)} %copy-done.6, bf16[4,576,256]{2,1,0:T(8,128)(2,1)S(1)} %bitcast.34, bf16[16,36,256]{2,1,0:T(8,128)(2,1)S(1)} %all-to-all-done.1.arrived_ref, bf16[4,576,2]{2,1,0:T(8,128)(2,1)S(1)} %bitcast.35, bf16[2,4,576,128]{3,2,1,0:T(8,128)(2,1)S(1)} %bitcast.36), custom_call_target="tpu_custom_call" | custom-call | tf_op jit(solution)/shard_map/attend/pallas_call | solution.py:121
  44.0 4.6 %all-to-all-start.2 = ((bf16[16,4,16,512]{3,2,1,0:T(8,128)(2,1)}), bf16[16,4,16,512]{3,2,1,0:T(8,128)(2,1)S(1)}, u32[]{:S(2)}, u32[]{:S(2)}) async-start(bf16[16,4,16,512]{3,2,1,0:T(8,128)(2,1)} %attend.1), calls=%async_computation.2 | async-start | bytes 2097152 | tf_op jit(solution)/shard_map/all_to_all | solution.py:29
  48.6 1.2 pad_maximum_fusion.2
  49.8 1.2 collective-permute-start
  51.0 3.3 %multiply_convert_fusion.1 = (bf16[896,576]{1,0:T(8,128)(2,1)S(1)}, bf16[896,576]{1,0:T(8,128)(2,1)S(1)}) fusion(f32[896]{0:T(1024)S(1)} %convert_element_type.73, bf16[896,1152]{1,0:T(8,128)(2,1)} %param.23, s32[]{:T(128)S(6)} %select_n.21, bf16[896,1152]{1,0:T(8,128)(2,1)} %param.24), kind=kLoop, calls=%fused_computation.3 | loop fusion | flops 3096576 | bytes 4132356 | tf_op jit(solution)/shard_map/convert.7
  54.4 2.0 pad_maximum_fusion.kept_ref
  56.4 20.3 %collective-permute-done.first_ref = bf16[384,1152]{1,0:T(8,128)(2,1)S(1)} collective-permute-done((bf16[384,1152]{1,0:T(8,128)(2,1)}, bf16[384,1152]{1,0:T(8,128)(2,1)S(1)}, u32[]{:S(2)}, u32[]{:S(2)}) %collective-permute-start) | collective-permute-done | bytes 884768 | tf_op jit(solution)/shard_map/ppermute | solution.py:37
  76.7 1.0 convolution_convert_fusion
  78.1 29.4 %all_to_all.45 = bf16[8,128,1024]{2,1,0:T(8,128)(2,1)S(1)} all-to-all(bf16[8,128,1024]{2,1,0:T(8,128)(2,1)S(1)} %broadcast_in_dim.14), channel_id=1, replica_groups=mesh['xh'=2,'xl'=2,'zl'=2,'zh'=2,'y'=4,'c'=2] {'xh','xl','zl'}, dimensions={0} | all-to-all | bytes 4194304 | tf_op jit(solution)/shard_map/all_to_all | solution.py:29
  107.6 2.1 project.4
  109.7 2.6 collective-permute-start.2
  112.2 2.1 collective-permute-done.2.refs_1_
  114.3 2.9 project.5
  117.2 7.1 %all-to-all-start.4 = ((bf16[8,64,896]{2,1,0:T(8,128)(2,1)}), bf16[8,64,896]{2,1,0:T(8,128)(2,1)S(1)}, u32[]{:S(2)}, u32[]{:S(2)}) async-start(bf16[8,64,896]{2,1,0:T(8,128)(2,1)} %bitcast.13), calls=%async_computation.4 | async-start | bytes 1835008 | tf_op jit(solution)/shard_map/all_to_all | solution.py:29
  126.3 14.0 %all-to-all-done.4 = bf16[8,64,896]{2,1,0:T(8,128)(2,1)S(1)} async-done(((bf16[8,64,896]{2,1,0:T(8,128)(2,1)}), bf16[8,64,896]{2,1,0:T(8,128)(2,1)S(1)}, u32[]{:S(2)}, u32[]{:S(2)}) %all-to-all-start.4) | async-done | bytes 917536 | tf_op jit(solution)/shard_map/all_to_all | solution.py:29
  141.4 28.4 %all_to_all.46 = bf16[16,64,896]{2,1,0:T(8,128)(2,1)S(1)} all-to-all(bf16[16,64,896]{2,1,0:T(8,128)(2,1)S(1)} %broadcast_in_dim.28), channel_id=1, replica_groups=mesh['xh'=2,'xl'=2,'zl'=2,'zh'=2,'y'=4,'c'=2] {'xl','zh','y'}, dimensions={0} | all-to-all | bytes 3670016 | tf_op jit(solution)/shard_map/all_to_all | solution.py:29
  169.8 1.9 collective-permute-start.3
  171.7 3.4 %collective-permute-done.3.other_ref = bf16[2,8,64,896]{3,2,1,0:T(8,128)(2,1)S(1)} collective-permute-done((bf16[2,8,64,896]{3,2,1,0:T(8,128)(2,1)S(1)}, bf16[2,8,64,896]{3,2,1,0:T(8,128)(2,1)S(1)}, u32[]{:S(2)}, u32[]{:S(2)}) %collective-permute-start.3) | collective-permute-done | bytes 1835040 | tf_op jit(solution)/shard_map/ppermute | solution.py:37
  175.1 9.6 %widen.1 = bf16[4,256,1280]{2,1,0:T(8,128)(2,1)} custom-call(s32[3]{0:T(128)S(1)} %pad_add_fusion.ids_ref, bf16[2,8,64,896]{3,2,1,0:T(8,128)(2,1)S(1)} %bitcast.32, bf16[2,8,64,896]{3,2,1,0:T(8,128)(2,1)S(1)} %collective-permute-done.3.other_ref, bf16[896,1152]{1,0:T(8,128)(2,1)} %pad_maximum_fusion.kept_ref, ...), custom_call_target="tpu_custom_call" | custom-call | tf_op jit(solution)/shard_map/widen/pallas_call | solution.py:204
  184.7 4.5 %all-to-all-start.6 = ((bf16[4,256,1280]{2,1,0:T(8,128)(2,1)}), bf16[4,256,1280]{2,1,0:T(8,128)(2,1)}, u32[]{:S(2)}, u32[]{:S(2)}) async-start(bf16[4,256,1280]{2,1,0:T(8,128)(2,1)} %widen.1), calls=%async_computation.6 | async-start | bytes 5242880 | tf_op jit(solution)/shard_map/all_to_all | solution.py:29
  189.2 2.7 constant_dynamic-slice_fusion
  192.1 28.9 %all-to-all-done.6 = bf16[4,256,1280]{2,1,0:T(8,128)(2,1)} async-done(((bf16[4,256,1280]{2,1,0:T(8,128)(2,1)}), bf16[4,256,1280]{2,1,0:T(8,128)(2,1)}, u32[]{:S(2)}, u32[]{:S(2)}) %all-to-all-start.6) | async-done | bytes 2621472 | tf_op jit(solution)/shard_map/all_to_all | solution.py:29
  221.0 2.3 convert_reduce_fusion
  224.1 31.9 %all_to_all.47 = bf16[4,256,576]{1,2,0:T(8,128)(2,1)} all-to-all(bf16[4,256,576]{1,2,0:T(8,128)(2,1)S(1)} %broadcast_in_dim.29), channel_id=1, replica_groups=mesh['xh'=2,'xl'=2,'zl'=2,'zh'=2,'y'=4,'c'=2] {'xh','zl'}, dimensions={0} | all-to-all | bytes 2359296 | tf_op jit(solution)/shard_map/all_to_all | solution.py:29
  255.9 1.7 copy.31
  257.7 3.9 %project.6 = bf16[2,512,896]{2,1,0:T(8,128)(2,1)S(1)} custom-call(s32[3]{0:T(128)S(1)} %pad_add_fusion.ids_ref, bf16[4,2,128,576]{3,2,1,0:T(8,128)(2,1)S(1)} %bitcast.28, bf16[576,896]{1,0:T(8,128)(2,1)S(1)} %get-tuple-element.18.refs_0_, bf16[576,896]{1,0:T(8,128)(2,1)} %collective-permute-done.4.refs_1_), custom_call_target="tpu_custom_call" | custom-call | tf_op jit(solution)/shard_map/project/pallas_call | solution.py:160
  261.6 1.6 collective-permute-start.5
  263.2 3.4 %collective-permute-done.5.refs_2_ = bf16[2,512,896]{2,1,0:T(8,128)(2,1)S(1)} collective-permute-done((bf16[2,512,896]{2,1,0:T(8,128)(2,1)S(1)}, bf16[2,512,896]{2,1,0:T(8,128)(2,1)S(1)}, u32[]{:S(2)}, u32[]{:S(2)}) %collective-permute-start.5) | collective-permute-done | bytes 1835040 | tf_op jit(solution)/shard_map/ppermute | solution.py:37
  266.6 1.3 copy-done.14
  267.9 4.2 %project.7 = bf16[2,512,896]{2,1,0:T(8,128)(2,1)S(1)} custom-call(s32[3]{0:T(128)S(1)} %pad_add_fusion.ids_ref, bf16[4,2,128,576]{3,2,1,0:T(8,128)(2,1)S(1)} %bitcast.29, bf16[576,896]{1,0:T(8,128)(2,1)S(1)} %get-tuple-element.18.refs_0_, bf16[576,896]{1,0:T(8,128)(2,1)} %collective-permute-done.4.refs_1_, bf16[2,512,896]{2,1,0:T(8,128)(2,1)} %copy-done.14), custom_call_target="tpu_custom_call" | custom-call | tf_op jit(solution)/shard_map/project/pallas_call | solution.py:160
  272.1 1.3 copy-done.1
  273.3 3.8 %all-to-all-start.8 = ((bf16[16,64,896]{2,1,0:T(8,128)(2,1)}), bf16[16,64,896]{2,1,0:T(8,128)(2,1)S(1)}, u32[]{:S(2)}, u32[]{:S(2)}) async-start(bf16[16,64,896]{2,1,0:T(8,128)(2,1)} %bitcast.30), calls=%async_computation.8 | async-start | bytes 3670016 | tf_op jit(solution)/shard_map/all_to_all | solution.py:29
  278.0 26.5 %all-to-all-done.8 = bf16[16,64,896]{2,1,0:T(8,128)(2,1)S(1)} async-done(((bf16[16,64,896]{2,1,0:T(8,128)(2,1)}), bf16[16,64,896]{2,1,0:T(8,128)(2,1)S(1)}, u32[]{:S(2)}, u32[]{:S(2)}) %all-to-all-start.8) | async-done | bytes 1835040 | tf_op jit(solution)/shard_map/all_to_all | solution.py:29
  304.5 0.9 convert_reduce_fusion.1
  305.5 1.1 reduce_sum.45
  (56 shorter events, 7.2 us)
Async XLA Ops:
  0.0 76.7 %copy-start = (bf16[8,512,128]{2,1,0:T(8,128)(2,1)S(1)}, bf16[8,512,128]{2,1,0:T(8,128)(2,1)}, u32[]{:S(2)}) copy-start(bf16[8,512,128]{2,1,0:T(8,128)(2,1)} %param.19) | copy-start | bytes 3145732
  0.0 14.0 %copy-start.16 = (bf16[896]{0:T(1024)(128)(2,1)S(1)}, bf16[896]{0:T(1024)(128)(2,1)}, u32[]{:S(2)}) copy-start(bf16[896]{0:T(1024)(128)(2,1)} %param.22) | copy-start | bytes 5380
  2.0 1.3 copy-start.3
  4.6 18.6 %copy-start.7 = (s32[1,16]{1,0:T(1,128)S(1)}, s32[1,16]{1,0:T(1,128)}, u32[]{:S(2)}) copy-start(s32[1,16]{1,0:T(1,128)} %param.16) | copy-start | bytes 196
  4.6 18.6 %all-to-all-start = ((bf16[16,36,256]{2,1,0:T(8,128)(2,1)}), bf16[16,36,256]{2,1,0:T(8,128)(2,1)S(1)}, u32[]{:S(2)}, u32[]{:S(2)}) async-start(bf16[16,36,256]{2,1,0:T(8,128)(2,1)} %leave.1), calls=%async_computation | async-start | bytes 655360 | tf_op jit(solution)/shard_map/all_to_all | solution.py:29
  24.5 13.6 %all-to-all-start.1 = ((bf16[16,36,256]{2,1,0:T(8,128)(2,1)}), bf16[16,36,256]{2,1,0:T(8,128)(2,1)S(1)}, u32[]{:S(2)}, u32[]{:S(2)}) async-start(bf16[16,36,256]{2,1,0:T(8,128)(2,1)} %route.1), calls=%async_computation.1 | async-start | bytes 655360 | tf_op jit(solution)/shard_map/all_to_all | solution.py:29
  28.8 5.4 %copy-start.17 = (bf16[2,4,576]{2,1,0:T(4,128)(2,1)S(1)}, bf16[2,4,576]{2,1,0:T(4,128)(2,1)}, u32[]{:S(2)}) copy-start(bf16[2,4,576]{2,1,0:T(4,128)(2,1)} %param.18) | copy-start | bytes 27652
  30.2 7.8 %copy-start.4 = (bf16[4,256,576]{1,2,0:T(8,128)(2,1)S(1)}, bf16[4,256,576]{1,2,0:T(8,128)(2,1)}, u32[]{:S(2)}) copy-start(bf16[4,256,576]{1,2,0:T(8,128)(2,1)} %param.13) | copy-start | bytes 3538948
  30.2 7.8 %copy-start.6 = (s32[4]{0:T(128)S(1)}, s32[4]{0:T(128)}, u32[]{:S(2)}) copy-start(s32[4]{0:T(128)} %lengths_ref.1) | copy-start | bytes 52
  30.2 46.5 %collective-permute-start.1 = (bf16[512,1152]{1,0:T(8,128)(2,1)}, bf16[512,1152]{1,0:T(8,128)(2,1)}, u32[]{:S(2)}, u32[]{:S(2)}) collective-permute-start(bf16[512,1152]{1,0:T(8,128)(2,1)} %pad_maximum_fusion.1), channel_id=1, source_target_pairs={{0,32},{32,0},{1,33},{33,1},{2,34},{34,2},{3,35},{35,3},{4,36},{36... | collective-permute-start | bytes 3538952 | tf_op jit(solution)/shard_map/ppermute | solution.py:37
  38.0 1.3 copy-start.5
  44.0 4.6 %copy-start.12 = (bf16[384,576]{1,0:T(8,128)(2,1)S(1)}, bf16[384,576]{1,0:T(8,128)(2,1)}, u32[]{:S(2)}) copy-start(bf16[384,576]{1,0:T(8,128)(2,1)} %get-tuple-element.23) | copy-start | bytes 1327108
  44.0 4.6 %copy-start.13 = (bf16[384,576]{1,0:T(8,128)(2,1)S(1)}, bf16[384,576]{1,0:T(8,128)(2,1)}, u32[]{:S(2)}) copy-start(bf16[384,576]{1,0:T(8,128)(2,1)} %get-tuple-element.24) | copy-start | bytes 1327108
  44.0 32.7 %all-to-all-start.2 = ((bf16[16,4,16,512]{3,2,1,0:T(8,128)(2,1)}), bf16[16,4,16,512]{3,2,1,0:T(8,128)(2,1)S(1)}, u32[]{:S(2)}, u32[]{:S(2)}) async-start(bf16[16,4,16,512]{3,2,1,0:T(8,128)(2,1)} %attend.1), calls=%async_computation.2 | async-start | bytes 2097152 | tf_op jit(solution)/shard_map/all_to_all | solution.py:29
  49.8 26.9 %collective-permute-start = (bf16[384,1152]{1,0:T(8,128)(2,1)}, bf16[384,1152]{1,0:T(8,128)(2,1)S(1)}, u32[]{:S(2)}, u32[]{:S(2)}) collective-permute-start(bf16[384,1152]{1,0:T(8,128)(2,1)} %pad_maximum_fusion.2), channel_id=1, source_target_pairs={{0,32},{32,0},{1,33},{33,1},{2,34},{34,2},{3,35},{35,3},{4,36},{36... | collective-permute-start | bytes 2654216 | tf_op jit(solution)/shard_map/ppermute | solution.py:37
  78.1 29.5 %copy-start.2 = (bf16[1024,896]{1,0:T(8,128)(2,1)S(1)}, bf16[1024,896]{1,0:T(8,128)(2,1)}, u32[]{:S(2)}) copy-start(bf16[1024,896]{1,0:T(8,128)(2,1)} %refs_0_.3) | copy-start | bytes 5505028
  109.7 4.7 %collective-permute-start.2 = (bf16[1,512,896]{2,1,0:T(8,128)(2,1)S(1)}, bf16[1,512,896]{2,1,0:T(8,128)(2,1)S(1)}, u32[]{:S(2)}, u32[]{:S(2)}) collective-permute-start(bf16[1,512,896]{2,1,0:T(8,128)(2,1)S(1)} %project.4), channel_id=1, source_target_pairs={{0,1},{1,0},{2,3},{3,2},{4,5},{5,4},{6,7},{7,6},{8,9},{9,8},{10,11... | collective-permute-start | bytes 2752520 | tf_op jit(solution)/shard_map/ppermute | solution.py:37
  117.2 23.1 %all-to-all-start.4 = ((bf16[8,64,896]{2,1,0:T(8,128)(2,1)}), bf16[8,64,896]{2,1,0:T(8,128)(2,1)S(1)}, u32[]{:S(2)}, u32[]{:S(2)}) async-start(bf16[8,64,896]{2,1,0:T(8,128)(2,1)} %bitcast.13), calls=%async_computation.4 | async-start | bytes 1835008 | tf_op jit(solution)/shard_map/all_to_all | solution.py:29
  125.2 0.7 copy-start.8
  140.4 0.7 copy-start.10
  169.8 5.3 %collective-permute-start.3 = (bf16[2,8,64,896]{3,2,1,0:T(8,128)(2,1)S(1)}, bf16[2,8,64,896]{3,2,1,0:T(8,128)(2,1)S(1)}, u32[]{:S(2)}, u32[]{:S(2)}) collective-permute-start(bf16[2,8,64,896]{3,2,1,0:T(8,128)(2,1)S(1)} %bitcast.31), channel_id=1, source_target_pairs={{0,1},{1,0},{2,3},{3,2},{4,5},{5,4},{6,7},{7,6},{8,9},{9,8},{10,11... | collective-permute-start | bytes 5505032 | tf_op jit(solution)/shard_map/ppermute | solution.py:37
  184.7 36.3 %all-to-all-start.6 = ((bf16[4,256,1280]{2,1,0:T(8,128)(2,1)}), bf16[4,256,1280]{2,1,0:T(8,128)(2,1)}, u32[]{:S(2)}, u32[]{:S(2)}) async-start(bf16[4,256,1280]{2,1,0:T(8,128)(2,1)} %widen.1), calls=%async_computation.6 | async-start | bytes 5242880 | tf_op jit(solution)/shard_map/all_to_all | solution.py:29
  191.9 65.8 %collective-permute-start.4 = (bf16[576,896]{1,0:T(8,128)(2,1)}, bf16[576,896]{1,0:T(8,128)(2,1)}, u32[]{:S(2)}, u32[]{:S(2)}) collective-permute-start(bf16[576,896]{1,0:T(8,128)(2,1)} %get-tuple-element.17), channel_id=1, source_target_pairs={{0,32},{32,0},{1,33},{33,1},{2,34},{34,2},{3,35},{35,3},{4,36},{36... | collective-permute-start | bytes 3096584 | tf_op jit(solution)/shard_map/ppermute | solution.py:37
  261.6 5.0 %collective-permute-start.5 = (bf16[2,512,896]{2,1,0:T(8,128)(2,1)S(1)}, bf16[2,512,896]{2,1,0:T(8,128)(2,1)S(1)}, u32[]{:S(2)}, u32[]{:S(2)}) collective-permute-start(bf16[2,512,896]{2,1,0:T(8,128)(2,1)S(1)} %project.6), channel_id=1, source_target_pairs={{0,1},{1,0},{2,3},{3,2},{4,5},{5,4},{6,7},{7,6},{8,9},{9,8},{10,11... | collective-permute-start | bytes 5505032 | tf_op jit(solution)/shard_map/ppermute | solution.py:37
  266.6 1.3 copy-start.14
  272.1 1.3 copy-start.1
  273.3 3.9 %copy-start.11 = (f32[64,896]{1,0:T(8,128)S(1)}, f32[64,896]{1,0:T(8,128)}, u32[]{:S(2)}) copy-start(f32[64,896]{1,0:T(8,128)} %copy-done.10) | copy-start | bytes 688132
  273.3 31.2 %all-to-all-start.8 = ((bf16[16,64,896]{2,1,0:T(8,128)(2,1)}), bf16[16,64,896]{2,1,0:T(8,128)(2,1)S(1)}, u32[]{:S(2)}, u32[]{:S(2)}) async-start(bf16[16,64,896]{2,1,0:T(8,128)(2,1)} %bitcast.30), calls=%async_computation.8 | async-start | bytes 3670016 | tf_op jit(solution)/shard_map/all_to_all | solution.py:29
  277.2 29.3 %copy-start.9 = (f32[2,32,896]{2,1,0:T(8,128)S(1)}, f32[2,32,896]{2,1,0:T(8,128)}, u32[]{:S(2)}) copy-start(f32[2,32,896]{2,1,0:T(8,128)} %copy-done.8) | copy-start | bytes 688132
  278.0 28.5 %copy-start.15 = (f32[32,2,896]{2,1,0:T(2,128)S(1)}, f32[32,2,896]{2,1,0:T(2,128)}, u32[]{:S(2)}) copy-start(f32[32,2,896]{2,1,0:T(2,128)} %reduce_sum.42) | copy-start | bytes 688132

commit v3 on v2

--- a/solution.py
+++ b/solution.py
@@ -19,7 +19,8 @@
 N_ZY = 8
 N_FOUR = 4
 SWAP = [(0, 1), (1, 0)]
-FIRST_ROWS = 384
+CUTS = (0, 384, 640, 896)
+TILE = 384
 bf16 = jnp.bfloat16
 f32 = jnp.float32
 VMEM = 48 * 1024 * 1024
@@ -87,17 +88,22 @@
     )(peer, pieces)
 
 
-def attend(ids, lengths, cache_t, arrived, fresh_t, queries_t, heads, latent_width):
+def attend(ids, lengths, cache_t, fresh_t, queries_t, heads, latent_width, arrived=None, done=None):
     rows, entries, length = cache_t.shape
     steps, _, _, all_heads = queries_t.shape
     parts = all_heads // heads
-
-    def body(ids_ref, lengths_ref, cache_ref, arrived_ref, fresh_ref, q_ref, out_ref):
-        r = pl.program_id(0)
-        here = r == ids_ref[0]
-        came = jnp.concatenate([arrived_ref[j].astype(f32) for j in range(N_TP)], axis=0)
-        latents = jnp.where(here, came, cache_ref[0].astype(f32))
-        current = lengths_ref[r]
+    again = arrived is not None
+
+    def slot(r, ids):
+        return ids[0] if again else r
+
+    def body(ids_ref, lengths_ref, cache_ref, fresh_ref, q_ref, *refs):
+        out_ref = refs[-1]
+        current = lengths_ref[slot(pl.program_id(0), ids_ref)]
+        if again:
+            latents = jnp.concatenate([refs[0][j].astype(f32) for j in range(N_TP)], axis=0)
+        else:
+            latents = cache_ref[0].astype(f32)
         position = lax.broadcasted_iota(jnp.int32, (entries, length), 1)
         for s in range(steps):
             token = fresh_ref[0, :, s : s + 1].astype(f32)
@@ -118,25 +124,31 @@
             outs.append(out.reshape(parts, heads, latent_width))
         out_ref[:, 0] = jnp.concatenate(outs, axis=1).astype(bf16)
 
+    extra_specs = [whole(arrived.shape), pl.BlockSpec(memory_space=pl.ANY)] if again else []
+    extra = [arrived, done] if again else []
     return pl.pallas_call(
         body,
         grid_spec=pltpu.PrefetchScalarGridSpec(
             num_scalar_prefetch=2,
-            grid=(rows,),
+            grid=(1 if again else rows,),
             in_specs=[
-                pl.BlockSpec((1, entries, length), lambda r, *_: (r, 0, 0)),
-                whole(arrived.shape),
-                pl.BlockSpec((1, entries, steps), lambda r, *_: (r, 0, 0)),
-                pl.BlockSpec((steps, 1, entries, all_heads), lambda r, *_: (0, r, 0, 0)),
-            ],
+                pl.BlockSpec((1, entries, length), lambda r, ids, _: (slot(r, ids), 0, 0)),
+                pl.BlockSpec((1, entries, steps), lambda r, ids, _: (slot(r, ids), 0, 0)),
+                pl.BlockSpec(
+                    (steps, 1, entries, all_heads), lambda r, ids, _: (0, slot(r, ids), 0, 0)
+                ),
+            ]
+            + extra_specs,
             out_specs=pl.BlockSpec(
-                (parts, 1, steps * heads, latent_width), lambda r, *_: (0, r, 0, 0)
+                (parts, 1, steps * heads, latent_width),
+                lambda r, ids, _: (0, slot(r, ids), 0, 0),
             ),
         ),
         out_shape=jax.ShapeDtypeStruct((parts, rows, steps * heads, latent_width), bf16),
-        compiler_params=params(),
-        name="attend",
-    )(ids, lengths, cache_t, arrived, fresh_t, queries_t)
+        input_output_aliases={6: 0} if again else {},
+        compiler_params=params(),
+        name="again" if again else "attend",
+    )(ids, lengths, cache_t, fresh_t, queries_t, *extra)
 
 
 def project(ids, half, rows, weights, near=None):
@@ -173,46 +185,56 @@
     )(ids, rows, *weights, *extra)
 
 
-def widen(ids, own, other, kept, came):
-    _, _, chunk, features = own.shape
+def widen(ids, rows, kept, came, side, done=None):
+    _, count, chunk, features = rows.shape
     columns = kept.shape[1]
-    per = 2 * chunk
-
-    def body(ids_ref, own_ref, other_ref, kept_ref, first_ref, second_ref, out_ref):
+    per = count * chunk // N_FOUR
+    starts = [0]
+    for w in came:
+        starts.append(starts[-1] + w.shape[0])
+
+    def body(ids_ref, rows_ref, kept_ref, *refs):
+        out_ref = refs[-1]
         pair = ids_ref[2]
-
-        def pick(at):
-            return jnp.concatenate(
-                [ref[at].reshape(per, features) for ref in (own_ref, other_ref)], axis=0
-            )
-
-        mine, near = pick(pair), pick(1 - pair)
-        total = jnp.dot(mine, kept_ref[...], preferred_element_type=f32)
-        total += jnp.dot(near[:, :FIRST_ROWS], first_ref[...], preferred_element_type=f32)
-        total += jnp.dot(near[:, FIRST_ROWS:], second_ref[...], preferred_element_type=f32)
-        out_ref[0, :, :columns] = total.astype(bf16)
-        squares = jnp.zeros((2 * per, 1), f32)
-        for rows in (mine, near):
-            wide = rows.astype(f32)
+        mine = rows_ref[pair].reshape(count * chunk, features)
+        near = rows_ref[1 - pair].reshape(count * chunk, features)
+        for at in range(0, columns, TILE):
+            tile = slice(at, at + TILE)
+            total = jnp.dot(mine, kept_ref[:, tile], preferred_element_type=f32)
+            for k in range(len(came)):
+                total += jnp.dot(
+                    near[:, starts[k] : starts[k + 1]],
+                    refs[k][:, tile],
+                    preferred_element_type=f32,
+                )
+            out_ref[:, 0, :, tile] = total.astype(bf16).reshape(N_FOUR, per, TILE)
+        squares = jnp.zeros((count * chunk, 1), f32)
+        for half in (mine, near):
+            wide = half.astype(f32)
             squares += jnp.sum(wide * wide, axis=1, keepdims=True)
         high = squares.astype(bf16).astype(f32)
-        lane = lax.broadcasted_iota(jnp.int32, (2 * per, 128), 1)
+        lane = lax.broadcasted_iota(jnp.int32, (count * chunk, 128), 1)
         extra = jnp.where(lane == 0, high, jnp.where(lane == 1, squares - high, 0.0))
-        out_ref[0, :, columns:] = extra.astype(bf16)
-
-    rows = pl.BlockSpec((2, 2, chunk, features), lambda q, ids: (0, q, 0, 0))
+        out_ref[:, 0, :, columns:] = extra.astype(bf16).reshape(N_FOUR, per, 128)
+
+    last = [] if done is None else [done]
     return pl.pallas_call(
         body,
         grid_spec=pltpu.PrefetchScalarGridSpec(
             num_scalar_prefetch=1,
-            grid=(N_FOUR,),
-            in_specs=[rows, rows] + [whole(w.shape) for w in (kept,) + came],
-            out_specs=pl.BlockSpec((1, 2 * per, columns + 128), lambda q, ids: (q, 0, 0)),
-        ),
-        out_shape=jax.ShapeDtypeStruct((N_FOUR, 2 * per, columns + 128), bf16),
+            grid=(1,),
+            in_specs=[whole(rows.shape)]
+            + [whole(w.shape) for w in (kept,) + came]
+            + [pl.BlockSpec(memory_space=pl.ANY) for _ in last],
+            out_specs=pl.BlockSpec(
+                (N_FOUR, 1, per, columns + 128), lambda i, ids: (0, side, 0, 0)
+            ),
+        ),
+        out_shape=jax.ShapeDtypeStruct((N_FOUR, 2, per, columns + 128), bf16),
+        input_output_aliases={3 + len(came): 0} if last else {},
         compiler_params=params(),
         name="widen",
-    )(ids, own, other, kept, *came)
+    )(ids, rows, kept, *came, *last)
 
 
 def local(
@@ -259,44 +281,45 @@
             axis=1,
         ).astype(bf16)
 
-    came = (
-        swap(columns(1 - pair, 0, FIRST_ROWS), "xl"),
-        swap(columns(1 - pair, FIRST_ROWS, features), "xl"),
+    sent = [columns(1 - pair, low, high) for low, high in zip(CUTS[:-1], CUTS[1:])]
+    kept = columns(pair, 0, features)
+    came = [swap(sent[0], "xl"), swap(sent[1], "xl")]
+
+    arrived = exchange(route(move_peer[0], pieces), TP)
+    fresh_t = new_latent.transpose(1, 2, 0)
+    queries_t = queries.transpose(0, 1, 3, 2)
+    out = attend(ids, cache_length, cache_t, fresh_t, queries_t, heads, latent_width)
+    out = attend(
+        ids, cache_length, cache_t, fresh_t, queries_t, heads, latent_width, arrived, out
     )
-    kept = columns(pair, 0, features)
-
-    arrived = exchange(route(move_peer[0], pieces), TP)
-    out = attend(
-        ids,
-        cache_length,
-        cache_t,
-        arrived,
-        new_latent.transpose(1, 2, 0),
-        queries.transpose(0, 1, 3, 2),
-        heads,
-        latent_width,
-    )
+    out, came[0] = lax.optimization_barrier((out, came[0]))
     by_head = exchange(out, TP).reshape(-1, heads, latent_width)
-    by_head, kept, came = lax.optimization_barrier((by_head, kept, came))
+    by_head, kept, came[1] = lax.optimization_barrier((by_head, kept, came[1]))
     value_heads = jnp.einsum(
         "thl,hlv->thv", by_head, value_up, preferred_element_type=f32
     ).astype(bf16)
     value_heads = value_heads.reshape(-1, heads * value_width)
 
     gathered = spread(value_heads, DP, N_DP).reshape(N_DP, 2, chunk, -1)
-    gathered, down_weight = lax.optimization_barrier((gathered, down_weight))
+    down_sent = lax.dynamic_slice_in_dim(down_weight, (1 - pair) * part, part, 0)
+    gathered, sent[2], down_sent = lax.optimization_barrier((gathered, sent[2], down_sent))
     down_kept = lax.dynamic_slice_in_dim(down_weight, pair * part, part, 0)
-    down_came = swap(lax.dynamic_slice_in_dim(down_weight, (1 - pair) * part, part, 0), "xl")
+    down_came = swap(down_sent, "xl")
+    came.append(swap(sent[2], "xl"))
     away = swap(project(ids, lambda i: 1 - i[1], gathered, [out_proj]), "c")
     total = project(ids, lambda i: i[1], gathered, [out_proj], away)
     parts = exchange(total.reshape(N_ZY, chunk, -1), ZY)
+    parts, down_came, came[2] = lax.optimization_barrier((parts, down_came, came[2]))
     residue = lax.dynamic_slice_in_dim(residual, member * rows_out, rows_out, 1)
     residue = residue.transpose(1, 0, 2).reshape(chunk, -1)
     hidden = residue.astype(f32) + jnp.sum(parts.astype(f32), axis=0)
 
     own = spread(hidden.astype(bf16), PAIR, 2 * N_ZY).reshape(2, N_ZY, chunk, features)
     other = swap(own, "c")
-    sums = exchange(widen(ids, own, other, kept, came), FOUR)
+    came = tuple(came)
+    wide = widen(ids, own, kept, came, 0)
+    wide = widen(ids, other, kept, came, 1, wide)
+    sums = exchange(wide.reshape(N_FOUR, 4 * chunk, -1), FOUR)
     sums = jnp.sum(sums.astype(f32), axis=0)
     squares = sums[:, units] + sums[:, units + 1]
     inverse = lax.rsqrt(squares / D + norm_eps)[:, None]

time: 309 us -> 304 us (0.984)
  waiting for transfers between devices: 109 us -> 93.3 us
  blocking collectives: 89.7 us -> 104 us
  starting transfers between devices: 42.6 us -> 33.2 us
  local copies, waits for them, and re-layouts: 15 us -> 20 us
  Pallas kernels: 29.9 us -> 33.2 us
    all_to_all x6 -> x5, waiting for transfers between devices: 79.8 us -> 55.3 us  [exchange(): return lax.all_to_all(blocks, axes, 0, 0, tiled=True)]
    all_to_all x3 -> x4, blocking collectives: 89.7 us -> 104 us  [exchange(): return lax.all_to_all(blocks, axes, 0, 0, tiled=True)]
    all_to_all x6 -> x5, starting transfers between devices: 33.8 us -> 23.8 us  [exchange(): return lax.all_to_all(blocks, axes, 0, 0, tiled=True)]
    ppermute x6 -> x7, waiting for transfers between devices: 29.3 us -> 38 us  [swap(): return lax.ppermute(block, axis, SWAP)]
    pallas_call x1 -> x2, Pallas kernels: 9.59 us -> 12.2 us  [widen(): pl.pallas_call(body, grid_spec=pltpu.PrefetchScalarGridSpec(num_scalar_pr...]
    unnamed x38 -> x48, local copies, waits for them, and re-layouts: 7.01 us -> 9.47 us
    pallas_call x1 -> x2, Pallas kernels: 4.72 us -> 6.8 us  [attend(): pl.pallas_call(body, grid_spec=pltpu.PrefetchScalarGridSpec(num_scalar_pr...]
    ppermute x6 -> x7, starting transfers between devices: 8.74 us -> 9.41 us  [swap(): return lax.ppermute(block, axis, SWAP)]
  transfers between devices with their start and end apart: 12 -> 12, of which waited for: 9 -> 7; matrix products, arithmetic and copies ran while one was open for 7% -> 6% of each run, Pallas kernels for 2% -> 6%
where the time goes in v3:
time: 304 us; the launch traced here: 303 us
  blocking collectives  104 us (34%)
  waiting for transfers between devices  93.3 us (31%)
  starting transfers between devices  33.2 us (11%)
  Pallas kernels  33.2 us (11%)
  local copies, waits for them, and re-layouts  20 us (7%)
  other arithmetic  17.9 us (6%)
    all_to_all x4, blocking collectives, exchange(): return lax.all_to_all(blocks, axes, 0, 0, tiled=True)  104 us
    all_to_all x5, waiting for transfers between devices, exchange(): return lax.all_to_all(blocks, axes, 0, 0, tiled=True)  55.3 us
    ppermute x7, waiting for transfers between devices, swap(): return lax.ppermute(block, axis, SWAP)  38 us
    all_to_all x5, starting transfers between devices, exchange(): return lax.all_to_all(blocks, axes, 0, 0, tiled=True)  23.8 us
    pallas_call x4, Pallas kernels, project(): pl.pallas_call(body, grid_spec=pltpu.PrefetchScalarGridSpec(num_scalar_pr...  12.3 us
    pallas_call x2, Pallas kernels, widen(): pl.pallas_call(body, grid_spec=pltpu.PrefetchScalarGridSpec(num_scalar_pr...  12.2 us
    unnamed x48, local copies, waits for them, and re-layouts  9.47 us
    ppermute x7, starting transfers between devices, swap(): return lax.ppermute(block, axis, SWAP)  9.41 us
  transfers between devices with their start and end apart: 12, of which 7 were waited for; matrix products, arithmetic and copies ran while one was open for 6% of the time, Pallas kernels for 6%

profile of v3, /device:TPU:1, one launch (start us, length us, event | category | flops | bytes accessed | tf_op | source)
XLA Modules:
  0.0 303.0 jit_solution(15461660057954036826)
XLA Ops:
  0.8 1.9 multiply_convert_fusion.3
  2.7 1.2 pad_maximum_fusion.1
  3.9 2.1 collective-permute-start
  8.1 17.7 %all_to_all.45.in_ref = bf16[16,36,256]{2,1,0:T(8,128)(2,1)S(1)} all-to-all(bf16[16,36,256]{2,1,0:T(8,128)(2,1)S(1)} %leave.1), channel_id=1, replica_groups=mesh['xh'=2,'xl'=2,'zl'=2,'zh'=2,'y'=4,'c'=2] {'zh','y','c'}, dimensions={0} | all-to-all | bytes 589824 | tf_op jit(solution)/shard_map/all_to_all | solution.py:30
  25.8 1.3 route.1
  27.0 4.3 %all-to-all-start.1 = ((bf16[16,36,256]{2,1,0:T(8,128)(2,1)}), bf16[16,36,256]{2,1,0:T(8,128)(2,1)S(1)}, u32[]{:S(2)}, u32[]{:S(2)}) async-start(bf16[16,36,256]{2,1,0:T(8,128)(2,1)} %route.1), calls=%async_computation.1 | async-start | bytes 655360 | tf_op jit(solution)/shard_map/all_to_all | solution.py:30
  31.8 1.3 copy-done.6
  33.0 4.7 %attend.1.refs_1_ = bf16[16,4,16,512]{3,2,1,0:T(8,128)(2,1)} custom-call(s32[3]{0:T(128)S(1)} %pad_add_fusion.ids_ref, s32[4]{0:T(128)S(1)} %copy-done.11, bf16[4,576,256]{2,1,0:T(8,128)(2,1)S(1)} %bitcast.32, bf16[4,576,2]{2,1,0:T(8,128)(2,1)S(1)} %bitcast.37, bf16[2,4,576,128]{3,2,1,0:T(8,128)(2,1)S(1)} %bitcast.39), custom_call_target="tpu_custom_call" | custom-call | tf_op jit(solution)/shard_map/attend/pallas_call | solution.py:129
  37.7 2.9 all-to-all-done.1.refs_0_
  40.6 1.3 copy-done.7
  41.9 2.1 again.1
  44.0 4.4 %all-to-all-start.2 = ((bf16[16,4,16,512]{3,2,1,0:T(8,128)(2,1)}), bf16[16,4,16,512]{3,2,1,0:T(8,128)(2,1)S(1)}, u32[]{:S(2)}, u32[]{:S(2)}) async-start(bf16[16,4,16,512]{3,2,1,0:T(8,128)(2,1)} %again.1), calls=%async_computation.2 | async-start | bytes 2097152 | tf_op jit(solution)/shard_map/all_to_all | solution.py:30
  48.4 2.8 multiply_convert_fusion.4
  51.2 1.0 pad_maximum_fusion.2
  52.5 3.3 %multiply_convert_fusion.1 = (bf16[896,576]{1,0:T(8,128)(2,1)S(1)}, bf16[896,576]{1,0:T(8,128)(2,1)S(1)}) fusion(f32[896]{0:T(1024)S(1)} %convert_element_type.80, bf16[896,1152]{1,0:T(8,128)(2,1)} %param.23, s32[]{:T(128)S(6)} %select_n.24, bf16[896,1152]{1,0:T(8,128)(2,1)} %param.24), kind=kLoop, calls=%fused_computation.3 | loop fusion | flops 3096576 | bytes 4132356 | tf_op jit(solution)/shard_map/convert.7
  55.8 2.0 pad_maximum_fusion.kept_ref
  57.8 9.3 %collective-permute-done.1.refs_1_ = bf16[256,1152]{1,0:T(8,128)(2,1)S(1)} collective-permute-done((bf16[256,1152]{1,0:T(8,128)(2,1)}, bf16[256,1152]{1,0:T(8,128)(2,1)S(1)}, u32[]{:S(2)}, u32[]{:S(2)}) %collective-permute-start.1) | collective-permute-done | bytes 589856 | tf_op jit(solution)/shard_map/ppermute | solution.py:38
  67.1 1.0 convolution_convert_fusion
  68.3 1.6 broadcast_in_dim.14
  69.9 4.2 %all-to-all-start.3 = ((bf16[8,128,1024]{2,1,0:T(8,128)(2,1)}), bf16[8,128,1024]{2,1,0:T(8,128)(2,1)S(1)}, u32[]{:S(2)}, u32[]{:S(2)}) async-start(bf16[8,128,1024]{2,1,0:T(8,128)(2,1)} %broadcast_in_dim.14), calls=%async_computation.3 | async-start | bytes 4194304 | tf_op jit(solution)/shard_map/all_to_all | solution.py:30
  74.1 3.0 %constant_dynamic-slice_fusion = (bf16[576,896]{1,0:T(8,128)(2,1)}, bf16[576,896]{1,0:T(8,128)(2,1)}) fusion(bf16[1152,896]{1,0:T(8,128)(2,1)} %param.25, s32[]{:T(128)S(6)} %select_n.24, s32[]{:T(128)S(6)} %select_n.12), kind=kLoop, calls=%fused_computation.32 | loop fusion | bytes 4128776 | tf_op jit(solution)/shard_map/dynamic_slice | solution.py:306
  77.1 1.0 pad_maximum_fusion.3
  78.1 26.0 %all-to-all-done.3 = bf16[8,128,1024]{2,1,0:T(8,128)(2,1)S(1)} async-done(((bf16[8,128,1024]{2,1,0:T(8,128)(2,1)}), bf16[8,128,1024]{2,1,0:T(8,128)(2,1)S(1)}, u32[]{:S(2)}, u32[]{:S(2)}) %all-to-all-start.3) | async-done | bytes 2097184 | tf_op jit(solution)/shard_map/all_to_all | solution.py:30
  104.1 1.5 copy-done.5
  105.6 2.1 project.4
  107.7 1.9 collective-permute-start.2
  109.6 2.1 collective-permute-done.2.refs_1_
  111.7 2.1 project.5
  113.8 0.9 copy-done.8
  114.7 6.9 %all-to-all-start.4 = ((bf16[8,64,896]{2,1,0:T(8,128)(2,1)}), bf16[8,64,896]{2,1,0:T(8,128)(2,1)S(1)}, u32[]{:S(2)}, u32[]{:S(2)}) async-start(bf16[8,64,896]{2,1,0:T(8,128)(2,1)} %bitcast.41), calls=%async_computation.4 | async-start | bytes 1835008 | tf_op jit(solution)/shard_map/all_to_all | solution.py:30
  123.6 23.2 %collective-permute-done.4.refs_2_ = bf16[256,1152]{1,0:T(8,128)(2,1)S(1)} collective-permute-done((bf16[256,1152]{1,0:T(8,128)(2,1)}, bf16[256,1152]{1,0:T(8,128)(2,1)S(1)}, u32[]{:S(2)}, u32[]{:S(2)}) %collective-permute-start.4) | collective-permute-done | bytes 589856 | tf_op jit(solution)/shard_map/ppermute | solution.py:38
  147.9 32.7 %all_to_all.46 = bf16[16,64,896]{2,1,0:T(8,128)(2,1)S(1)} all-to-all(bf16[16,64,896]{2,1,0:T(8,128)(2,1)S(1)} %broadcast_in_dim.28), channel_id=1, replica_groups=mesh['xh'=2,'xl'=2,'zl'=2,'zh'=2,'y'=4,'c'=2] {'xl','zh','y'}, dimensions={0} | all-to-all | bytes 3670016 | tf_op jit(solution)/shard_map/all_to_all | solution.py:30
  180.6 2.1 collective-permute-start.5
  182.7 6.1 %widen.2.refs_3_ = bf16[4,2,128,1280]{3,2,1,0:T(8,128)(2,1)} custom-call(s32[3]{0:T(128)S(1)} %pad_add_fusion.ids_ref, bf16[2,8,64,896]{3,2,1,0:T(8,128)(2,1)S(1)} %bitcast.36, bf16[896,1152]{1,0:T(8,128)(2,1)S(1)} %copy-done.1, bf16[384,1152]{1,0:T(8,128)(2,1)} %collective-permute-done.refs_0_, bf16[256,1152]{1,0:T(8,128)(2,1)S(1)} %copy-done.10, ...), custom_call_target="tpu_custom_call" | custom-call | tf_op jit(solution)/shard_map/widen/pallas_call | solution.py:221
  188.9 6.1 %widen.3 = bf16[4,2,128,1280]{3,2,1,0:T(8,128)(2,1)} custom-call(s32[3]{0:T(128)S(1)} %pad_add_fusion.ids_ref, bf16[2,8,64,896]{3,2,1,0:T(8,128)(2,1)S(1)} %collective-permute-done.5.rows_ref, bf16[896,1152]{1,0:T(8,128)(2,1)S(1)} %copy-done.1, bf16[384,1152]{1,0:T(8,128)(2,1)} %collective-permute-done.refs_0_, ...), custom_call_target="tpu_custom_call", output_to_operand_aliasing={{}: (6, {})} | custom-call | tf_op jit(solution)/shard_map/widen/pallas_call | solution.py:221
  195.0 35.6 %all_to_all.47 = bf16[4,256,1280]{2,1,0:T(8,128)(2,1)S(1)} all-to-all(bf16[4,256,1280]{2,1,0:T(8,128)(2,1)} %bitcast.43), channel_id=1, replica_groups=mesh['xh'=2,'xl'=2,'zl'=2,'zh'=2,'y'=4,'c'=2] {'xh','zl'}, dimensions={0} | all-to-all | bytes 5242880 | tf_op jit(solution)/shard_map/all_to_all | solution.py:30
  231.8 18.2 %all_to_all.48 = bf16[4,256,576]{1,2,0:T(8,128)(2,1)} all-to-all(bf16[4,256,576]{1,2,0:T(8,128)(2,1)S(1)} %broadcast_in_dim.29), channel_id=1, replica_groups=mesh['xh'=2,'xl'=2,'zl'=2,'zh'=2,'y'=4,'c'=2] {'xh','zl'}, dimensions={0} | all-to-all | bytes 2359296 | tf_op jit(solution)/shard_map/all_to_all | solution.py:30
  249.9 1.8 copy.33
  251.7 3.9 %project.6 = bf16[2,512,896]{2,1,0:T(8,128)(2,1)S(1)} custom-call(s32[3]{0:T(128)S(1)} %pad_add_fusion.ids_ref, bf16[4,2,128,576]{3,2,1,0:T(8,128)(2,1)S(1)} %bitcast.29, bf16[576,896]{1,0:T(8,128)(2,1)S(1)} %copy-done.3, bf16[576,896]{1,0:T(8,128)(2,1)} %collective-permute-done.3.refs_1_), custom_call_target="tpu_custom_call" | custom-call | tf_op jit(solution)/shard_map/project/pallas_call | solution.py:172
  255.6 3.1 %collective-permute-start.6 = (bf16[2,512,896]{2,1,0:T(8,128)(2,1)S(1)}, bf16[2,512,896]{2,1,0:T(8,128)(2,1)S(1)}, u32[]{:S(2)}, u32[]{:S(2)}) collective-permute-start(bf16[2,512,896]{2,1,0:T(8,128)(2,1)S(1)} %project.6), channel_id=1, source_target_pairs={{0,1},{1,0},{2,3},{3,2},{4,5},{5,4},{6,7},{7,6},{8,9},{9,8},{10,11... | collective-permute-start | bytes 5505032 | tf_op jit(solution)/shard_map/ppermute | solution.py:38
  258.7 3.4 %collective-permute-done.6.refs_2_ = bf16[2,512,896]{2,1,0:T(8,128)(2,1)S(1)} collective-permute-done((bf16[2,512,896]{2,1,0:T(8,128)(2,1)S(1)}, bf16[2,512,896]{2,1,0:T(8,128)(2,1)S(1)}, u32[]{:S(2)}, u32[]{:S(2)}) %collective-permute-start.6) | collective-permute-done | bytes 1835040 | tf_op jit(solution)/shard_map/ppermute | solution.py:38
  262.1 1.3 copy-done.17
  263.4 4.2 %project.7 = bf16[2,512,896]{2,1,0:T(8,128)(2,1)S(1)} custom-call(s32[3]{0:T(128)S(1)} %pad_add_fusion.ids_ref, bf16[4,2,128,576]{3,2,1,0:T(8,128)(2,1)S(1)} %bitcast.30, bf16[576,896]{1,0:T(8,128)(2,1)S(1)} %copy-done.3, bf16[576,896]{1,0:T(8,128)(2,1)} %collective-permute-done.3.refs_1_, bf16[2,512,896]{2,1,0:T(8,128)(2,1)} %copy-done.17), custom_call_target="tpu_custom_call" | custom-call | tf_op jit(solution)/shard_map/project/pallas_call | solution.py:172
  267.6 1.3 copy-done.4
  268.9 3.8 %all-to-all-start.8 = ((bf16[16,64,896]{2,1,0:T(8,128)(2,1)}), bf16[16,64,896]{2,1,0:T(8,128)(2,1)S(1)}, u32[]{:S(2)}, u32[]{:S(2)}) async-start(bf16[16,64,896]{2,1,0:T(8,128)(2,1)} %bitcast.34), calls=%async_computation.8 | async-start | bytes 3670016 | tf_op jit(solution)/shard_map/all_to_all | solution.py:30
  273.5 26.5 %all-to-all-done.8 = bf16[16,64,896]{2,1,0:T(8,128)(2,1)S(1)} async-done(((bf16[16,64,896]{2,1,0:T(8,128)(2,1)}), bf16[16,64,896]{2,1,0:T(8,128)(2,1)S(1)}, u32[]{:S(2)}, u32[]{:S(2)}) %all-to-all-start.8) | async-done | bytes 1835040 | tf_op jit(solution)/shard_map/all_to_all | solution.py:30
  300.0 0.9 convert_reduce_fusion.1
  301.0 1.1 reduce_sum.45
  (70 shorter events, 9.6 us)
Async XLA Ops:
  0.0 67.1 %copy-start = (bf16[8,512,128]{2,1,0:T(8,128)(2,1)S(1)}, bf16[8,512,128]{2,1,0:T(8,128)(2,1)}, u32[]{:S(2)}) copy-start(bf16[8,512,128]{2,1,0:T(8,128)(2,1)} %param.19) | copy-start | bytes 3145732
  0.8 5.2 %copy-start.22 = (s32[1,16]{1,0:T(1,128)S(1)}, s32[1,16]{1,0:T(1,128)}, u32[]{:S(2)}) copy-start(s32[1,16]{1,0:T(1,128)} %param.15) | copy-start | bytes 196
  0.8 6.7 %copy-start.2 = (bf16[4,256,576]{1,2,0:T(8,128)(2,1)S(1)}, bf16[4,256,576]{1,2,0:T(8,128)(2,1)}, u32[]{:S(2)}) copy-start(bf16[4,256,576]{1,2,0:T(8,128)(2,1)} %param.13) | copy-start | bytes 3538948
  2.7 23.0 %copy-start.12 = (s32[1,16]{1,0:T(1,128)S(1)}, s32[1,16]{1,0:T(1,128)}, u32[]{:S(2)}) copy-start(s32[1,16]{1,0:T(1,128)} %param.16) | copy-start | bytes 196
  3.9 27.5 %copy-start.21 = (bf16[2,4,576]{2,1,0:T(4,128)(2,1)S(1)}, bf16[2,4,576]{2,1,0:T(4,128)(2,1)}, u32[]{:S(2)}) copy-start(bf16[2,4,576]{2,1,0:T(4,128)(2,1)} %param.18) | copy-start | bytes 27652
  3.9 40.1 %collective-permute-start = (bf16[384,1152]{1,0:T(8,128)(2,1)}, bf16[384,1152]{1,0:T(8,128)(2,1)}, u32[]{:S(2)}, u32[]{:S(2)}) collective-permute-start(bf16[384,1152]{1,0:T(8,128)(2,1)} %pad_maximum_fusion.1), channel_id=1, source_target_pairs={{0,32},{32,0},{1,33},{33,1},{2,34},{34,2},{3,35},{35,3},{4,36},{36... | collective-permute-start | bytes 2654216 | tf_op jit(solution)/shard_map/ppermute | solution.py:38
  7.5 24.3 %copy-start.11 = (s32[4]{0:T(128)S(1)}, s32[4]{0:T(128)}, u32[]{:S(2)}) copy-start(s32[4]{0:T(128)} %lengths_ref.3) | copy-start | bytes 52
  27.0 13.6 %all-to-all-start.1 = ((bf16[16,36,256]{2,1,0:T(8,128)(2,1)}), bf16[16,36,256]{2,1,0:T(8,128)(2,1)S(1)}, u32[]{:S(2)}, u32[]{:S(2)}) async-start(bf16[16,36,256]{2,1,0:T(8,128)(2,1)} %route.1), calls=%async_computation.1 | async-start | bytes 655360 | tf_op jit(solution)/shard_map/all_to_all | solution.py:30
  31.8 1.3 copy-start.6
  33.0 4.7 %copy-start.20 = (bf16[896]{0:T(1024)(128)(2,1)S(1)}, bf16[896]{0:T(1024)(128)(2,1)}, u32[]{:S(2)}) copy-start(bf16[896]{0:T(1024)(128)(2,1)} %param.22) | copy-start | bytes 5380
  40.6 1.3 copy-start.7
  44.0 23.2 %all-to-all-start.2 = ((bf16[16,4,16,512]{3,2,1,0:T(8,128)(2,1)}), bf16[16,4,16,512]{3,2,1,0:T(8,128)(2,1)S(1)}, u32[]{:S(2)}, u32[]{:S(2)}) async-start(bf16[16,4,16,512]{3,2,1,0:T(8,128)(2,1)} %again.1), calls=%async_computation.2 | async-start | bytes 2097152 | tf_op jit(solution)/shard_map/all_to_all | solution.py:30
  52.2 14.9 %collective-permute-start.1 = (bf16[256,1152]{1,0:T(8,128)(2,1)}, bf16[256,1152]{1,0:T(8,128)(2,1)S(1)}, u32[]{:S(2)}, u32[]{:S(2)}) collective-permute-start(bf16[256,1152]{1,0:T(8,128)(2,1)} %pad_maximum_fusion.2), channel_id=1, source_target_pairs={{0,32},{32,0},{1,33},{33,1},{2,34},{34,2},{3,35},{35,3},{4,36},{36... | collective-permute-start | bytes 1769480 | tf_op jit(solution)/shard_map/ppermute | solution.py:38
  67.1 2.7 copy-start.9
  69.9 34.2 %all-to-all-start.3 = ((bf16[8,128,1024]{2,1,0:T(8,128)(2,1)}), bf16[8,128,1024]{2,1,0:T(8,128)(2,1)S(1)}, u32[]{:S(2)}, u32[]{:S(2)}) async-start(bf16[8,128,1024]{2,1,0:T(8,128)(2,1)} %broadcast_in_dim.14), calls=%async_computation.3 | async-start | bytes 4194304 | tf_op jit(solution)/shard_map/all_to_all | solution.py:30
  74.1 3.1 %copy-start.18 = (bf16[256,576]{1,0:T(8,128)(2,1)S(1)}, bf16[256,576]{1,0:T(8,128)(2,1)}, u32[]{:S(2)}) copy-start(bf16[256,576]{1,0:T(8,128)(2,1)} %get-tuple-element.36) | copy-start | bytes 884740
  104.1 1.5 copy-start.5
  107.7 4.0 %collective-permute-start.2 = (bf16[1,512,896]{2,1,0:T(8,128)(2,1)S(1)}, bf16[1,512,896]{2,1,0:T(8,128)(2,1)S(1)}, u32[]{:S(2)}, u32[]{:S(2)}) collective-permute-start(bf16[1,512,896]{2,1,0:T(8,128)(2,1)S(1)} %project.4), channel_id=1, source_target_pairs={{0,1},{1,0},{2,3},{3,2},{4,5},{5,4},{6,7},{7,6},{8,9},{9,8},{10,11... | collective-permute-start | bytes 2752520 | tf_op jit(solution)/shard_map/ppermute | solution.py:38
  109.6 37.2 %collective-permute-start.3 = (bf16[576,896]{1,0:T(8,128)(2,1)}, bf16[576,896]{1,0:T(8,128)(2,1)}, u32[]{:S(2)}, u32[]{:S(2)}) collective-permute-start(bf16[576,896]{1,0:T(8,128)(2,1)} %get-tuple-element.19), channel_id=1, source_target_pairs={{0,32},{32,0},{1,33},{33,1},{2,34},{34,2},{3,35},{35,3},{4,36},{36... | collective-permute-start | bytes 3096584 | tf_op jit(solution)/shard_map/ppermute | solution.py:38
  113.8 1.0 copy-start.8
  114.7 32.1 %all-to-all-start.4 = ((bf16[8,64,896]{2,1,0:T(8,128)(2,1)}), bf16[8,64,896]{2,1,0:T(8,128)(2,1)S(1)}, u32[]{:S(2)}, u32[]{:S(2)}) async-start(bf16[8,64,896]{2,1,0:T(8,128)(2,1)} %bitcast.41), calls=%async_computation.4 | async-start | bytes 1835008 | tf_op jit(solution)/shard_map/all_to_all | solution.py:30
  121.7 25.1 %collective-permute-start.4 = (bf16[256,1152]{1,0:T(8,128)(2,1)}, bf16[256,1152]{1,0:T(8,128)(2,1)S(1)}, u32[]{:S(2)}, u32[]{:S(2)}) collective-permute-start(bf16[256,1152]{1,0:T(8,128)(2,1)} %pad_maximum_fusion.3), channel_id=1, source_target_pairs={{0,32},{32,0},{1,33},{33,1},{2,34},{34,2},{3,35},{35,3},{4,36},{36... | collective-permute-start | bytes 1769480 | tf_op jit(solution)/shard_map/ppermute | solution.py:38
  122.6 0.7 copy-start.13
  146.9 0.7 copy-start.15
  147.9 34.8 %copy-start.1 = (bf16[896,1152]{1,0:T(8,128)(2,1)S(1)}, bf16[896,1152]{1,0:T(8,128)(2,1)}, u32[]{:S(2)}) copy-start(bf16[896,1152]{1,0:T(8,128)(2,1)} %pad_maximum_fusion.kept_ref) | copy-start | bytes 6193156
  147.9 34.8 %copy-start.10 = (bf16[256,1152]{1,0:T(8,128)(2,1)S(1)}, bf16[256,1152]{1,0:T(8,128)(2,1)}, u32[]{:S(2)}) copy-start(bf16[256,1152]{1,0:T(8,128)(2,1)} %copy-done.9) | copy-start | bytes 1769476
  180.6 8.2 %collective-permute-start.5 = (bf16[2,8,64,896]{3,2,1,0:T(8,128)(2,1)S(1)}, bf16[2,8,64,896]{3,2,1,0:T(8,128)(2,1)S(1)}, u32[]{:S(2)}, u32[]{:S(2)}) collective-permute-start(bf16[2,8,64,896]{3,2,1,0:T(8,128)(2,1)S(1)} %bitcast.35), channel_id=1, source_target_pairs={{0,1},{1,0},{2,3},{3,2},{4,5},{5,4},{6,7},{7,6},{8,9},{9,8},{10,11... | collective-permute-start | bytes 5505032 | tf_op jit(solution)/shard_map/ppermute | solution.py:38
  249.9 1.8 copy-start.3
  255.6 6.5 %collective-permute-start.6 = (bf16[2,512,896]{2,1,0:T(8,128)(2,1)S(1)}, bf16[2,512,896]{2,1,0:T(8,128)(2,1)S(1)}, u32[]{:S(2)}, u32[]{:S(2)}) collective-permute-start(bf16[2,512,896]{2,1,0:T(8,128)(2,1)S(1)} %project.6), channel_id=1, source_target_pairs={{0,1},{1,0},{2,3},{3,2},{4,5},{5,4},{6,7},{7,6},{8,9},{9,8},{10,11... | collective-permute-start | bytes 5505032 | tf_op jit(solution)/shard_map/ppermute | solution.py:38
  262.1 1.3 copy-start.17
  267.6 1.3 copy-start.4
  268.9 3.9 %copy-start.16 = (f32[64,896]{1,0:T(8,128)S(1)}, f32[64,896]{1,0:T(8,128)}, u32[]{:S(2)}) copy-start(f32[64,896]{1,0:T(8,128)} %copy-done.15) | copy-start | bytes 688132
  268.9 31.2 %all-to-all-start.8 = ((bf16[16,64,896]{2,1,0:T(8,128)(2,1)}), bf16[16,64,896]{2,1,0:T(8,128)(2,1)S(1)}, u32[]{:S(2)}, u32[]{:S(2)}) async-start(bf16[16,64,896]{2,1,0:T(8,128)(2,1)} %bitcast.34), calls=%async_computation.8 | async-start | bytes 3670016 | tf_op jit(solution)/shard_map/all_to_all | solution.py:30
  272.7 29.3 %copy-start.14 = (f32[2,32,896]{2,1,0:T(8,128)S(1)}, f32[2,32,896]{2,1,0:T(8,128)}, u32[]{:S(2)}) copy-start(f32[2,32,896]{2,1,0:T(8,128)} %copy-done.13) | copy-start | bytes 688132
  273.5 28.5 %copy-start.19 = (f32[32,2,896]{2,1,0:T(2,128)S(1)}, f32[32,2,896]{2,1,0:T(2,128)}, u32[]{:S(2)}) copy-start(f32[32,2,896]{2,1,0:T(2,128)} %reduce_sum.42) | copy-start | bytes 688132

commit v4 on v3

--- a/solution.py
+++ b/solution.py
@@ -19,7 +19,7 @@
 N_ZY = 8
 N_FOUR = 4
 SWAP = [(0, 1), (1, 0)]
-CUTS = (0, 384, 640, 896)
+CUTS = (0, 640, 896)
 TILE = 384
 bf16 = jnp.bfloat16
 f32 = jnp.float32
@@ -267,7 +267,10 @@
     own_slot = jnp.sum(jnp.where(lanes == member, move_slot[0], 0))
     ids = jnp.stack([own_slot, core, pair]).astype(jnp.int32)
     cache_t = cache.transpose(0, 2, 1)
-    pieces = exchange(leave(ids, cache_t), TP)
+    leaving, gate_weight, up_weight = lax.optimization_barrier(
+        (leave(ids, cache_t), gate_weight, up_weight)
+    )
+    pieces = exchange(leaving, TP)
 
     gain = norm_gain.astype(f32)[:, None]
 
@@ -301,15 +304,9 @@
     value_heads = value_heads.reshape(-1, heads * value_width)
 
     gathered = spread(value_heads, DP, N_DP).reshape(N_DP, 2, chunk, -1)
-    down_sent = lax.dynamic_slice_in_dim(down_weight, (1 - pair) * part, part, 0)
-    gathered, sent[2], down_sent = lax.optimization_barrier((gathered, sent[2], down_sent))
-    down_kept = lax.dynamic_slice_in_dim(down_weight, pair * part, part, 0)
-    down_came = swap(down_sent, "xl")
-    came.append(swap(sent[2], "xl"))
     away = swap(project(ids, lambda i: 1 - i[1], gathered, [out_proj]), "c")
     total = project(ids, lambda i: i[1], gathered, [out_proj], away)
     parts = exchange(total.reshape(N_ZY, chunk, -1), ZY)
-    parts, down_came, came[2] = lax.optimization_barrier((parts, down_came, came[2]))
     residue = lax.dynamic_slice_in_dim(residual, member * rows_out, rows_out, 1)
     residue = residue.transpose(1, 0, 2).reshape(chunk, -1)
     hidden = residue.astype(f32) + jnp.sum(parts.astype(f32), axis=0)
@@ -324,12 +321,13 @@
     squares = sums[:, units] + sums[:, units + 1]
     inverse = lax.rsqrt(squares / D + norm_eps)[:, None]
     active = jax.nn.silu(sums[:, :part] * inverse) * (sums[:, part:units] * inverse)
-    active = spread(active.astype(bf16), FOUR, N_FOUR).reshape(N_FOUR, 2, 2 * chunk, part)
-
-    weights = [down_kept, down_came]
-    away = swap(project(ids, lambda i: 1, active, weights), "c")
-    total = project(ids, lambda i: 0, active, weights, away)
-    parts = exchange(total.reshape(2 * N_ZY, chunk, -1), PAIR)
+    active = active.astype(bf16).reshape(2, 2 * chunk, part)
+    active = spread(active, DP, N_DP).reshape(2, 2, 2, 2, 2 * chunk, part)
+    active = jnp.concatenate([active[:, 0], active[:, 1]], axis=-1)
+    active = active.reshape(N_FOUR, 2, 2 * chunk, units)
+    away = swap(project(ids, lambda i: 1, active, [down_weight]), "c")
+    total = project(ids, lambda i: 0, active, [down_weight], away)
+    parts = exchange(total.reshape(N_ZY, chunk, -1), ZY)
     result = (hidden + jnp.sum(parts.astype(f32), axis=0)).astype(bf16)
     return result.reshape(rows_out, steps, -1).transpose(1, 0, 2)
 

time: 304 us -> 290 us (0.954)
  waiting for transfers between devices: 93.3 us -> 45.4 us
  blocking collectives: 104 us -> 142 us
    all_to_all x4 -> x5, blocking collectives: 104 us -> 142 us  [exchange(): return lax.all_to_all(blocks, axes, 0, 0, tiled=True)]
    all_to_all x5 -> x4, waiting for transfers between devices: 55.3 us -> 31.1 us  [exchange(): return lax.all_to_all(blocks, axes, 0, 0, tiled=True)]
    ppermute x7 -> x5, waiting for transfers between devices: 38 us -> 14.4 us  [swap(): return lax.ppermute(block, axis, SWAP)]
    slice x0 -> x3, local copies, waits for them, and re-layouts: none -> 4.34 us  [local(): active = jnp.concatenate([active[:, 0], active[:, 1]], axis=-1)]
    all_to_all x5 -> x4, starting transfers between devices: 23.8 us -> 20.6 us  [exchange(): return lax.all_to_all(blocks, axes, 0, 0, tiled=True)]
    dynamic_slice x1 -> x0, local copies, waits for them, and re-layouts: 3.05 us -> none  [local(): down_kept = lax.dynamic_slice_in_dim(down_weight, pair * part, part, 0)]
    unnamed x48 -> x38, local copies, waits for them, and re-layouts: 9.47 us -> 7.43 us
    ppermute x7 -> x5, starting transfers between devices: 9.41 us -> 10.4 us  [swap(): return lax.ppermute(block, axis, SWAP)]
  transfers between devices with their start and end apart: 12 -> 9, of which waited for: 7 -> 6; matrix products, arithmetic and copies ran while one was open for 6% -> 3% of each run, Pallas kernels for 6% -> 5%
where the time goes in v4:
time: 290 us; the launch traced here: 288 us
  blocking collectives  142 us (49%)
  waiting for transfers between devices  45.4 us (16%)
  Pallas kernels  32.3 us (11%)
  starting transfers between devices  31 us (11%)
  other arithmetic  17.9 us (6%)
  local copies, waits for them, and re-layouts  17.6 us (6%)
    all_to_all x5, blocking collectives, exchange(): return lax.all_to_all(blocks, axes, 0, 0, tiled=True)  142 us
    all_to_all x4, waiting for transfers between devices, exchange(): return lax.all_to_all(blocks, axes, 0, 0, tiled=True)  31.1 us
    all_to_all x4, starting transfers between devices, exchange(): return lax.all_to_all(blocks, axes, 0, 0, tiled=True)  20.6 us
    ppermute x5, waiting for transfers between devices, swap(): return lax.ppermute(block, axis, SWAP)  14.4 us
    pallas_call x2, Pallas kernels, widen(): pl.pallas_call(body, grid_spec=pltpu.PrefetchScalarGridSpec(num_scalar_pr...  13 us
    pallas_call x4, Pallas kernels, project(): pl.pallas_call(body, grid_spec=pltpu.PrefetchScalarGridSpec(num_scalar_pr...  10.6 us
    ppermute x5, starting transfers between devices, swap(): return lax.ppermute(block, axis, SWAP)  10.4 us
    unnamed x38, local copies, waits for them, and re-layouts  7.43 us
  transfers between devices with their start and end apart: 9, of which 6 were waited for; matrix products, arithmetic and copies ran while one was open for 3% of the time, Pallas kernels for 5%

profile of v4, /device:TPU:1, one launch (start us, length us, event | category | flops | bytes accessed | tf_op | source)
XLA Modules:
  0.0 288.3 jit_solution(12093276657752192519)
XLA Ops:
  0.8 1.3 fusion.8
  2.8 1.3 copy-done.2
  4.6 2.4 multiply_convert_fusion.3
  7.1 1.6 pad_maximum_fusion.2
  8.7 2.1 collective-permute-start
  10.8 17.7 %all_to_all.45.in_ref = bf16[16,36,256]{2,1,0:T(8,128)(2,1)S(1)} all-to-all(bf16[16,36,256]{2,1,0:T(8,128)(2,1)S(1)} %leave.1), channel_id=1, replica_groups=mesh['xh'=2,'xl'=2,'zl'=2,'zh'=2,'y'=4,'c'=2] {'zh','y','c'}, dimensions={0} | all-to-all | bytes 589824 | tf_op jit(solution)/shard_map/all_to_all | solution.py:30
  28.5 1.3 route.1
  29.8 4.3 %all-to-all-start.1 = ((bf16[16,36,256]{2,1,0:T(8,128)(2,1)}), bf16[16,36,256]{2,1,0:T(8,128)(2,1)S(1)}, u32[]{:S(2)}, u32[]{:S(2)}) async-start(bf16[16,36,256]{2,1,0:T(8,128)(2,1)} %route.1), calls=%async_computation.1 | async-start | bytes 655360 | tf_op jit(solution)/shard_map/all_to_all | solution.py:30
  34.5 1.3 copy-done.6
  35.8 4.7 %attend.1.refs_1_ = bf16[16,4,16,512]{3,2,1,0:T(8,128)(2,1)} custom-call(s32[3]{0:T(128)S(1)} %pad_add_fusion.ids_ref, s32[4]{0:T(128)S(1)} %copy-done.9, bf16[4,576,256]{2,1,0:T(8,128)(2,1)S(1)} %bitcast.33, bf16[4,576,2]{2,1,0:T(8,128)(2,1)S(1)} %bitcast.37, bf16[2,4,576,128]{3,2,1,0:T(8,128)(2,1)S(1)} %bitcast.39), custom_call_target="tpu_custom_call" | custom-call | tf_op jit(solution)/shard_map/attend/pallas_call | solution.py:129
  40.5 2.8 all-to-all-done.1.refs_0_
  43.3 1.3 copy-done.7
  44.6 2.1 again.1
  46.7 5.6 %all-to-all-start.2 = ((bf16[16,4,16,512]{3,2,1,0:T(8,128)(2,1)}), bf16[16,4,16,512]{3,2,1,0:T(8,128)(2,1)}, u32[]{:S(2)}, u32[]{:S(2)}) async-start(bf16[16,4,16,512]{3,2,1,0:T(8,128)(2,1)} %again.1), calls=%async_computation.2 | async-start | bytes 2097152 | tf_op jit(solution)/shard_map/all_to_all | solution.py:30
  52.3 1.4 multiply_convert_fusion.5
  53.8 1.0 pad_maximum_fusion.3
  54.8 1.3 collective-permute-start.1
  56.1 2.9 %multiply_convert_fusion.1 = (bf16[896,576]{1,0:T(8,128)(2,1)S(1)}, bf16[896,576]{1,0:T(8,128)(2,1)S(1)}) fusion(f32[896]{0:T(1024)S(1)} %convert_element_type.73, bf16[896,1152]{1,0:T(8,128)(2,1)S(1)} %copy-done.11, s32[]{:T(128)S(6)} %select_n.20, bf16[896,1152]{1,0:T(8,128)(2,1)} %param.24), kind=kLoop, calls=%fused_computation.3 | loop fusion | flops 3096576 | bytes 4132356 | tf_op jit(solution)/shard_map/convert.5
  59.7 10.2 %collective-permute-done.1.refs_1_ = bf16[256,1152]{1,0:T(8,128)(2,1)} collective-permute-done((bf16[256,1152]{1,0:T(8,128)(2,1)}, bf16[256,1152]{1,0:T(8,128)(2,1)}, u32[]{:S(2)}, u32[]{:S(2)}) %collective-permute-start.1) | collective-permute-done | bytes 589856 | tf_op jit(solution)/shard_map/ppermute | solution.py:38
  69.9 2.1 convolution_convert_fusion
  72.8 1.2 broadcast_in_dim.28
  74.1 29.5 %all_to_all.46 = bf16[8,128,1024]{2,1,0:T(8,128)(2,1)S(1)} all-to-all(bf16[8,128,1024]{2,1,0:T(8,128)(2,1)S(1)} %broadcast_in_dim.28), channel_id=1, replica_groups=mesh['xh'=2,'xl'=2,'zl'=2,'zh'=2,'y'=4,'c'=2] {'xh','xl','zl'}, dimensions={0} | all-to-all | bytes 4194304 | tf_op jit(solution)/shard_map/all_to_all | solution.py:30
  103.6 2.1 project.4
  105.7 2.5 collective-permute-start.2
  108.2 2.1 collective-permute-done.2.refs_1_
  110.3 2.1 project.5
  112.4 0.9 copy-done.8
  113.4 6.9 %all-to-all-start.4 = ((bf16[8,64,896]{2,1,0:T(8,128)(2,1)}), bf16[8,64,896]{2,1,0:T(8,128)(2,1)}, u32[]{:S(2)}, u32[]{:S(2)}) async-start(bf16[8,64,896]{2,1,0:T(8,128)(2,1)} %bitcast.41), calls=%async_computation.4 | async-start | bytes 1835008 | tf_op jit(solution)/shard_map/all_to_all | solution.py:30
  120.3 0.9 dynamic-slice_convert_fusion
  122.8 1.1 reshape.55
  123.9 12.5 %all-to-all-done.4 = bf16[8,64,896]{2,1,0:T(8,128)(2,1)} async-done(((bf16[8,64,896]{2,1,0:T(8,128)(2,1)}), bf16[8,64,896]{2,1,0:T(8,128)(2,1)}, u32[]{:S(2)}, u32[]{:S(2)}) %all-to-all-start.4) | async-done | bytes 917536 | tf_op jit(solution)/shard_map/all_to_all | solution.py:30
  136.4 1.3 convert_reduce_fusion.2
  138.7 28.4 %all_to_all.47 = bf16[16,64,896]{2,1,0:T(8,128)(2,1)S(1)} all-to-all(bf16[16,64,896]{2,1,0:T(8,128)(2,1)S(1)} %broadcast_in_dim.29), channel_id=1, replica_groups=mesh['xh'=2,'xl'=2,'zl'=2,'zh'=2,'y'=4,'c'=2] {'xl','zh','y'}, dimensions={0} | all-to-all | bytes 3670016 | tf_op jit(solution)/shard_map/all_to_all | solution.py:30
  167.1 1.9 collective-permute-start.3
  169.0 6.5 %widen.2.refs_2_ = bf16[4,2,128,1280]{3,2,1,0:T(8,128)(2,1)} custom-call(s32[3]{0:T(128)S(1)} %pad_add_fusion.ids_ref, bf16[2,8,64,896]{3,2,1,0:T(8,128)(2,1)S(1)} %bitcast.36, bf16[896,1152]{1,0:T(8,128)(2,1)S(1)} %pad_maximum_fusion.1.kept_ref, bf16[640,1152]{1,0:T(8,128)(2,1)} %collective-permute-done.refs_0_, ...), custom_call_target="tpu_custom_call" | custom-call | tf_op jit(solution)/shard_map/widen/pallas_call | solution.py:221
  175.5 6.5 %widen.3 = bf16[4,2,128,1280]{3,2,1,0:T(8,128)(2,1)} custom-call(s32[3]{0:T(128)S(1)} %pad_add_fusion.ids_ref, bf16[2,8,64,896]{3,2,1,0:T(8,128)(2,1)S(1)} %collective-permute-done.3.rows_ref, bf16[896,1152]{1,0:T(8,128)(2,1)S(1)} %pad_maximum_fusion.1.kept_ref, bf16[640,1152]{1,0:T(8,128)(2,1)} %collective-permute-done.refs_0_, ...), custom_call_target="tpu_custom_call", output_to_operand_aliasing={{}: (5, {})} | custom-call | tf_op jit(solution)/shard_map/widen/pallas_call | solution.py:221
  182.0 35.6 %all_to_all.48 = bf16[4,256,1280]{2,1,0:T(8,128)(2,1)S(1)} all-to-all(bf16[4,256,1280]{2,1,0:T(8,128)(2,1)} %bitcast.43), channel_id=1, replica_groups=mesh['xh'=2,'xl'=2,'zl'=2,'zh'=2,'y'=4,'c'=2] {'xh','zl'}, dimensions={0} | all-to-all | bytes 5242880 | tf_op jit(solution)/shard_map/all_to_all | solution.py:30
  219.2 30.5 %all_to_all.49 = bf16[8,2,128,576]{2,3,1,0:T(8,128)(2,1)S(1)} all-to-all(bf16[8,2,128,576]{2,3,1,0:T(8,128)(2,1)S(1)} %broadcast_in_dim.31), channel_id=1, replica_groups=mesh['xh'=2,'xl'=2,'zl'=2,'zh'=2,'y'=4,'c'=2] {'xh','xl','zl'}, dimensions={0} | all-to-all | bytes 4718592 | tf_op jit(solution)/shard_map/all_to_all | solution.py:30
  249.8 1.2 fusion.9
  251.0 1.7 copy.35
  252.7 1.5 copy.36
  254.1 2.3 pad_maximum_fusion.rows_ref
  256.4 2.3 project.6
  258.8 2.5 collective-permute-start.4
  261.3 2.1 collective-permute-done.4.refs_1_
  263.4 4.1 %project.7 = bf16[1,512,896]{2,1,0:T(8,128)(2,1)} custom-call(s32[3]{0:T(128)S(1)} %pad_add_fusion.ids_ref, bf16[4,2,128,1152]{3,2,1,0:T(8,128)(2,1)} %copy-done.1, bf16[1152,896]{1,0:T(8,128)(2,1)S(1)} %copy-done.4, bf16[1,512,896]{2,1,0:T(8,128)(2,1)S(1)} %collective-permute-done.4.refs_1_), custom_call_target="tpu_custom_call" | custom-call | tf_op jit(solution)/shard_map/project/pallas_call | solution.py:172
  267.5 3.7 %all-to-all-start.8 = ((bf16[8,64,896]{2,1,0:T(8,128)(2,1)}), bf16[8,64,896]{2,1,0:T(8,128)(2,1)S(1)}, u32[]{:S(2)}, u32[]{:S(2)}) async-start(bf16[8,64,896]{2,1,0:T(8,128)(2,1)} %bitcast.20), calls=%async_computation.8 | async-start | bytes 1835008 | tf_op jit(solution)/shard_map/all_to_all | solution.py:30
  271.3 15.8 %all-to-all-done.8 = bf16[8,64,896]{2,1,0:T(8,128)(2,1)S(1)} async-done(((bf16[8,64,896]{2,1,0:T(8,128)(2,1)}), bf16[8,64,896]{2,1,0:T(8,128)(2,1)S(1)}, u32[]{:S(2)}, u32[]{:S(2)}) %all-to-all-start.8) | async-done | bytes 917536 | tf_op jit(solution)/shard_map/all_to_all | solution.py:30
  (56 shorter events, 9.4 us)
Async XLA Ops:
  0.0 69.9 %copy-start = (bf16[8,512,128]{2,1,0:T(8,128)(2,1)S(1)}, bf16[8,512,128]{2,1,0:T(8,128)(2,1)}, u32[]{:S(2)}) copy-start(bf16[8,512,128]{2,1,0:T(8,128)(2,1)} %param.19) | copy-start | bytes 3145732
  2.8 1.3 copy-start.2
  7.1 21.4 %copy-start.10 = (s32[1,16]{1,0:T(1,128)S(1)}, s32[1,16]{1,0:T(1,128)}, u32[]{:S(2)}) copy-start(s32[1,16]{1,0:T(1,128)} %param.16) | copy-start | bytes 196
  7.1 27.0 %copy-start.16 = (bf16[896]{0:T(1024)(128)(2,1)S(1)}, bf16[896]{0:T(1024)(128)(2,1)}, u32[]{:S(2)}) copy-start(bf16[896]{0:T(1024)(128)(2,1)} %param.22) | copy-start | bytes 5380
  7.1 27.0 %copy-start.17 = (bf16[2,4,576]{2,1,0:T(4,128)(2,1)S(1)}, bf16[2,4,576]{2,1,0:T(4,128)(2,1)}, u32[]{:S(2)}) copy-start(bf16[2,4,576]{2,1,0:T(4,128)(2,1)} %param.18) | copy-start | bytes 27652
  8.7 25.8 %copy-start.3 = (bf16[4,256,576]{1,2,0:T(8,128)(2,1)S(1)}, bf16[4,256,576]{1,2,0:T(8,128)(2,1)}, u32[]{:S(2)}) copy-start(bf16[4,256,576]{1,2,0:T(8,128)(2,1)} %param.13) | copy-start | bytes 3538948
  8.7 25.8 %copy-start.9 = (s32[4]{0:T(128)S(1)}, s32[4]{0:T(128)}, u32[]{:S(2)}) copy-start(s32[4]{0:T(128)} %lengths_ref.3) | copy-start | bytes 52
  8.7 38.0 %collective-permute-start = (bf16[640,1152]{1,0:T(8,128)(2,1)}, bf16[640,1152]{1,0:T(8,128)(2,1)}, u32[]{:S(2)}, u32[]{:S(2)}) collective-permute-start(bf16[640,1152]{1,0:T(8,128)(2,1)} %pad_maximum_fusion.2), channel_id=1, source_target_pairs={{0,32},{32,0},{1,33},{33,1},{2,34},{34,2},{3,35},{35,3},{4,36},{36... | collective-permute-start | bytes 4423688 | tf_op jit(solution)/shard_map/ppermute | solution.py:38
  29.8 13.6 %all-to-all-start.1 = ((bf16[16,36,256]{2,1,0:T(8,128)(2,1)}), bf16[16,36,256]{2,1,0:T(8,128)(2,1)S(1)}, u32[]{:S(2)}, u32[]{:S(2)}) async-start(bf16[16,36,256]{2,1,0:T(8,128)(2,1)} %route.1), calls=%async_computation.1 | async-start | bytes 655360 | tf_op jit(solution)/shard_map/all_to_all | solution.py:30
  34.5 1.3 copy-start.6
  43.3 1.3 copy-start.7
  46.7 5.6 %copy-start.11 = (bf16[896,1152]{1,0:T(8,128)(2,1)S(1)}, bf16[896,1152]{1,0:T(8,128)(2,1)}, u32[]{:S(2)}) copy-start(bf16[896,1152]{1,0:T(8,128)(2,1)} %param.23) | copy-start | bytes 6193156
  46.7 23.2 %all-to-all-start.2 = ((bf16[16,4,16,512]{3,2,1,0:T(8,128)(2,1)}), bf16[16,4,16,512]{3,2,1,0:T(8,128)(2,1)}, u32[]{:S(2)}, u32[]{:S(2)}) async-start(bf16[16,4,16,512]{3,2,1,0:T(8,128)(2,1)} %again.1), calls=%async_computation.2 | async-start | bytes 2097152 | tf_op jit(solution)/shard_map/all_to_all | solution.py:30
  54.8 15.1 %collective-permute-start.1 = (bf16[256,1152]{1,0:T(8,128)(2,1)}, bf16[256,1152]{1,0:T(8,128)(2,1)}, u32[]{:S(2)}, u32[]{:S(2)}) collective-permute-start(bf16[256,1152]{1,0:T(8,128)(2,1)} %pad_maximum_fusion.3), channel_id=1, source_target_pairs={{0,32},{32,0},{1,33},{33,1},{2,34},{34,2},{3,35},{35,3},{4,36},{36... | collective-permute-start | bytes 1769480 | tf_op jit(solution)/shard_map/ppermute | solution.py:38
  74.0 29.5 %copy-start.5 = (bf16[1024,896]{1,0:T(8,128)(2,1)S(1)}, bf16[1024,896]{1,0:T(8,128)(2,1)}, u32[]{:S(2)}) copy-start(bf16[1024,896]{1,0:T(8,128)(2,1)} %refs_0_.5) | copy-start | bytes 5505028
  105.7 4.6 %collective-permute-start.2 = (bf16[1,512,896]{2,1,0:T(8,128)(2,1)S(1)}, bf16[1,512,896]{2,1,0:T(8,128)(2,1)S(1)}, u32[]{:S(2)}, u32[]{:S(2)}) collective-permute-start(bf16[1,512,896]{2,1,0:T(8,128)(2,1)S(1)} %project.4), channel_id=1, source_target_pairs={{0,1},{1,0},{2,3},{3,2},{4,5},{5,4},{6,7},{7,6},{8,9},{9,8},{10,11... | collective-permute-start | bytes 2752520 | tf_op jit(solution)/shard_map/ppermute | solution.py:38
  112.4 1.0 copy-start.8
  113.4 23.0 %all-to-all-start.4 = ((bf16[8,64,896]{2,1,0:T(8,128)(2,1)}), bf16[8,64,896]{2,1,0:T(8,128)(2,1)}, u32[]{:S(2)}, u32[]{:S(2)}) async-start(bf16[8,64,896]{2,1,0:T(8,128)(2,1)} %bitcast.41), calls=%async_computation.4 | async-start | bytes 1835008 | tf_op jit(solution)/shard_map/all_to_all | solution.py:30
  121.2 0.7 copy-start.12
  137.7 0.7 copy-start.14
  167.1 8.4 %collective-permute-start.3 = (bf16[2,8,64,896]{3,2,1,0:T(8,128)(2,1)S(1)}, bf16[2,8,64,896]{3,2,1,0:T(8,128)(2,1)S(1)}, u32[]{:S(2)}, u32[]{:S(2)}) collective-permute-start(bf16[2,8,64,896]{3,2,1,0:T(8,128)(2,1)S(1)} %bitcast.35), channel_id=1, source_target_pairs={{0,1},{1,0},{2,3},{3,2},{4,5},{5,4},{6,7},{7,6},{8,9},{9,8},{10,11... | collective-permute-start | bytes 5505032 | tf_op jit(solution)/shard_map/ppermute | solution.py:38
  254.1 2.3 copy-start.4
  256.4 2.4 copy-start.1
  258.8 4.6 %collective-permute-start.4 = (bf16[1,512,896]{2,1,0:T(8,128)(2,1)S(1)}, bf16[1,512,896]{2,1,0:T(8,128)(2,1)S(1)}, u32[]{:S(2)}, u32[]{:S(2)}) collective-permute-start(bf16[1,512,896]{2,1,0:T(8,128)(2,1)S(1)} %project.6), channel_id=1, source_target_pairs={{0,1},{1,0},{2,3},{3,2},{4,5},{5,4},{6,7},{7,6},{8,9},{9,8},{10,11... | collective-permute-start | bytes 2752520 | tf_op jit(solution)/shard_map/ppermute | solution.py:38
  267.5 3.7 %copy-start.15 = (f32[64,896]{1,0:T(8,128)S(1)}, f32[64,896]{1,0:T(8,128)}, u32[]{:S(2)}) copy-start(f32[64,896]{1,0:T(8,128)} %copy-done.14) | copy-start | bytes 688132
  267.5 19.9 %copy-start.13 = (f32[2,32,896]{2,1,0:T(8,128)S(1)}, f32[2,32,896]{2,1,0:T(8,128)}, u32[]{:S(2)}) copy-start(f32[2,32,896]{2,1,0:T(8,128)} %copy-done.12) | copy-start | bytes 688132
  267.5 19.6 %all-to-all-start.8 = ((bf16[8,64,896]{2,1,0:T(8,128)(2,1)}), bf16[8,64,896]{2,1,0:T(8,128)(2,1)S(1)}, u32[]{:S(2)}, u32[]{:S(2)}) async-start(bf16[8,64,896]{2,1,0:T(8,128)(2,1)} %bitcast.20), calls=%async_computation.8 | async-start | bytes 1835008 | tf_op jit(solution)/shard_map/all_to_all | solution.py:30

commit v5 on v4

--- a/solution.py
+++ b/solution.py
@@ -12,14 +12,12 @@
 DP = ("xh", "xl", "zl")
 TP = ("zh", "y", "c")
 ZY = ("zh", "y")
-FOUR = ("xh", "zl")
 PAIR = ("xl",) + ZY
 N_DP = 8
 N_TP = 16
 N_ZY = 8
-N_FOUR = 4
 SWAP = [(0, 1), (1, 0)]
-CUTS = (0, 640, 896)
+CUTS = (0, 384, 896)
 TILE = 384
 bf16 = jnp.bfloat16
 f32 = jnp.float32
@@ -151,11 +149,11 @@
     )(ids, lengths, cache_t, fresh_t, queries_t, *extra)
 
 
-def project(ids, half, rows, weights, near=None):
+def project(ids, half, rows, weights, cuts, near=None):
     groups, _, count, depth = rows.shape
     width = weights[0].shape[1]
     blocks = len(weights)
-    per = groups // 2
+    per = groups // cuts
 
     def body(ids_ref, rows_ref, *refs):
         out_ref = refs[-1]
@@ -163,32 +161,33 @@
         for k in range(blocks):
             at = lax.rem(ids_ref[2] + k, blocks)
             total = jnp.dot(lhs, refs[k][...], preferred_element_type=f32)
+            total = total.reshape(per, count, width)
             if near is not None:
-                total = total + refs[blocks][at].astype(f32)
-            out_ref[at] = total.astype(bf16)
-
-    block = pl.BlockSpec((blocks, per * count, width), lambda i, ids: (0, i, 0))
+                total = total + refs[blocks][:, at].astype(f32)
+            out_ref[:, at] = total.astype(bf16)
+
+    block = pl.BlockSpec((per, blocks, count, width), lambda i, ids: (i, 0, 0, 0))
     extra = [] if near is None else [near]
     return pl.pallas_call(
         body,
         grid_spec=pltpu.PrefetchScalarGridSpec(
             num_scalar_prefetch=1,
-            grid=(2,),
+            grid=(cuts,),
             in_specs=[pl.BlockSpec((per, 1, count, depth), lambda i, ids: (i, half(ids), 0, 0))]
             + [whole(w.shape) for w in weights]
             + [block for _ in extra],
             out_specs=block,
         ),
-        out_shape=jax.ShapeDtypeStruct((blocks, groups * count, width), bf16),
+        out_shape=jax.ShapeDtypeStruct((groups, blocks, count, width), bf16),
         compiler_params=params(),
         name="project",
     )(ids, rows, *weights, *extra)
 
 
 def widen(ids, rows, kept, came, side, done=None):
-    _, count, chunk, features = rows.shape
+    halves, chunks, _, count, features = rows.shape
     columns = kept.shape[1]
-    per = count * chunk // N_FOUR
+    every = halves * chunks * count
     starts = [0]
     for w in came:
         starts.append(starts[-1] + w.shape[0])
@@ -196,8 +195,14 @@
     def body(ids_ref, rows_ref, kept_ref, *refs):
         out_ref = refs[-1]
         pair = ids_ref[2]
-        mine = rows_ref[pair].reshape(count * chunk, features)
-        near = rows_ref[1 - pair].reshape(count * chunk, features)
+        mine = rows_ref[:, :, pair].reshape(every, features)
+        near = rows_ref[:, :, 1 - pair].reshape(every, features)
+
+        def put(tile, value):
+            value = value.astype(bf16).reshape(halves, chunks, count, value.shape[1])
+            for h in range(halves):
+                out_ref[:, 0, h, :, tile] = value[h]
+
         for at in range(0, columns, TILE):
             tile = slice(at, at + TILE)
             total = jnp.dot(mine, kept_ref[:, tile], preferred_element_type=f32)
@@ -207,15 +212,15 @@
                     refs[k][:, tile],
                     preferred_element_type=f32,
                 )
-            out_ref[:, 0, :, tile] = total.astype(bf16).reshape(N_FOUR, per, TILE)
-        squares = jnp.zeros((count * chunk, 1), f32)
-        for half in (mine, near):
-            wide = half.astype(f32)
+            put(tile, total)
+        squares = jnp.zeros((every, 1), f32)
+        for block in (mine, near):
+            wide = block.astype(f32)
             squares += jnp.sum(wide * wide, axis=1, keepdims=True)
         high = squares.astype(bf16).astype(f32)
-        lane = lax.broadcasted_iota(jnp.int32, (count * chunk, 128), 1)
+        lane = lax.broadcasted_iota(jnp.int32, (every, 128), 1)
         extra = jnp.where(lane == 0, high, jnp.where(lane == 1, squares - high, 0.0))
-        out_ref[:, 0, :, columns:] = extra.astype(bf16).reshape(N_FOUR, per, 128)
+        put(slice(columns, columns + 128), extra)
 
     last = [] if done is None else [done]
     return pl.pallas_call(
@@ -227,10 +232,10 @@
             + [whole(w.shape) for w in (kept,) + came]
             + [pl.BlockSpec(memory_space=pl.ANY) for _ in last],
             out_specs=pl.BlockSpec(
-                (N_FOUR, 1, per, columns + 128), lambda i, ids: (0, side, 0, 0)
+                (chunks, 1, halves, count, columns + 128), lambda i, ids: (0, side, 0, 0, 0)
             ),
         ),
-        out_shape=jax.ShapeDtypeStruct((N_FOUR, 2, per, columns + 128), bf16),
+        out_shape=jax.ShapeDtypeStruct((chunks, 2, halves, count, columns + 128), bf16),
         input_output_aliases={3 + len(came): 0} if last else {},
         compiler_params=params(),
         name="widen",
@@ -255,38 +260,42 @@
     member = lax.axis_index(TP)
     core = lax.axis_index("c")
     pair = lax.axis_index("xl")
-    rows_dev = cache.shape[0]
     steps = new_latent.shape[0]
     heads, latent_width, value_width = value_up.shape
     rows_out = residual.shape[1] // N_TP
     chunk = rows_out * steps
-    features, units = gate_weight.shape
-    part = units // 2
-
+    count = chunk // 2
+    units = gate_weight.shape[1]
+
+    def by_pair(mine, other):
+        first = pair == 0
+        return jnp.stack([jnp.where(first, mine, other), jnp.where(first, other, mine)])
+
+    def at_pair(blocks):
+        return lax.dynamic_index_in_dim(blocks, pair, 0, False)
+
+    def at_other(blocks):
+        return lax.dynamic_index_in_dim(blocks, 1 - pair, 0, False)
+
+    out_came = swap(out_proj, "xl")
     lanes = jnp.arange(N_TP, dtype=jnp.int32)
     own_slot = jnp.sum(jnp.where(lanes == member, move_slot[0], 0))
     ids = jnp.stack([own_slot, core, pair]).astype(jnp.int32)
     cache_t = cache.transpose(0, 2, 1)
-    leaving, gate_weight, up_weight = lax.optimization_barrier(
-        (leave(ids, cache_t), gate_weight, up_weight)
-    )
-    pieces = exchange(leaving, TP)
+    pieces = exchange(leave(ids, cache_t), TP)
+    pieces, gate_weight, up_weight = lax.optimization_barrier((pieces, gate_weight, up_weight))
 
     gain = norm_gain.astype(f32)[:, None]
 
-    def columns(index, low, high):
-        return jnp.concatenate(
-            [
-                lax.dynamic_slice(w, (low, index * part), (high - low, part)).astype(f32)
-                * gain[low:high]
-                for w in (gate_weight, up_weight)
-            ],
-            axis=1,
-        ).astype(bf16)
-
-    sent = [columns(1 - pair, low, high) for low, high in zip(CUTS[:-1], CUTS[1:])]
-    kept = columns(pair, 0, features)
-    came = [swap(sent[0], "xl"), swap(sent[1], "xl")]
+    def scaled(low, high, first, second):
+        weight = jnp.where(pair == 0, first[low:high], second[low:high])
+        return (weight.astype(f32) * gain[low:high]).astype(bf16)
+
+    sent = [
+        scaled(low, high, up_weight, gate_weight) for low, high in zip(CUTS[:-1], CUTS[1:])
+    ]
+    kept = scaled(0, CUTS[-1], gate_weight, up_weight)
+    came = [swap(sent[0], "xl")]
 
     arrived = exchange(route(move_peer[0], pieces), TP)
     fresh_t = new_latent.transpose(1, 2, 0)
@@ -295,39 +304,46 @@
     out = attend(
         ids, cache_length, cache_t, fresh_t, queries_t, heads, latent_width, arrived, out
     )
-    out, came[0] = lax.optimization_barrier((out, came[0]))
+    out, out_came = lax.optimization_barrier((out, out_came))
     by_head = exchange(out, TP).reshape(-1, heads, latent_width)
-    by_head, kept, came[1] = lax.optimization_barrier((by_head, kept, came[1]))
+    by_head, kept, came[0] = lax.optimization_barrier((by_head, kept, came[0]))
     value_heads = jnp.einsum(
         "thl,hlv->thv", by_head, value_up, preferred_element_type=f32
     ).astype(bf16)
-    value_heads = value_heads.reshape(-1, heads * value_width)
-
-    gathered = spread(value_heads, DP, N_DP).reshape(N_DP, 2, chunk, -1)
-    away = swap(project(ids, lambda i: 1 - i[1], gathered, [out_proj]), "c")
-    total = project(ids, lambda i: i[1], gathered, [out_proj], away)
-    parts = exchange(total.reshape(N_ZY, chunk, -1), ZY)
+
+    value_heads = value_heads.reshape(2, 2, count, heads * value_width).transpose(1, 0, 2, 3)
+    value_heads = jnp.broadcast_to(
+        value_heads[None, :, None], (2, 2, 2) + value_heads.shape[1:]
+    ).reshape((N_DP,) + value_heads.shape[1:])
+    gathered = exchange(value_heads, DP)
+    gathered, sent[1] = lax.optimization_barrier((gathered, sent[1]))
+    came.append(swap(sent[1], "xl"))
+    weights = [out_proj, out_came]
+    away = swap(project(ids, lambda i: 1 - i[1], gathered, weights, 1), "c")
+    total = project(ids, lambda i: i[1], gathered, weights, 1, away)
+    parts = exchange(total, ZY)
+    parts, came[1] = lax.optimization_barrier((parts, came[1]))
     residue = lax.dynamic_slice_in_dim(residual, member * rows_out, rows_out, 1)
-    residue = residue.transpose(1, 0, 2).reshape(chunk, -1)
+    residue = residue.transpose(1, 0, 2).reshape(2, count, -1)
+    residue = by_pair(at_pair(residue), swap(at_other(residue), "xl"))
     hidden = residue.astype(f32) + jnp.sum(parts.astype(f32), axis=0)
 
-    own = spread(hidden.astype(bf16), PAIR, 2 * N_ZY).reshape(2, N_ZY, chunk, features)
+    own = spread(hidden.astype(bf16), PAIR, 2 * N_ZY).reshape((2, N_ZY) + hidden.shape)
     other = swap(own, "c")
     came = tuple(came)
     wide = widen(ids, own, kept, came, 0)
     wide = widen(ids, other, kept, came, 1, wide)
-    sums = exchange(wide.reshape(N_FOUR, 4 * chunk, -1), FOUR)
-    sums = jnp.sum(sums.astype(f32), axis=0)
-    squares = sums[:, units] + sums[:, units + 1]
+    sums = exchange(wide.reshape(N_DP, 2 * chunk, -1), DP)
+    sums = jnp.sum(sums.reshape(2, 2, 2, 2 * chunk, -1).astype(f32), axis=(0, 2))
+    squares = sums[0, :, units] + sums[0, :, units + 1]
     inverse = lax.rsqrt(squares / D + norm_eps)[:, None]
-    active = jax.nn.silu(sums[:, :part] * inverse) * (sums[:, part:units] * inverse)
-    active = active.astype(bf16).reshape(2, 2 * chunk, part)
-    active = spread(active, DP, N_DP).reshape(2, 2, 2, 2, 2 * chunk, part)
-    active = jnp.concatenate([active[:, 0], active[:, 1]], axis=-1)
-    active = active.reshape(N_FOUR, 2, 2 * chunk, units)
-    away = swap(project(ids, lambda i: 1, active, [down_weight]), "c")
-    total = project(ids, lambda i: 0, active, [down_weight], away)
+    active = jax.nn.silu(sums[0, :, :units] * inverse) * (sums[1, :, :units] * inverse)
+    active = spread(active.astype(bf16), DP, N_DP).reshape(N_DP, 2, chunk, units)
+
+    away = swap(project(ids, lambda i: 1, active, [down_weight], 2), "c")
+    total = project(ids, lambda i: 0, active, [down_weight], 2, away)
     parts = exchange(total.reshape(N_ZY, chunk, -1), ZY)
+    hidden = by_pair(at_pair(hidden), swap(at_other(hidden), "xl")).reshape(chunk, -1)
     result = (hidden + jnp.sum(parts.astype(f32), axis=0)).astype(bf16)
     return result.reshape(rows_out, steps, -1).transpose(1, 0, 2)
 

time: 290 us -> 282 us (0.972)
  blocking collectives: 142 us -> 117 us
  waiting for transfers between devices: 45.4 us -> 65.2 us
  other arithmetic: 17.9 us -> 10.1 us
  starting transfers between devices: 31 us -> 36.8 us
    ppermute x5 -> x8, waiting for transfers between devices: 14.4 us -> 41.3 us  [swap(): return lax.ppermute(block, axis, SWAP)]
    all_to_all x5 -> x4, blocking collectives: 142 us -> 117 us  [exchange(): return lax.all_to_all(blocks, axes, 0, 0, tiled=True)]
    all_to_all x4 -> x5, waiting for transfers between devices: 31.1 us -> 23.9 us  [exchange(): return lax.all_to_all(blocks, axes, 0, 0, tiled=True)]
    unnamed x38 -> x47, local copies, waits for them, and re-layouts: 7.43 us -> 14.4 us
    another operation x3, other arithmetic: 6.81 us -> 0.06 us  [by_pair(): jnp.stack([jnp.where(first, mine, other), jnp.where(first, other, mine)])]
    convert_element_type x2 -> x3, other arithmetic: 1.25 us -> 6.81 us  [scaled(): return (weight.astype(f32) * gain[low:high]).astype(bf16)]
    all_to_all x4 -> x5, starting transfers between devices: 20.6 us -> 26.1 us  [exchange(): return lax.all_to_all(blocks, axes, 0, 0, tiled=True)]
    concatenate x4 -> x0, other arithmetic: 5.47 us -> none  [the longest x3 3.21 us: columns(): jnp.concatenate([lax.dynamic_slice(w, (low, index * part), (high - low, p...]
  transfers between devices with their start and end apart: 9 -> 13, of which waited for: 6 -> 8; matrix products, arithmetic and copies ran while one was open for 3% -> 4% of each run, Pallas kernels for 5% -> 6%
where the time goes in v5:
time: 282 us; the launch traced here: 281 us
  blocking collectives  117 us (41%)
  waiting for transfers between devices  65.2 us (23%)
  starting transfers between devices  36.8 us (13%)
  Pallas kernels  31.9 us (11%)
  local copies, waits for them, and re-layouts  17.4 us (6%)
  other arithmetic  10.1 us (4%)
    all_to_all x4, blocking collectives, exchange(): return lax.all_to_all(blocks, axes, 0, 0, tiled=True)  117 us
    ppermute x8, waiting for transfers between devices, swap(): return lax.ppermute(block, axis, SWAP)  41.3 us
    all_to_all x5, starting transfers between devices, exchange(): return lax.all_to_all(blocks, axes, 0, 0, tiled=True)  26.1 us
    all_to_all x5, waiting for transfers between devices, exchange(): return lax.all_to_all(blocks, axes, 0, 0, tiled=True)  23.9 us
    unnamed x47, local copies, waits for them, and re-layouts  14.4 us
    pallas_call x4, Pallas kernels, project(): pl.pallas_call(body, grid_spec=pltpu.PrefetchScalarGridSpec(num_scalar_pr...  13 us
    pallas_call x2, Pallas kernels, widen(): pl.pallas_call(body, grid_spec=pltpu.PrefetchScalarGridSpec(num_scalar_pr...  12.4 us
    ppermute x8, starting transfers between devices, swap(): return lax.ppermute(block, axis, SWAP)  10.7 us
  transfers between devices with their start and end apart: 13, of which 8 were waited for; matrix products, arithmetic and copies ran while one was open for 4% of the time, Pallas kernels for 6%

profile of v5, /device:TPU:1, one launch (start us, length us, event | category | flops | bytes accessed | tf_op | source)
XLA Modules:
  0.0 280.8 jit_solution(7265360002532398465)
XLA Ops:
  0.0 2.1 collective-permute-start.1
  2.2 1.3 fusion.14
  4.2 1.3 copy-done.3
  6.0 17.7 %all_to_all.45.in_ref = bf16[16,36,256]{2,1,0:T(8,128)(2,1)S(1)} all-to-all(bf16[16,36,256]{2,1,0:T(8,128)(2,1)S(1)} %leave.1), channel_id=1, replica_groups=mesh['xh'=2,'xl'=2,'zl'=2,'zh'=2,'y'=4,'c'=2] {'zh','y','c'}, dimensions={0} | all-to-all | bytes 589824 | tf_op jit(solution)/shard_map/all_to_all | solution.py:28
  24.3 0.7 copy-done.17
  25.0 4.3 %all-to-all-start.1 = ((bf16[16,36,256]{2,1,0:T(8,128)(2,1)}), bf16[16,36,256]{2,1,0:T(8,128)(2,1)S(1)}, u32[]{:S(2)}, u32[]{:S(2)}) async-start(bf16[16,36,256]{2,1,0:T(8,128)(2,1)} %copy-done.17), calls=%async_computation.1 | async-start | bytes 655360 | tf_op jit(solution)/shard_map/all_to_all | solution.py:28
  29.4 1.1 copy.33
  30.5 1.1 copy-done.10
  31.6 1.3 copy-done.12
  32.8 4.0 %attend.1.refs_1_ = bf16[16,4,16,512]{3,2,1,0:T(8,128)(2,1)S(1)} custom-call(s32[3]{0:T(128)S(1)} %pad_add_fusion.ids_ref, s32[4]{0:T(128)S(1)} %copy-done.18, bf16[4,576,256]{2,1,0:T(8,128)(2,1)S(1)} %bitcast.56, bf16[4,576,2]{2,1,0:T(8,128)(2,1)S(1)} %bitcast.60, bf16[2,4,576,128]{3,2,1,0:T(8,128)(2,1)S(1)} %bitcast.62), custom_call_target="tpu_custom_call" | custom-call | tf_op jit(solution)/shard_map/attend/pallas_call | solution.py:127
  36.9 1.0 copy-done.5
  38.6 1.2 copy-done.6
  39.8 1.1 copy-done.11
  40.9 1.3 copy-done.13
  42.1 1.4 again.1
  43.5 1.0 copy-done.7
  44.5 7.0 %all-to-all-start.2 = ((bf16[16,4,16,512]{3,2,1,0:T(8,128)(2,1)}), bf16[16,4,16,512]{3,2,1,0:T(8,128)(2,1)S(1)}, u32[]{:S(2)}, u32[]{:S(2)}) async-start(bf16[16,4,16,512]{3,2,1,0:T(8,128)(2,1)} %copy-done.7), calls=%async_computation.2 | async-start | bytes 2097152 | tf_op jit(solution)/shard_map/all_to_all | solution.py:28
  51.5 1.8 multiply_convert_fusion.2
  53.3 1.3 collective-permute-start.2
  54.7 1.9 multiply_convert_fusion.kept_ref
  56.6 18.0 %collective-permute-done.2.refs_0_ = bf16[384,1152]{1,0:T(8,128)(2,1)S(1)} collective-permute-done((bf16[384,1152]{1,0:T(8,128)(2,1)S(1)}, bf16[384,1152]{1,0:T(8,128)(2,1)S(1)}, u32[]{:S(2)}, u32[]{:S(2)}) %collective-permute-start.2) | collective-permute-done | bytes 884768 | tf_op jit(solution)/shard_map/ppermute | solution.py:36
  74.6 0.9 copy-done.15
  75.6 2.1 fusion
  78.0 1.1 broadcast_in_dim.13
  79.1 4.5 %all-to-all-start.3 = ((bf16[8,2,32,1024]{3,2,1,0:T(8,128)(2,1)}), bf16[8,2,32,1024]{3,2,1,0:T(8,128)(2,1)S(1)}, u32[]{:S(2)}, u32[]{:S(2)}) async-start(bf16[8,2,32,1024]{3,2,1,0:T(8,128)(2,1)} %bitcast.67), calls=%async_computation.3 | async-start | bytes 2097152 | tf_op jit(solution)/shard_map/all_to_all | solution.py:28
  83.6 3.0 %multiply_convert_fusion.1 = bf16[512,1152]{1,0:T(8,128)(2,1)} fusion(f32[512]{0:T(512)S(1)} %slice.37, bf16[896,1152]{1,0:T(8,128)(2,1)} %param.23, bf16[896,1152]{1,0:T(8,128)(2,1)} %param.24, pred[]{:T(512)S(6)} %eq.6), kind=kLoop, calls=%fused_computation.2 | loop fusion | flops 2359296 | bytes 3540993 | tf_op jit(solution)/shard_map/convert_element_type | solution.py:292
  86.6 11.9 %all-to-all-done.3.rows_ref = bf16[8,2,32,1024]{3,2,1,0:T(8,128)(2,1)S(1)} async-done(((bf16[8,2,32,1024]{3,2,1,0:T(8,128)(2,1)}), bf16[8,2,32,1024]{3,2,1,0:T(8,128)(2,1)S(1)}, u32[]{:S(2)}, u32[]{:S(2)}) %all-to-all-start.3) | async-done | bytes 1048608 | tf_op jit(solution)/shard_map/all_to_all | solution.py:28
  98.5 1.5 copy-done.9
  100.0 3.3 %project.4 = bf16[8,2,32,896]{3,2,1,0:T(8,128)(2,1)S(1)} custom-call(s32[3]{0:T(128)S(1)} %pad_add_fusion.ids_ref, bf16[8,2,32,1024]{3,2,1,0:T(8,128)(2,1)S(1)} %all-to-all-done.3.rows_ref, bf16[1024,896]{1,0:T(8,128)(2,1)S(1)} %copy-done.9, bf16[1024,896]{1,0:T(8,128)(2,1)} %collective-permute-done.1.refs_1_), custom_call_target="tpu_custom_call" | custom-call | tf_op jit(solution)/shard_map/project/pallas_call | solution.py:171
  103.2 1.8 collective-permute-start.3
  105.3 1.8 collective-permute-done.3.refs_2_
  107.1 3.3 %project.5 = bf16[8,2,32,896]{3,2,1,0:T(8,128)(2,1)S(1)} custom-call(s32[3]{0:T(128)S(1)} %pad_add_fusion.ids_ref, bf16[8,2,32,1024]{3,2,1,0:T(8,128)(2,1)S(1)} %all-to-all-done.3.rows_ref, bf16[1024,896]{1,0:T(8,128)(2,1)S(1)} %copy-done.9, bf16[1024,896]{1,0:T(8,128)(2,1)} %collective-permute-done.1.refs_1_, ...), custom_call_target="tpu_custom_call" | custom-call | tf_op jit(solution)/shard_map/project/pallas_call | solution.py:171
  110.5 0.9 copy-done.14
  111.4 6.8 %all-to-all-start.4 = ((bf16[8,2,32,896]{3,2,1,0:T(8,128)(2,1)}), bf16[8,2,32,896]{3,2,1,0:T(8,128)(2,1)S(1)}, u32[]{:S(2)}, u32[]{:S(2)}) async-start(bf16[8,2,32,896]{3,2,1,0:T(8,128)(2,1)} %copy-done.14), calls=%async_computation.4 | async-start | bytes 1835008 | tf_op jit(solution)/shard_map/all_to_all | solution.py:28
  118.7 15.3 %collective-permute-done = bf16[32,896]{1,0:T(8,128)(2,1)S(1)} collective-permute-done((bf16[32,896]{1,0:T(8,128)(2,1)S(1)}, bf16[32,896]{1,0:T(8,128)(2,1)S(1)}, u32[]{:S(2)}, u32[]{:S(2)}) %collective-permute-start) | collective-permute-done | bytes 57376 | tf_op jit(solution)/shard_map/ppermute | solution.py:36
  134.5 32.5 %all_to_all.46 = bf16[16,2,32,896]{3,2,1,0:T(8,128)(2,1)S(1)} all-to-all(bf16[16,2,32,896]{3,2,1,0:T(8,128)(2,1)S(1)} %broadcast_in_dim.14), channel_id=1, replica_groups=mesh['xh'=2,'xl'=2,'zl'=2,'zh'=2,'y'=4,'c'=2] {'xl','zh','y'}, dimensions={0} | all-to-all | bytes 3670016 | tf_op jit(solution)/shard_map/all_to_all | solution.py:28
  167.0 2.1 collective-permute-start.6
  169.1 6.2 %widen.2.refs_2_ = bf16[8,2,2,32,1280]{4,3,2,1,0:T(8,128)(2,1)} custom-call(s32[3]{0:T(128)S(1)} %pad_add_fusion.ids_ref, bf16[2,8,2,32,896]{4,3,2,1,0:T(8,128)(2,1)S(1)} %bitcast.59, bf16[896,1152]{1,0:T(8,128)(2,1)S(1)} %copy-done.2, bf16[384,1152]{1,0:T(8,128)(2,1)S(1)} %copy-done.16, bf16[512,1152]{1,0:T(8,128)(2,1)} %collective-permute-done.4.refs_1_), custom_call_target="tpu_custom_call" | custom-call | tf_op jit(solution)/shard_map/widen/pallas_call | solution.py:226
  175.3 6.2 %widen.3 = bf16[8,2,2,32,1280]{4,3,2,1,0:T(8,128)(2,1)} custom-call(s32[3]{0:T(128)S(1)} %pad_add_fusion.ids_ref, bf16[2,8,2,32,896]{4,3,2,1,0:T(8,128)(2,1)S(1)} %collective-permute-done.6.rows_ref, bf16[896,1152]{1,0:T(8,128)(2,1)S(1)} %copy-done.2, bf16[384,1152]{1,0:T(8,128)(2,1)S(1)} %copy-done.16, ...), custom_call_target="tpu_custom_call", output_to_operand_aliasing={{}: (5, {})} | custom-call | tf_op jit(solution)/shard_map/widen/pallas_call | solution.py:226
  181.5 35.6 %all_to_all.47 = bf16[8,128,1280]{2,1,0:T(8,128)(2,1)S(1)} all-to-all(bf16[8,128,1280]{2,1,0:T(8,128)(2,1)} %bitcast.65), channel_id=1, replica_groups=mesh['xh'=2,'xl'=2,'zl'=2,'zh'=2,'y'=4,'c'=2] {'xh','xl','zl'}, dimensions={0} | all-to-all | bytes 5242880 | tf_op jit(solution)/shard_map/all_to_all | solution.py:28
  218.3 31.1 %all_to_all.48 = bf16[8,128,1152]{2,1,0:T(8,128)(2,1)S(1)} all-to-all(bf16[8,128,1152]{2,1,0:T(8,128)(2,1)S(1)} %broadcast_in_dim.30), channel_id=1, replica_groups=mesh['xh'=2,'xl'=2,'zl'=2,'zh'=2,'y'=4,'c'=2] {'xh','xl','zl'}, dimensions={0} | all-to-all | bytes 4718592 | tf_op jit(solution)/shard_map/all_to_all | solution.py:28
  249.4 2.3 project.6
  251.8 2.3 collective-permute-start.7
  254.1 2.1 collective-permute-done.7.refs_1_
  256.2 4.1 %project.7 = bf16[8,1,64,896]{3,2,1,0:T(8,128)(2,1)} custom-call(s32[3]{0:T(128)S(1)} %pad_add_fusion.ids_ref, bf16[8,2,64,1152]{3,2,1,0:T(8,128)(2,1)} %bitcast.54, bf16[1152,896]{1,0:T(8,128)(2,1)S(1)} %copy-done.8, bf16[8,1,64,896]{3,2,1,0:T(8,128)(2,1)S(1)} %collective-permute-done.7.refs_1_), custom_call_target="tpu_custom_call" | custom-call | tf_op jit(solution)/shard_map/project/pallas_call | solution.py:171
  260.2 3.6 %all-to-all-start.8 = ((bf16[8,64,896]{2,1,0:T(8,128)(2,1)}), bf16[8,64,896]{2,1,0:T(8,128)(2,1)S(1)}, u32[]{:S(2)}, u32[]{:S(2)}) async-start(bf16[8,64,896]{2,1,0:T(8,128)(2,1)} %bitcast.26), calls=%async_computation.8 | async-start | bytes 1835008 | tf_op jit(solution)/shard_map/all_to_all | solution.py:28
  264.2 4.0 %collective-permute-done.5 = f32[32,896]{1,0:T(8,128)S(1)} collective-permute-done((f32[32,896]{1,0:T(8,128)S(1)}, f32[32,896]{1,0:T(8,128)S(1)}, u32[]{:S(2)}, u32[]{:S(2)}) %collective-permute-start.5) | collective-permute-done | bytes 114720 | tf_op jit(solution)/shard_map/ppermute | solution.py:36
  268.4 11.3 %all-to-all-done.8 = bf16[8,64,896]{2,1,0:T(8,128)(2,1)S(1)} async-done(((bf16[8,64,896]{2,1,0:T(8,128)(2,1)}), bf16[8,64,896]{2,1,0:T(8,128)(2,1)S(1)}, u32[]{:S(2)}, u32[]{:S(2)}) %all-to-all-start.8) | async-done | bytes 917536 | tf_op jit(solution)/shard_map/all_to_all | solution.py:28
  (72 shorter events, 6.9 us)
Async XLA Ops:
  0.0 118.1 %copy-start = (bf16[2,512,896]{2,1,0:T(8,128)(2,1)S(1)}, bf16[2,512,896]{2,1,0:T(8,128)(2,1)}, u32[]{:S(2)}) copy-start(bf16[2,512,896]{2,1,0:T(8,128)(2,1)} %param.21) | copy-start | bytes 5505028
  0.0 23.7 %copy-start.19 = (s32[1,16]{1,0:T(1,128)S(1)}, s32[1,16]{1,0:T(1,128)}, u32[]{:S(2)}) copy-start(s32[1,16]{1,0:T(1,128)} %param.16) | copy-start | bytes 196
  0.0 29.4 %copy-start.21 = (bf16[896]{0:T(1024)(128)(2,1)S(1)}, bf16[896]{0:T(1024)(128)(2,1)}, u32[]{:S(2)}) copy-start(bf16[896]{0:T(1024)(128)(2,1)} %param.22) | copy-start | bytes 5380
  0.0 29.4 %copy-start.22 = (bf16[2,4,576]{2,1,0:T(4,128)(2,1)S(1)}, bf16[2,4,576]{2,1,0:T(4,128)(2,1)}, u32[]{:S(2)}) copy-start(bf16[2,4,576]{2,1,0:T(4,128)(2,1)} %param.18) | copy-start | bytes 27652
  0.0 30.5 %copy-start.18 = (s32[4]{0:T(128)S(1)}, s32[4]{0:T(128)}, u32[]{:S(2)}) copy-start(s32[4]{0:T(128)} %lengths_ref.3) | copy-start | bytes 52
  0.0 44.5 %collective-permute-start.1 = (bf16[1024,896]{1,0:T(8,128)(2,1)}, bf16[1024,896]{1,0:T(8,128)(2,1)}, u32[]{:S(2)}, u32[]{:S(2)}) collective-permute-start(bf16[1024,896]{1,0:T(8,128)(2,1)} %refs_0_.5), channel_id=1, source_target_pairs={{0,32},{32,0},{1,33},{33,1},{2,34},{34,2},{3,35},{35,3},{4,36},{36... | collective-permute-start | bytes 5505032 | tf_op jit(solution)/shard_map/ppermute | solution.py:36
  4.2 1.3 copy-start.3
  5.4 25.1 %copy-start.4 = (bf16[4,256,576]{1,2,0:T(8,128)(2,1)S(1)}, bf16[4,256,576]{1,2,0:T(8,128)(2,1)}, u32[]{:S(2)}) copy-start(bf16[4,256,576]{1,2,0:T(8,128)(2,1)} %param.13) | copy-start | bytes 3538948
  24.3 0.8 copy-start.17
  25.0 13.6 %all-to-all-start.1 = ((bf16[16,36,256]{2,1,0:T(8,128)(2,1)}), bf16[16,36,256]{2,1,0:T(8,128)(2,1)S(1)}, u32[]{:S(2)}, u32[]{:S(2)}) async-start(bf16[16,36,256]{2,1,0:T(8,128)(2,1)} %copy-done.17), calls=%async_computation.1 | async-start | bytes 655360 | tf_op jit(solution)/shard_map/all_to_all | solution.py:28
  30.5 1.1 copy-start.10
  31.6 1.3 copy-start.12
  36.9 1.0 copy-start.5
  38.6 1.2 copy-start.6
  39.8 1.1 copy-start.11
  40.9 1.3 copy-start.13
  43.5 1.0 copy-start.7
  44.5 31.1 %all-to-all-start.2 = ((bf16[16,4,16,512]{3,2,1,0:T(8,128)(2,1)}), bf16[16,4,16,512]{3,2,1,0:T(8,128)(2,1)S(1)}, u32[]{:S(2)}, u32[]{:S(2)}) async-start(bf16[16,4,16,512]{3,2,1,0:T(8,128)(2,1)} %copy-done.7), calls=%async_computation.2 | async-start | bytes 2097152 | tf_op jit(solution)/shard_map/all_to_all | solution.py:28
  51.5 3.2 %copy-start.20 = (bf16[896,1152]{1,0:T(8,128)(2,1)S(1)}, bf16[896,1152]{1,0:T(8,128)(2,1)}, u32[]{:S(2)}) copy-start(bf16[896,1152]{1,0:T(8,128)(2,1)} %param.23) | copy-start | bytes 6193156
  53.3 21.3 %collective-permute-start.2 = (bf16[384,1152]{1,0:T(8,128)(2,1)S(1)}, bf16[384,1152]{1,0:T(8,128)(2,1)S(1)}, u32[]{:S(2)}, u32[]{:S(2)}) collective-permute-start(bf16[384,1152]{1,0:T(8,128)(2,1)S(1)} %multiply_convert_fusion.2), channel_id=1, source_target_pairs={{0,32},{32,0},{1,33},{33,1},{2,34},{34,2},{3,35},{35,3},{4,36},{36... | collective-permute-start | bytes 2654216 | tf_op jit(solution)/shard_map/ppermute | solution.py:36
  74.6 0.9 copy-start.15
  79.1 19.4 %all-to-all-start.3 = ((bf16[8,2,32,1024]{3,2,1,0:T(8,128)(2,1)}), bf16[8,2,32,1024]{3,2,1,0:T(8,128)(2,1)S(1)}, u32[]{:S(2)}, u32[]{:S(2)}) async-start(bf16[8,2,32,1024]{3,2,1,0:T(8,128)(2,1)} %bitcast.67), calls=%async_computation.3 | async-start | bytes 2097152 | tf_op jit(solution)/shard_map/all_to_all | solution.py:28
  98.5 1.5 copy-start.9
  103.2 3.9 %collective-permute-start.3 = (bf16[8,2,32,896]{3,2,1,0:T(8,128)(2,1)S(1)}, bf16[8,2,32,896]{3,2,1,0:T(8,128)(2,1)S(1)}, u32[]{:S(2)}, u32[]{:S(2)}) collective-permute-start(bf16[8,2,32,896]{3,2,1,0:T(8,128)(2,1)S(1)} %project.4), channel_id=1, source_target_pairs={{0,1},{1,0},{2,3},{3,2},{4,5},{5,4},{6,7},{7,6},{8,9},{9,8},{10,11... | collective-permute-start | bytes 2752520 | tf_op jit(solution)/shard_map/ppermute | solution.py:36
  105.0 29.0 %collective-permute-start.4 = (bf16[512,1152]{1,0:T(8,128)(2,1)}, bf16[512,1152]{1,0:T(8,128)(2,1)}, u32[]{:S(2)}, u32[]{:S(2)}) collective-permute-start(bf16[512,1152]{1,0:T(8,128)(2,1)} %multiply_convert_fusion.1), channel_id=1, source_target_pairs={{0,32},{32,0},{1,33},{33,1},{2,34},{34,2},{3,35},{35,3},{4,36},{36... | collective-permute-start | bytes 3538952 | tf_op jit(solution)/shard_map/ppermute | solution.py:36
  110.4 0.9 copy-start.14
  111.4 22.7 %all-to-all-start.4 = ((bf16[8,2,32,896]{3,2,1,0:T(8,128)(2,1)}), bf16[8,2,32,896]{3,2,1,0:T(8,128)(2,1)S(1)}, u32[]{:S(2)}, u32[]{:S(2)}) async-start(bf16[8,2,32,896]{3,2,1,0:T(8,128)(2,1)} %copy-done.14), calls=%async_computation.4 | async-start | bytes 1835008 | tf_op jit(solution)/shard_map/all_to_all | solution.py:28
  118.3 15.7 %collective-permute-start = (bf16[32,896]{1,0:T(8,128)(2,1)S(1)}, bf16[32,896]{1,0:T(8,128)(2,1)S(1)}, u32[]{:S(2)}, u32[]{:S(2)}) collective-permute-start(bf16[32,896]{1,0:T(8,128)(2,1)S(1)} %dynamic-slice_bitcast_fusion.2), channel_id=1, source_target_pairs={{0,32},{32,0},{1,33},{33,1},{2,34},{34,2},{3,35},{35,3},{4,36},{36... | collective-permute-start | bytes 172040 | tf_op jit(solution)/shard_map/ppermute | solution.py:36
  134.5 34.6 %copy-start.2 = (bf16[896,1152]{1,0:T(8,128)(2,1)S(1)}, bf16[896,1152]{1,0:T(8,128)(2,1)}, u32[]{:S(2)}) copy-start(bf16[896,1152]{1,0:T(8,128)(2,1)} %multiply_convert_fusion.kept_ref) | copy-start | bytes 6193156
  134.5 34.6 %copy-start.16 = (bf16[384,1152]{1,0:T(8,128)(2,1)S(1)}, bf16[384,1152]{1,0:T(8,128)(2,1)}, u32[]{:S(2)}) copy-start(bf16[384,1152]{1,0:T(8,128)(2,1)} %copy-done.15) | copy-start | bytes 2654212
  167.0 8.3 %collective-permute-start.6 = (bf16[2,8,2,32,896]{4,3,2,1,0:T(8,128)(2,1)S(1)}, bf16[2,8,2,32,896]{4,3,2,1,0:T(8,128)(2,1)S(1)}, u32[]{:S(2)}, u32[]{:S(2)}) collective-permute-start(bf16[2,8,2,32,896]{4,3,2,1,0:T(8,128)(2,1)S(1)} %bitcast.58), channel_id=1, source_target_pairs={{0,1},{1,0},{2,3},{3,2},{4,5},{5,4},{6,7},{7,6},{8,9},{9,8},{10,11... | collective-permute-start | bytes 5505032 | tf_op jit(solution)/shard_map/ppermute | solution.py:36
  218.3 31.2 %copy-start.8 = (bf16[1152,896]{1,0:T(8,128)(2,1)S(1)}, bf16[1152,896]{1,0:T(8,128)(2,1)}, u32[]{:S(2)}) copy-start(bf16[1152,896]{1,0:T(8,128)(2,1)} %refs_0_.7) | copy-start | bytes 6193156
  249.4 2.3 copy-start.1
  251.8 4.4 %collective-permute-start.7 = (bf16[8,1,64,896]{3,2,1,0:T(8,128)(2,1)S(1)}, bf16[8,1,64,896]{3,2,1,0:T(8,128)(2,1)S(1)}, u32[]{:S(2)}, u32[]{:S(2)}) collective-permute-start(bf16[8,1,64,896]{3,2,1,0:T(8,128)(2,1)S(1)} %project.6), channel_id=1, source_target_pairs={{0,1},{1,0},{2,3},{3,2},{4,5},{5,4},{6,7},{7,6},{8,9},{9,8},{10,11... | collective-permute-start | bytes 2752520 | tf_op jit(solution)/shard_map/ppermute | solution.py:36
  260.2 19.5 %all-to-all-start.8 = ((bf16[8,64,896]{2,1,0:T(8,128)(2,1)}), bf16[8,64,896]{2,1,0:T(8,128)(2,1)S(1)}, u32[]{:S(2)}, u32[]{:S(2)}) async-start(bf16[8,64,896]{2,1,0:T(8,128)(2,1)} %bitcast.26), calls=%async_computation.8 | async-start | bytes 1835008 | tf_op jit(solution)/shard_map/all_to_all | solution.py:28
  263.8 4.4 %collective-permute-start.5 = (f32[32,896]{1,0:T(8,128)S(1)}, f32[32,896]{1,0:T(8,128)S(1)}, u32[]{:S(2)}, u32[]{:S(2)}) collective-permute-start(f32[32,896]{1,0:T(8,128)S(1)} %dynamic-slice_bitcast_fusion), channel_id=1, source_target_pairs={{0,32},{32,0},{1,33},{33,1},{2,34},{34,2},{3,35},{35,3},{4,36},{36... | collective-permute-start | bytes 344072 | tf_op jit(solution)/shard_map/ppermute | solution.py:36

commit v6 on v5

--- a/solution.py
+++ b/solution.py
@@ -17,11 +17,11 @@
 N_TP = 16
 N_ZY = 8
 SWAP = [(0, 1), (1, 0)]
-CUTS = (0, 384, 896)
+CUTS = (0, 256, 896)
 TILE = 384
 bf16 = jnp.bfloat16
 f32 = jnp.float32
-VMEM = 48 * 1024 * 1024
+VMEM = 60 * 1024 * 1024
 
 
 def exchange(blocks, axes):
@@ -89,7 +89,7 @@
 def attend(ids, lengths, cache_t, fresh_t, queries_t, heads, latent_width, arrived=None, done=None):
     rows, entries, length = cache_t.shape
     steps, _, _, all_heads = queries_t.shape
-    parts = all_heads // heads
+    chips = all_heads // (2 * heads)
     again = arrived is not None
 
     def slot(r, ids):
@@ -97,7 +97,8 @@
 
     def body(ids_ref, lengths_ref, cache_ref, fresh_ref, q_ref, *refs):
         out_ref = refs[-1]
-        current = lengths_ref[slot(pl.program_id(0), ids_ref)]
+        row = slot(pl.program_id(0), ids_ref)
+        current = lengths_ref[row]
         if again:
             latents = jnp.concatenate([refs[0][j].astype(f32) for j in range(N_TP)], axis=0)
         else:
@@ -119,8 +120,11 @@
             out = lax.dot_general(
                 probs, latents[:latent_width], (((1,), (1,)), ((), ())), preferred_element_type=f32
             )
-            outs.append(out.reshape(parts, heads, latent_width))
-        out_ref[:, 0] = jnp.concatenate(outs, axis=1).astype(bf16)
+            out = out.reshape(chips, 2, heads, latent_width)
+            turned = jnp.concatenate([out[:, 1:], out[:, :1]], axis=1)
+            out = jnp.where(row >= rows // 2, turned, out)
+            outs.append(out.reshape(chips, 2 * heads, latent_width))
+        out_ref[:, 0, 0] = jnp.concatenate(outs, axis=1).astype(bf16)
 
     extra_specs = [whole(arrived.shape), pl.BlockSpec(memory_space=pl.ANY)] if again else []
     extra = [arrived, done] if again else []
@@ -138,81 +142,92 @@
             ]
             + extra_specs,
             out_specs=pl.BlockSpec(
-                (parts, 1, steps * heads, latent_width),
-                lambda r, ids, _: (0, slot(r, ids), 0, 0),
+                (chips, 1, 1, 2 * steps * heads, latent_width),
+                lambda r, ids, _: (
+                    0,
+                    lax.div(slot(r, ids), rows // 2),
+                    lax.rem(slot(r, ids), rows // 2),
+                    0,
+                    0,
+                ),
             ),
         ),
-        out_shape=jax.ShapeDtypeStruct((parts, rows, steps * heads, latent_width), bf16),
+        out_shape=jax.ShapeDtypeStruct(
+            (chips, 2, rows // 2, 2 * steps * heads, latent_width), bf16
+        ),
         input_output_aliases={6: 0} if again else {},
         compiler_params=params(),
         name="again" if again else "attend",
     )(ids, lengths, cache_t, fresh_t, queries_t, *extra)
 
 
-def project(ids, half, rows, weights, cuts, near=None):
-    groups, _, count, depth = rows.shape
-    width = weights[0].shape[1]
+def project(ids, rows, weights, cuts):
+    groups, count, depth = rows.shape
+    width = weights[0][0].shape[1]
     blocks = len(weights)
     per = groups // cuts
+    flat = [w for weight in weights for w in weight]
 
     def body(ids_ref, rows_ref, *refs):
         out_ref = refs[-1]
         lhs = rows_ref[...].reshape(per * count, depth)
+        n = 0
         for k in range(blocks):
-            at = lax.rem(ids_ref[2] + k, blocks)
-            total = jnp.dot(lhs, refs[k][...], preferred_element_type=f32)
-            total = total.reshape(per, count, width)
-            if near is not None:
-                total = total + refs[blocks][:, at].astype(f32)
-            out_ref[:, at] = total.astype(bf16)
-
-    block = pl.BlockSpec((per, blocks, count, width), lambda i, ids: (i, 0, 0, 0))
-    extra = [] if near is None else [near]
+            total, start = 0.0, 0
+            for w in weights[k]:
+                stop = start + w.shape[0]
+                total += jnp.dot(lhs[:, start:stop], refs[n][...], preferred_element_type=f32)
+                n, start = n + 1, stop
+            at = lax.rem(ids_ref[1] + k, blocks)
+            out_ref[:, at] = total.astype(bf16).reshape(per, count, width)
+
     return pl.pallas_call(
         body,
         grid_spec=pltpu.PrefetchScalarGridSpec(
             num_scalar_prefetch=1,
             grid=(cuts,),
-            in_specs=[pl.BlockSpec((per, 1, count, depth), lambda i, ids: (i, half(ids), 0, 0))]
-            + [whole(w.shape) for w in weights]
-            + [block for _ in extra],
-            out_specs=block,
+            in_specs=[pl.BlockSpec((per, count, depth), lambda i, ids: (i, 0, 0))]
+            + [whole(w.shape) for w in flat],
+            out_specs=pl.BlockSpec((per, blocks, count, width), lambda i, ids: (i, 0, 0, 0)),
         ),
         out_shape=jax.ShapeDtypeStruct((groups, blocks, count, width), bf16),
         compiler_params=params(),
         name="project",
-    )(ids, rows, *weights, *extra)
-
-
-def widen(ids, rows, kept, came, side, done=None):
+    )(ids, rows, *flat)
+
+
+def widen(ids, rows, kept, came):
     halves, chunks, _, count, features = rows.shape
-    columns = kept.shape[1]
+    width = kept[0].shape[1]
+    columns = width * len(kept)
     every = halves * chunks * count
-    starts = [0]
-    for w in came:
-        starts.append(starts[-1] + w.shape[0])
-
-    def body(ids_ref, rows_ref, kept_ref, *refs):
+    weights = [w for own, rest in zip(kept, came) for w in [own] + rest]
+
+    def body(ids_ref, rows_ref, *refs):
         out_ref = refs[-1]
-        pair = ids_ref[2]
+        pair = ids_ref[1]
         mine = rows_ref[:, :, pair].reshape(every, features)
         near = rows_ref[:, :, 1 - pair].reshape(every, features)
 
         def put(tile, value):
             value = value.astype(bf16).reshape(halves, chunks, count, value.shape[1])
             for h in range(halves):
-                out_ref[:, 0, h, :, tile] = value[h]
-
-        for at in range(0, columns, TILE):
-            tile = slice(at, at + TILE)
-            total = jnp.dot(mine, kept_ref[:, tile], preferred_element_type=f32)
-            for k in range(len(came)):
-                total += jnp.dot(
-                    near[:, starts[k] : starts[k + 1]],
-                    refs[k][:, tile],
-                    preferred_element_type=f32,
-                )
-            put(tile, total)
+                out_ref[:, h, :, tile] = value[h]
+
+        n = 0
+        for k in range(len(kept)):
+            for at in range(0, width, TILE):
+                tile = slice(at, at + TILE)
+                total = jnp.dot(mine, refs[n][:, tile], preferred_element_type=f32)
+                start = 0
+                for m, w in enumerate(came[k]):
+                    stop = start + w.shape[0]
+                    total += jnp.dot(
+                        near[:, start:stop], refs[n + 1 + m][:, tile], preferred_element_type=f32
+                    )
+                    start = stop
+                put(slice(k * width + at, k * width + at + TILE), total)
+            n += 1 + len(came[k])
         squares = jnp.zeros((every, 1), f32)
         for block in (mine, near):
             wide = block.astype(f32)
@@ -222,24 +237,18 @@
         extra = jnp.where(lane == 0, high, jnp.where(lane == 1, squares - high, 0.0))
         put(slice(columns, columns + 128), extra)
 
-    last = [] if done is None else [done]
     return pl.pallas_call(
         body,
         grid_spec=pltpu.PrefetchScalarGridSpec(
             num_scalar_prefetch=1,
             grid=(1,),
-            in_specs=[whole(rows.shape)]
-            + [whole(w.shape) for w in (kept,) + came]
-            + [pl.BlockSpec(memory_space=pl.ANY) for _ in last],
-            out_specs=pl.BlockSpec(
-                (chunks, 1, halves, count, columns + 128), lambda i, ids: (0, side, 0, 0, 0)
-            ),
-        ),
-        out_shape=jax.ShapeDtypeStruct((chunks, 2, halves, count, columns + 128), bf16),
-        input_output_aliases={3 + len(came): 0} if last else {},
+            in_specs=[whole(rows.shape)] + [whole(w.shape) for w in weights],
+            out_specs=whole((chunks, halves, count, columns + 128)),
+        ),
+        out_shape=jax.ShapeDtypeStruct((chunks, halves, count, columns + 128), bf16),
         compiler_params=params(),
         name="widen",
-    )(ids, rows, kept, *came, *last)
+    )(ids, rows, *weights)
 
 
 def local(
@@ -265,7 +274,7 @@
     rows_out = residual.shape[1] // N_TP
     chunk = rows_out * steps
     count = chunk // 2
-    units = gate_weight.shape[1]
+    features, units = gate_weight.shape
 
     def by_pair(mine, other):
         first = pair == 0
@@ -278,9 +287,11 @@
         return lax.dynamic_index_in_dim(blocks, 1 - pair, 0, False)
 
     out_came = swap(out_proj, "xl")
+    value_ups = jnp.concatenate([value_up, swap(value_up, "c")], axis=0)
+    downs = [down_weight, swap(down_weight, "c")]
     lanes = jnp.arange(N_TP, dtype=jnp.int32)
     own_slot = jnp.sum(jnp.where(lanes == member, move_slot[0], 0))
-    ids = jnp.stack([own_slot, core, pair]).astype(jnp.int32)
+    ids = jnp.stack([own_slot, pair]).astype(jnp.int32)
     cache_t = cache.transpose(0, 2, 1)
     pieces = exchange(leave(ids, cache_t), TP)
     pieces, gate_weight, up_weight = lax.optimization_barrier((pieces, gate_weight, up_weight))
@@ -295,8 +306,6 @@
         scaled(low, high, up_weight, gate_weight) for low, high in zip(CUTS[:-1], CUTS[1:])
     ]
     kept = scaled(0, CUTS[-1], gate_weight, up_weight)
-    came = [swap(sent[0], "xl")]
-
     arrived = exchange(route(move_peer[0], pieces), TP)
     fresh_t = new_latent.transpose(1, 2, 0)
     queries_t = queries.transpose(0, 1, 3, 2)
@@ -304,48 +313,54 @@
     out = attend(
         ids, cache_length, cache_t, fresh_t, queries_t, heads, latent_width, arrived, out
     )
-    out, out_came = lax.optimization_barrier((out, out_came))
-    by_head = exchange(out, TP).reshape(-1, heads, latent_width)
-    by_head, kept, came[0] = lax.optimization_barrier((by_head, kept, came[0]))
+    out, out_came, sent[0] = lax.optimization_barrier((out, out_came, sent[0]))
+    came = [swap(sent[0], "xl")]
+    out_weights = [[w, swap(w, "c")] for w in (out_proj, out_came)]
+    kept = [kept, swap(kept, "c")]
+    out = out.reshape((N_TP,) + out.shape[2:])
+    by_head = exchange(out, TP).reshape(-1, 2 * heads, latent_width)
+    by_head, kept, came, out_weights, value_ups = lax.optimization_barrier(
+        (by_head, kept, came, out_weights, value_ups)
+    )
     value_heads = jnp.einsum(
-        "thl,hlv->thv", by_head, value_up, preferred_element_type=f32
+        "thl,hlv->thv", by_head, value_ups, preferred_element_type=f32
     ).astype(bf16)
 
-    value_heads = value_heads.reshape(2, 2, count, heads * value_width).transpose(1, 0, 2, 3)
+    value_heads = value_heads.reshape(2, 2, count // 2, 2 * heads * value_width)
+    value_heads = value_heads.transpose(1, 0, 2, 3).reshape(2, count, -1)
     value_heads = jnp.broadcast_to(
         value_heads[None, :, None], (2, 2, 2) + value_heads.shape[1:]
     ).reshape((N_DP,) + value_heads.shape[1:])
     gathered = exchange(value_heads, DP)
     gathered, sent[1] = lax.optimization_barrier((gathered, sent[1]))
     came.append(swap(sent[1], "xl"))
-    weights = [out_proj, out_came]
-    away = swap(project(ids, lambda i: 1 - i[1], gathered, weights, 1), "c")
-    total = project(ids, lambda i: i[1], gathered, weights, 1, away)
-    parts = exchange(total, ZY)
+    parts = exchange(project(ids, gathered, out_weights, 1), ZY)
     parts, came[1] = lax.optimization_barrier((parts, came[1]))
-    residue = lax.dynamic_slice_in_dim(residual, member * rows_out, rows_out, 1)
-    residue = residue.transpose(1, 0, 2).reshape(2, count, -1)
+    came = [came, [swap(w, "c") for w in came]]
+    residue = lax.dynamic_slice_in_dim(residual, lax.div(member, 2) * 2 * rows_out, 2 * rows_out, 1)
+    residue = residue.reshape(steps, 2, 2, rows_out // 8, 2, 2, features)
+    residue = lax.dynamic_index_in_dim(residue, core, 4, False)
+    residue = residue.transpose(2, 1, 3, 4, 0, 5).reshape(2, count, features)
     residue = by_pair(at_pair(residue), swap(at_other(residue), "xl"))
     hidden = residue.astype(f32) + jnp.sum(parts.astype(f32), axis=0)
 
-    own = spread(hidden.astype(bf16), PAIR, 2 * N_ZY).reshape((2, N_ZY) + hidden.shape)
-    other = swap(own, "c")
-    came = tuple(came)
-    wide = widen(ids, own, kept, came, 0)
-    wide = widen(ids, other, kept, came, 1, wide)
-    sums = exchange(wide.reshape(N_DP, 2 * chunk, -1), DP)
-    sums = jnp.sum(sums.reshape(2, 2, 2, 2 * chunk, -1).astype(f32), axis=(0, 2))
-    squares = sums[0, :, units] + sums[0, :, units + 1]
+    rows = spread(hidden.astype(bf16), PAIR, 2 * N_ZY).reshape((2, N_ZY) + hidden.shape)
+    sums = exchange(widen(ids, rows, kept, came).reshape(N_DP, chunk, -1), DP)
+    sums = jnp.sum(sums.reshape(2, 2, 2, chunk, -1).astype(f32), axis=(0, 2))
+    squares = sums[0, :, 2 * units] + sums[0, :, 2 * units + 1]
     inverse = lax.rsqrt(squares / D + norm_eps)[:, None]
-    active = jax.nn.silu(sums[0, :, :units] * inverse) * (sums[1, :, :units] * inverse)
-    active = spread(active.astype(bf16), DP, N_DP).reshape(N_DP, 2, chunk, units)
-
-    away = swap(project(ids, lambda i: 1, active, [down_weight], 2), "c")
-    total = project(ids, lambda i: 0, active, [down_weight], 2, away)
-    parts = exchange(total.reshape(N_ZY, chunk, -1), ZY)
+    active = sums[:, :, : 2 * units] * inverse
+    active = (jax.nn.silu(active[0]) * active[1]).astype(bf16)
+    parts = exchange(project(ids, spread(active, DP, N_DP), [downs], 2)[:, 0], ZY)
     hidden = by_pair(at_pair(hidden), swap(at_other(hidden), "xl")).reshape(chunk, -1)
     result = (hidden + jnp.sum(parts.astype(f32), axis=0)).astype(bf16)
-    return result.reshape(rows_out, steps, -1).transpose(1, 0, 2)
+
+    result = result.reshape(2, 2, rows_out // 8, 2, steps, features)
+    mine = lax.dynamic_index_in_dim(result, core, 1, False)
+    near = swap(lax.dynamic_index_in_dim(result, 1 - core, 1, False), "c")
+    first = core == 0
+    result = jnp.stack([jnp.where(first, mine, near), jnp.where(first, near, mine)])
+    return result.transpose(4, 1, 2, 0, 3, 5).reshape(steps, rows_out, features)
 
 
 def solution(mesh):

time: 282 us -> 284 us (level)
  blocking collectives: 117 us -> 0 us
  waiting for transfers between devices: 65.2 us -> 152 us
  starting transfers between devices: 36.8 us -> 59 us
  Pallas kernels: 31.9 us -> 41.3 us
  local copies, waits for them, and re-layouts: 17.4 us -> 9.67 us
  other arithmetic: 10.1 us -> 17.5 us
    all_to_all x4 -> x0, blocking collectives: 117 us -> none  [exchange(): return lax.all_to_all(blocks, axes, 0, 0, tiled=True)]
    all_to_all x5 -> x9, waiting for transfers between devices: 23.9 us -> 113 us  [exchange(): return lax.all_to_all(blocks, axes, 0, 0, tiled=True)]
    all_to_all x5 -> x9, starting transfers between devices: 26.1 us -> 46.7 us  [exchange(): return lax.all_to_all(blocks, axes, 0, 0, tiled=True)]
    unnamed x47 -> x16, local copies, waits for them, and re-layouts: 14.4 us -> 3.4 us
    pallas_call x2, Pallas kernels: 5.38 us -> 9.69 us  [attend(): pl.pallas_call(body, grid_spec=pltpu.PrefetchScalarGridSpec(num_scalar_pr...]
    concatenate x0 -> x1, other arithmetic: none -> 3.1 us  [local(): value_ups = jnp.concatenate([value_up, swap(value_up, 'c')], axis=0)]
    ppermute x8 -> x13, waiting for transfers between devices: 41.3 us -> 38.9 us  [swap(): return lax.ppermute(block, axis, SWAP)]
    ppermute x8 -> x13, starting transfers between devices: 10.7 us -> 12.3 us  [swap(): return lax.ppermute(block, axis, SWAP)]
  transfers between devices with their start and end apart: 13 -> 22, of which waited for: 8 -> 14; matrix products, arithmetic and copies ran while one was open for 4% -> 7% of each run, Pallas kernels for 6% -> 8%
where the time goes in v6:
time: 284 us; the launch traced here: 283 us
  waiting for transfers between devices  152 us (54%)
  starting transfers between devices  59 us (21%)
  Pallas kernels  41.3 us (15%)
  other arithmetic  17.5 us (6%)
  local copies, waits for them, and re-layouts  9.67 us (3%)
  matrix products  2.91 us (1%)
    all_to_all x9, waiting for transfers between devices, exchange(): return lax.all_to_all(blocks, axes, 0, 0, tiled=True)  113 us
    all_to_all x9, starting transfers between devices, exchange(): return lax.all_to_all(blocks, axes, 0, 0, tiled=True)  46.7 us
    ppermute x13, waiting for transfers between devices, swap(): return lax.ppermute(block, axis, SWAP)  38.9 us
    pallas_call x2, Pallas kernels, project(): pl.pallas_call(body, grid_spec=pltpu.PrefetchScalarGridSpec(num_scalar_pr...  14.5 us
    pallas_call x1, Pallas kernels, widen(): pl.pallas_call(body, grid_spec=pltpu.PrefetchScalarGridSpec(num_scalar_pr...  12.4 us
    ppermute x13, starting transfers between devices, swap(): return lax.ppermute(block, axis, SWAP)  12.3 us
    pallas_call x2, Pallas kernels, attend(): pl.pallas_call(body, grid_spec=pltpu.PrefetchScalarGridSpec(num_scalar_pr...  9.69 us
    convert_element_type x3, other arithmetic, scaled(): return (weight.astype(f32) * gain[low:high]).astype(bf16)  8.37 us
  transfers between devices with their start and end apart: 22, of which 14 were waited for; matrix products, arithmetic and copies ran while one was open for 7% of the time, Pallas kernels for 8%

profile of v6, /device:TPU:1, one launch (start us, length us, event | category | flops | bytes accessed | tf_op | source)
XLA Modules:
  0.0 282.8 jit_solution(13110120542839291118)
XLA Ops:
  0.0 2.1 collective-permute-start.1
  2.1 1.3 fusion.13
  3.4 1.3 pad_add_fusion.ids_ref
  4.7 2.4 leave.1
  7.1 8.8 %all-to-all-start = ((bf16[16,36,256]{2,1,0:T(8,128)(2,1)}), bf16[16,36,256]{2,1,0:T(8,128)(2,1)S(1)}, u32[]{:S(2)}, u32[]{:S(2)}) async-start(bf16[16,36,256]{2,1,0:T(8,128)(2,1)} %leave.1), calls=%async_computation | async-start | bytes 655360 | tf_op jit(solution)/shard_map/all_to_all | solution.py:28
  16.1 1.2 copy.55
  17.2 6.3 %attend.1.refs_1_ = bf16[8,2,2,32,512]{4,3,2,1,0:T(8,128)(2,1)} custom-call(s32[2]{0:T(128)} %pad_add_fusion.ids_ref, s32[4]{0:T(128)} %lengths_ref.3, bf16[4,576,256]{2,1,0:T(8,128)(2,1)} %bitcast.61, bf16[4,576,2]{2,1,0:T(8,128)(2,1)} %bitcast.65, bf16[2,4,576,128]{3,2,1,0:T(8,128)(2,1)} %bitcast.67), custom_call_target="tpu_custom_call" | custom-call | tf_op jit(solution)/shard_map/attend/pallas_call | solution.py:131
  23.5 1.5 all-to-all-done.in_ref
  25.7 2.4 route.1
  28.1 5.8 %all-to-all-start.1 = ((bf16[16,36,256]{2,1,0:T(8,128)(2,1)}), bf16[16,36,256]{2,1,0:T(8,128)(2,1)S(1)}, u32[]{:S(2)}, u32[]{:S(2)}) async-start(bf16[16,36,256]{2,1,0:T(8,128)(2,1)} %route.1), calls=%async_computation.1 | async-start | bytes 655360 | tf_op jit(solution)/shard_map/all_to_all | solution.py:28
  33.9 3.5 %multiply_convert_fusion.refs_0_ = bf16[896,1152]{1,0:T(8,128)(2,1)} fusion(f32[896]{0:T(1024)S(1)} %convert_element_type.63, bf16[896,1152]{1,0:T(8,128)(2,1)} %param.23, bf16[896,1152]{1,0:T(8,128)(2,1)} %param.24, pred[]{:T(512)S(6)} %eq.17), kind=kLoop, calls=%fused_computation.1 | loop fusion | flops 4128768 | bytes 6196737 | tf_op jit(solution)/shard_map/convert_element_type | solution.py:303
  37.5 1.4 multiply_convert_fusion.2
  38.9 4.1 %all-to-all-done.1.refs_0_ = bf16[16,36,256]{2,1,0:T(8,128)(2,1)S(1)} async-done(((bf16[16,36,256]{2,1,0:T(8,128)(2,1)}), bf16[16,36,256]{2,1,0:T(8,128)(2,1)S(1)}, u32[]{:S(2)}, u32[]{:S(2)}) %all-to-all-start.1) | async-done | bytes 294944 | tf_op jit(solution)/shard_map/all_to_all | solution.py:28
  43.0 0.7 copy-done.3
  43.7 3.4 %again.1 = bf16[8,2,2,32,512]{4,3,2,1,0:T(8,128)(2,1)} custom-call(s32[2]{0:T(128)} %pad_add_fusion.ids_ref, s32[4]{0:T(128)} %lengths_ref.3, bf16[4,576,256]{2,1,0:T(8,128)(2,1)} %bitcast.62, bf16[4,576,2]{2,1,0:T(8,128)(2,1)} %bitcast.66, bf16[2,4,576,128]{3,2,1,0:T(8,128)(2,1)} %bitcast.68, ...), custom_call_target="tpu_custom_call", output_to_operand_aliasing={{}: (6, {})} | custom-call | tf_op jit(solution)/shard_map/again/pallas_call | solution.py:131
  47.1 1.0 collective-permute-start.5
  48.3 3.9 %all-to-all-start.2 = ((bf16[16,2,32,512]{3,2,1,0:T(8,128)(2,1)}), bf16[16,2,32,512]{3,2,1,0:T(8,128)(2,1)S(1)}, u32[]{:S(2)}, u32[]{:S(2)}) async-start(bf16[16,2,32,512]{3,2,1,0:T(8,128)(2,1)} %bitcast.64), calls=%async_computation.2 | async-start | bytes 2097152 | tf_op jit(solution)/shard_map/all_to_all | solution.py:28
  52.1 1.0 collective-permute-start.3
  53.4 3.1 %pad_maximum_fusion = bf16[16,512,128]{2,1,0:T(8,128)(2,1)} fusion(bf16[8,512,128]{2,1,0:T(8,128)(2,1)} %collective-permute-done.6, bf16[8,512,128]{2,1,0:T(8,128)(2,1)} %param.19), kind=kLoop, calls=%fused_computation.3 | loop fusion | flops 1048576 | bytes 4194304 | tf_op jit(solution)/shard_map/concatenate | solution.py:290
  56.5 10.3 %collective-permute-done.3.refs_1_ = bf16[256,1152]{1,0:T(8,128)(2,1)} collective-permute-done((bf16[256,1152]{1,0:T(8,128)(2,1)S(1)}, bf16[256,1152]{1,0:T(8,128)(2,1)}, u32[]{:S(2)}, u32[]{:S(2)}) %collective-permute-start.3) | collective-permute-done | bytes 589856 | tf_op jit(solution)/shard_map/ppermute | solution.py:36
  66.9 2.7 all-to-all-done.2
  69.6 2.9 %fusion = bf16[64,16,128]{2,0,1:T(8,128)(2,1)S(1)} fusion(bf16[16,512,128]{2,1,0:T(8,128)(2,1)} %pad_maximum_fusion, bf16[64,16,512]{2,1,0:T(8,128)(2,1)S(1)} %bitcast.70), kind=kOutput, calls=%fused_computation.9 | convolution fusion | flops 134348800 | bytes 3407872 | tf_op jit(solution)/shard_map/thl,hlv->thv/dot_general | solution.py:325
  72.8 1.2 broadcast_in_dim.28
  74.0 4.2 %all-to-all-start.3 = ((bf16[8,32,2048]{2,1,0:T(8,128)(2,1)}), bf16[8,32,2048]{2,1,0:T(8,128)(2,1)S(1)}, u32[]{:S(2)}, u32[]{:S(2)}) async-start(bf16[8,32,2048]{2,1,0:T(8,128)(2,1)} %bitcast.69), calls=%async_computation.3 | async-start | bytes 2097152 | tf_op jit(solution)/shard_map/all_to_all | solution.py:28
  78.2 3.4 %multiply_convert_fusion.1 = bf16[640,1152]{1,0:T(8,128)(2,1)} fusion(f32[640]{0:T(1024)S(1)} %slice.40, bf16[896,1152]{1,0:T(8,128)(2,1)} %param.23, bf16[896,1152]{1,0:T(8,128)(2,1)} %param.24, pred[]{:T(512)S(6)} %eq.17), kind=kLoop, calls=%fused_computation.2 | loop fusion | flops 2949120 | bytes 4426241 | tf_op jit(solution)/shard_map/convert_element_type | solution.py:303
  81.7 11.7 %all-to-all-done.3.rows_ref = bf16[8,32,2048]{2,1,0:T(8,128)(2,1)S(1)} async-done(((bf16[8,32,2048]{2,1,0:T(8,128)(2,1)}), bf16[8,32,2048]{2,1,0:T(8,128)(2,1)S(1)}, u32[]{:S(2)}, u32[]{:S(2)}) %all-to-all-start.3) | async-done | bytes 1048608 | tf_op jit(solution)/shard_map/all_to_all | solution.py:28
  94.3 7.4 %project.2 = bf16[8,2,32,896]{3,2,1,0:T(8,128)(2,1)} custom-call(s32[2]{0:T(128)} %pad_add_fusion.ids_ref, bf16[8,32,2048]{2,1,0:T(8,128)(2,1)} %copy-done.1, bf16[1024,896]{1,0:T(8,128)(2,1)} %refs_0_.1, bf16[1024,896]{1,0:T(8,128)(2,1)} %collective-permute-done.4.refs_1_, bf16[1024,896]{1,0:T(8,128)(2,1)} %collective-permute-done.1.refs_2_, ...), custom_call_target="tpu_custom_call" | custom-call | tf_op jit(solution)/shard_map/project/pallas_call | solution.py:184
  101.7 4.0 %all-to-all-start.4 = ((bf16[8,2,32,896]{3,2,1,0:T(8,128)(2,1)}), bf16[8,2,32,896]{3,2,1,0:T(8,128)(2,1)S(1)}, u32[]{:S(2)}, u32[]{:S(2)}) async-start(bf16[8,2,32,896]{3,2,1,0:T(8,128)(2,1)} %project.2), calls=%async_computation.4 | async-start | bytes 1835008 | tf_op jit(solution)/shard_map/all_to_all | solution.py:28
  107.0 20.0 %collective-permute-done = bf16[32,896]{1,0:T(8,128)(2,1)S(1)} collective-permute-done((bf16[32,896]{1,0:T(8,128)(2,1)S(1)}, bf16[32,896]{1,0:T(8,128)(2,1)S(1)}, u32[]{:S(2)}, u32[]{:S(2)}) %collective-permute-start) | collective-permute-done | bytes 57376 | tf_op jit(solution)/shard_map/ppermute | solution.py:36
  127.2 1.4 broadcast_in_dim.29
  128.7 4.4 %all-to-all-start.5 = ((bf16[16,2,32,896]{3,2,1,0:T(8,128)(2,1)}), bf16[16,2,32,896]{3,2,1,0:T(8,128)(2,1)}, u32[]{:S(2)}, u32[]{:S(2)}) async-start(bf16[16,2,32,896]{3,2,1,0:T(8,128)(2,1)} %broadcast_in_dim.29), calls=%async_computation.5 | async-start | bytes 3670016 | tf_op jit(solution)/shard_map/all_to_all | solution.py:28
  133.1 2.6 collective-permute-start.10
  135.9 3.8 %collective-permute-done.9.refs_4_ = bf16[256,1152]{1,0:T(8,128)(2,1)} collective-permute-done((bf16[256,1152]{1,0:T(8,128)(2,1)}, bf16[256,1152]{1,0:T(8,128)(2,1)}, u32[]{:S(2)}, u32[]{:S(2)}) %collective-permute-start.9) | collective-permute-done | bytes 589856 | tf_op jit(solution)/shard_map/ppermute | solution.py:36
  139.7 18.1 %all-to-all-done.5 = bf16[16,2,32,896]{3,2,1,0:T(8,128)(2,1)} async-done(((bf16[16,2,32,896]{3,2,1,0:T(8,128)(2,1)}), bf16[16,2,32,896]{3,2,1,0:T(8,128)(2,1)}, u32[]{:S(2)}, u32[]{:S(2)}) %all-to-all-start.5) | async-done | bytes 1835040 | tf_op jit(solution)/shard_map/all_to_all | solution.py:28
  157.9 12.4 %widen.1 = bf16[8,2,32,2432]{3,2,1,0:T(8,128)(2,1)} custom-call(s32[2]{0:T(128)} %pad_add_fusion.ids_ref, bf16[2,8,2,32,896]{4,3,2,1,0:T(8,128)(2,1)} %bitcast.22.rows_ref, bf16[896,1152]{1,0:T(8,128)(2,1)} %multiply_convert_fusion.refs_0_, bf16[256,1152]{1,0:T(8,128)(2,1)} %collective-permute-done.3.refs_1_, ...), custom_call_target="tpu_custom_call" | custom-call | tf_op jit(solution)/shard_map/widen/pallas_call | solution.py:240
  170.3 4.9 %all-to-all-start.6 = ((bf16[8,64,2432]{2,1,0:T(8,128)(2,1)}), bf16[8,64,2432]{2,1,0:T(8,128)(2,1)}, u32[]{:S(2)}, u32[]{:S(2)}) async-start(bf16[8,64,2432]{2,1,0:T(8,128)(2,1)} %bitcast.63), calls=%async_computation.6 | async-start | bytes 4980736 | tf_op jit(solution)/shard_map/all_to_all | solution.py:28
  175.2 3.0 %collective-permute-start.11 = (bf16[1152,896]{1,0:T(8,128)(2,1)}, bf16[1152,896]{1,0:T(8,128)(2,1)}, u32[]{:S(2)}, u32[]{:S(2)}) collective-permute-start(bf16[1152,896]{1,0:T(8,128)(2,1)} %refs_0_.2), channel_id=1, source_target_pairs={{0,1},{1,0},{2,3},{3,2},{4,5},{5,4},{6,7},{7,6},{8,9},{9,8},{10,11... | collective-permute-start | bytes 6193160 | tf_op jit(solution)/shard_map/ppermute | solution.py:36
  178.2 30.9 %all-to-all-done.6 = bf16[8,64,2432]{2,1,0:T(8,128)(2,1)} async-done(((bf16[8,64,2432]{2,1,0:T(8,128)(2,1)}), bf16[8,64,2432]{2,1,0:T(8,128)(2,1)}, u32[]{:S(2)}, u32[]{:S(2)}) %all-to-all-start.6) | async-done | bytes 2490400 | tf_op jit(solution)/shard_map/all_to_all | solution.py:28
  209.1 2.2 convert_reduce_fusion
  211.8 1.6 broadcast_in_dim.31
  213.4 4.4 %all-to-all-start.7 = ((bf16[8,64,2304]{2,1,0:T(8,128)(2,1)}), bf16[8,64,2304]{2,1,0:T(8,128)(2,1)}, u32[]{:S(2)}, u32[]{:S(2)}) async-start(bf16[8,64,2304]{2,1,0:T(8,128)(2,1)} %broadcast_in_dim.31), calls=%async_computation.7 | async-start | bytes 4718592 | tf_op jit(solution)/shard_map/all_to_all | solution.py:28
  217.8 32.2 %all-to-all-done.7.rows_ref = bf16[8,64,2304]{2,1,0:T(8,128)(2,1)} async-done(((bf16[8,64,2304]{2,1,0:T(8,128)(2,1)}), bf16[8,64,2304]{2,1,0:T(8,128)(2,1)}, u32[]{:S(2)}, u32[]{:S(2)}) %all-to-all-start.7) | async-done | bytes 2359328 | tf_op jit(solution)/shard_map/all_to_all | solution.py:28
  250.0 7.1 %project.3 = bf16[8,1,64,896]{3,2,1,0:T(8,128)(2,1)} custom-call(s32[2]{0:T(128)} %pad_add_fusion.ids_ref, bf16[8,64,2304]{2,1,0:T(8,128)(2,1)} %all-to-all-done.7.rows_ref, bf16[1152,896]{1,0:T(8,128)(2,1)} %refs_0_.2, bf16[1152,896]{1,0:T(8,128)(2,1)} %collective-permute-done.11.refs_1_), custom_call_target="tpu_custom_call" | custom-call | tf_op jit(solution)/shard_map/project/pallas_call | solution.py:184
  257.1 6.4 %all-to-all-start.8 = ((bf16[8,64,896]{2,1,0:T(8,128)(2,1)}), bf16[8,64,896]{2,1,0:T(8,128)(2,1)S(1)}, u32[]{:S(2)}, u32[]{:S(2)}) async-start(bf16[8,64,896]{2,1,0:T(8,128)(2,1)} %bitcast.71), calls=%async_computation.8 | async-start | bytes 1835008 | tf_op jit(solution)/shard_map/all_to_all | solution.py:28
  263.6 3.6 %collective-permute-done.8 = f32[32,896]{1,0:T(8,128)S(1)} collective-permute-done((f32[32,896]{1,0:T(8,128)S(1)}, f32[32,896]{1,0:T(8,128)S(1)}, u32[]{:S(2)}, u32[]{:S(2)}) %collective-permute-start.8) | collective-permute-done | bytes 114720 | tf_op jit(solution)/shard_map/ppermute | solution.py:36
  267.4 12.0 %all-to-all-done.8 = bf16[8,64,896]{2,1,0:T(8,128)(2,1)S(1)} async-done(((bf16[8,64,896]{2,1,0:T(8,128)(2,1)}), bf16[8,64,896]{2,1,0:T(8,128)(2,1)S(1)}, u32[]{:S(2)}, u32[]{:S(2)}) %all-to-all-start.8) | async-done | bytes 917536 | tf_op jit(solution)/shard_map/all_to_all | solution.py:28
  279.9 0.9 collective-permute-start.12
  280.9 0.9 collective-permute-done.12
  (59 shorter events, 6.6 us)
Async XLA Ops:
  0.0 105.7 %copy-start = (bf16[2,512,896]{2,1,0:T(8,128)(2,1)S(1)}, bf16[2,512,896]{2,1,0:T(8,128)(2,1)}, u32[]{:S(2)}) copy-start(bf16[2,512,896]{2,1,0:T(8,128)(2,1)} %param.21) | copy-start | bytes 5505028
  0.0 16.0 %copy-start.5 = (bf16[896]{0:T(1024)(128)(2,1)S(1)}, bf16[896]{0:T(1024)(128)(2,1)}, u32[]{:S(2)}) copy-start(bf16[896]{0:T(1024)(128)(2,1)} %param.22) | copy-start | bytes 5380
  0.0 16.0 %copy-start.6 = (bf16[2,4,576]{2,1,0:T(4,128)(2,1)S(1)}, bf16[2,4,576]{2,1,0:T(4,128)(2,1)}, u32[]{:S(2)}) copy-start(bf16[2,4,576]{2,1,0:T(4,128)(2,1)} %param.18) | copy-start | bytes 27652
  0.0 47.1 %collective-permute-start.1 = (bf16[1024,896]{1,0:T(8,128)(2,1)}, bf16[1024,896]{1,0:T(8,128)(2,1)}, u32[]{:S(2)}, u32[]{:S(2)}) collective-permute-start(bf16[1024,896]{1,0:T(8,128)(2,1)} %refs_0_.1), channel_id=1, source_target_pairs={{0,32},{32,0},{1,33},{33,1},{2,34},{34,2},{3,35},{35,3},{4,36},{36... | collective-permute-start | bytes 5505032 | tf_op jit(solution)/shard_map/ppermute | solution.py:36
  7.1 17.9 %all-to-all-start = ((bf16[16,36,256]{2,1,0:T(8,128)(2,1)}), bf16[16,36,256]{2,1,0:T(8,128)(2,1)S(1)}, u32[]{:S(2)}, u32[]{:S(2)}) async-start(bf16[16,36,256]{2,1,0:T(8,128)(2,1)} %leave.1), calls=%async_computation | async-start | bytes 655360 | tf_op jit(solution)/shard_map/all_to_all | solution.py:28
  15.9 40.7 %collective-permute-start.4 = (bf16[1024,896]{1,0:T(8,128)(2,1)}, bf16[1024,896]{1,0:T(8,128)(2,1)}, u32[]{:S(2)}, u32[]{:S(2)}) collective-permute-start(bf16[1024,896]{1,0:T(8,128)(2,1)} %refs_0_.1), channel_id=1, source_target_pairs={{0,1},{1,0},{2,3},{3,2},{4,5},{5,4},{6,7},{7,6},{8,9},{9,8},{10,11... | collective-permute-start | bytes 5505032 | tf_op jit(solution)/shard_map/ppermute | solution.py:36
  25.0 0.7 copy-start.4
  28.1 14.9 %all-to-all-start.1 = ((bf16[16,36,256]{2,1,0:T(8,128)(2,1)}), bf16[16,36,256]{2,1,0:T(8,128)(2,1)S(1)}, u32[]{:S(2)}, u32[]{:S(2)}) async-start(bf16[16,36,256]{2,1,0:T(8,128)(2,1)} %route.1), calls=%async_computation.1 | async-start | bytes 655360 | tf_op jit(solution)/shard_map/all_to_all | solution.py:28
  37.4 19.2 %collective-permute-start.2 = (bf16[896,1152]{1,0:T(8,128)(2,1)}, bf16[896,1152]{1,0:T(8,128)(2,1)}, u32[]{:S(2)}, u32[]{:S(2)}) collective-permute-start(bf16[896,1152]{1,0:T(8,128)(2,1)} %multiply_convert_fusion.refs_0_), channel_id=1, source_target_pairs={{0,1},{1,0},{2,3},{3,2},{4,5},{5,4},{6,7},{7,6},{8,9},{9,8},{10,11... | collective-permute-start | bytes 6193160 | tf_op jit(solution)/shard_map/ppermute | solution.py:36
  43.0 0.7 copy-start.3
  47.1 22.5 %collective-permute-start.5 = (bf16[1024,896]{1,0:T(8,128)(2,1)}, bf16[1024,896]{1,0:T(8,128)(2,1)}, u32[]{:S(2)}, u32[]{:S(2)}) collective-permute-start(bf16[1024,896]{1,0:T(8,128)(2,1)} %collective-permute-done.1.refs_2_), channel_id=1, source_target_pairs={{0,1},{1,0},{2,3},{3,2},{4,5},{5,4},{6,7},{7,6},{8,9},{9,8},{10,11... | collective-permute-start | bytes 5505032 | tf_op jit(solution)/shard_map/ppermute | solution.py:36
  48.2 5.3 %collective-permute-start.6 = (bf16[8,512,128]{2,1,0:T(8,128)(2,1)}, bf16[8,512,128]{2,1,0:T(8,128)(2,1)}, u32[]{:S(2)}, u32[]{:S(2)}) collective-permute-start(bf16[8,512,128]{2,1,0:T(8,128)(2,1)} %param.19), channel_id=1, source_target_pairs={{0,1},{1,0},{2,3},{3,2},{4,5},{5,4},{6,7},{7,6},{8,9},{9,8},{10,11... | collective-permute-start | bytes 3145736 | tf_op jit(solution)/shard_map/ppermute | solution.py:36
  48.3 21.3 %all-to-all-start.2 = ((bf16[16,2,32,512]{3,2,1,0:T(8,128)(2,1)}), bf16[16,2,32,512]{3,2,1,0:T(8,128)(2,1)S(1)}, u32[]{:S(2)}, u32[]{:S(2)}) async-start(bf16[16,2,32,512]{3,2,1,0:T(8,128)(2,1)} %bitcast.64), calls=%async_computation.2 | async-start | bytes 2097152 | tf_op jit(solution)/shard_map/all_to_all | solution.py:28
  52.1 14.7 %collective-permute-start.3 = (bf16[256,1152]{1,0:T(8,128)(2,1)S(1)}, bf16[256,1152]{1,0:T(8,128)(2,1)}, u32[]{:S(2)}, u32[]{:S(2)}) collective-permute-start(bf16[256,1152]{1,0:T(8,128)(2,1)S(1)} %multiply_convert_fusion.2), channel_id=1, source_target_pairs={{0,32},{32,0},{1,33},{33,1},{2,34},{34,2},{3,35},{35,3},{4,36},{36... | collective-permute-start | bytes 1769480 | tf_op jit(solution)/shard_map/ppermute | solution.py:36
  74.0 19.3 %all-to-all-start.3 = ((bf16[8,32,2048]{2,1,0:T(8,128)(2,1)}), bf16[8,32,2048]{2,1,0:T(8,128)(2,1)S(1)}, u32[]{:S(2)}, u32[]{:S(2)}) async-start(bf16[8,32,2048]{2,1,0:T(8,128)(2,1)} %bitcast.69), calls=%async_computation.3 | async-start | bytes 2097152 | tf_op jit(solution)/shard_map/all_to_all | solution.py:28
  93.3 1.0 copy-start.1
  93.3 33.7 %collective-permute-start.7 = (bf16[640,1152]{1,0:T(8,128)(2,1)}, bf16[640,1152]{1,0:T(8,128)(2,1)}, u32[]{:S(2)}, u32[]{:S(2)}) collective-permute-start(bf16[640,1152]{1,0:T(8,128)(2,1)} %multiply_convert_fusion.1), channel_id=1, source_target_pairs={{0,32},{32,0},{1,33},{33,1},{2,34},{34,2},{3,35},{35,3},{4,36},{36... | collective-permute-start | bytes 4423688 | tf_op jit(solution)/shard_map/ppermute | solution.py:36
  101.7 25.3 %all-to-all-start.4 = ((bf16[8,2,32,896]{3,2,1,0:T(8,128)(2,1)}), bf16[8,2,32,896]{3,2,1,0:T(8,128)(2,1)S(1)}, u32[]{:S(2)}, u32[]{:S(2)}) async-start(bf16[8,2,32,896]{3,2,1,0:T(8,128)(2,1)} %project.2), calls=%async_computation.4 | async-start | bytes 1835008 | tf_op jit(solution)/shard_map/all_to_all | solution.py:28
  106.4 20.6 %collective-permute-start = (bf16[32,896]{1,0:T(8,128)(2,1)S(1)}, bf16[32,896]{1,0:T(8,128)(2,1)S(1)}, u32[]{:S(2)}, u32[]{:S(2)}) collective-permute-start(bf16[32,896]{1,0:T(8,128)(2,1)S(1)} %bitcast.77), channel_id=1, source_target_pairs={{0,32},{32,0},{1,33},{33,1},{2,34},{34,2},{3,35},{35,3},{4,36},{36... | collective-permute-start | bytes 172040 | tf_op jit(solution)/shard_map/ppermute | solution.py:36
  128.7 29.2 %all-to-all-start.5 = ((bf16[16,2,32,896]{3,2,1,0:T(8,128)(2,1)}), bf16[16,2,32,896]{3,2,1,0:T(8,128)(2,1)}, u32[]{:S(2)}, u32[]{:S(2)}) async-start(bf16[16,2,32,896]{3,2,1,0:T(8,128)(2,1)} %broadcast_in_dim.29), calls=%async_computation.5 | async-start | bytes 3670016 | tf_op jit(solution)/shard_map/all_to_all | solution.py:28
  133.1 6.7 %collective-permute-start.10 = (bf16[640,1152]{1,0:T(8,128)(2,1)}, bf16[640,1152]{1,0:T(8,128)(2,1)S(1)}, u32[]{:S(2)}, u32[]{:S(2)}) collective-permute-start(bf16[640,1152]{1,0:T(8,128)(2,1)} %collective-permute-done.7.refs_2_), channel_id=1, source_target_pairs={{0,1},{1,0},{2,3},{3,2},{4,5},{5,4},{6,7},{7,6},{8,9},{9,8},{10,11... | collective-permute-start | bytes 4423688 | tf_op jit(solution)/shard_map/ppermute | solution.py:36
  135.7 4.1 %collective-permute-start.9 = (bf16[256,1152]{1,0:T(8,128)(2,1)}, bf16[256,1152]{1,0:T(8,128)(2,1)}, u32[]{:S(2)}, u32[]{:S(2)}) collective-permute-start(bf16[256,1152]{1,0:T(8,128)(2,1)} %collective-permute-done.3.refs_1_), channel_id=1, source_target_pairs={{0,1},{1,0},{2,3},{3,2},{4,5},{5,4},{6,7},{7,6},{8,9},{9,8},{10,11... | collective-permute-start | bytes 1769480 | tf_op jit(solution)/shard_map/ppermute | solution.py:36
  139.7 18.2 %copy-start.2 = (bf16[640,1152]{1,0:T(8,128)(2,1)}, bf16[640,1152]{1,0:T(8,128)(2,1)S(1)}, u32[]{:S(2)}) copy-start(bf16[640,1152]{1,0:T(8,128)(2,1)S(1)} %collective-permute-done.10.refs_5_) | copy-start | bytes 4423684
  170.3 38.8 %all-to-all-start.6 = ((bf16[8,64,2432]{2,1,0:T(8,128)(2,1)}), bf16[8,64,2432]{2,1,0:T(8,128)(2,1)}, u32[]{:S(2)}, u32[]{:S(2)}) async-start(bf16[8,64,2432]{2,1,0:T(8,128)(2,1)} %bitcast.63), calls=%async_computation.6 | async-start | bytes 4980736 | tf_op jit(solution)/shard_map/all_to_all | solution.py:28
  175.2 42.6 %collective-permute-start.11 = (bf16[1152,896]{1,0:T(8,128)(2,1)}, bf16[1152,896]{1,0:T(8,128)(2,1)}, u32[]{:S(2)}, u32[]{:S(2)}) collective-permute-start(bf16[1152,896]{1,0:T(8,128)(2,1)} %refs_0_.2), channel_id=1, source_target_pairs={{0,1},{1,0},{2,3},{3,2},{4,5},{5,4},{6,7},{7,6},{8,9},{9,8},{10,11... | collective-permute-start | bytes 6193160 | tf_op jit(solution)/shard_map/ppermute | solution.py:36
  213.4 36.6 %all-to-all-start.7 = ((bf16[8,64,2304]{2,1,0:T(8,128)(2,1)}), bf16[8,64,2304]{2,1,0:T(8,128)(2,1)}, u32[]{:S(2)}, u32[]{:S(2)}) async-start(bf16[8,64,2304]{2,1,0:T(8,128)(2,1)} %broadcast_in_dim.31), calls=%async_computation.7 | async-start | bytes 4718592 | tf_op jit(solution)/shard_map/all_to_all | solution.py:28
  257.1 22.3 %all-to-all-start.8 = ((bf16[8,64,896]{2,1,0:T(8,128)(2,1)}), bf16[8,64,896]{2,1,0:T(8,128)(2,1)S(1)}, u32[]{:S(2)}, u32[]{:S(2)}) async-start(bf16[8,64,896]{2,1,0:T(8,128)(2,1)} %bitcast.71), calls=%async_computation.8 | async-start | bytes 1835008 | tf_op jit(solution)/shard_map/all_to_all | solution.py:28
  263.5 3.7 %collective-permute-start.8 = (f32[32,896]{1,0:T(8,128)S(1)}, f32[32,896]{1,0:T(8,128)S(1)}, u32[]{:S(2)}, u32[]{:S(2)}) collective-permute-start(f32[32,896]{1,0:T(8,128)S(1)} %dynamic-slice_bitcast_fusion), channel_id=1, source_target_pairs={{0,32},{32,0},{1,33},{33,1},{2,34},{34,2},{3,35},{35,3},{4,36},{36... | collective-permute-start | bytes 344072 | tf_op jit(solution)/shard_map/ppermute | solution.py:36
  279.9 1.8 collective-permute-start.12

commit v7 on v6

--- a/solution.py
+++ b/solution.py
@@ -17,11 +17,11 @@
 N_TP = 16
 N_ZY = 8
 SWAP = [(0, 1), (1, 0)]
-CUTS = (0, 256, 896)
-TILE = 384
+CUTS = (0, 384, 896)
+TILE = 768
 bf16 = jnp.bfloat16
 f32 = jnp.float32
-VMEM = 60 * 1024 * 1024
+MIB = 1024 * 1024
 
 
 def exchange(blocks, axes):
@@ -36,20 +36,24 @@
     return lax.ppermute(block, axis, SWAP)
 
 
-def params():
-    return pltpu.CompilerParams(vmem_limit_bytes=VMEM)
+def params(mib):
+    return pltpu.CompilerParams(vmem_limit_bytes=mib * MIB)
 
 
 def whole(shape):
     return pl.BlockSpec(shape, lambda *_: (0,) * len(shape))
 
 
-def leave(ids, cache_t):
+def leave(slots, cache_t):
     _, entries, length = cache_t.shape
     piece = entries // N_TP
 
-    def body(ids_ref, row_ref, out_ref):
-        row = row_ref[0].astype(f32)
+    def body(slots_ref, cache_ref, out_ref, row_ref, sem):
+        slot = slots_ref[lax.axis_index(TP)]
+        copy = pltpu.make_async_copy(cache_ref.at[slot], row_ref, sem)
+        copy.start()
+        copy.wait()
+        row = row_ref[...].astype(f32)
         for j in range(N_TP):
             out_ref[j] = row[j * piece : (j + 1) * piece].astype(bf16)
 
@@ -58,13 +62,14 @@
         grid_spec=pltpu.PrefetchScalarGridSpec(
             num_scalar_prefetch=1,
             grid=(1,),
-            in_specs=[pl.BlockSpec((1, entries, length), lambda i, ids: (ids[0], 0, 0))],
+            in_specs=[pl.BlockSpec(memory_space=pl.ANY)],
             out_specs=whole((N_TP, piece, length)),
+            scratch_shapes=[pltpu.VMEM((entries, length), bf16), pltpu.SemaphoreType.DMA],
         ),
         out_shape=jax.ShapeDtypeStruct((N_TP, piece, length), bf16),
-        compiler_params=params(),
+        compiler_params=params(60),
         name="leave",
-    )(ids, cache_t)
+    )(slots, cache_t)
 
 
 def route(peer, pieces):
@@ -81,7 +86,7 @@
             out_specs=whole(pieces.shape),
         ),
         out_shape=jax.ShapeDtypeStruct(pieces.shape, bf16),
-        compiler_params=params(),
+        compiler_params=params(40),
         name="route",
     )(peer, pieces)
 
@@ -95,14 +100,14 @@
     def slot(r, ids):
         return ids[0] if again else r
 
-    def body(ids_ref, lengths_ref, cache_ref, fresh_ref, q_ref, *refs):
+    def body(ids_ref, lengths_ref, fresh_ref, q_ref, *refs):
         out_ref = refs[-1]
         row = slot(pl.program_id(0), ids_ref)
         current = lengths_ref[row]
         if again:
             latents = jnp.concatenate([refs[0][j].astype(f32) for j in range(N_TP)], axis=0)
         else:
-            latents = cache_ref[0].astype(f32)
+            latents = refs[0][0].astype(f32)
         position = lax.broadcasted_iota(jnp.int32, (entries, length), 1)
         for s in range(steps):
             token = fresh_ref[0, :, s : s + 1].astype(f32)
@@ -126,15 +131,18 @@
             outs.append(out.reshape(chips, 2 * heads, latent_width))
         out_ref[:, 0, 0] = jnp.concatenate(outs, axis=1).astype(bf16)
 
-    extra_specs = [whole(arrived.shape), pl.BlockSpec(memory_space=pl.ANY)] if again else []
-    extra = [arrived, done] if again else []
+    if again:
+        extra_specs = [whole(arrived.shape), pl.BlockSpec(memory_space=pl.ANY)]
+        extra = [arrived, done]
+    else:
+        extra_specs = [pl.BlockSpec((1, entries, length), lambda r, *_: (r, 0, 0))]
+        extra = [cache_t]
     return pl.pallas_call(
         body,
         grid_spec=pltpu.PrefetchScalarGridSpec(
             num_scalar_prefetch=2,
             grid=(1 if again else rows,),
             in_specs=[
-                pl.BlockSpec((1, entries, length), lambda r, ids, _: (slot(r, ids), 0, 0)),
                 pl.BlockSpec((1, entries, steps), lambda r, ids, _: (slot(r, ids), 0, 0)),
                 pl.BlockSpec(
                     (steps, 1, entries, all_heads), lambda r, ids, _: (0, slot(r, ids), 0, 0)
@@ -155,100 +163,85 @@
         out_shape=jax.ShapeDtypeStruct(
             (chips, 2, rows // 2, 2 * steps * heads, latent_width), bf16
         ),
-        input_output_aliases={6: 0} if again else {},
-        compiler_params=params(),
+        input_output_aliases={5: 0} if again else {},
+        compiler_params=params(60),
         name="again" if again else "attend",
-    )(ids, lengths, cache_t, fresh_t, queries_t, *extra)
-
-
-def project(ids, rows, weights, cuts):
+    )(ids, lengths, fresh_t, queries_t, *extra)
+
+
+def project(ids, rows, weight, blocks):
     groups, count, depth = rows.shape
-    width = weights[0][0].shape[1]
-    blocks = len(weights)
-    per = groups // cuts
-    flat = [w for weight in weights for w in weight]
-
-    def body(ids_ref, rows_ref, *refs):
-        out_ref = refs[-1]
-        lhs = rows_ref[...].reshape(per * count, depth)
-        n = 0
-        for k in range(blocks):
-            total, start = 0.0, 0
-            for w in weights[k]:
-                stop = start + w.shape[0]
-                total += jnp.dot(lhs[:, start:stop], refs[n][...], preferred_element_type=f32)
-                n, start = n + 1, stop
-            at = lax.rem(ids_ref[1] + k, blocks)
-            out_ref[:, at] = total.astype(bf16).reshape(per, count, width)
+    width = weight.shape[1] // blocks
+
+    def body(ids_ref, rows_ref, weight_ref, out_ref):
+        lhs = rows_ref[...].reshape(groups * count, depth)
+        total = jnp.dot(lhs, weight_ref[...], preferred_element_type=f32)
+        out_ref[:, 0] = total.astype(bf16).reshape(groups, count, width)
 
     return pl.pallas_call(
         body,
         grid_spec=pltpu.PrefetchScalarGridSpec(
             num_scalar_prefetch=1,
-            grid=(cuts,),
-            in_specs=[pl.BlockSpec((per, count, depth), lambda i, ids: (i, 0, 0))]
-            + [whole(w.shape) for w in flat],
-            out_specs=pl.BlockSpec((per, blocks, count, width), lambda i, ids: (i, 0, 0, 0)),
+            grid=(blocks,),
+            in_specs=[
+                whole(rows.shape),
+                pl.BlockSpec((depth, width), lambda k, ids: (0, k)),
+            ],
+            out_specs=pl.BlockSpec(
+                (groups, 1, count, width), lambda k, ids: (0, lax.rem(ids[1] + k, blocks), 0, 0)
+            ),
         ),
         out_shape=jax.ShapeDtypeStruct((groups, blocks, count, width), bf16),
-        compiler_params=params(),
+        compiler_params=params(40),
         name="project",
-    )(ids, rows, *flat)
-
-
-def widen(ids, rows, kept, came):
-    halves, chunks, _, count, features = rows.shape
-    width = kept[0].shape[1]
-    columns = width * len(kept)
+    )(ids, rows, weight)
+
+
+def widen(ids, rows, weight):
+    halves, chunks, blocks, count, features = rows.shape
+    depth, columns = weight.shape
     every = halves * chunks * count
-    weights = [w for own, rest in zip(kept, came) for w in [own] + rest]
-
-    def body(ids_ref, rows_ref, *refs):
-        out_ref = refs[-1]
-        pair = ids_ref[1]
-        mine = rows_ref[:, :, pair].reshape(every, features)
-        near = rows_ref[:, :, 1 - pair].reshape(every, features)
-
-        def put(tile, value):
+
+    def body(ids_ref, rows_ref, weight_ref, out_ref, lhs_ref):
+        tile = pl.program_id(0)
+
+        def put(at, value):
             value = value.astype(bf16).reshape(halves, chunks, count, value.shape[1])
             for h in range(halves):
-                out_ref[:, h, :, tile] = value[h]
-
-        n = 0
-        for k in range(len(kept)):
-            for at in range(0, width, TILE):
-                tile = slice(at, at + TILE)
-                total = jnp.dot(mine, refs[n][:, tile], preferred_element_type=f32)
-                start = 0
-                for m, w in enumerate(came[k]):
-                    stop = start + w.shape[0]
-                    total += jnp.dot(
-                        near[:, start:stop], refs[n + 1 + m][:, tile], preferred_element_type=f32
-                    )
-                    start = stop
-                put(slice(k * width + at, k * width + at + TILE), total)
-            n += 1 + len(came[k])
-        squares = jnp.zeros((every, 1), f32)
-        for block in (mine, near):
-            wide = block.astype(f32)
-            squares += jnp.sum(wide * wide, axis=1, keepdims=True)
-        high = squares.astype(bf16).astype(f32)
-        lane = lax.broadcasted_iota(jnp.int32, (every, 128), 1)
-        extra = jnp.where(lane == 0, high, jnp.where(lane == 1, squares - high, 0.0))
-        put(slice(columns, columns + 128), extra)
+                out_ref[:, h, :, at] = value[h]
+
+        @pl.when(tile == 0)
+        def _():
+            squares = jnp.zeros((every, 1), f32)
+            for k in range(blocks):
+                block = rows_ref[:, :, lax.rem(ids_ref[1] + k, blocks)].reshape(every, features)
+                lhs_ref[:, k * features : (k + 1) * features] = block
+                wide = block.astype(f32)
+                squares += jnp.sum(wide * wide, axis=1, keepdims=True)
+            high = squares.astype(bf16).astype(f32)
+            lane = lax.broadcasted_iota(jnp.int32, (every, 128), 1)
+            extra = jnp.where(lane == 0, high, jnp.where(lane == 1, squares - high, 0.0))
+            put(slice(columns, columns + 128), extra)
+
+        total = jnp.dot(lhs_ref[...], weight_ref[...], preferred_element_type=f32)
+        put(pl.ds(pl.multiple_of(tile * TILE, 128), TILE), total)
 
     return pl.pallas_call(
         body,
         grid_spec=pltpu.PrefetchScalarGridSpec(
             num_scalar_prefetch=1,
-            grid=(1,),
-            in_specs=[whole(rows.shape)] + [whole(w.shape) for w in weights],
+            grid=(columns // TILE,),
+            in_specs=[
+                whole(rows.shape),
+                pl.BlockSpec((depth, TILE), lambda k, ids: (0, k)),
+            ],
             out_specs=whole((chunks, halves, count, columns + 128)),
+            scratch_shapes=[pltpu.VMEM((every, depth), bf16)],
         ),
         out_shape=jax.ShapeDtypeStruct((chunks, halves, count, columns + 128), bf16),
-        compiler_params=params(),
+        compiler_params=params(40),
         name="widen",
-    )(ids, rows, *weights)
+    )(ids, rows, weight)
 
 
 def local(
@@ -288,12 +281,17 @@
 
     out_came = swap(out_proj, "xl")
     value_ups = jnp.concatenate([value_up, swap(value_up, "c")], axis=0)
-    downs = [down_weight, swap(down_weight, "c")]
+    downs = jnp.concatenate([down_weight, swap(down_weight, "c")], axis=0)
+    residue = lax.dynamic_slice_in_dim(residual, lax.div(member, 2) * 2 * rows_out, 2 * rows_out, 1)
+    residue = residue.reshape(steps, 2, 2, rows_out // 8, 2, 2, features)
+    residue = lax.dynamic_index_in_dim(residue, core, 4, False)
+    residue = residue.transpose(2, 1, 3, 4, 0, 5).reshape(2, count, features)
+    residue_came = swap(at_other(residue), "xl")
     lanes = jnp.arange(N_TP, dtype=jnp.int32)
     own_slot = jnp.sum(jnp.where(lanes == member, move_slot[0], 0))
     ids = jnp.stack([own_slot, pair]).astype(jnp.int32)
     cache_t = cache.transpose(0, 2, 1)
-    pieces = exchange(leave(ids, cache_t), TP)
+    pieces = exchange(leave(move_slot[0], cache_t), TP)
     pieces, gate_weight, up_weight = lax.optimization_barrier((pieces, gate_weight, up_weight))
 
     gain = norm_gain.astype(f32)[:, None]
@@ -315,12 +313,14 @@
     )
     out, out_came, sent[0] = lax.optimization_barrier((out, out_came, sent[0]))
     came = [swap(sent[0], "xl")]
-    out_weights = [[w, swap(w, "c")] for w in (out_proj, out_came)]
+    out_weights = jnp.concatenate(
+        [jnp.concatenate([w, swap(w, "c")], axis=0) for w in (out_proj, out_came)], axis=1
+    )
     kept = [kept, swap(kept, "c")]
     out = out.reshape((N_TP,) + out.shape[2:])
     by_head = exchange(out, TP).reshape(-1, 2 * heads, latent_width)
-    by_head, kept, came, out_weights, value_ups = lax.optimization_barrier(
-        (by_head, kept, came, out_weights, value_ups)
+    by_head, kept, came, out_weights, value_ups, residue_came, downs = lax.optimization_barrier(
+        (by_head, kept, came, out_weights, value_ups, residue_came, downs)
     )
     value_heads = jnp.einsum(
         "thl,hlv->thv", by_head, value_ups, preferred_element_type=f32
@@ -334,24 +334,27 @@
     gathered = exchange(value_heads, DP)
     gathered, sent[1] = lax.optimization_barrier((gathered, sent[1]))
     came.append(swap(sent[1], "xl"))
-    parts = exchange(project(ids, gathered, out_weights, 1), ZY)
+    parts = exchange(project(ids, gathered, out_weights, 2), ZY)
     parts, came[1] = lax.optimization_barrier((parts, came[1]))
-    came = [came, [swap(w, "c") for w in came]]
-    residue = lax.dynamic_slice_in_dim(residual, lax.div(member, 2) * 2 * rows_out, 2 * rows_out, 1)
-    residue = residue.reshape(steps, 2, 2, rows_out // 8, 2, 2, features)
-    residue = lax.dynamic_index_in_dim(residue, core, 4, False)
-    residue = residue.transpose(2, 1, 3, 4, 0, 5).reshape(2, count, features)
-    residue = by_pair(at_pair(residue), swap(at_other(residue), "xl"))
+    in_weight = jnp.concatenate(
+        [
+            jnp.concatenate([own, swap(own, "c") if k else kept[1]], axis=1)
+            for k, own in enumerate([kept[0]] + came)
+        ],
+        axis=0,
+    )
+    residue = by_pair(at_pair(residue), residue_came)
     hidden = residue.astype(f32) + jnp.sum(parts.astype(f32), axis=0)
 
     rows = spread(hidden.astype(bf16), PAIR, 2 * N_ZY).reshape((2, N_ZY) + hidden.shape)
-    sums = exchange(widen(ids, rows, kept, came).reshape(N_DP, chunk, -1), DP)
+    rows, in_weight = lax.optimization_barrier((rows, in_weight))
+    sums = exchange(widen(ids, rows, in_weight).reshape(N_DP, chunk, -1), DP)
     sums = jnp.sum(sums.reshape(2, 2, 2, chunk, -1).astype(f32), axis=(0, 2))
     squares = sums[0, :, 2 * units] + sums[0, :, 2 * units + 1]
     inverse = lax.rsqrt(squares / D + norm_eps)[:, None]
     active = sums[:, :, : 2 * units] * inverse
     active = (jax.nn.silu(active[0]) * active[1]).astype(bf16)
-    parts = exchange(project(ids, spread(active, DP, N_DP), [downs], 2)[:, 0], ZY)
+    parts = exchange(project(ids, spread(active, DP, N_DP), downs, 1)[:, 0], ZY)
     hidden = by_pair(at_pair(hidden), swap(at_other(hidden), "xl")).reshape(chunk, -1)
     result = (hidden + jnp.sum(parts.astype(f32), axis=0)).astype(bf16)
 

time: 284 us -> 268 us (0.944)
  waiting for transfers between devices: 152 us -> 40.8 us
  blocking collectives: 0 us -> 79.8 us
  other arithmetic: 17.5 us -> 53.6 us
  Pallas kernels: 41.3 us -> 27.6 us
  starting transfers between devices: 59 us -> 50.1 us
  local copies, waits for them, and re-layouts: 9.67 us -> 13.1 us
    all_to_all x0 -> x3, blocking collectives: none -> 79.8 us  [exchange(): return lax.all_to_all(blocks, axes, 0, 0, tiled=True)]
    all_to_all x9 -> x6, waiting for transfers between devices: 113 us -> 35.3 us  [exchange(): return lax.all_to_all(blocks, axes, 0, 0, tiled=True)]
    concatenate x0 -> x3, other arithmetic: none -> 39.6 us  [the longest x1 19.9 us: local(): jnp.concatenate([jnp.concatenate([own, swap(own, 'c') if k else kept[1]],...]
    ppermute x13, waiting for transfers between devices: 38.9 us -> 5.46 us  [swap(): return lax.ppermute(block, axis, SWAP)]
    all_to_all x9 -> x6, starting transfers between devices: 46.7 us -> 37.8 us  [exchange(): return lax.all_to_all(blocks, axes, 0, 0, tiled=True)]
    pallas_call x2, Pallas kernels: 14.5 us -> 7.88 us  [project(): pl.pallas_call(body, grid_spec=pltpu.PrefetchScalarGridSpec(num_scalar_pr...]
    pallas_call x1, Pallas kernels: 12.4 us -> 6.38 us  [widen(): pl.pallas_call(body, grid_spec=pltpu.PrefetchScalarGridSpec(num_scalar_pr...]
    unnamed x16 -> x28, local copies, waits for them, and re-layouts: 3.4 us -> 8.34 us
  transfers between devices with their start and end apart: 22 -> 19, of which waited for: 14 -> 7; matrix products, arithmetic and copies ran while one was open for 7% -> 21% of each run, Pallas kernels for 8% -> 6%
where the time goes in v7:
time: 268 us; the launch traced here: 267 us
  blocking collectives  79.8 us (30%)
  other arithmetic  53.6 us (20%)
  starting transfers between devices  50.1 us (19%)
  waiting for transfers between devices  40.8 us (15%)
  Pallas kernels  27.6 us (10%)
  local copies, waits for them, and re-layouts  13.1 us (5%)
    all_to_all x3, blocking collectives, exchange(): return lax.all_to_all(blocks, axes, 0, 0, tiled=True)  79.8 us
    all_to_all x6, starting transfers between devices, exchange(): return lax.all_to_all(blocks, axes, 0, 0, tiled=True)  37.8 us
    all_to_all x6, waiting for transfers between devices, exchange(): return lax.all_to_all(blocks, axes, 0, 0, tiled=True)  35.3 us
    concatenate x1, other arithmetic, local(): jnp.concatenate([jnp.concatenate([own, swap(own, 'c') if k else kept[1]],...  19.9 us
    concatenate x1, other arithmetic, local(): jnp.concatenate([jnp.concatenate([w, swap(w, 'c')], axis=0) for w in (out...  15.3 us
    ppermute x13, starting transfers between devices, swap(): return lax.ppermute(block, axis, SWAP)  12.3 us
    pallas_call x2, Pallas kernels, attend(): pl.pallas_call(body, grid_spec=pltpu.PrefetchScalarGridSpec(num_scalar_pr...  9.66 us
    convert_element_type x3, other arithmetic, scaled(): return (weight.astype(f32) * gain[low:high]).astype(bf16)  9.2 us
  transfers between devices with their start and end apart: 19, of which 7 were waited for; matrix products, arithmetic and copies ran while one was open for 21% of the time, Pallas kernels for 6%

profile of v7, /device:TPU:1, one launch (start us, length us, event | category | flops | bytes accessed | tf_op | source)
XLA Modules:
  0.0 266.7 jit_solution(2317737520025553249)
XLA Ops:
  0.0 2.1 collective-permute-start
  2.2 2.4 leave.1
  4.6 8.8 %all-to-all-start = ((bf16[16,36,256]{2,1,0:T(8,128)(2,1)}), bf16[16,36,256]{2,1,0:T(8,128)(2,1)S(1)}, u32[]{:S(2)}, u32[]{:S(2)}) async-start(bf16[16,36,256]{2,1,0:T(8,128)(2,1)} %leave.1), calls=%async_computation | async-start | bytes 655360 | tf_op jit(solution)/shard_map/all_to_all | solution.py:28
  14.0 1.1 copy.55
  15.2 0.6 fusion.13
  15.8 1.2 pad_add_fusion.ids_ref
  17.0 6.3 %attend.1.refs_1_ = bf16[8,2,2,32,512]{4,3,2,1,0:T(8,128)(2,1)} custom-call(s32[2]{0:T(128)} %pad_add_fusion.ids_ref, s32[4]{0:T(128)} %lengths_ref.3, bf16[4,576,2]{2,1,0:T(8,128)(2,1)} %bitcast.64, bf16[2,4,576,128]{3,2,1,0:T(8,128)(2,1)} %bitcast.66, bf16[4,576,256]{2,1,0:T(8,128)(2,1)} %bitcast.69), custom_call_target="tpu_custom_call" | custom-call | tf_op jit(solution)/shard_map/attend/pallas_call | solution.py:140
  23.3 1.3 route.1
  24.6 7.2 %all-to-all-start.1 = ((bf16[16,36,256]{2,1,0:T(8,128)(2,1)}), bf16[16,36,256]{2,1,0:T(8,128)(2,1)S(1)}, u32[]{:S(2)}, u32[]{:S(2)}) async-start(bf16[16,36,256]{2,1,0:T(8,128)(2,1)} %route.1), calls=%async_computation.1 | async-start | bytes 655360 | tf_op jit(solution)/shard_map/all_to_all | solution.py:28
  31.8 2.7 %multiply_convert_fusion.2 = bf16[384,1152]{1,0:T(8,128)(2,1)} fusion(f32[384]{0:T(512)S(1)} %slice.37, bf16[896,1152]{1,0:T(8,128)(2,1)} %param.23, bf16[896,1152]{1,0:T(8,128)(2,1)} %param.24, pred[]{:T(512)S(6)} %eq.17), kind=kLoop, calls=%fused_computation.9 | loop fusion | flops 1769472 | bytes 2655745 | tf_op jit(solution)/shard_map/convert_element_type | solution.py:301
  34.5 6.4 %all-to-all-done.1.refs_0_ = bf16[16,36,256]{2,1,0:T(8,128)(2,1)S(1)} async-done(((bf16[16,36,256]{2,1,0:T(8,128)(2,1)}), bf16[16,36,256]{2,1,0:T(8,128)(2,1)S(1)}, u32[]{:S(2)}, u32[]{:S(2)}) %all-to-all-start.1) | async-done | bytes 294944 | tf_op jit(solution)/shard_map/all_to_all | solution.py:28
  40.9 0.7 copy-done.8
  41.7 3.4 %again.1 = bf16[8,2,2,32,512]{4,3,2,1,0:T(8,128)(2,1)} custom-call(s32[2]{0:T(128)} %pad_add_fusion.ids_ref, s32[4]{0:T(128)} %lengths_ref.3, bf16[4,576,2]{2,1,0:T(8,128)(2,1)} %bitcast.65, bf16[2,4,576,128]{3,2,1,0:T(8,128)(2,1)} %bitcast.67, bf16[16,36,256]{2,1,0:T(8,128)(2,1)} %copy-done.8, ...), custom_call_target="tpu_custom_call", output_to_operand_aliasing={{}: (5, {})} | custom-call | tf_op jit(solution)/shard_map/again/pallas_call | solution.py:140
  45.0 1.1 collective-permute-start.4
  46.1 3.5 %multiply_convert_fusion = bf16[896,1152]{1,0:T(8,128)(2,1)} fusion(f32[896]{0:T(1024)S(1)} %convert_element_type.62, bf16[896,1152]{1,0:T(8,128)(2,1)} %param.23, bf16[896,1152]{1,0:T(8,128)(2,1)} %param.24, pred[]{:T(512)S(6)} %eq.17), kind=kLoop, calls=%fused_computation.4 | loop fusion | flops 4128768 | bytes 6196737 | tf_op jit(solution)/shard_map/convert_element_type | solution.py:301
  50.4 0.5 collective-permute-start.6
  50.8 1.4 pad_maximum_fusion.1
  52.2 7.0 %all-to-all-start.2 = ((bf16[16,2,32,512]{3,2,1,0:T(8,128)(2,1)}), bf16[16,2,32,512]{3,2,1,0:T(8,128)(2,1)S(1)}, u32[]{:S(2)}, u32[]{:S(2)}) async-start(bf16[16,2,32,512]{3,2,1,0:T(8,128)(2,1)} %bitcast.12), calls=%async_computation.2 | async-start | bytes 2097152 | tf_op jit(solution)/shard_map/all_to_all | solution.py:28
  59.3 0.5 collective-permute-start.2
  59.8 4.5 %pad_maximum_fusion.weight_ref = bf16[2304,896]{1,0:T(8,128)(2,1)} fusion(bf16[1152,896]{1,0:T(8,128)(2,1)} %collective-permute-done.7, bf16[1152,896]{1,0:T(8,128)(2,1)} %param.25), kind=kLoop, calls=%fused_computation.3 | loop fusion | flops 8257536 | bytes 8257536 | tf_op jit(solution)/shard_map/concatenate | solution.py:284
  64.3 15.3 %maximum_maximum_fusion.1.weight_ref = bf16[2048,1792]{1,0:T(8,128)(2,1)} fusion(bf16[1024,896]{1,0:T(8,128)(2,1)} %collective-permute-done.4, bf16[1024,896]{1,0:T(8,128)(2,1)} %collective-permute-done, bf16[1024,896]{1,0:T(8,128)(2,1)} %collective-permute-done.3, bf16[1024,896]{1,0:T(8,128)(2,1)S(1)} %copy-done.7), kind=kLoop, calls=%fused_computation.1 | loop fusion | flops 29360128 | bytes 14680064 | tf_op jit(solution)/shard_map/concatenate | solution.py:316
  79.6 1.5 collective-permute-done.2
  81.1 1.3 fusion
  82.7 1.1 broadcast_in_dim.28
  83.8 4.2 %all-to-all-start.3 = ((bf16[8,32,2048]{2,1,0:T(8,128)(2,1)}), bf16[8,32,2048]{2,1,0:T(8,128)(2,1)S(1)}, u32[]{:S(2)}, u32[]{:S(2)}) async-start(bf16[8,32,2048]{2,1,0:T(8,128)(2,1)} %bitcast.19), calls=%async_computation.3 | async-start | bytes 2097152 | tf_op jit(solution)/shard_map/all_to_all | solution.py:28
  88.0 3.0 %multiply_convert_fusion.1 = bf16[512,1152]{1,0:T(8,128)(2,1)} fusion(f32[512]{0:T(512)S(1)} %slice.40, bf16[896,1152]{1,0:T(8,128)(2,1)} %param.23, bf16[896,1152]{1,0:T(8,128)(2,1)} %param.24, pred[]{:T(512)S(6)} %eq.17), kind=kLoop, calls=%fused_computation.5 | loop fusion | flops 2359296 | bytes 3540993 | tf_op jit(solution)/shard_map/convert_element_type | solution.py:301
  91.0 11.9 %all-to-all-done.3.rows_ref = bf16[8,32,2048]{2,1,0:T(8,128)(2,1)S(1)} async-done(((bf16[8,32,2048]{2,1,0:T(8,128)(2,1)}), bf16[8,32,2048]{2,1,0:T(8,128)(2,1)S(1)}, u32[]{:S(2)}, u32[]{:S(2)}) %all-to-all-start.3) | async-done | bytes 1048608 | tf_op jit(solution)/shard_map/all_to_all | solution.py:28
  103.2 3.1 %copy-done.3 = bf16[2048,1792]{1,0:T(8,128)(2,1)S(1)} copy-done((bf16[2048,1792]{1,0:T(8,128)(2,1)S(1)}, bf16[2048,1792]{1,0:T(8,128)(2,1)}, u32[]{:S(2)}) %copy-start.3) | copy-done | bytes 7340056
  106.3 3.8 %project.2 = bf16[8,2,32,896]{3,2,1,0:T(8,128)(2,1)S(1)} custom-call(s32[2]{0:T(128)S(1)} %copy-done.5, bf16[8,32,2048]{2,1,0:T(8,128)(2,1)S(1)} %all-to-all-done.3.rows_ref, bf16[2048,1792]{1,0:T(8,128)(2,1)S(1)} %copy-done.3), custom_call_target="tpu_custom_call" | custom-call | tf_op jit(solution)/shard_map/project/pallas_call | solution.py:181
  110.0 19.0 %all_to_all.45 = bf16[8,2,32,896]{3,2,1,0:T(8,128)(2,1)S(1)} all-to-all(bf16[8,2,32,896]{3,2,1,0:T(8,128)(2,1)S(1)} %project.2), channel_id=1, replica_groups=mesh['xh'=2,'xl'=2,'zl'=2,'zh'=2,'y'=4,'c'=2] {'zh','y'}, dimensions={0} | all-to-all | bytes 1835008 | tf_op jit(solution)/shard_map/all_to_all | solution.py:28
  129.1 3.9 %collective-permute-start.11 = (bf16[512,1152]{1,0:T(8,128)(2,1)S(1)}, bf16[512,1152]{1,0:T(8,128)(2,1)}, u32[]{:S(2)}, u32[]{:S(2)}) collective-permute-start(bf16[512,1152]{1,0:T(8,128)(2,1)S(1)} %collective-permute-done.8), channel_id=1, source_target_pairs={{0,1},{1,0},{2,3},{3,2},{4,5},{5,4},{6,7},{7,6},{8,9},{9,8},{10,11... | collective-permute-start | bytes 3538952 | tf_op jit(solution)/shard_map/ppermute | solution.py:36
  133.2 1.5 broadcast_in_dim.29
  134.6 5.2 %all-to-all-start.5 = ((bf16[16,2,32,896]{3,2,1,0:T(8,128)(2,1)}), bf16[16,2,32,896]{3,2,1,0:T(8,128)(2,1)S(1)}, u32[]{:S(2)}, u32[]{:S(2)}) async-start(bf16[16,2,32,896]{3,2,1,0:T(8,128)(2,1)} %broadcast_in_dim.29), calls=%async_computation.5 | async-start | bytes 3670016 | tf_op jit(solution)/shard_map/all_to_all | solution.py:28
  139.8 19.9 %maximum_maximum_fusion.weight_ref = bf16[1792,2304]{1,0:T(8,128)(2,1)} fusion(bf16[512,1152]{1,0:T(8,128)(2,1)} %collective-permute-done.11, bf16[512,1152]{1,0:T(8,128)(2,1)S(1)} %collective-permute-done.8, bf16[384,1152]{1,0:T(8,128)(2,1)} %collective-permute-done.10, bf16[384,1152]{1,0:T(8,128)(2,1)} %collective-permute-done.2, ...), kind=kLoop, calls=%fused_computation | loop fusion | flops 49545216 | bytes 16515072 | tf_op jit(solution)/shard_map/concatenate | solution.py:339
  159.7 6.6 %all-to-all-done.5 = bf16[16,2,32,896]{3,2,1,0:T(8,128)(2,1)S(1)} async-done(((bf16[16,2,32,896]{3,2,1,0:T(8,128)(2,1)}), bf16[16,2,32,896]{3,2,1,0:T(8,128)(2,1)S(1)}, u32[]{:S(2)}, u32[]{:S(2)}) %all-to-all-start.5) | async-done | bytes 1835040 | tf_op jit(solution)/shard_map/all_to_all | solution.py:28
  166.3 3.3 %copy-done.2 = bf16[1792,2304]{1,0:T(8,128)(2,1)S(1)} copy-done((bf16[1792,2304]{1,0:T(8,128)(2,1)S(1)}, bf16[1792,2304]{1,0:T(8,128)(2,1)}, u32[]{:S(2)}) %copy-start.2) | copy-done | bytes 8257560
  169.7 6.4 %widen.1 = bf16[8,2,32,2432]{3,2,1,0:T(8,128)(2,1)S(1)} custom-call(s32[2]{0:T(128)S(1)} %copy-done.5, bf16[2,8,2,32,896]{4,3,2,1,0:T(8,128)(2,1)S(1)} %bitcast.61, bf16[1792,2304]{1,0:T(8,128)(2,1)S(1)} %copy-done.2), custom_call_target="tpu_custom_call" | custom-call | tf_op jit(solution)/shard_map/widen/pallas_call | solution.py:229
  176.1 31.4 %all_to_all.46 = bf16[8,64,2432]{2,1,0:T(8,128)(2,1)S(1)} all-to-all(bf16[8,64,2432]{2,1,0:T(8,128)(2,1)S(1)} %bitcast.60), channel_id=1, replica_groups=mesh['xh'=2,'xl'=2,'zl'=2,'zh'=2,'y'=4,'c'=2] {'xh','xl','zl'}, dimensions={0} | all-to-all | bytes 4980736 | tf_op jit(solution)/shard_map/all_to_all | solution.py:28
  207.5 0.3 convert_reduce_fusion
  208.5 29.4 %all_to_all.47.rows_ref = bf16[8,64,2304]{2,1,0:T(8,128)(2,1)S(1)} all-to-all(bf16[8,64,2304]{2,1,0:T(8,128)(2,1)S(1)} %broadcast_in_dim.31), channel_id=1, replica_groups=mesh['xh'=2,'xl'=2,'zl'=2,'zh'=2,'y'=4,'c'=2] {'xh','xl','zl'}, dimensions={0} | all-to-all | bytes 4718592 | tf_op jit(solution)/shard_map/all_to_all | solution.py:28
  237.9 4.1 %project.3 = bf16[8,1,64,896]{3,2,1,0:T(8,128)(2,1)} custom-call(s32[2]{0:T(128)S(1)} %copy-done.5, bf16[8,64,2304]{2,1,0:T(8,128)(2,1)S(1)} %all_to_all.47.rows_ref, bf16[2304,896]{1,0:T(8,128)(2,1)S(1)} %copy-done.4), custom_call_target="tpu_custom_call" | custom-call | tf_op jit(solution)/shard_map/project/pallas_call | solution.py:181
  242.0 5.5 %all-to-all-start.8 = ((bf16[8,64,896]{2,1,0:T(8,128)(2,1)}), bf16[8,64,896]{2,1,0:T(8,128)(2,1)S(1)}, u32[]{:S(2)}, u32[]{:S(2)}) async-start(bf16[8,64,896]{2,1,0:T(8,128)(2,1)} %bitcast.26), calls=%async_computation.8 | async-start | bytes 1835008 | tf_op jit(solution)/shard_map/all_to_all | solution.py:28
  247.5 0.7 collective-permute-start.9
  248.2 3.1 %collective-permute-done.9 = f32[32,896]{1,0:T(8,128)S(1)} collective-permute-done((f32[32,896]{1,0:T(8,128)S(1)}, f32[32,896]{1,0:T(8,128)S(1)}, u32[]{:S(2)}, u32[]{:S(2)}) %collective-permute-start.9) | collective-permute-done | bytes 114720 | tf_op jit(solution)/shard_map/ppermute | solution.py:36
  251.4 10.4 %all-to-all-done.8 = bf16[8,64,896]{2,1,0:T(8,128)(2,1)S(1)} async-done(((bf16[8,64,896]{2,1,0:T(8,128)(2,1)}), bf16[8,64,896]{2,1,0:T(8,128)(2,1)S(1)}, u32[]{:S(2)}, u32[]{:S(2)}) %all-to-all-start.8) | async-done | bytes 917536 | tf_op jit(solution)/shard_map/all_to_all | solution.py:28
  262.3 2.5 collective-permute-start.12
  264.8 0.9 collective-permute-done.12
  266.0 0.7 copy.60
  (71 shorter events, 3.9 us)
Async XLA Ops:
  0.0 49.6 %copy-start = (bf16[2,512,896]{2,1,0:T(8,128)(2,1)S(1)}, bf16[2,512,896]{2,1,0:T(8,128)(2,1)}, u32[]{:S(2)}) copy-start(bf16[2,512,896]{2,1,0:T(8,128)(2,1)} %param.21) | copy-start | bytes 5505028
  0.0 15.2 %copy-start.12 = (s32[1,16]{1,0:T(1,128)S(1)}, s32[1,16]{1,0:T(1,128)}, u32[]{:S(2)}) copy-start(s32[1,16]{1,0:T(1,128)} %param.15) | copy-start | bytes 196
  0.0 13.8 %copy-start.9 = (bf16[8,512,128]{2,1,0:T(8,128)(2,1)S(1)}, bf16[8,512,128]{2,1,0:T(8,128)(2,1)}, u32[]{:S(2)}) copy-start(bf16[8,512,128]{2,1,0:T(8,128)(2,1)} %param.19) | copy-start | bytes 3145732
  0.0 14.0 %copy-start.10 = (bf16[896]{0:T(1024)(128)(2,1)S(1)}, bf16[896]{0:T(1024)(128)(2,1)}, u32[]{:S(2)}) copy-start(bf16[896]{0:T(1024)(128)(2,1)} %param.22) | copy-start | bytes 5380
  0.0 14.0 %copy-start.11 = (bf16[2,4,576]{2,1,0:T(4,128)(2,1)S(1)}, bf16[2,4,576]{2,1,0:T(4,128)(2,1)}, u32[]{:S(2)}) copy-start(bf16[2,4,576]{2,1,0:T(4,128)(2,1)} %param.18) | copy-start | bytes 27652
  0.0 45.0 %collective-permute-start = (bf16[1024,896]{1,0:T(8,128)(2,1)}, bf16[1024,896]{1,0:T(8,128)(2,1)}, u32[]{:S(2)}, u32[]{:S(2)}) collective-permute-start(bf16[1024,896]{1,0:T(8,128)(2,1)} %param.20), channel_id=1, source_target_pairs={{0,32},{32,0},{1,33},{33,1},{2,34},{34,2},{3,35},{35,3},{4,36},{36... | collective-permute-start | bytes 5505032 | tf_op jit(solution)/shard_map/ppermute | solution.py:36
  4.6 18.7 %all-to-all-start = ((bf16[16,36,256]{2,1,0:T(8,128)(2,1)}), bf16[16,36,256]{2,1,0:T(8,128)(2,1)S(1)}, u32[]{:S(2)}, u32[]{:S(2)}) async-start(bf16[16,36,256]{2,1,0:T(8,128)(2,1)} %leave.1), calls=%async_computation | async-start | bytes 655360 | tf_op jit(solution)/shard_map/all_to_all | solution.py:28
  13.3 51.0 %collective-permute-start.3 = (bf16[1024,896]{1,0:T(8,128)(2,1)}, bf16[1024,896]{1,0:T(8,128)(2,1)}, u32[]{:S(2)}, u32[]{:S(2)}) collective-permute-start(bf16[1024,896]{1,0:T(8,128)(2,1)} %param.20), channel_id=1, source_target_pairs={{0,1},{1,0},{2,3},{3,2},{4,5},{5,4},{6,7},{7,6},{8,9},{9,8},{10,11... | collective-permute-start | bytes 5505032 | tf_op jit(solution)/shard_map/ppermute | solution.py:36
  13.5 45.7 %collective-permute-start.7 = (bf16[1152,896]{1,0:T(8,128)(2,1)}, bf16[1152,896]{1,0:T(8,128)(2,1)}, u32[]{:S(2)}, u32[]{:S(2)}) collective-permute-start(bf16[1152,896]{1,0:T(8,128)(2,1)} %param.25), channel_id=1, source_target_pairs={{0,1},{1,0},{2,3},{3,2},{4,5},{5,4},{6,7},{7,6},{8,9},{9,8},{10,11... | collective-permute-start | bytes 6193160 | tf_op jit(solution)/shard_map/ppermute | solution.py:36
  13.8 36.5 %collective-permute-start.5 = (bf16[8,512,128]{2,1,0:T(8,128)(2,1)S(1)}, bf16[8,512,128]{2,1,0:T(8,128)(2,1)}, u32[]{:S(2)}, u32[]{:S(2)}) collective-permute-start(bf16[8,512,128]{2,1,0:T(8,128)(2,1)S(1)} %copy-done.9), channel_id=1, source_target_pairs={{0,1},{1,0},{2,3},{3,2},{4,5},{5,4},{6,7},{7,6},{8,9},{9,8},{10,11... | collective-permute-start | bytes 3145736 | tf_op jit(solution)/shard_map/ppermute | solution.py:36
  15.2 8.1 %copy-start.6 = (s32[1,16]{1,0:T(1,128)S(1)}, s32[1,16]{1,0:T(1,128)}, u32[]{:S(2)}) copy-start(s32[1,16]{1,0:T(1,128)} %param.16) | copy-start | bytes 196
  24.6 16.3 %all-to-all-start.1 = ((bf16[16,36,256]{2,1,0:T(8,128)(2,1)}), bf16[16,36,256]{2,1,0:T(8,128)(2,1)S(1)}, u32[]{:S(2)}, u32[]{:S(2)}) async-start(bf16[16,36,256]{2,1,0:T(8,128)(2,1)} %route.1), calls=%async_computation.1 | async-start | bytes 655360 | tf_op jit(solution)/shard_map/all_to_all | solution.py:28
  40.9 0.7 copy-start.8
  45.0 19.2 %collective-permute-start.4 = (bf16[1024,896]{1,0:T(8,128)(2,1)}, bf16[1024,896]{1,0:T(8,128)(2,1)}, u32[]{:S(2)}, u32[]{:S(2)}) collective-permute-start(bf16[1024,896]{1,0:T(8,128)(2,1)} %collective-permute-done), channel_id=1, source_target_pairs={{0,1},{1,0},{2,3},{3,2},{4,5},{5,4},{6,7},{7,6},{8,9},{9,8},{10,11... | collective-permute-start | bytes 5505032 | tf_op jit(solution)/shard_map/ppermute | solution.py:36
  49.6 30.0 %collective-permute-start.1 = (bf16[896,1152]{1,0:T(8,128)(2,1)}, bf16[896,1152]{1,0:T(8,128)(2,1)}, u32[]{:S(2)}, u32[]{:S(2)}) collective-permute-start(bf16[896,1152]{1,0:T(8,128)(2,1)} %multiply_convert_fusion), channel_id=1, source_target_pairs={{0,1},{1,0},{2,3},{3,2},{4,5},{5,4},{6,7},{7,6},{8,9},{9,8},{10,11... | collective-permute-start | bytes 6193160 | tf_op jit(solution)/shard_map/ppermute | solution.py:36
  50.4 29.2 %collective-permute-start.6 = (bf16[32,896]{1,0:T(8,128)(2,1)S(1)}, bf16[32,896]{1,0:T(8,128)(2,1)S(1)}, u32[]{:S(2)}, u32[]{:S(2)}) collective-permute-start(bf16[32,896]{1,0:T(8,128)(2,1)S(1)} %bitcast.76), channel_id=1, source_target_pairs={{0,32},{32,0},{1,33},{33,1},{2,34},{34,2},{3,35},{35,3},{4,36},{36... | collective-permute-start | bytes 172040 | tf_op jit(solution)/shard_map/ppermute | solution.py:36
  52.2 28.8 %all-to-all-start.2 = ((bf16[16,2,32,512]{3,2,1,0:T(8,128)(2,1)}), bf16[16,2,32,512]{3,2,1,0:T(8,128)(2,1)S(1)}, u32[]{:S(2)}, u32[]{:S(2)}) async-start(bf16[16,2,32,512]{3,2,1,0:T(8,128)(2,1)} %bitcast.12), calls=%async_computation.2 | async-start | bytes 2097152 | tf_op jit(solution)/shard_map/all_to_all | solution.py:28
  59.2 5.0 %copy-start.7 = (bf16[1024,896]{1,0:T(8,128)(2,1)S(1)}, bf16[1024,896]{1,0:T(8,128)(2,1)}, u32[]{:S(2)}) copy-start(bf16[1024,896]{1,0:T(8,128)(2,1)} %param.20) | copy-start | bytes 5505028
  59.3 21.8 %collective-permute-start.2 = (bf16[384,1152]{1,0:T(8,128)(2,1)}, bf16[384,1152]{1,0:T(8,128)(2,1)}, u32[]{:S(2)}, u32[]{:S(2)}) collective-permute-start(bf16[384,1152]{1,0:T(8,128)(2,1)} %multiply_convert_fusion.2), channel_id=1, source_target_pairs={{0,32},{32,0},{1,33},{33,1},{2,34},{34,2},{3,35},{35,3},{4,36},{36... | collective-permute-start | bytes 2654216 | tf_op jit(solution)/shard_map/ppermute | solution.py:36
  83.8 19.1 %all-to-all-start.3 = ((bf16[8,32,2048]{2,1,0:T(8,128)(2,1)}), bf16[8,32,2048]{2,1,0:T(8,128)(2,1)S(1)}, u32[]{:S(2)}, u32[]{:S(2)}) async-start(bf16[8,32,2048]{2,1,0:T(8,128)(2,1)} %bitcast.19), calls=%async_computation.3 | async-start | bytes 2097152 | tf_op jit(solution)/shard_map/all_to_all | solution.py:28
  88.0 15.2 %copy-start.5 = (s32[2]{0:T(128)S(1)}, s32[2]{0:T(128)}, u32[]{:S(2)}) copy-start(s32[2]{0:T(128)} %pad_add_fusion.ids_ref) | copy-start | bytes 28
  102.9 26.2 %collective-permute-start.8 = (bf16[512,1152]{1,0:T(8,128)(2,1)}, bf16[512,1152]{1,0:T(8,128)(2,1)S(1)}, u32[]{:S(2)}, u32[]{:S(2)}) collective-permute-start(bf16[512,1152]{1,0:T(8,128)(2,1)} %multiply_convert_fusion.1), channel_id=1, source_target_pairs={{0,32},{32,0},{1,33},{33,1},{2,34},{34,2},{3,35},{35,3},{4,36},{36... | collective-permute-start | bytes 3538952 | tf_op jit(solution)/shard_map/ppermute | solution.py:36
  103.2 3.1 %copy-start.3 = (bf16[2048,1792]{1,0:T(8,128)(2,1)S(1)}, bf16[2048,1792]{1,0:T(8,128)(2,1)}, u32[]{:S(2)}) copy-start(bf16[2048,1792]{1,0:T(8,128)(2,1)} %maximum_maximum_fusion.1.weight_ref) | copy-start | bytes 22020100
  129.1 10.8 %collective-permute-start.11 = (bf16[512,1152]{1,0:T(8,128)(2,1)S(1)}, bf16[512,1152]{1,0:T(8,128)(2,1)}, u32[]{:S(2)}, u32[]{:S(2)}) collective-permute-start(bf16[512,1152]{1,0:T(8,128)(2,1)S(1)} %collective-permute-done.8), channel_id=1, source_target_pairs={{0,1},{1,0},{2,3},{3,2},{4,5},{5,4},{6,7},{7,6},{8,9},{9,8},{10,11... | collective-permute-start | bytes 3538952 | tf_op jit(solution)/shard_map/ppermute | solution.py:36
  133.0 6.8 %collective-permute-start.10 = (bf16[384,1152]{1,0:T(8,128)(2,1)}, bf16[384,1152]{1,0:T(8,128)(2,1)}, u32[]{:S(2)}, u32[]{:S(2)}) collective-permute-start(bf16[384,1152]{1,0:T(8,128)(2,1)} %collective-permute-done.2), channel_id=1, source_target_pairs={{0,1},{1,0},{2,3},{3,2},{4,5},{5,4},{6,7},{7,6},{8,9},{9,8},{10,11... | collective-permute-start | bytes 2654216 | tf_op jit(solution)/shard_map/ppermute | solution.py:36
  134.6 31.7 %all-to-all-start.5 = ((bf16[16,2,32,896]{3,2,1,0:T(8,128)(2,1)}), bf16[16,2,32,896]{3,2,1,0:T(8,128)(2,1)S(1)}, u32[]{:S(2)}, u32[]{:S(2)}) async-start(bf16[16,2,32,896]{3,2,1,0:T(8,128)(2,1)} %broadcast_in_dim.29), calls=%async_computation.5 | async-start | bytes 3670016 | tf_op jit(solution)/shard_map/all_to_all | solution.py:28
  166.3 3.3 %copy-start.2 = (bf16[1792,2304]{1,0:T(8,128)(2,1)S(1)}, bf16[1792,2304]{1,0:T(8,128)(2,1)}, u32[]{:S(2)}) copy-start(bf16[1792,2304]{1,0:T(8,128)(2,1)} %maximum_maximum_fusion.weight_ref) | copy-start | bytes 24772612
  208.5 29.4 %copy-start.4 = (bf16[2304,896]{1,0:T(8,128)(2,1)S(1)}, bf16[2304,896]{1,0:T(8,128)(2,1)}, u32[]{:S(2)}) copy-start(bf16[2304,896]{1,0:T(8,128)(2,1)} %pad_maximum_fusion.weight_ref) | copy-start | bytes 12386308
  242.0 19.8 %all-to-all-start.8 = ((bf16[8,64,896]{2,1,0:T(8,128)(2,1)}), bf16[8,64,896]{2,1,0:T(8,128)(2,1)S(1)}, u32[]{:S(2)}, u32[]{:S(2)}) async-start(bf16[8,64,896]{2,1,0:T(8,128)(2,1)} %bitcast.26), calls=%async_computation.8 | async-start | bytes 1835008 | tf_op jit(solution)/shard_map/all_to_all | solution.py:28
  247.5 19.2 %copy-start.1 = (bf16[2,512,896]{2,1,0:T(8,128)(2,1)S(1)}, bf16[2,512,896]{2,1,0:T(8,128)(2,1)}, u32[]{:S(2)}) copy-start(bf16[2,512,896]{2,1,0:T(8,128)(2,1)} %param.21) | copy-start | bytes 5505028
  247.5 3.7 %collective-permute-start.9 = (f32[32,896]{1,0:T(8,128)S(1)}, f32[32,896]{1,0:T(8,128)S(1)}, u32[]{:S(2)}, u32[]{:S(2)}) collective-permute-start(f32[32,896]{1,0:T(8,128)S(1)} %dynamic-slice_bitcast_fusion), channel_id=1, source_target_pairs={{0,32},{32,0},{1,33},{33,1},{2,34},{34,2},{3,35},{35,3},{4,36},{36... | collective-permute-start | bytes 344072 | tf_op jit(solution)/shard_map/ppermute | solution.py:36
  262.3 3.4 %collective-permute-start.12 = (bf16[2,4,2,2,896]{4,3,2,1,0:T(2,128)(2,1)S(1)}, bf16[2,4,2,2,896]{4,3,2,1,0:T(2,128)(2,1)S(1)}, u32[]{:S(2)}, u32[]{:S(2)}) collective-permute-start(bf16[2,4,2,2,896]{4,3,2,1,0:T(2,128)(2,1)S(1)} %dynamic-slice_bitcast_fusion.2), channel_id=1, source_target_pairs={{0,1},{1,0},{2,3},{3,2},{4,5},{5,4},{6,7},{7,6},{8,9},{9,8},{10,11... | collective-permute-start | bytes 172040 | tf_op jit(solution)/shard_map/ppermute | solution.py:36

commit v8 on v7

--- a/solution.py
+++ b/solution.py
@@ -197,51 +197,113 @@
     )(ids, rows, weight)
 
 
-def widen(ids, rows, weight):
-    halves, chunks, blocks, count, features = rows.shape
-    depth, columns = weight.shape
+def fetches(refs, blocks, weight_ref, sems):
+    copies, n, left = [], 0, 0
+    for column in blocks:
+        top = 0
+        for w in column:
+            at = weight_ref.at[pl.ds(top, w.shape[0]), pl.ds(left, w.shape[1])]
+            copies.append(pltpu.make_async_copy(refs[n], at, sems.at[n]))
+            n, top = n + 1, top + w.shape[0]
+        left += column[0].shape[1]
+    return copies
+
+
+def combine(ids, rows, blocks):
+    groups, count, depth = rows.shape
+    width = blocks[0][0].shape[1]
+    flat = [w for column in blocks for w in column]
+    half = len(flat) // 2
+
+    def body(ids_ref, rows_ref, *refs):
+        out_ref, weight_ref, sems = refs[len(flat) :]
+        copies = fetches(refs, blocks, weight_ref, sems)
+        for copy in copies:
+            copy.start()
+        lhs = rows_ref[...].reshape(groups * count, depth)
+        for k in range(2):
+            for copy in copies[k * half : (k + 1) * half]:
+                copy.wait()
+            total = jnp.dot(
+                lhs, weight_ref[:, k * width : (k + 1) * width], preferred_element_type=f32
+            )
+            at = lax.rem(ids_ref[1] + k, 2)
+            out_ref[:, at] = total.astype(bf16).reshape(groups, count, width)
+
+    return pl.pallas_call(
+        body,
+        grid_spec=pltpu.PrefetchScalarGridSpec(
+            num_scalar_prefetch=1,
+            grid=(1,),
+            in_specs=[whole(rows.shape)] + [pl.BlockSpec(memory_space=pl.ANY) for _ in flat],
+            out_specs=whole((groups, 2, count, width)),
+            scratch_shapes=[
+                pltpu.VMEM((depth, 2 * width), bf16),
+                pltpu.SemaphoreType.DMA((len(flat),)),
+            ],
+        ),
+        out_shape=jax.ShapeDtypeStruct((groups, 2, count, width), bf16),
+        compiler_params=params(60),
+        name="combine",
+    )(ids, rows, *flat)
+
+
+def widen(ids, rows, blocks):
+    halves, chunks, parts, count, features = rows.shape
+    depth = parts * features
+    columns = sum(column[0].shape[1] for column in blocks)
     every = halves * chunks * count
-
-    def body(ids_ref, rows_ref, weight_ref, out_ref, lhs_ref):
-        tile = pl.program_id(0)
+    flat = [w for column in blocks for w in column]
+    half = len(flat) // 2
+
+    def body(ids_ref, rows_ref, *refs):
+        out_ref, lhs_ref, weight_ref, sems = refs[len(flat) :]
+        copies = fetches(refs, blocks, weight_ref, sems)
+        for copy in copies:
+            copy.start()
 
         def put(at, value):
             value = value.astype(bf16).reshape(halves, chunks, count, value.shape[1])
             for h in range(halves):
                 out_ref[:, h, :, at] = value[h]
 
-        @pl.when(tile == 0)
-        def _():
-            squares = jnp.zeros((every, 1), f32)
-            for k in range(blocks):
-                block = rows_ref[:, :, lax.rem(ids_ref[1] + k, blocks)].reshape(every, features)
-                lhs_ref[:, k * features : (k + 1) * features] = block
-                wide = block.astype(f32)
-                squares += jnp.sum(wide * wide, axis=1, keepdims=True)
-            high = squares.astype(bf16).astype(f32)
-            lane = lax.broadcasted_iota(jnp.int32, (every, 128), 1)
-            extra = jnp.where(lane == 0, high, jnp.where(lane == 1, squares - high, 0.0))
-            put(slice(columns, columns + 128), extra)
-
-        total = jnp.dot(lhs_ref[...], weight_ref[...], preferred_element_type=f32)
-        put(pl.ds(pl.multiple_of(tile * TILE, 128), TILE), total)
+        squares = jnp.zeros((every, 1), f32)
+        for k in range(parts):
+            block = rows_ref[:, :, lax.rem(ids_ref[1] + k, parts)].reshape(every, features)
+            lhs_ref[:, k * features : (k + 1) * features] = block
+            wide = block.astype(f32)
+            squares += jnp.sum(wide * wide, axis=1, keepdims=True)
+        high = squares.astype(bf16).astype(f32)
+        lane = lax.broadcasted_iota(jnp.int32, (every, 128), 1)
+        extra = jnp.where(lane == 0, high, jnp.where(lane == 1, squares - high, 0.0))
+        put(slice(columns, columns + 128), extra)
+
+        for copy in copies[:half]:
+            copy.wait()
+        for at in range(0, columns, TILE):
+            if at == TILE:
+                for copy in copies[half:]:
+                    copy.wait()
+            tile = slice(at, at + TILE)
+            put(tile, jnp.dot(lhs_ref[...], weight_ref[:, tile], preferred_element_type=f32))
 
     return pl.pallas_call(
         body,
         grid_spec=pltpu.PrefetchScalarGridSpec(
             num_scalar_prefetch=1,
-            grid=(columns // TILE,),
-            in_specs=[
-                whole(rows.shape),
-                pl.BlockSpec((depth, TILE), lambda k, ids: (0, k)),
+            grid=(1,),
+            in_specs=[whole(rows.shape)] + [pl.BlockSpec(memory_space=pl.ANY) for _ in flat],
+            out_specs=whole((chunks, halves, count, columns + 128)),
+            scratch_shapes=[
+                pltpu.VMEM((every, depth), bf16),
+                pltpu.VMEM((depth, columns), bf16),
+                pltpu.SemaphoreType.DMA((len(flat),)),
             ],
-            out_specs=whole((chunks, halves, count, columns + 128)),
-            scratch_shapes=[pltpu.VMEM((every, depth), bf16)],
         ),
         out_shape=jax.ShapeDtypeStruct((chunks, halves, count, columns + 128), bf16),
-        compiler_params=params(40),
+        compiler_params=params(60),
         name="widen",
-    )(ids, rows, weight)
+    )(ids, rows, *flat)
 
 
 def local(
@@ -305,22 +367,23 @@
     ]
     kept = scaled(0, CUTS[-1], gate_weight, up_weight)
     arrived = exchange(route(move_peer[0], pieces), TP)
+    arrived, kept, sent[0], value_ups = lax.optimization_barrier(
+        (arrived, kept, sent[0], value_ups)
+    )
     fresh_t = new_latent.transpose(1, 2, 0)
     queries_t = queries.transpose(0, 1, 3, 2)
     out = attend(ids, cache_length, cache_t, fresh_t, queries_t, heads, latent_width)
     out = attend(
         ids, cache_length, cache_t, fresh_t, queries_t, heads, latent_width, arrived, out
     )
-    out, out_came, sent[0] = lax.optimization_barrier((out, out_came, sent[0]))
+    out, out_came = lax.optimization_barrier((out, out_came))
     came = [swap(sent[0], "xl")]
-    out_weights = jnp.concatenate(
-        [jnp.concatenate([w, swap(w, "c")], axis=0) for w in (out_proj, out_came)], axis=1
-    )
+    out_weights = [[w, swap(w, "c")] for w in (out_proj, out_came)]
     kept = [kept, swap(kept, "c")]
     out = out.reshape((N_TP,) + out.shape[2:])
     by_head = exchange(out, TP).reshape(-1, 2 * heads, latent_width)
-    by_head, kept, came, out_weights, value_ups, residue_came, downs = lax.optimization_barrier(
-        (by_head, kept, came, out_weights, value_ups, residue_came, downs)
+    by_head, kept, came, out_weights, residue_came = lax.optimization_barrier(
+        (by_head, kept, came, out_weights, residue_came)
     )
     value_heads = jnp.einsum(
         "thl,hlv->thv", by_head, value_ups, preferred_element_type=f32
@@ -334,21 +397,16 @@
     gathered = exchange(value_heads, DP)
     gathered, sent[1] = lax.optimization_barrier((gathered, sent[1]))
     came.append(swap(sent[1], "xl"))
-    parts = exchange(project(ids, gathered, out_weights, 2), ZY)
+    parts = exchange(combine(ids, gathered, out_weights), ZY)
     parts, came[1] = lax.optimization_barrier((parts, came[1]))
-    in_weight = jnp.concatenate(
-        [
-            jnp.concatenate([own, swap(own, "c") if k else kept[1]], axis=1)
-            for k, own in enumerate([kept[0]] + came)
-        ],
-        axis=0,
-    )
+    in_weights = [[kept[0]] + came, [kept[1]] + [swap(w, "c") for w in came]]
     residue = by_pair(at_pair(residue), residue_came)
     hidden = residue.astype(f32) + jnp.sum(parts.astype(f32), axis=0)
 
     rows = spread(hidden.astype(bf16), PAIR, 2 * N_ZY).reshape((2, N_ZY) + hidden.shape)
-    rows, in_weight = lax.optimization_barrier((rows, in_weight))
-    sums = exchange(widen(ids, rows, in_weight).reshape(N_DP, chunk, -1), DP)
+    rows, in_weights = lax.optimization_barrier((rows, in_weights))
+    sums = exchange(widen(ids, rows, in_weights).reshape(N_DP, chunk, -1), DP)
+    sums, downs = lax.optimization_barrier((sums, downs))
     sums = jnp.sum(sums.reshape(2, 2, 2, chunk, -1).astype(f32), axis=(0, 2))
     squares = sums[0, :, 2 * units] + sums[0, :, 2 * units + 1]
     inverse = lax.rsqrt(squares / D + norm_eps)[:, None]

time: 268 us -> 282 us (1.052)
  waiting for transfers between devices: 40.8 us -> 129 us
  blocking collectives: 79.8 us -> 30.1 us
  other arithmetic: 53.6 us -> 21.7 us
  Pallas kernels: 27.6 us -> 35.5 us
  local copies, waits for them, and re-layouts: 13.1 us -> 8.81 us
    all_to_all x6 -> x8, waiting for transfers between devices: 35.3 us -> 95.8 us  [exchange(): return lax.all_to_all(blocks, axes, 0, 0, tiled=True)]
    all_to_all x3 -> x1, blocking collectives: 79.8 us -> 30.1 us  [exchange(): return lax.all_to_all(blocks, axes, 0, 0, tiled=True)]
    concatenate x2 -> x0, other arithmetic: 35.1 us -> none  [the longest x1 19.9 us: local(): jnp.concatenate([jnp.concatenate([own, swap(own, 'c') if k else kept[1]],...]
    ppermute x13, waiting for transfers between devices: 5.46 us -> 33.1 us  [swap(): return lax.ppermute(block, axis, SWAP)]
    pallas_call x0 -> x1, Pallas kernels: none -> 7.41 us  [combine(): pl.pallas_call(body, grid_spec=pltpu.PrefetchScalarGridSpec(num_scalar_pr...]
    all_to_all x6 -> x8, starting transfers between devices: 37.8 us -> 43.7 us  [exchange(): return lax.all_to_all(blocks, axes, 0, 0, tiled=True)]
    unnamed x28 -> x30, local copies, waits for them, and re-layouts: 8.34 us -> 4.03 us
    pallas_call x1, Pallas kernels: 6.38 us -> 10.4 us  [widen(): pl.pallas_call(body, grid_spec=pltpu.PrefetchScalarGridSpec(num_scalar_pr...]
  transfers between devices with their start and end apart: 19 -> 21, of which waited for: 7 -> 12; matrix products, arithmetic and copies ran while one was open for 21% -> 7% of each run, Pallas kernels for 6% -> 10%
where the time goes in v8:
time: 282 us; the launch traced here: 281 us
  waiting for transfers between devices  129 us (46%)
  starting transfers between devices  52.9 us (19%)
  Pallas kernels  35.5 us (13%)
  blocking collectives  30.1 us (11%)
  other arithmetic  21.7 us (8%)
  local copies, waits for them, and re-layouts  8.81 us (3%)
  matrix products  2.91 us (1%)
    all_to_all x8, waiting for transfers between devices, exchange(): return lax.all_to_all(blocks, axes, 0, 0, tiled=True)  95.8 us
    all_to_all x8, starting transfers between devices, exchange(): return lax.all_to_all(blocks, axes, 0, 0, tiled=True)  43.7 us
    ppermute x13, waiting for transfers between devices, swap(): return lax.ppermute(block, axis, SWAP)  33.1 us
    all_to_all x1, blocking collectives, exchange(): return lax.all_to_all(blocks, axes, 0, 0, tiled=True)  30.1 us
    pallas_call x1, Pallas kernels, widen(): pl.pallas_call(body, grid_spec=pltpu.PrefetchScalarGridSpec(num_scalar_pr...  10.4 us
    pallas_call x2, Pallas kernels, attend(): pl.pallas_call(body, grid_spec=pltpu.PrefetchScalarGridSpec(num_scalar_pr...  9.72 us
    ppermute x13, starting transfers between devices, swap(): return lax.ppermute(block, axis, SWAP)  9.18 us
    convert_element_type x3, other arithmetic, scaled(): return (weight.astype(f32) * gain[low:high]).astype(bf16)  9.14 us
  transfers between devices with their start and end apart: 21, of which 12 were waited for; matrix products, arithmetic and copies ran while one was open for 7% of the time, Pallas kernels for 10%

profile of v8, /device:TPU:1, one launch (start us, length us, event | category | flops | bytes accessed | tf_op | source)
XLA Modules:
  0.0 281.1 jit_solution(5184936513350194360)
XLA Ops:
  0.0 2.6 leave.1
  2.6 9.3 %all-to-all-start = ((bf16[16,36,256]{2,1,0:T(8,128)(2,1)}), bf16[16,36,256]{2,1,0:T(8,128)(2,1)S(1)}, u32[]{:S(2)}, u32[]{:S(2)}) async-start(bf16[16,36,256]{2,1,0:T(8,128)(2,1)} %leave.1), calls=%async_computation | async-start | bytes 655360 | tf_op jit(solution)/shard_map/all_to_all | solution.py:28
  11.9 1.2 collective-permute-start.1
  13.6 7.4 %all-to-all-done.in_ref = bf16[16,36,256]{2,1,0:T(8,128)(2,1)S(1)} async-done(((bf16[16,36,256]{2,1,0:T(8,128)(2,1)}), bf16[16,36,256]{2,1,0:T(8,128)(2,1)S(1)}, u32[]{:S(2)}, u32[]{:S(2)}) %all-to-all-start) | async-done | bytes 294944 | tf_op jit(solution)/shard_map/all_to_all | solution.py:28
  21.0 1.3 route.1
  22.3 4.3 %all-to-all-start.1 = ((bf16[16,36,256]{2,1,0:T(8,128)(2,1)}), bf16[16,36,256]{2,1,0:T(8,128)(2,1)S(1)}, u32[]{:S(2)}, u32[]{:S(2)}) async-start(bf16[16,36,256]{2,1,0:T(8,128)(2,1)} %route.1), calls=%async_computation.1 | async-start | bytes 655360 | tf_op jit(solution)/shard_map/all_to_all | solution.py:28
  26.6 3.5 %multiply_convert_fusion.refs_0_ = bf16[896,1152]{1,0:T(8,128)(2,1)} fusion(f32[896]{0:T(1024)S(1)} %convert_element_type.62, bf16[896,1152]{1,0:T(8,128)(2,1)} %param.23, bf16[896,1152]{1,0:T(8,128)(2,1)} %param.24, pred[]{:T(512)S(6)} %eq.17), kind=kLoop, calls=%fused_computation.2 | loop fusion | flops 4128768 | bytes 6196737 | tf_op jit(solution)/shard_map/convert_element_type | solution.py:363
  30.2 2.6 multiply_convert_fusion.2
  32.8 2.7 pad_maximum_fusion.1
  35.9 1.0 collective-permute-start.2
  36.9 1.1 copy.55
  38.6 1.3 pad_add_fusion.ids_ref
  39.9 6.3 %attend.1.refs_1_ = bf16[8,2,2,32,512]{4,3,2,1,0:T(8,128)(2,1)} custom-call(s32[2]{0:T(128)} %pad_add_fusion.ids_ref, s32[4]{0:T(128)} %lengths_ref.3, bf16[4,576,2]{2,1,0:T(8,128)(2,1)} %bitcast.64, bf16[2,4,576,128]{3,2,1,0:T(8,128)(2,1)} %bitcast.66, bf16[4,576,256]{2,1,0:T(8,128)(2,1)} %bitcast.69), custom_call_target="tpu_custom_call" | custom-call | tf_op jit(solution)/shard_map/attend/pallas_call | solution.py:140
  46.3 3.4 %again.1 = bf16[8,2,2,32,512]{4,3,2,1,0:T(8,128)(2,1)} custom-call(s32[2]{0:T(128)} %pad_add_fusion.ids_ref, s32[4]{0:T(128)} %lengths_ref.3, bf16[4,576,2]{2,1,0:T(8,128)(2,1)} %bitcast.65, bf16[2,4,576,128]{3,2,1,0:T(8,128)(2,1)} %bitcast.67, bf16[16,36,256]{2,1,0:T(8,128)(2,1)} %copy-done.7, ...), custom_call_target="tpu_custom_call", output_to_operand_aliasing={{}: (5, {})} | custom-call | tf_op jit(solution)/shard_map/again/pallas_call | solution.py:140
  49.6 4.0 %collective-permute-done.1.refs_2_ = bf16[1024,896]{1,0:T(8,128)(2,1)} collective-permute-done((bf16[1024,896]{1,0:T(8,128)(2,1)}, bf16[1024,896]{1,0:T(8,128)(2,1)}, u32[]{:S(2)}, u32[]{:S(2)}) %collective-permute-start.1) | collective-permute-done | bytes 1835040 | tf_op jit(solution)/shard_map/ppermute | solution.py:36
  53.7 1.0 collective-permute-start.5
  54.6 7.0 %all-to-all-start.2 = ((bf16[16,2,32,512]{3,2,1,0:T(8,128)(2,1)}), bf16[16,2,32,512]{3,2,1,0:T(8,128)(2,1)S(1)}, u32[]{:S(2)}, u32[]{:S(2)}) async-start(bf16[16,2,32,512]{3,2,1,0:T(8,128)(2,1)} %bitcast.62), calls=%async_computation.2 | async-start | bytes 2097152 | tf_op jit(solution)/shard_map/all_to_all | solution.py:28
  61.6 1.2 collective-permute-start.3
  63.9 20.3 %collective-permute-done.6 = bf16[32,896]{1,0:T(8,128)(2,1)S(1)} collective-permute-done((bf16[32,896]{1,0:T(8,128)(2,1)S(1)}, bf16[32,896]{1,0:T(8,128)(2,1)S(1)}, u32[]{:S(2)}, u32[]{:S(2)}) %collective-permute-start.6) | collective-permute-done | bytes 57376 | tf_op jit(solution)/shard_map/ppermute | solution.py:36
  84.2 2.9 %fusion = bf16[64,16,128]{2,0,1:T(8,128)(2,1)S(1)} fusion(bf16[16,512,128]{2,1,0:T(8,128)(2,1)} %pad_maximum_fusion.1, bf16[64,16,512]{2,1,0:T(8,128)(2,1)S(1)} %bitcast.70), kind=kOutput, calls=%fused_computation.10 | convolution fusion | flops 134348800 | bytes 3407872 | tf_op jit(solution)/shard_map/thl,hlv->thv/dot_general | solution.py:388
  87.5 1.1 broadcast_in_dim.28
  88.5 4.5 %all-to-all-start.3 = ((bf16[8,32,2048]{2,1,0:T(8,128)(2,1)}), bf16[8,32,2048]{2,1,0:T(8,128)(2,1)S(1)}, u32[]{:S(2)}, u32[]{:S(2)}) async-start(bf16[8,32,2048]{2,1,0:T(8,128)(2,1)} %bitcast.19), calls=%async_computation.3 | async-start | bytes 2097152 | tf_op jit(solution)/shard_map/all_to_all | solution.py:28
  93.0 3.0 %multiply_convert_fusion.1 = bf16[512,1152]{1,0:T(8,128)(2,1)} fusion(f32[512]{0:T(512)S(1)} %slice.40, bf16[896,1152]{1,0:T(8,128)(2,1)} %param.23, bf16[896,1152]{1,0:T(8,128)(2,1)} %param.24, pred[]{:T(512)S(6)} %eq.17), kind=kLoop, calls=%fused_computation.3 | loop fusion | flops 2359296 | bytes 3540993 | tf_op jit(solution)/shard_map/convert_element_type | solution.py:363
  96.0 11.8 %all-to-all-done.3.rows_ref = bf16[8,32,2048]{2,1,0:T(8,128)(2,1)S(1)} async-done(((bf16[8,32,2048]{2,1,0:T(8,128)(2,1)}), bf16[8,32,2048]{2,1,0:T(8,128)(2,1)S(1)}, u32[]{:S(2)}, u32[]{:S(2)}) %all-to-all-start.3) | async-done | bytes 1048608 | tf_op jit(solution)/shard_map/all_to_all | solution.py:28
  108.1 0.7 copy-done.6
  108.8 7.4 %combine.1 = bf16[8,2,32,896]{3,2,1,0:T(8,128)(2,1)} custom-call(s32[2]{0:T(128)} %pad_add_fusion.ids_ref, bf16[8,32,2048]{2,1,0:T(8,128)(2,1)} %copy-done.6, bf16[1024,896]{1,0:T(8,128)(2,1)} %refs_0_, bf16[1024,896]{1,0:T(8,128)(2,1)} %collective-permute-done.4.refs_1_, bf16[1024,896]{1,0:T(8,128)(2,1)} %collective-permute-done.1.refs_2_, ...), custom_call_target="tpu_custom_call" | custom-call | tf_op jit(solution)/shard_map/combine/pallas_call | solution.py:233
  116.2 6.9 %all-to-all-start.4 = ((bf16[8,2,32,896]{3,2,1,0:T(8,128)(2,1)}), bf16[8,2,32,896]{3,2,1,0:T(8,128)(2,1)S(1)}, u32[]{:S(2)}, u32[]{:S(2)}) async-start(bf16[8,2,32,896]{3,2,1,0:T(8,128)(2,1)} %combine.1), calls=%async_computation.4 | async-start | bytes 1835008 | tf_op jit(solution)/shard_map/all_to_all | solution.py:28
  123.2 15.9 %all-to-all-done.4 = bf16[8,2,32,896]{3,2,1,0:T(8,128)(2,1)S(1)} async-done(((bf16[8,2,32,896]{3,2,1,0:T(8,128)(2,1)}), bf16[8,2,32,896]{3,2,1,0:T(8,128)(2,1)S(1)}, u32[]{:S(2)}, u32[]{:S(2)}) %all-to-all-start.4) | async-done | bytes 917536 | tf_op jit(solution)/shard_map/all_to_all | solution.py:28
  139.2 1.5 broadcast_in_dim.29
  140.7 3.7 %all-to-all-start.5 = ((bf16[16,2,32,896]{3,2,1,0:T(8,128)(2,1)}), bf16[16,2,32,896]{3,2,1,0:T(8,128)(2,1)S(1)}, u32[]{:S(2)}, u32[]{:S(2)}) async-start(bf16[16,2,32,896]{3,2,1,0:T(8,128)(2,1)} %broadcast_in_dim.29), calls=%async_computation.5 | async-start | bytes 3670016 | tf_op jit(solution)/shard_map/all_to_all | solution.py:28
  144.4 1.2 collective-permute-start.10
  146.2 4.6 %collective-permute-done.9.refs_4_ = bf16[384,1152]{1,0:T(8,128)(2,1)S(1)} collective-permute-done((bf16[384,1152]{1,0:T(8,128)(2,1)}, bf16[384,1152]{1,0:T(8,128)(2,1)S(1)}, u32[]{:S(2)}, u32[]{:S(2)}) %collective-permute-start.9) | collective-permute-done | bytes 884768 | tf_op jit(solution)/shard_map/ppermute | solution.py:36
  150.7 1.0 copy-done.10
  151.7 18.7 %all-to-all-done.5 = bf16[16,2,32,896]{3,2,1,0:T(8,128)(2,1)S(1)} async-done(((bf16[16,2,32,896]{3,2,1,0:T(8,128)(2,1)}), bf16[16,2,32,896]{3,2,1,0:T(8,128)(2,1)S(1)}, u32[]{:S(2)}, u32[]{:S(2)}) %all-to-all-start.5) | async-done | bytes 1835040 | tf_op jit(solution)/shard_map/all_to_all | solution.py:28
  170.4 1.2 copy-done.5
  171.6 10.4 %widen.1 = bf16[8,2,32,2432]{3,2,1,0:T(8,128)(2,1)} custom-call(s32[2]{0:T(128)} %pad_add_fusion.ids_ref, bf16[2,8,2,32,896]{4,3,2,1,0:T(8,128)(2,1)} %bitcast.63, bf16[896,1152]{1,0:T(8,128)(2,1)} %multiply_convert_fusion.refs_0_, bf16[384,1152]{1,0:T(8,128)(2,1)} %collective-permute-done.3.refs_1_, bf16[512,1152]{1,0:T(8,128)(2,1)} %copy-done.8, ...), custom_call_target="tpu_custom_call" | custom-call | tf_op jit(solution)/shard_map/widen/pallas_call | solution.py:290
  182.0 4.4 %all-to-all-start.6 = ((bf16[8,64,2432]{2,1,0:T(8,128)(2,1)}), bf16[8,64,2432]{2,1,0:T(8,128)(2,1)}, u32[]{:S(2)}, u32[]{:S(2)}) async-start(bf16[8,64,2432]{2,1,0:T(8,128)(2,1)} %bitcast.61), calls=%async_computation.6 | async-start | bytes 4980736 | tf_op jit(solution)/shard_map/all_to_all | solution.py:28
  186.4 4.5 %pad_maximum_fusion.weight_ref = bf16[2304,896]{1,0:T(8,128)(2,1)} fusion(bf16[1152,896]{1,0:T(8,128)(2,1)} %collective-permute-done.11, bf16[1152,896]{1,0:T(8,128)(2,1)} %param.25), kind=kLoop, calls=%fused_computation.1 | loop fusion | flops 8257536 | bytes 8257536 | tf_op jit(solution)/shard_map/concatenate | solution.py:346
  190.9 30.4 %all-to-all-done.6 = bf16[8,64,2432]{2,1,0:T(8,128)(2,1)} async-done(((bf16[8,64,2432]{2,1,0:T(8,128)(2,1)}), bf16[8,64,2432]{2,1,0:T(8,128)(2,1)}, u32[]{:S(2)}, u32[]{:S(2)}) %all-to-all-start.6) | async-done | bytes 2490400 | tf_op jit(solution)/shard_map/all_to_all | solution.py:28
  221.3 2.2 convert_reduce_fusion
  224.2 30.1 %all_to_all.45.rows_ref = bf16[8,64,2304]{2,1,0:T(8,128)(2,1)S(1)} all-to-all(bf16[8,64,2304]{2,1,0:T(8,128)(2,1)S(1)} %broadcast_in_dim.31), channel_id=1, replica_groups=mesh['xh'=2,'xl'=2,'zl'=2,'zh'=2,'y'=4,'c'=2] {'xh','xl','zl'}, dimensions={0} | all-to-all | bytes 4718592 | tf_op jit(solution)/shard_map/all_to_all | solution.py:28
  254.3 4.1 %project.1 = bf16[8,1,64,896]{3,2,1,0:T(8,128)(2,1)} custom-call(s32[2]{0:T(128)S(1)} %copy-done.3, bf16[8,64,2304]{2,1,0:T(8,128)(2,1)S(1)} %all_to_all.45.rows_ref, bf16[2304,896]{1,0:T(8,128)(2,1)S(1)} %copy-done.2), custom_call_target="tpu_custom_call" | custom-call | tf_op jit(solution)/shard_map/project/pallas_call | solution.py:181
  258.3 3.6 %all-to-all-start.8 = ((bf16[8,64,896]{2,1,0:T(8,128)(2,1)}), bf16[8,64,896]{2,1,0:T(8,128)(2,1)S(1)}, u32[]{:S(2)}, u32[]{:S(2)}) async-start(bf16[8,64,896]{2,1,0:T(8,128)(2,1)} %bitcast.26), calls=%async_computation.8 | async-start | bytes 1835008 | tf_op jit(solution)/shard_map/all_to_all | solution.py:28
  262.3 3.4 %collective-permute-done.8 = f32[32,896]{1,0:T(8,128)S(1)} collective-permute-done((f32[32,896]{1,0:T(8,128)S(1)}, f32[32,896]{1,0:T(8,128)S(1)}, u32[]{:S(2)}, u32[]{:S(2)}) %collective-permute-start.8) | collective-permute-done | bytes 114720 | tf_op jit(solution)/shard_map/ppermute | solution.py:36
  265.8 11.3 %all-to-all-done.8 = bf16[8,64,896]{2,1,0:T(8,128)(2,1)S(1)} async-done(((bf16[8,64,896]{2,1,0:T(8,128)(2,1)}), bf16[8,64,896]{2,1,0:T(8,128)(2,1)S(1)}, u32[]{:S(2)}, u32[]{:S(2)}) %all-to-all-start.8) | async-done | bytes 917536 | tf_op jit(solution)/shard_map/all_to_all | solution.py:28
  277.5 1.6 collective-permute-start.12
  279.1 0.9 collective-permute-done.12
  280.4 0.7 copy.60
  (73 shorter events, 5.8 us)
Async XLA Ops:
  0.0 62.8 %copy-start = (bf16[2,512,896]{2,1,0:T(8,128)(2,1)S(1)}, bf16[2,512,896]{2,1,0:T(8,128)(2,1)}, u32[]{:S(2)}) copy-start(bf16[2,512,896]{2,1,0:T(8,128)(2,1)} %param.21) | copy-start | bytes 5505028
  0.0 13.1 %copy-start.9 = (bf16[8,512,128]{2,1,0:T(8,128)(2,1)S(1)}, bf16[8,512,128]{2,1,0:T(8,128)(2,1)}, u32[]{:S(2)}) copy-start(bf16[8,512,128]{2,1,0:T(8,128)(2,1)} %param.19) | copy-start | bytes 3145732
  0.0 13.6 %copy-start.11 = (bf16[896]{0:T(1024)(128)(2,1)S(1)}, bf16[896]{0:T(1024)(128)(2,1)}, u32[]{:S(2)}) copy-start(bf16[896]{0:T(1024)(128)(2,1)} %param.22) | copy-start | bytes 5380
  0.0 21.0 %copy-start.4 = (s32[1,16]{1,0:T(1,128)S(1)}, s32[1,16]{1,0:T(1,128)}, u32[]{:S(2)}) copy-start(s32[1,16]{1,0:T(1,128)} %param.16) | copy-start | bytes 196
  2.6 18.4 %all-to-all-start = ((bf16[16,36,256]{2,1,0:T(8,128)(2,1)}), bf16[16,36,256]{2,1,0:T(8,128)(2,1)S(1)}, u32[]{:S(2)}, u32[]{:S(2)}) async-start(bf16[16,36,256]{2,1,0:T(8,128)(2,1)} %leave.1), calls=%async_computation | async-start | bytes 655360 | tf_op jit(solution)/shard_map/all_to_all | solution.py:28
  11.9 41.8 %collective-permute-start.1 = (bf16[1024,896]{1,0:T(8,128)(2,1)}, bf16[1024,896]{1,0:T(8,128)(2,1)}, u32[]{:S(2)}, u32[]{:S(2)}) collective-permute-start(bf16[1024,896]{1,0:T(8,128)(2,1)} %refs_0_), channel_id=1, source_target_pairs={{0,32},{32,0},{1,33},{33,1},{2,34},{34,2},{3,35},{35,3},{4,36},{36... | collective-permute-start | bytes 5505032 | tf_op jit(solution)/shard_map/ppermute | solution.py:36
  13.1 19.7 %collective-permute-start = (bf16[8,512,128]{2,1,0:T(8,128)(2,1)S(1)}, bf16[8,512,128]{2,1,0:T(8,128)(2,1)}, u32[]{:S(2)}, u32[]{:S(2)}) collective-permute-start(bf16[8,512,128]{2,1,0:T(8,128)(2,1)S(1)} %copy-done.9), channel_id=1, source_target_pairs={{0,1},{1,0},{2,3},{3,2},{4,5},{5,4},{6,7},{7,6},{8,9},{9,8},{10,11... | collective-permute-start | bytes 3145736 | tf_op jit(solution)/shard_map/ppermute | solution.py:36
  22.3 13.6 %all-to-all-start.1 = ((bf16[16,36,256]{2,1,0:T(8,128)(2,1)}), bf16[16,36,256]{2,1,0:T(8,128)(2,1)S(1)}, u32[]{:S(2)}, u32[]{:S(2)}) async-start(bf16[16,36,256]{2,1,0:T(8,128)(2,1)} %route.1), calls=%async_computation.1 | async-start | bytes 655360 | tf_op jit(solution)/shard_map/all_to_all | solution.py:28
  32.8 4.1 %copy-start.12 = (bf16[2,4,576]{2,1,0:T(4,128)(2,1)S(1)}, bf16[2,4,576]{2,1,0:T(4,128)(2,1)}, u32[]{:S(2)}) copy-start(bf16[2,4,576]{2,1,0:T(4,128)(2,1)} %param.18) | copy-start | bytes 27652
  32.8 5.2 %copy-start.13 = (s32[1,16]{1,0:T(1,128)S(1)}, s32[1,16]{1,0:T(1,128)}, u32[]{:S(2)}) copy-start(s32[1,16]{1,0:T(1,128)} %param.15) | copy-start | bytes 196
  35.9 10.4 %copy-start.7 = (bf16[16,36,256]{2,1,0:T(8,128)(2,1)}, bf16[16,36,256]{2,1,0:T(8,128)(2,1)S(1)}, u32[]{:S(2)}) copy-start(bf16[16,36,256]{2,1,0:T(8,128)(2,1)S(1)} %all-to-all-done.1.refs_0_) | copy-start | bytes 884740
  35.9 48.3 %collective-permute-start.2 = (bf16[896,1152]{1,0:T(8,128)(2,1)}, bf16[896,1152]{1,0:T(8,128)(2,1)}, u32[]{:S(2)}, u32[]{:S(2)}) collective-permute-start(bf16[896,1152]{1,0:T(8,128)(2,1)} %multiply_convert_fusion.refs_0_), channel_id=1, source_target_pairs={{0,1},{1,0},{2,3},{3,2},{4,5},{5,4},{6,7},{7,6},{8,9},{9,8},{10,11... | collective-permute-start | bytes 6193160 | tf_op jit(solution)/shard_map/ppermute | solution.py:36
  36.9 47.3 %collective-permute-start.4 = (bf16[1024,896]{1,0:T(8,128)(2,1)}, bf16[1024,896]{1,0:T(8,128)(2,1)}, u32[]{:S(2)}, u32[]{:S(2)}) collective-permute-start(bf16[1024,896]{1,0:T(8,128)(2,1)} %refs_0_), channel_id=1, source_target_pairs={{0,1},{1,0},{2,3},{3,2},{4,5},{5,4},{6,7},{7,6},{8,9},{9,8},{10,11... | collective-permute-start | bytes 5505032 | tf_op jit(solution)/shard_map/ppermute | solution.py:36
  53.7 30.6 %collective-permute-start.5 = (bf16[1024,896]{1,0:T(8,128)(2,1)}, bf16[1024,896]{1,0:T(8,128)(2,1)}, u32[]{:S(2)}, u32[]{:S(2)}) collective-permute-start(bf16[1024,896]{1,0:T(8,128)(2,1)} %collective-permute-done.1.refs_2_), channel_id=1, source_target_pairs={{0,1},{1,0},{2,3},{3,2},{4,5},{5,4},{6,7},{7,6},{8,9},{9,8},{10,11... | collective-permute-start | bytes 5505032 | tf_op jit(solution)/shard_map/ppermute | solution.py:36
  54.6 29.6 %all-to-all-start.2 = ((bf16[16,2,32,512]{3,2,1,0:T(8,128)(2,1)}), bf16[16,2,32,512]{3,2,1,0:T(8,128)(2,1)S(1)}, u32[]{:S(2)}, u32[]{:S(2)}) async-start(bf16[16,2,32,512]{3,2,1,0:T(8,128)(2,1)} %bitcast.62), calls=%async_computation.2 | async-start | bytes 2097152 | tf_op jit(solution)/shard_map/all_to_all | solution.py:28
  61.6 22.6 %collective-permute-start.3 = (bf16[384,1152]{1,0:T(8,128)(2,1)}, bf16[384,1152]{1,0:T(8,128)(2,1)}, u32[]{:S(2)}, u32[]{:S(2)}) collective-permute-start(bf16[384,1152]{1,0:T(8,128)(2,1)} %multiply_convert_fusion.2), channel_id=1, source_target_pairs={{0,32},{32,0},{1,33},{33,1},{2,34},{34,2},{3,35},{35,3},{4,36},{36... | collective-permute-start | bytes 2654216 | tf_op jit(solution)/shard_map/ppermute | solution.py:36
  63.6 20.6 %collective-permute-start.6 = (bf16[32,896]{1,0:T(8,128)(2,1)S(1)}, bf16[32,896]{1,0:T(8,128)(2,1)S(1)}, u32[]{:S(2)}, u32[]{:S(2)}) collective-permute-start(bf16[32,896]{1,0:T(8,128)(2,1)S(1)} %bitcast.76), channel_id=1, source_target_pairs={{0,32},{32,0},{1,33},{33,1},{2,34},{34,2},{3,35},{35,3},{4,36},{36... | collective-permute-start | bytes 172040 | tf_op jit(solution)/shard_map/ppermute | solution.py:36
  88.5 19.3 %all-to-all-start.3 = ((bf16[8,32,2048]{2,1,0:T(8,128)(2,1)}), bf16[8,32,2048]{2,1,0:T(8,128)(2,1)S(1)}, u32[]{:S(2)}, u32[]{:S(2)}) async-start(bf16[8,32,2048]{2,1,0:T(8,128)(2,1)} %bitcast.19), calls=%async_computation.3 | async-start | bytes 2097152 | tf_op jit(solution)/shard_map/all_to_all | solution.py:28
  107.9 1.0 copy-start.6
  107.9 31.2 %collective-permute-start.7 = (bf16[512,1152]{1,0:T(8,128)(2,1)}, bf16[512,1152]{1,0:T(8,128)(2,1)S(1)}, u32[]{:S(2)}, u32[]{:S(2)}) collective-permute-start(bf16[512,1152]{1,0:T(8,128)(2,1)} %multiply_convert_fusion.1), channel_id=1, source_target_pairs={{0,32},{32,0},{1,33},{33,1},{2,34},{34,2},{3,35},{35,3},{4,36},{36... | collective-permute-start | bytes 3538952 | tf_op jit(solution)/shard_map/ppermute | solution.py:36
  116.2 22.8 %all-to-all-start.4 = ((bf16[8,2,32,896]{3,2,1,0:T(8,128)(2,1)}), bf16[8,2,32,896]{3,2,1,0:T(8,128)(2,1)S(1)}, u32[]{:S(2)}, u32[]{:S(2)}) async-start(bf16[8,2,32,896]{3,2,1,0:T(8,128)(2,1)} %combine.1), calls=%async_computation.4 | async-start | bytes 1835008 | tf_op jit(solution)/shard_map/all_to_all | solution.py:28
  139.1 5.4 %copy-start.8 = (bf16[512,1152]{1,0:T(8,128)(2,1)}, bf16[512,1152]{1,0:T(8,128)(2,1)S(1)}, u32[]{:S(2)}) copy-start(bf16[512,1152]{1,0:T(8,128)(2,1)S(1)} %collective-permute-done.7.refs_2_) | copy-start | bytes 3538948
  140.7 29.7 %all-to-all-start.5 = ((bf16[16,2,32,896]{3,2,1,0:T(8,128)(2,1)}), bf16[16,2,32,896]{3,2,1,0:T(8,128)(2,1)S(1)}, u32[]{:S(2)}, u32[]{:S(2)}) async-start(bf16[16,2,32,896]{3,2,1,0:T(8,128)(2,1)} %broadcast_in_dim.29), calls=%async_computation.5 | async-start | bytes 3670016 | tf_op jit(solution)/shard_map/all_to_all | solution.py:28
  144.4 7.3 %collective-permute-start.10 = (bf16[512,1152]{1,0:T(8,128)(2,1)S(1)}, bf16[512,1152]{1,0:T(8,128)(2,1)}, u32[]{:S(2)}, u32[]{:S(2)}) collective-permute-start(bf16[512,1152]{1,0:T(8,128)(2,1)S(1)} %collective-permute-done.7.refs_2_), channel_id=1, source_target_pairs={{0,1},{1,0},{2,3},{3,2},{4,5},{5,4},{6,7},{7,6},{8,9},{9,8},{10,11... | collective-permute-start | bytes 3538952 | tf_op jit(solution)/shard_map/ppermute | solution.py:36
  145.7 5.1 %collective-permute-start.9 = (bf16[384,1152]{1,0:T(8,128)(2,1)}, bf16[384,1152]{1,0:T(8,128)(2,1)S(1)}, u32[]{:S(2)}, u32[]{:S(2)}) collective-permute-start(bf16[384,1152]{1,0:T(8,128)(2,1)} %collective-permute-done.3.refs_1_), channel_id=1, source_target_pairs={{0,1},{1,0},{2,3},{3,2},{4,5},{5,4},{6,7},{7,6},{8,9},{9,8},{10,11... | collective-permute-start | bytes 2654216 | tf_op jit(solution)/shard_map/ppermute | solution.py:36
  145.7 40.7 %collective-permute-start.11 = (bf16[1152,896]{1,0:T(8,128)(2,1)}, bf16[1152,896]{1,0:T(8,128)(2,1)}, u32[]{:S(2)}, u32[]{:S(2)}) collective-permute-start(bf16[1152,896]{1,0:T(8,128)(2,1)} %param.25), channel_id=1, source_target_pairs={{0,1},{1,0},{2,3},{3,2},{4,5},{5,4},{6,7},{7,6},{8,9},{9,8},{10,11... | collective-permute-start | bytes 6193160 | tf_op jit(solution)/shard_map/ppermute | solution.py:36
  150.7 1.0 copy-start.10
  170.4 1.2 copy-start.5
  182.0 39.3 %all-to-all-start.6 = ((bf16[8,64,2432]{2,1,0:T(8,128)(2,1)}), bf16[8,64,2432]{2,1,0:T(8,128)(2,1)}, u32[]{:S(2)}, u32[]{:S(2)}) async-start(bf16[8,64,2432]{2,1,0:T(8,128)(2,1)} %bitcast.61), calls=%async_computation.6 | async-start | bytes 4980736 | tf_op jit(solution)/shard_map/all_to_all | solution.py:28
  224.2 30.1 %copy-start.2 = (bf16[2304,896]{1,0:T(8,128)(2,1)S(1)}, bf16[2304,896]{1,0:T(8,128)(2,1)}, u32[]{:S(2)}) copy-start(bf16[2304,896]{1,0:T(8,128)(2,1)} %pad_maximum_fusion.weight_ref) | copy-start | bytes 12386308
  224.2 30.1 %copy-start.3 = (s32[2]{0:T(128)S(1)}, s32[2]{0:T(128)}, u32[]{:S(2)}) copy-start(s32[2]{0:T(128)} %pad_add_fusion.ids_ref) | copy-start | bytes 28
  258.3 18.7 %all-to-all-start.8 = ((bf16[8,64,896]{2,1,0:T(8,128)(2,1)}), bf16[8,64,896]{2,1,0:T(8,128)(2,1)S(1)}, u32[]{:S(2)}, u32[]{:S(2)}) async-start(bf16[8,64,896]{2,1,0:T(8,128)(2,1)} %bitcast.26), calls=%async_computation.8 | async-start | bytes 1835008 | tf_op jit(solution)/shard_map/all_to_all | solution.py:28
  261.9 3.7 %collective-permute-start.8 = (f32[32,896]{1,0:T(8,128)S(1)}, f32[32,896]{1,0:T(8,128)S(1)}, u32[]{:S(2)}, u32[]{:S(2)}) collective-permute-start(f32[32,896]{1,0:T(8,128)S(1)} %dynamic-slice_bitcast_fusion), channel_id=1, source_target_pairs={{0,32},{32,0},{1,33},{33,1},{2,34},{34,2},{3,35},{35,3},{4,36},{36... | collective-permute-start | bytes 344072 | tf_op jit(solution)/shard_map/ppermute | solution.py:36
  262.3 18.8 %copy-start.1 = (bf16[2,512,896]{2,1,0:T(8,128)(2,1)S(1)}, bf16[2,512,896]{2,1,0:T(8,128)(2,1)}, u32[]{:S(2)}) copy-start(bf16[2,512,896]{2,1,0:T(8,128)(2,1)} %param.21) | copy-start | bytes 5505028
  277.5 2.5 collective-permute-start.12

commit v9 on v7

--- a/solution.py
+++ b/solution.py
@@ -17,7 +17,7 @@
 N_TP = 16
 N_ZY = 8
 SWAP = [(0, 1), (1, 0)]
-CUTS = (0, 384, 896)
+CUTS = (0, 256, 768, 896)
 TILE = 768
 bf16 = jnp.bfloat16
 f32 = jnp.float32
@@ -169,6 +169,38 @@
     )(ids, lengths, fresh_t, queries_t, *extra)
 
 
+def join(blocks):
+    flat = [w for column in blocks for w in column]
+    depth = sum(w.shape[0] for w in blocks[0])
+    width = sum(column[0].shape[1] for column in blocks)
+
+    def body(*refs):
+        out_ref, sems = refs[len(flat) :]
+        copies, left = [], 0
+        for column in blocks:
+            top = 0
+            for w in column:
+                at = out_ref.at[pl.ds(top, w.shape[0]), pl.ds(left, w.shape[1])]
+                n = len(copies)
+                copies.append(pltpu.make_async_copy(refs[n], at, sems.at[n]))
+                top += w.shape[0]
+            left += column[0].shape[1]
+        for copy in copies:
+            copy.start()
+        for copy in copies:
+            copy.wait()
+
+    return pl.pallas_call(
+        body,
+        in_specs=[pl.BlockSpec(memory_space=pl.ANY) for _ in flat],
+        out_specs=pl.BlockSpec(memory_space=pl.ANY),
+        scratch_shapes=[pltpu.SemaphoreType.DMA((len(flat),))],
+        out_shape=jax.ShapeDtypeStruct((depth, width), bf16),
+        compiler_params=params(8),
+        name="join",
+    )(*flat)
+
+
 def project(ids, rows, weight, blocks):
     groups, count, depth = rows.shape
     width = weight.shape[1] // blocks
@@ -291,8 +323,14 @@
     own_slot = jnp.sum(jnp.where(lanes == member, move_slot[0], 0))
     ids = jnp.stack([own_slot, pair]).astype(jnp.int32)
     cache_t = cache.transpose(0, 2, 1)
-    pieces = exchange(leave(move_slot[0], cache_t), TP)
-    pieces, gate_weight, up_weight = lax.optimization_barrier((pieces, gate_weight, up_weight))
+    leaving, ids = lax.optimization_barrier((leave(move_slot[0], cache_t), ids))
+    pieces = exchange(leaving, TP)
+    fresh_t = new_latent.transpose(1, 2, 0)
+    queries_t = queries.transpose(0, 1, 3, 2)
+    out = attend(ids, cache_length, cache_t, fresh_t, queries_t, heads, latent_width)
+    pieces, out, gate_weight, up_weight = lax.optimization_barrier(
+        (pieces, out, gate_weight, up_weight)
+    )
 
     gain = norm_gain.astype(f32)[:, None]
 
@@ -305,22 +343,20 @@
     ]
     kept = scaled(0, CUTS[-1], gate_weight, up_weight)
     arrived = exchange(route(move_peer[0], pieces), TP)
-    fresh_t = new_latent.transpose(1, 2, 0)
-    queries_t = queries.transpose(0, 1, 3, 2)
-    out = attend(ids, cache_length, cache_t, fresh_t, queries_t, heads, latent_width)
+    arrived, kept, sent[0], value_ups = lax.optimization_barrier(
+        (arrived, kept, sent[0], value_ups)
+    )
     out = attend(
         ids, cache_length, cache_t, fresh_t, queries_t, heads, latent_width, arrived, out
     )
-    out, out_came, sent[0] = lax.optimization_barrier((out, out_came, sent[0]))
+    out, out_came = lax.optimization_barrier((out, out_came))
     came = [swap(sent[0], "xl")]
-    out_weights = jnp.concatenate(
-        [jnp.concatenate([w, swap(w, "c")], axis=0) for w in (out_proj, out_came)], axis=1
-    )
+    out_weights = join([[w, swap(w, "c")] for w in (out_proj, out_came)])
     kept = [kept, swap(kept, "c")]
     out = out.reshape((N_TP,) + out.shape[2:])
     by_head = exchange(out, TP).reshape(-1, 2 * heads, latent_width)
-    by_head, kept, came, out_weights, value_ups, residue_came, downs = lax.optimization_barrier(
-        (by_head, kept, came, out_weights, value_ups, residue_came, downs)
+    by_head, kept, came, out_weights, residue_came = lax.optimization_barrier(
+        (by_head, kept, came, out_weights, residue_came)
     )
     value_heads = jnp.einsum(
         "thl,hlv->thv", by_head, value_ups, preferred_element_type=f32
@@ -335,20 +371,16 @@
     gathered, sent[1] = lax.optimization_barrier((gathered, sent[1]))
     came.append(swap(sent[1], "xl"))
     parts = exchange(project(ids, gathered, out_weights, 2), ZY)
-    parts, came[1] = lax.optimization_barrier((parts, came[1]))
-    in_weight = jnp.concatenate(
-        [
-            jnp.concatenate([own, swap(own, "c") if k else kept[1]], axis=1)
-            for k, own in enumerate([kept[0]] + came)
-        ],
-        axis=0,
-    )
+    parts, came[1], sent[2] = lax.optimization_barrier((parts, came[1], sent[2]))
+    came.append(swap(sent[2], "xl"))
+    in_weight = join([[kept[0]] + came, [kept[1]] + [swap(w, "c") for w in came]])
     residue = by_pair(at_pair(residue), residue_came)
     hidden = residue.astype(f32) + jnp.sum(parts.astype(f32), axis=0)
 
     rows = spread(hidden.astype(bf16), PAIR, 2 * N_ZY).reshape((2, N_ZY) + hidden.shape)
     rows, in_weight = lax.optimization_barrier((rows, in_weight))
     sums = exchange(widen(ids, rows, in_weight).reshape(N_DP, chunk, -1), DP)
+    sums, downs = lax.optimization_barrier((sums, downs))
     sums = jnp.sum(sums.reshape(2, 2, 2, chunk, -1).astype(f32), axis=(0, 2))
     squares = sums[0, :, 2 * units] + sums[0, :, 2 * units + 1]
     inverse = lax.rsqrt(squares / D + norm_eps)[:, None]

time: 268 us -> 296 us (1.10)
  waiting for transfers between devices: 40.8 us -> 117 us
  blocking collectives: 79.8 us -> 30.3 us
  other arithmetic: 53.6 us -> 23.5 us
  starting transfers between devices: 50.1 us -> 62 us
  local copies, waits for them, and re-layouts: 13.1 us -> 22.4 us
  Pallas kernels: 27.6 us -> 36 us
    all_to_all x3 -> x1, blocking collectives: 79.8 us -> 30.3 us  [exchange(): return lax.all_to_all(blocks, axes, 0, 0, tiled=True)]
    ppermute x13 -> x15, waiting for transfers between devices: 5.46 us -> 45.5 us  [swap(): return lax.ppermute(block, axis, SWAP)]
    all_to_all x6 -> x8, waiting for transfers between devices: 35.3 us -> 71.4 us  [exchange(): return lax.all_to_all(blocks, axes, 0, 0, tiled=True)]
    concatenate x2 -> x0, other arithmetic: 35.1 us -> none  [the longest x1 19.9 us: local(): jnp.concatenate([jnp.concatenate([own, swap(own, 'c') if k else kept[1]],...]
    all_to_all x6 -> x8, starting transfers between devices: 37.8 us -> 49 us  [exchange(): return lax.all_to_all(blocks, axes, 0, 0, tiled=True)]
    unnamed x28 -> x38, local copies, waits for them, and re-layouts: 8.34 us -> 16.9 us
    pallas_call x0 -> x2, Pallas kernels: none -> 4.76 us  [join(): pl.pallas_call(body, in_specs=[pl.BlockSpec(memory_space=pl.ANY) for _ in...]
    ppermute x13 -> x15, starting transfers between devices: 12.3 us -> 13 us  [swap(): return lax.ppermute(block, axis, SWAP)]
  transfers between devices with their start and end apart: 19 -> 23, of which waited for: 7 -> 12; matrix products, arithmetic and copies ran while one was open for 21% -> 7% of each run, Pallas kernels for 6% -> 10%
where the time goes in v9:
time: 296 us; the launch traced here: 294 us
  waiting for transfers between devices  117 us (40%)
  starting transfers between devices  62 us (21%)
  Pallas kernels  36 us (12%)
  blocking collectives  30.3 us (10%)
  other arithmetic  23.5 us (8%)
  local copies, waits for them, and re-layouts  22.4 us (8%)
    all_to_all x8, waiting for transfers between devices, exchange(): return lax.all_to_all(blocks, axes, 0, 0, tiled=True)  71.4 us
    all_to_all x8, starting transfers between devices, exchange(): return lax.all_to_all(blocks, axes, 0, 0, tiled=True)  49 us
    ppermute x15, waiting for transfers between devices, swap(): return lax.ppermute(block, axis, SWAP)  45.5 us
    all_to_all x1, blocking collectives, exchange(): return lax.all_to_all(blocks, axes, 0, 0, tiled=True)  30.3 us
    unnamed x38, local copies, waits for them, and re-layouts  16.9 us
    ppermute x15, starting transfers between devices, swap(): return lax.ppermute(block, axis, SWAP)  13 us
    convert_element_type x4, other arithmetic, scaled(): return (weight.astype(f32) * gain[low:high]).astype(bf16)  9.96 us
    pallas_call x2, Pallas kernels, attend(): pl.pallas_call(body, grid_spec=pltpu.PrefetchScalarGridSpec(num_scalar_pr...  9.85 us
  transfers between devices with their start and end apart: 23, of which 12 were waited for; matrix products, arithmetic and copies ran while one was open for 7% of the time, Pallas kernels for 10%

profile of v9, /device:TPU:1, one launch (start us, length us, event | category | flops | bytes accessed | tf_op | source)
XLA Modules:
  0.0 294.5 jit_solution(2246277846780469387)
XLA Ops:
  0.0 1.5 fusion.13
  1.5 1.3 pad_add_fusion.ids_ref
  2.8 2.4 leave.1
  5.2 9.3 %all-to-all-start = ((bf16[16,36,256]{2,1,0:T(8,128)(2,1)}), bf16[16,36,256]{2,1,0:T(8,128)(2,1)S(1)}, u32[]{:S(2)}, u32[]{:S(2)}) async-start(bf16[16,36,256]{2,1,0:T(8,128)(2,1)} %leave.1), calls=%async_computation | async-start | bytes 655360 | tf_op jit(solution)/shard_map/all_to_all | solution.py:28
  14.5 1.2 collective-permute-start.1
  17.3 6.5 %attend.1.refs_1_ = bf16[8,2,2,32,512]{4,3,2,1,0:T(8,128)(2,1)} custom-call(s32[2]{0:T(128)} %pad_add_fusion.ids_ref, s32[4]{0:T(128)} %lengths_ref.3, bf16[4,576,2]{2,1,0:T(8,128)(2,1)} %bitcast.62, bf16[2,4,576,128]{3,2,1,0:T(8,128)(2,1)} %bitcast.64, bf16[4,576,256]{2,1,0:T(8,128)(2,1)} %bitcast.67), custom_call_target="tpu_custom_call" | custom-call | tf_op jit(solution)/shard_map/attend/pallas_call | solution.py:140
  23.8 1.3 route.1
  25.1 7.2 %all-to-all-start.1 = ((bf16[16,36,256]{2,1,0:T(8,128)(2,1)}), bf16[16,36,256]{2,1,0:T(8,128)(2,1)S(1)}, u32[]{:S(2)}, u32[]{:S(2)}) async-start(bf16[16,36,256]{2,1,0:T(8,128)(2,1)} %route.1), calls=%async_computation.1 | async-start | bytes 655360 | tf_op jit(solution)/shard_map/all_to_all | solution.py:28
  32.3 3.5 %multiply_convert_fusion.refs_0_ = bf16[896,1152]{1,0:T(8,128)(2,1)} fusion(f32[896]{0:T(1024)S(1)} %convert_element_type.68, bf16[896,1152]{1,0:T(8,128)(2,1)} %param.23, bf16[896,1152]{1,0:T(8,128)(2,1)} %param.24, pred[]{:T(512)S(6)} %eq.18), kind=kLoop, calls=%fused_computation.2 | loop fusion | flops 4128768 | bytes 6196737 | tf_op jit(solution)/shard_map/convert_element_type | solution.py:339
  35.8 2.2 multiply_convert_fusion.2
  38.1 2.8 pad_maximum_fusion.1
  42.4 3.4 %again.1 = bf16[8,2,2,32,512]{4,3,2,1,0:T(8,128)(2,1)} custom-call(s32[2]{0:T(128)} %pad_add_fusion.ids_ref, s32[4]{0:T(128)} %lengths_ref.3, bf16[4,576,2]{2,1,0:T(8,128)(2,1)} %bitcast.63, bf16[2,4,576,128]{3,2,1,0:T(8,128)(2,1)} %bitcast.65, bf16[16,36,256]{2,1,0:T(8,128)(2,1)} %copy-done.13, ...), custom_call_target="tpu_custom_call", output_to_operand_aliasing={{}: (5, {})} | custom-call | tf_op jit(solution)/shard_map/again/pallas_call | solution.py:140
  45.8 10.5 %collective-permute-done.1.refs_2_ = bf16[1024,896]{1,0:T(8,128)(2,1)} collective-permute-done((bf16[1024,896]{1,0:T(8,128)(2,1)}, bf16[1024,896]{1,0:T(8,128)(2,1)}, u32[]{:S(2)}, u32[]{:S(2)}) %collective-permute-start.1) | collective-permute-done | bytes 1835040 | tf_op jit(solution)/shard_map/ppermute | solution.py:36
  57.2 7.0 %all-to-all-start.2 = ((bf16[16,2,32,512]{3,2,1,0:T(8,128)(2,1)}), bf16[16,2,32,512]{3,2,1,0:T(8,128)(2,1)S(1)}, u32[]{:S(2)}, u32[]{:S(2)}) async-start(bf16[16,2,32,512]{3,2,1,0:T(8,128)(2,1)} %bitcast.61), calls=%async_computation.2 | async-start | bytes 2097152 | tf_op jit(solution)/shard_map/all_to_all | solution.py:28
  64.2 1.2 collective-permute-start.3
  67.1 1.5 copy-done.8
  68.6 2.8 join.2.weight_ref
  71.4 3.0 %copy-done.4 = bf16[2048,1792]{1,0:T(8,128)(2,1)} copy-done((bf16[2048,1792]{1,0:T(8,128)(2,1)}, bf16[2048,1792]{1,0:T(8,128)(2,1)S(1)}, u32[]{:S(2)}) %copy-start.4) | copy-done | bytes 7340056
  74.4 6.0 %collective-permute-done.6 = bf16[32,896]{1,0:T(8,128)(2,1)S(1)} collective-permute-done((bf16[32,896]{1,0:T(8,128)(2,1)S(1)}, bf16[32,896]{1,0:T(8,128)(2,1)S(1)}, u32[]{:S(2)}, u32[]{:S(2)}) %collective-permute-start.6) | collective-permute-done | bytes 57376 | tf_op jit(solution)/shard_map/ppermute | solution.py:36
  81.6 2.9 fusion
  86.0 4.5 %all-to-all-start.3 = ((bf16[8,32,2048]{2,1,0:T(8,128)(2,1)}), bf16[8,32,2048]{2,1,0:T(8,128)(2,1)S(1)}, u32[]{:S(2)}, u32[]{:S(2)}) async-start(bf16[8,32,2048]{2,1,0:T(8,128)(2,1)} %bitcast.19), calls=%async_computation.3 | async-start | bytes 2097152 | tf_op jit(solution)/shard_map/all_to_all | solution.py:28
  90.5 3.0 %multiply_convert_fusion.1 = bf16[512,1152]{1,0:T(8,128)(2,1)} fusion(f32[512]{0:T(512)S(1)} %slice.50, bf16[896,1152]{1,0:T(8,128)(2,1)} %param.23, bf16[896,1152]{1,0:T(8,128)(2,1)} %param.24, pred[]{:T(512)S(6)} %eq.18), kind=kLoop, calls=%fused_computation.3 | loop fusion | flops 2359296 | bytes 3540993 | tf_op jit(solution)/shard_map/convert_element_type | solution.py:339
  93.5 12.1 %all-to-all-done.3.rows_ref = bf16[8,32,2048]{2,1,0:T(8,128)(2,1)S(1)} async-done(((bf16[8,32,2048]{2,1,0:T(8,128)(2,1)}), bf16[8,32,2048]{2,1,0:T(8,128)(2,1)S(1)}, u32[]{:S(2)}, u32[]{:S(2)}) %all-to-all-start.3) | async-done | bytes 1048608 | tf_op jit(solution)/shard_map/all_to_all | solution.py:28
  105.8 3.1 %copy-done.5 = bf16[2048,1792]{1,0:T(8,128)(2,1)S(1)} copy-done((bf16[2048,1792]{1,0:T(8,128)(2,1)S(1)}, bf16[2048,1792]{1,0:T(8,128)(2,1)}, u32[]{:S(2)}) %copy-start.5) | copy-done | bytes 7340056
  108.9 4.5 %project.2 = bf16[8,2,32,896]{3,2,1,0:T(8,128)(2,1)} custom-call(s32[2]{0:T(128)S(1)} %copy-done.11, bf16[8,32,2048]{2,1,0:T(8,128)(2,1)S(1)} %all-to-all-done.3.rows_ref, bf16[2048,1792]{1,0:T(8,128)(2,1)S(1)} %copy-done.5), custom_call_target="tpu_custom_call" | custom-call | tf_op jit(solution)/shard_map/project/pallas_call | solution.py:213
  113.4 5.6 %all-to-all-start.4 = ((bf16[8,2,32,896]{3,2,1,0:T(8,128)(2,1)}), bf16[8,2,32,896]{3,2,1,0:T(8,128)(2,1)S(1)}, u32[]{:S(2)}, u32[]{:S(2)}) async-start(bf16[8,2,32,896]{3,2,1,0:T(8,128)(2,1)} %project.2), calls=%async_computation.4 | async-start | bytes 1835008 | tf_op jit(solution)/shard_map/all_to_all | solution.py:28
  120.1 14.4 %all-to-all-done.4 = bf16[8,2,32,896]{3,2,1,0:T(8,128)(2,1)S(1)} async-done(((bf16[8,2,32,896]{3,2,1,0:T(8,128)(2,1)}), bf16[8,2,32,896]{3,2,1,0:T(8,128)(2,1)S(1)}, u32[]{:S(2)}, u32[]{:S(2)}) %all-to-all-start.4) | async-done | bytes 917536 | tf_op jit(solution)/shard_map/all_to_all | solution.py:28
  134.7 1.5 broadcast_in_dim.29
  136.2 4.5 %all-to-all-start.5 = ((bf16[16,2,32,896]{3,2,1,0:T(8,128)(2,1)}), bf16[16,2,32,896]{3,2,1,0:T(8,128)(2,1)}, u32[]{:S(2)}, u32[]{:S(2)}) async-start(bf16[16,2,32,896]{3,2,1,0:T(8,128)(2,1)} %broadcast_in_dim.29), calls=%async_computation.5 | async-start | bytes 3670016 | tf_op jit(solution)/shard_map/all_to_all | solution.py:28
  140.8 1.3 collective-permute-start.11
  142.1 1.5 collective-permute-start.9
  144.3 23.7 %collective-permute-done.9.refs_3_ = bf16[128,1152]{1,0:T(8,128)(2,1)S(1)} collective-permute-done((bf16[128,1152]{1,0:T(8,128)(2,1)S(1)}, bf16[128,1152]{1,0:T(8,128)(2,1)S(1)}, u32[]{:S(2)}, u32[]{:S(2)}) %collective-permute-start.9) | collective-permute-done | bytes 294944 | tf_op jit(solution)/shard_map/ppermute | solution.py:36
  168.0 2.0 collective-permute-start.12
  171.2 1.6 copy-done.7
  172.7 2.0 join.3.weight_ref
  174.7 3.3 %copy-done.2 = bf16[1792,2304]{1,0:T(8,128)(2,1)} copy-done((bf16[1792,2304]{1,0:T(8,128)(2,1)}, bf16[1792,2304]{1,0:T(8,128)(2,1)S(1)}, u32[]{:S(2)}) %copy-start.2) | copy-done | bytes 8257560
  178.0 3.3 %copy-done.3 = bf16[1792,2304]{1,0:T(8,128)(2,1)S(1)} copy-done((bf16[1792,2304]{1,0:T(8,128)(2,1)S(1)}, bf16[1792,2304]{1,0:T(8,128)(2,1)}, u32[]{:S(2)}) %copy-start.3) | copy-done | bytes 8257560
  181.4 9.1 %widen.1 = bf16[8,2,32,2432]{3,2,1,0:T(8,128)(2,1)} custom-call(s32[2]{0:T(128)S(1)} %copy-done.11, bf16[2,8,2,32,896]{4,3,2,1,0:T(8,128)(2,1)} %bitcast.22.rows_ref, bf16[1792,2304]{1,0:T(8,128)(2,1)S(1)} %copy-done.3), custom_call_target="tpu_custom_call" | custom-call | tf_op jit(solution)/shard_map/widen/pallas_call | solution.py:261
  190.5 4.4 %all-to-all-start.6 = ((bf16[8,64,2432]{2,1,0:T(8,128)(2,1)}), bf16[8,64,2432]{2,1,0:T(8,128)(2,1)}, u32[]{:S(2)}, u32[]{:S(2)}) async-start(bf16[8,64,2432]{2,1,0:T(8,128)(2,1)} %bitcast.23), calls=%async_computation.6 | async-start | bytes 4980736 | tf_op jit(solution)/shard_map/all_to_all | solution.py:28
  194.9 4.6 %pad_maximum_fusion.weight_ref = bf16[2304,896]{1,0:T(8,128)(2,1)} fusion(bf16[1152,896]{1,0:T(8,128)(2,1)} %collective-permute-done.13, bf16[1152,896]{1,0:T(8,128)(2,1)} %param.25), kind=kLoop, calls=%fused_computation.1 | loop fusion | flops 8257536 | bytes 8257536 | tf_op jit(solution)/shard_map/concatenate | solution.py:316
  199.5 31.9 %all-to-all-done.6 = bf16[8,64,2432]{2,1,0:T(8,128)(2,1)} async-done(((bf16[8,64,2432]{2,1,0:T(8,128)(2,1)}), bf16[8,64,2432]{2,1,0:T(8,128)(2,1)}, u32[]{:S(2)}, u32[]{:S(2)}) %all-to-all-start.6) | async-done | bytes 2490400 | tf_op jit(solution)/shard_map/all_to_all | solution.py:28
  231.4 2.2 convert_reduce_fusion
  234.3 30.3 %all_to_all.45.rows_ref = bf16[8,64,2304]{2,1,0:T(8,128)(2,1)S(1)} all-to-all(bf16[8,64,2304]{2,1,0:T(8,128)(2,1)S(1)} %broadcast_in_dim.31), channel_id=1, replica_groups=mesh['xh'=2,'xl'=2,'zl'=2,'zh'=2,'y'=4,'c'=2] {'xh','xl','zl'}, dimensions={0} | all-to-all | bytes 4718592 | tf_op jit(solution)/shard_map/all_to_all | solution.py:28
  264.6 4.1 %project.3 = bf16[8,1,64,896]{3,2,1,0:T(8,128)(2,1)} custom-call(s32[2]{0:T(128)S(1)} %copy-done.11, bf16[8,64,2304]{2,1,0:T(8,128)(2,1)S(1)} %all_to_all.45.rows_ref, bf16[2304,896]{1,0:T(8,128)(2,1)S(1)} %copy-done.6), custom_call_target="tpu_custom_call" | custom-call | tf_op jit(solution)/shard_map/project/pallas_call | solution.py:213
  268.7 6.5 %all-to-all-start.8 = ((bf16[8,64,896]{2,1,0:T(8,128)(2,1)}), bf16[8,64,896]{2,1,0:T(8,128)(2,1)S(1)}, u32[]{:S(2)}, u32[]{:S(2)}) async-start(bf16[8,64,896]{2,1,0:T(8,128)(2,1)} %bitcast.26), calls=%async_computation.8 | async-start | bytes 1835008 | tf_op jit(solution)/shard_map/all_to_all | solution.py:28
  275.7 3.2 %collective-permute-done.8 = f32[32,896]{1,0:T(8,128)S(1)} collective-permute-done((f32[32,896]{1,0:T(8,128)S(1)}, f32[32,896]{1,0:T(8,128)S(1)}, u32[]{:S(2)}, u32[]{:S(2)}) %collective-permute-start.8) | collective-permute-done | bytes 114720 | tf_op jit(solution)/shard_map/ppermute | solution.py:36
  279.1 11.4 %all-to-all-done.8 = bf16[8,64,896]{2,1,0:T(8,128)(2,1)S(1)} async-done(((bf16[8,64,896]{2,1,0:T(8,128)(2,1)}), bf16[8,64,896]{2,1,0:T(8,128)(2,1)S(1)}, u32[]{:S(2)}, u32[]{:S(2)}) %all-to-all-start.8) | async-done | bytes 917536 | tf_op jit(solution)/shard_map/all_to_all | solution.py:28
  291.0 1.6 collective-permute-start.14
  (89 shorter events, 15.7 us)
Async XLA Ops:
  0.0 65.4 %copy-start = (bf16[2,512,896]{2,1,0:T(8,128)(2,1)S(1)}, bf16[2,512,896]{2,1,0:T(8,128)(2,1)}, u32[]{:S(2)}) copy-start(bf16[2,512,896]{2,1,0:T(8,128)(2,1)} %param.21) | copy-start | bytes 5505028
  0.0 15.7 %copy-start.14 = (bf16[8,512,128]{2,1,0:T(8,128)(2,1)S(1)}, bf16[8,512,128]{2,1,0:T(8,128)(2,1)}, u32[]{:S(2)}) copy-start(bf16[8,512,128]{2,1,0:T(8,128)(2,1)} %param.19) | copy-start | bytes 3145732
  0.0 16.2 %copy-start.16 = (bf16[896]{0:T(1024)(128)(2,1)S(1)}, bf16[896]{0:T(1024)(128)(2,1)}, u32[]{:S(2)}) copy-start(bf16[896]{0:T(1024)(128)(2,1)} %param.22) | copy-start | bytes 5380
  0.0 16.2 %copy-start.17 = (bf16[2,4,576]{2,1,0:T(4,128)(2,1)S(1)}, bf16[2,4,576]{2,1,0:T(4,128)(2,1)}, u32[]{:S(2)}) copy-start(bf16[2,4,576]{2,1,0:T(4,128)(2,1)} %param.18) | copy-start | bytes 27652
  5.2 18.6 %all-to-all-start = ((bf16[16,36,256]{2,1,0:T(8,128)(2,1)}), bf16[16,36,256]{2,1,0:T(8,128)(2,1)S(1)}, u32[]{:S(2)}, u32[]{:S(2)}) async-start(bf16[16,36,256]{2,1,0:T(8,128)(2,1)} %leave.1), calls=%async_computation | async-start | bytes 655360 | tf_op jit(solution)/shard_map/all_to_all | solution.py:28
  14.5 41.8 %collective-permute-start.1 = (bf16[1024,896]{1,0:T(8,128)(2,1)}, bf16[1024,896]{1,0:T(8,128)(2,1)}, u32[]{:S(2)}, u32[]{:S(2)}) collective-permute-start(bf16[1024,896]{1,0:T(8,128)(2,1)} %refs_0_.1), channel_id=1, source_target_pairs={{0,32},{32,0},{1,33},{33,1},{2,34},{34,2},{3,35},{35,3},{4,36},{36... | collective-permute-start | bytes 5505032 | tf_op jit(solution)/shard_map/ppermute | solution.py:36
  15.7 22.4 %collective-permute-start = (bf16[8,512,128]{2,1,0:T(8,128)(2,1)S(1)}, bf16[8,512,128]{2,1,0:T(8,128)(2,1)}, u32[]{:S(2)}, u32[]{:S(2)}) collective-permute-start(bf16[8,512,128]{2,1,0:T(8,128)(2,1)S(1)} %copy-done.14), channel_id=1, source_target_pairs={{0,1},{1,0},{2,3},{3,2},{4,5},{5,4},{6,7},{7,6},{8,9},{9,8},{10,11... | collective-permute-start | bytes 3145736 | tf_op jit(solution)/shard_map/ppermute | solution.py:36
  17.3 6.5 %copy-start.12 = (s32[1,16]{1,0:T(1,128)S(1)}, s32[1,16]{1,0:T(1,128)}, u32[]{:S(2)}) copy-start(s32[1,16]{1,0:T(1,128)} %param.16) | copy-start | bytes 196
  25.1 16.3 %all-to-all-start.1 = ((bf16[16,36,256]{2,1,0:T(8,128)(2,1)}), bf16[16,36,256]{2,1,0:T(8,128)(2,1)S(1)}, u32[]{:S(2)}, u32[]{:S(2)}) async-start(bf16[16,36,256]{2,1,0:T(8,128)(2,1)} %route.1), calls=%async_computation.1 | async-start | bytes 655360 | tf_op jit(solution)/shard_map/all_to_all | solution.py:28
  41.4 1.0 copy-start.13
  41.4 40.2 %collective-permute-start.2 = (bf16[896,1152]{1,0:T(8,128)(2,1)}, bf16[896,1152]{1,0:T(8,128)(2,1)}, u32[]{:S(2)}, u32[]{:S(2)}) collective-permute-start(bf16[896,1152]{1,0:T(8,128)(2,1)} %multiply_convert_fusion.refs_0_), channel_id=1, source_target_pairs={{0,1},{1,0},{2,3},{3,2},{4,5},{5,4},{6,7},{7,6},{8,9},{9,8},{10,11... | collective-permute-start | bytes 6193160 | tf_op jit(solution)/shard_map/ppermute | solution.py:36
  42.4 24.7 %collective-permute-start.4 = (bf16[1024,896]{1,0:T(8,128)(2,1)}, bf16[1024,896]{1,0:T(8,128)(2,1)}, u32[]{:S(2)}, u32[]{:S(2)}) collective-permute-start(bf16[1024,896]{1,0:T(8,128)(2,1)} %refs_0_.1), channel_id=1, source_target_pairs={{0,1},{1,0},{2,3},{3,2},{4,5},{5,4},{6,7},{7,6},{8,9},{9,8},{10,11... | collective-permute-start | bytes 5505032 | tf_op jit(solution)/shard_map/ppermute | solution.py:36
  56.2 10.9 %collective-permute-start.5 = (bf16[1024,896]{1,0:T(8,128)(2,1)}, bf16[1024,896]{1,0:T(8,128)(2,1)}, u32[]{:S(2)}, u32[]{:S(2)}) collective-permute-start(bf16[1024,896]{1,0:T(8,128)(2,1)} %collective-permute-done.1.refs_2_), channel_id=1, source_target_pairs={{0,1},{1,0},{2,3},{3,2},{4,5},{5,4},{6,7},{7,6},{8,9},{9,8},{10,11... | collective-permute-start | bytes 5505032 | tf_op jit(solution)/shard_map/ppermute | solution.py:36
  57.2 24.3 %all-to-all-start.2 = ((bf16[16,2,32,512]{3,2,1,0:T(8,128)(2,1)}), bf16[16,2,32,512]{3,2,1,0:T(8,128)(2,1)S(1)}, u32[]{:S(2)}, u32[]{:S(2)}) async-start(bf16[16,2,32,512]{3,2,1,0:T(8,128)(2,1)} %bitcast.61), calls=%async_computation.2 | async-start | bytes 2097152 | tf_op jit(solution)/shard_map/all_to_all | solution.py:28
  64.2 16.2 %collective-permute-start.3 = (bf16[256,1152]{1,0:T(8,128)(2,1)}, bf16[256,1152]{1,0:T(8,128)(2,1)S(1)}, u32[]{:S(2)}, u32[]{:S(2)}) collective-permute-start(bf16[256,1152]{1,0:T(8,128)(2,1)} %multiply_convert_fusion.2), channel_id=1, source_target_pairs={{0,32},{32,0},{1,33},{33,1},{2,34},{34,2},{3,35},{35,3},{4,36},{36... | collective-permute-start | bytes 1769480 | tf_op jit(solution)/shard_map/ppermute | solution.py:36
  66.8 13.6 %collective-permute-start.6 = (bf16[32,896]{1,0:T(8,128)(2,1)S(1)}, bf16[32,896]{1,0:T(8,128)(2,1)S(1)}, u32[]{:S(2)}, u32[]{:S(2)}) collective-permute-start(bf16[32,896]{1,0:T(8,128)(2,1)S(1)} %bitcast.74), channel_id=1, source_target_pairs={{0,32},{32,0},{1,33},{33,1},{2,34},{34,2},{3,35},{35,3},{4,36},{36... | collective-permute-start | bytes 172040 | tf_op jit(solution)/shard_map/ppermute | solution.py:36
  67.1 1.5 copy-start.8
  71.4 3.0 %copy-start.4 = (bf16[2048,1792]{1,0:T(8,128)(2,1)}, bf16[2048,1792]{1,0:T(8,128)(2,1)S(1)}, u32[]{:S(2)}) copy-start(bf16[2048,1792]{1,0:T(8,128)(2,1)S(1)} %join.2.weight_ref) | copy-start | bytes 22020100
  80.4 4.4 %copy-start.9 = (bf16[256,1152]{1,0:T(8,128)(2,1)}, bf16[256,1152]{1,0:T(8,128)(2,1)S(1)}, u32[]{:S(2)}) copy-start(bf16[256,1152]{1,0:T(8,128)(2,1)S(1)} %collective-permute-done.3.refs_1_) | copy-start | bytes 1769476
  86.0 19.6 %all-to-all-start.3 = ((bf16[8,32,2048]{2,1,0:T(8,128)(2,1)}), bf16[8,32,2048]{2,1,0:T(8,128)(2,1)S(1)}, u32[]{:S(2)}, u32[]{:S(2)}) async-start(bf16[8,32,2048]{2,1,0:T(8,128)(2,1)} %bitcast.19), calls=%async_computation.3 | async-start | bytes 2097152 | tf_op jit(solution)/shard_map/all_to_all | solution.py:28
  90.4 15.3 %copy-start.11 = (s32[2]{0:T(128)S(1)}, s32[2]{0:T(128)}, u32[]{:S(2)}) copy-start(s32[2]{0:T(128)} %pad_add_fusion.ids_ref) | copy-start | bytes 28
  105.5 29.0 %collective-permute-start.7 = (bf16[512,1152]{1,0:T(8,128)(2,1)}, bf16[512,1152]{1,0:T(8,128)(2,1)S(1)}, u32[]{:S(2)}, u32[]{:S(2)}) collective-permute-start(bf16[512,1152]{1,0:T(8,128)(2,1)} %multiply_convert_fusion.1), channel_id=1, source_target_pairs={{0,32},{32,0},{1,33},{33,1},{2,34},{34,2},{3,35},{35,3},{4,36},{36... | collective-permute-start | bytes 3538952 | tf_op jit(solution)/shard_map/ppermute | solution.py:36
  105.8 3.1 %copy-start.5 = (bf16[2048,1792]{1,0:T(8,128)(2,1)S(1)}, bf16[2048,1792]{1,0:T(8,128)(2,1)}, u32[]{:S(2)}) copy-start(bf16[2048,1792]{1,0:T(8,128)(2,1)} %copy-done.4) | copy-start | bytes 22020100
  113.4 6.7 %copy-start.15 = (bf16[1,32,896]{2,0,1:T(2,128)(2,1)S(1)}, bf16[1,32,896]{2,0,1:T(2,128)(2,1)}, u32[]{:S(2)}) copy-start(bf16[1,32,896]{2,0,1:T(2,128)(2,1)} %get-tuple-element.67) | copy-start | bytes 172036
  113.4 21.2 %all-to-all-start.4 = ((bf16[8,2,32,896]{3,2,1,0:T(8,128)(2,1)}), bf16[8,2,32,896]{3,2,1,0:T(8,128)(2,1)S(1)}, u32[]{:S(2)}, u32[]{:S(2)}) async-start(bf16[8,2,32,896]{3,2,1,0:T(8,128)(2,1)} %project.2), calls=%async_computation.4 | async-start | bytes 1835008 | tf_op jit(solution)/shard_map/all_to_all | solution.py:28
  136.2 5.8 %copy-start.10 = (bf16[256,1152]{1,0:T(8,128)(2,1)S(1)}, bf16[256,1152]{1,0:T(8,128)(2,1)}, u32[]{:S(2)}) copy-start(bf16[256,1152]{1,0:T(8,128)(2,1)} %copy-done.9) | copy-start | bytes 1769476
  136.2 41.8 %all-to-all-start.5 = ((bf16[16,2,32,896]{3,2,1,0:T(8,128)(2,1)}), bf16[16,2,32,896]{3,2,1,0:T(8,128)(2,1)}, u32[]{:S(2)}, u32[]{:S(2)}) async-start(bf16[16,2,32,896]{3,2,1,0:T(8,128)(2,1)} %broadcast_in_dim.29), calls=%async_computation.5 | async-start | bytes 3670016 | tf_op jit(solution)/shard_map/all_to_all | solution.py:28
  140.8 30.4 %collective-permute-start.11 = (bf16[512,1152]{1,0:T(8,128)(2,1)S(1)}, bf16[512,1152]{1,0:T(8,128)(2,1)S(1)}, u32[]{:S(2)}, u32[]{:S(2)}) collective-permute-start(bf16[512,1152]{1,0:T(8,128)(2,1)S(1)} %collective-permute-done.7.refs_2_), channel_id=1, source_target_pairs={{0,1},{1,0},{2,3},{3,2},{4,5},{5,4},{6,7},{7,6},{8,9},{9,8},{10,11... | collective-permute-start | bytes 3538952 | tf_op jit(solution)/shard_map/ppermute | solution.py:36
  142.0 27.9 %collective-permute-start.10 = (bf16[256,1152]{1,0:T(8,128)(2,1)S(1)}, bf16[256,1152]{1,0:T(8,128)(2,1)S(1)}, u32[]{:S(2)}, u32[]{:S(2)}) collective-permute-start(bf16[256,1152]{1,0:T(8,128)(2,1)S(1)} %copy-done.10), channel_id=1, source_target_pairs={{0,1},{1,0},{2,3},{3,2},{4,5},{5,4},{6,7},{7,6},{8,9},{9,8},{10,11... | collective-permute-start | bytes 1769480 | tf_op jit(solution)/shard_map/ppermute | solution.py:36
  142.1 25.9 %collective-permute-start.9 = (bf16[128,1152]{1,0:T(8,128)(2,1)S(1)}, bf16[128,1152]{1,0:T(8,128)(2,1)S(1)}, u32[]{:S(2)}, u32[]{:S(2)}) collective-permute-start(bf16[128,1152]{1,0:T(8,128)(2,1)S(1)} %multiply_convert_fusion.3), channel_id=1, source_target_pairs={{0,32},{32,0},{1,33},{33,1},{2,34},{34,2},{3,35},{35,3},{4,36},{36... | collective-permute-start | bytes 884744 | tf_op jit(solution)/shard_map/ppermute | solution.py:36
  143.6 51.3 %collective-permute-start.13 = (bf16[1152,896]{1,0:T(8,128)(2,1)}, bf16[1152,896]{1,0:T(8,128)(2,1)}, u32[]{:S(2)}, u32[]{:S(2)}) collective-permute-start(bf16[1152,896]{1,0:T(8,128)(2,1)} %param.25), channel_id=1, source_target_pairs={{0,1},{1,0},{2,3},{3,2},{4,5},{5,4},{6,7},{7,6},{8,9},{9,8},{10,11... | collective-permute-start | bytes 6193160 | tf_op jit(solution)/shard_map/ppermute | solution.py:36
  168.0 3.2 %collective-permute-start.12 = (bf16[128,1152]{1,0:T(8,128)(2,1)S(1)}, bf16[128,1152]{1,0:T(8,128)(2,1)S(1)}, u32[]{:S(2)}, u32[]{:S(2)}) collective-permute-start(bf16[128,1152]{1,0:T(8,128)(2,1)S(1)} %collective-permute-done.9.refs_3_), channel_id=1, source_target_pairs={{0,1},{1,0},{2,3},{3,2},{4,5},{5,4},{6,7},{7,6},{8,9},{9,8},{10,11... | collective-permute-start | bytes 884744 | tf_op jit(solution)/shard_map/ppermute | solution.py:36
  171.2 1.6 copy-start.7
  174.7 3.3 %copy-start.2 = (bf16[1792,2304]{1,0:T(8,128)(2,1)}, bf16[1792,2304]{1,0:T(8,128)(2,1)S(1)}, u32[]{:S(2)}) copy-start(bf16[1792,2304]{1,0:T(8,128)(2,1)S(1)} %join.3.weight_ref) | copy-start | bytes 24772612
  178.0 3.3 %copy-start.3 = (bf16[1792,2304]{1,0:T(8,128)(2,1)S(1)}, bf16[1792,2304]{1,0:T(8,128)(2,1)}, u32[]{:S(2)}) copy-start(bf16[1792,2304]{1,0:T(8,128)(2,1)} %copy-done.2) | copy-start | bytes 24772612
  190.5 40.9 %all-to-all-start.6 = ((bf16[8,64,2432]{2,1,0:T(8,128)(2,1)}), bf16[8,64,2432]{2,1,0:T(8,128)(2,1)}, u32[]{:S(2)}, u32[]{:S(2)}) async-start(bf16[8,64,2432]{2,1,0:T(8,128)(2,1)} %bitcast.23), calls=%async_computation.6 | async-start | bytes 4980736 | tf_op jit(solution)/shard_map/all_to_all | solution.py:28
  234.3 30.3 %copy-start.6 = (bf16[2304,896]{1,0:T(8,128)(2,1)S(1)}, bf16[2304,896]{1,0:T(8,128)(2,1)}, u32[]{:S(2)}) copy-start(bf16[2304,896]{1,0:T(8,128)(2,1)} %pad_maximum_fusion.weight_ref) | copy-start | bytes 12386308
  268.7 21.8 %all-to-all-start.8 = ((bf16[8,64,896]{2,1,0:T(8,128)(2,1)}), bf16[8,64,896]{2,1,0:T(8,128)(2,1)S(1)}, u32[]{:S(2)}, u32[]{:S(2)}) async-start(bf16[8,64,896]{2,1,0:T(8,128)(2,1)} %bitcast.26), calls=%async_computation.8 | async-start | bytes 1835008 | tf_op jit(solution)/shard_map/all_to_all | solution.py:28
  275.2 3.7 %collective-permute-start.8 = (f32[32,896]{1,0:T(8,128)S(1)}, f32[32,896]{1,0:T(8,128)S(1)}, u32[]{:S(2)}, u32[]{:S(2)}) collective-permute-start(f32[32,896]{1,0:T(8,128)S(1)} %dynamic-slice_bitcast_fusion), channel_id=1, source_target_pairs={{0,32},{32,0},{1,33},{33,1},{2,34},{34,2},{3,35},{35,3},{4,36},{36... | collective-permute-start | bytes 344072 | tf_op jit(solution)/shard_map/ppermute | solution.py:36
  275.7 18.7 %copy-start.1 = (bf16[2,512,896]{2,1,0:T(8,128)(2,1)S(1)}, bf16[2,512,896]{2,1,0:T(8,128)(2,1)}, u32[]{:S(2)}) copy-start(bf16[2,512,896]{2,1,0:T(8,128)(2,1)} %param.21) | copy-start | bytes 5505028
  291.0 2.4 collective-permute-start.14

commit v10 on v8

--- a/solution.py
+++ b/solution.py
@@ -18,6 +18,7 @@
 N_ZY = 8
 SWAP = [(0, 1), (1, 0)]
 CUTS = (0, 384, 896)
+OUT_CUTS = (0, 480, 864, 1024)
 TILE = 768
 bf16 = jnp.bfloat16
 f32 = jnp.float32
@@ -213,7 +214,7 @@
     groups, count, depth = rows.shape
     width = blocks[0][0].shape[1]
     flat = [w for column in blocks for w in column]
-    half = len(flat) // 2
+    ends = [0, len(blocks[0]), len(flat)]
 
     def body(ids_ref, rows_ref, *refs):
         out_ref, weight_ref, sems = refs[len(flat) :]
@@ -222,7 +223,7 @@
             copy.start()
         lhs = rows_ref[...].reshape(groups * count, depth)
         for k in range(2):
-            for copy in copies[k * half : (k + 1) * half]:
+            for copy in copies[ends[k] : ends[k + 1]]:
                 copy.wait()
             total = jnp.dot(
                 lhs, weight_ref[:, k * width : (k + 1) * width], preferred_element_type=f32
@@ -301,7 +302,7 @@
             ],
         ),
         out_shape=jax.ShapeDtypeStruct((chunks, halves, count, columns + 128), bf16),
-        compiler_params=params(60),
+        compiler_params=params(32),
         name="widen",
     )(ids, rows, *flat)
 
@@ -341,20 +342,24 @@
     def at_other(blocks):
         return lax.dynamic_index_in_dim(blocks, 1 - pair, 0, False)
 
-    out_came = swap(out_proj, "xl")
+    out_came = [swap(out_proj[: OUT_CUTS[1]], "xl")]
     value_ups = jnp.concatenate([value_up, swap(value_up, "c")], axis=0)
-    downs = jnp.concatenate([down_weight, swap(down_weight, "c")], axis=0)
-    residue = lax.dynamic_slice_in_dim(residual, lax.div(member, 2) * 2 * rows_out, 2 * rows_out, 1)
-    residue = residue.reshape(steps, 2, 2, rows_out // 8, 2, 2, features)
-    residue = lax.dynamic_index_in_dim(residue, core, 4, False)
-    residue = residue.transpose(2, 1, 3, 4, 0, 5).reshape(2, count, features)
-    residue_came = swap(at_other(residue), "xl")
     lanes = jnp.arange(N_TP, dtype=jnp.int32)
-    own_slot = jnp.sum(jnp.where(lanes == member, move_slot[0], 0))
+    cache_t = cache.transpose(0, 2, 1)
+    leaving, slots, out_late = lax.optimization_barrier(
+        (leave(move_slot[0], cache_t), move_slot[0], out_proj)
+    )
+    for low, high in zip(OUT_CUTS[1:-1], OUT_CUTS[2:]):
+        out_came.append(swap(out_late[low:high], "xl"))
+    pieces = exchange(leaving, TP)
+    own_slot = jnp.sum(jnp.where(lanes == member, slots, 0))
     ids = jnp.stack([own_slot, pair]).astype(jnp.int32)
-    cache_t = cache.transpose(0, 2, 1)
-    pieces = exchange(leave(move_slot[0], cache_t), TP)
-    pieces, gate_weight, up_weight = lax.optimization_barrier((pieces, gate_weight, up_weight))
+    fresh_t = new_latent.transpose(1, 2, 0)
+    queries_t = queries.transpose(0, 1, 3, 2)
+    out = attend(ids, cache_length, cache_t, fresh_t, queries_t, heads, latent_width)
+    pieces, out, out_came[0], gate_weight, up_weight = lax.optimization_barrier(
+        (pieces, out, out_came[0], gate_weight, up_weight)
+    )
 
     gain = norm_gain.astype(f32)[:, None]
 
@@ -367,24 +372,26 @@
     ]
     kept = scaled(0, CUTS[-1], gate_weight, up_weight)
     arrived = exchange(route(move_peer[0], pieces), TP)
-    arrived, kept, sent[0], value_ups = lax.optimization_barrier(
-        (arrived, kept, sent[0], value_ups)
-    )
-    fresh_t = new_latent.transpose(1, 2, 0)
-    queries_t = queries.transpose(0, 1, 3, 2)
-    out = attend(ids, cache_length, cache_t, fresh_t, queries_t, heads, latent_width)
+    arrived, kept, sent[0], value_ups, out_came[1] = lax.optimization_barrier(
+        (arrived, kept, sent[0], value_ups, out_came[1])
+    )
     out = attend(
         ids, cache_length, cache_t, fresh_t, queries_t, heads, latent_width, arrived, out
     )
-    out, out_came = lax.optimization_barrier((out, out_came))
+    out, out_came[2] = lax.optimization_barrier((out, out_came[2]))
     came = [swap(sent[0], "xl")]
-    out_weights = [[w, swap(w, "c")] for w in (out_proj, out_came)]
-    kept = [kept, swap(kept, "c")]
     out = out.reshape((N_TP,) + out.shape[2:])
     by_head = exchange(out, TP).reshape(-1, 2 * heads, latent_width)
-    by_head, kept, came, out_weights, residue_came = lax.optimization_barrier(
-        (by_head, kept, came, out_weights, residue_came)
-    )
+    by_head, kept, came[0], out_came, out_late, residual = lax.optimization_barrier(
+        (by_head, kept, came[0], out_came, out_late, residual)
+    )
+    out_weights = [ws + [swap(w, "c") for w in ws] for ws in ([out_late], out_came)]
+    out_weights[0][1], residual = lax.optimization_barrier((out_weights[0][1], residual))
+    residue = lax.dynamic_slice_in_dim(residual, lax.div(member, 2) * 2 * rows_out, 2 * rows_out, 1)
+    residue = residue.reshape(steps, 2, 2, rows_out // 8, 2, 2, features)
+    residue = lax.dynamic_index_in_dim(residue, core, 4, False)
+    residue = residue.transpose(2, 1, 3, 4, 0, 5).reshape(2, count, features)
+    residue = by_pair(at_pair(residue), swap(at_other(residue), "xl"))
     value_heads = jnp.einsum(
         "thl,hlv->thv", by_head, value_ups, preferred_element_type=f32
     ).astype(bf16)
@@ -395,18 +402,20 @@
         value_heads[None, :, None], (2, 2, 2) + value_heads.shape[1:]
     ).reshape((N_DP,) + value_heads.shape[1:])
     gathered = exchange(value_heads, DP)
-    gathered, sent[1] = lax.optimization_barrier((gathered, sent[1]))
+    gathered, sent[1], kept, down_weight, residue, out_weights = lax.optimization_barrier(
+        (gathered, sent[1], kept, down_weight, residue, out_weights)
+    )
+    kept = [kept, swap(kept, "c")]
     came.append(swap(sent[1], "xl"))
     parts = exchange(combine(ids, gathered, out_weights), ZY)
     parts, came[1] = lax.optimization_barrier((parts, came[1]))
     in_weights = [[kept[0]] + came, [kept[1]] + [swap(w, "c") for w in came]]
-    residue = by_pair(at_pair(residue), residue_came)
     hidden = residue.astype(f32) + jnp.sum(parts.astype(f32), axis=0)
 
     rows = spread(hidden.astype(bf16), PAIR, 2 * N_ZY).reshape((2, N_ZY) + hidden.shape)
-    rows, in_weights = lax.optimization_barrier((rows, in_weights))
+    rows, in_weights, down_weight = lax.optimization_barrier((rows, in_weights, down_weight))
+    downs = jnp.concatenate([down_weight, swap(down_weight, "c")], axis=0)
     sums = exchange(widen(ids, rows, in_weights).reshape(N_DP, chunk, -1), DP)
-    sums, downs = lax.optimization_barrier((sums, downs))
     sums = jnp.sum(sums.reshape(2, 2, 2, chunk, -1).astype(f32), axis=(0, 2))
     squares = sums[0, :, 2 * units] + sums[0, :, 2 * units + 1]
     inverse = lax.rsqrt(squares / D + norm_eps)[:, None]

time: 282 us -> 295 us (1.046)
  blocking collectives: 30.1 us -> 0 us
  waiting for transfers between devices: 129 us -> 144 us
  starting transfers between devices: 52.9 us -> 66.5 us
  local copies, waits for them, and re-layouts: 8.81 us -> 21.7 us
    all_to_all x1 -> x0, blocking collectives: 30.1 us -> none  [exchange(): return lax.all_to_all(blocks, axes, 0, 0, tiled=True)]
    all_to_all x8 -> x9, waiting for transfers between devices: 95.8 us -> 107 us  [exchange(): return lax.all_to_all(blocks, axes, 0, 0, tiled=True)]
    all_to_all x8 -> x9, starting transfers between devices: 43.7 us -> 51.8 us  [exchange(): return lax.all_to_all(blocks, axes, 0, 0, tiled=True)]
    slice x0 -> x3, local copies, waits for them, and re-layouts: none -> 5.97 us  [the longest x2 3.72 us: local(): out_came.append(swap(out_late[low:high], 'xl'))]
    ppermute x13 -> x17, starting transfers between devices: 9.18 us -> 14.7 us  [swap(): return lax.ppermute(block, axis, SWAP)]
    unnamed x30 -> x38, local copies, waits for them, and re-layouts: 4.03 us -> 9.45 us
    ppermute x13 -> x17, waiting for transfers between devices: 33.1 us -> 37.2 us  [swap(): return lax.ppermute(block, axis, SWAP)]
  transfers between devices with their start and end apart: 21 -> 26, of which waited for: 12 -> 11; matrix products, arithmetic and copies ran while one was open for 7% -> 12% of each run, Pallas kernels for 10% -> 7%
where the time goes in v10:
time: 295 us; the launch traced here: 293 us
  waiting for transfers between devices  144 us (49%)
  starting transfers between devices  66.5 us (23%)
  Pallas kernels  34.5 us (12%)
  other arithmetic  22.7 us (8%)
  local copies, waits for them, and re-layouts  21.7 us (7%)
    all_to_all x9, waiting for transfers between devices, exchange(): return lax.all_to_all(blocks, axes, 0, 0, tiled=True)  107 us
    all_to_all x9, starting transfers between devices, exchange(): return lax.all_to_all(blocks, axes, 0, 0, tiled=True)  51.8 us
    ppermute x17, waiting for transfers between devices, swap(): return lax.ppermute(block, axis, SWAP)  37.2 us
    ppermute x17, starting transfers between devices, swap(): return lax.ppermute(block, axis, SWAP)  14.7 us
    pallas_call x2, Pallas kernels, attend(): pl.pallas_call(body, grid_spec=pltpu.PrefetchScalarGridSpec(num_scalar_pr...  9.62 us
    pallas_call x1, Pallas kernels, widen(): pl.pallas_call(body, grid_spec=pltpu.PrefetchScalarGridSpec(num_scalar_pr...  9.47 us
    unnamed x38, local copies, waits for them, and re-layouts  9.45 us
    convert_element_type x3, other arithmetic, scaled(): return (weight.astype(f32) * gain[low:high]).astype(bf16)  9.14 us
  transfers between devices with their start and end apart: 26, of which 11 were waited for; matrix products, arithmetic and copies ran while one was open for 12% of the time, Pallas kernels for 7%

profile of v10, /device:TPU:1, one launch (start us, length us, event | category | flops | bytes accessed | tf_op | source)
XLA Modules:
  0.0 293.1 jit_solution(14472487041542520143)
XLA Ops:
  0.0 2.3 slice.44
  2.3 2.0 collective-permute-start
  4.3 2.6 leave.1
  6.9 8.8 %all-to-all-start = ((bf16[16,36,256]{2,1,0:T(8,128)(2,1)}), bf16[16,36,256]{2,1,0:T(8,128)(2,1)S(1)}, u32[]{:S(2)}, u32[]{:S(2)}) async-start(bf16[16,36,256]{2,1,0:T(8,128)(2,1)} %leave.1), calls=%async_computation | async-start | bytes 655360 | tf_op jit(solution)/shard_map/all_to_all | solution.py:29
  15.6 1.7 slice.49
  17.6 2.0 slice.48
  19.6 1.2 collective-permute-start.2
  21.5 1.2 copy.52
  23.3 1.3 pad_add_fusion.ids_ref
  24.6 6.3 %attend.1.refs_1_ = bf16[8,2,2,32,512]{4,3,2,1,0:T(8,128)(2,1)} custom-call(s32[2]{0:T(128)} %pad_add_fusion.ids_ref, s32[4]{0:T(128)} %lengths_ref.3, bf16[4,576,2]{2,1,0:T(8,128)(2,1)} %bitcast.62, bf16[2,4,576,128]{3,2,1,0:T(8,128)(2,1)} %bitcast.64, bf16[4,576,256]{2,1,0:T(8,128)(2,1)} %bitcast.67), custom_call_target="tpu_custom_call" | custom-call | tf_op jit(solution)/shard_map/attend/pallas_call | solution.py:141
  30.9 1.3 route.1
  32.2 7.2 %all-to-all-start.1 = ((bf16[16,36,256]{2,1,0:T(8,128)(2,1)}), bf16[16,36,256]{2,1,0:T(8,128)(2,1)S(1)}, u32[]{:S(2)}, u32[]{:S(2)}) async-start(bf16[16,36,256]{2,1,0:T(8,128)(2,1)} %route.1), calls=%async_computation.1 | async-start | bytes 655360 | tf_op jit(solution)/shard_map/all_to_all | solution.py:29
  39.5 3.5 %multiply_convert_fusion.refs_0_ = bf16[896,1152]{1,0:T(8,128)(2,1)} fusion(f32[896]{0:T(1024)S(1)} %convert_element_type.54, bf16[896,1152]{1,0:T(8,128)(2,1)} %param.23, bf16[896,1152]{1,0:T(8,128)(2,1)} %param.24, pred[]{:T(512)S(6)} %eq.17), kind=kLoop, calls=%fused_computation.2 | loop fusion | flops 4128768 | bytes 6196737 | tf_op jit(solution)/shard_map/convert_element_type | solution.py:368
  43.0 2.6 multiply_convert_fusion.2
  45.6 2.8 pad_maximum_fusion.1
  49.3 3.3 %again.1 = bf16[8,2,2,32,512]{4,3,2,1,0:T(8,128)(2,1)} custom-call(s32[2]{0:T(128)} %pad_add_fusion.ids_ref, s32[4]{0:T(128)} %lengths_ref.3, bf16[4,576,2]{2,1,0:T(8,128)(2,1)} %bitcast.63, bf16[2,4,576,128]{3,2,1,0:T(8,128)(2,1)} %bitcast.65, bf16[16,36,256]{2,1,0:T(8,128)(2,1)} %copy-done.10, ...), custom_call_target="tpu_custom_call", output_to_operand_aliasing={{}: (5, {})} | custom-call | tf_op jit(solution)/shard_map/again/pallas_call | solution.py:141
  52.7 7.0 %all-to-all-start.2 = ((bf16[16,2,32,512]{3,2,1,0:T(8,128)(2,1)}), bf16[16,2,32,512]{3,2,1,0:T(8,128)(2,1)S(1)}, u32[]{:S(2)}, u32[]{:S(2)}) async-start(bf16[16,2,32,512]{3,2,1,0:T(8,128)(2,1)} %bitcast.61), calls=%async_computation.2 | async-start | bytes 2097152 | tf_op jit(solution)/shard_map/all_to_all | solution.py:29
  60.0 21.2 %collective-permute-done.4.refs_1_ = bf16[384,1152]{1,0:T(8,128)(2,1)} collective-permute-done((bf16[384,1152]{1,0:T(8,128)(2,1)}, bf16[384,1152]{1,0:T(8,128)(2,1)}, u32[]{:S(2)}, u32[]{:S(2)}) %collective-permute-start.4) | collective-permute-done | bytes 884768 | tf_op jit(solution)/shard_map/ppermute | solution.py:37
  82.1 2.9 fusion
  85.5 1.2 broadcast_in_dim.28
  86.6 4.2 %all-to-all-start.3 = ((bf16[8,32,2048]{2,1,0:T(8,128)(2,1)}), bf16[8,32,2048]{2,1,0:T(8,128)(2,1)}, u32[]{:S(2)}, u32[]{:S(2)}) async-start(bf16[8,32,2048]{2,1,0:T(8,128)(2,1)} %bitcast.12), calls=%async_computation.3 | async-start | bytes 2097152 | tf_op jit(solution)/shard_map/all_to_all | solution.py:29
  92.3 1.8 collective-permute-start.6
  94.2 3.0 %multiply_convert_fusion.1 = bf16[512,1152]{1,0:T(8,128)(2,1)} fusion(f32[512]{0:T(512)S(1)} %slice.52, bf16[896,1152]{1,0:T(8,128)(2,1)} %param.23, bf16[896,1152]{1,0:T(8,128)(2,1)} %param.24, pred[]{:T(512)S(6)} %eq.17), kind=kLoop, calls=%fused_computation.3 | loop fusion | flops 2359296 | bytes 3540993 | tf_op jit(solution)/shard_map/convert_element_type | solution.py:368
  97.5 7.6 %collective-permute-done.6 = bf16[32,896]{1,0:T(8,128)(2,1)S(1)} collective-permute-done((bf16[32,896]{1,0:T(8,128)(2,1)S(1)}, bf16[32,896]{1,0:T(8,128)(2,1)S(1)}, u32[]{:S(2)}, u32[]{:S(2)}) %collective-permute-start.6) | collective-permute-done | bytes 57376 | tf_op jit(solution)/shard_map/ppermute | solution.py:37
  107.3 7.5 %combine.1 = bf16[8,2,32,896]{3,2,1,0:T(8,128)(2,1)} custom-call(s32[2]{0:T(128)} %pad_add_fusion.ids_ref, bf16[8,32,2048]{2,1,0:T(8,128)(2,1)} %all-to-all-done.3.rows_ref, bf16[1024,896]{1,0:T(8,128)(2,1)} %refs_0_, bf16[1024,896]{1,0:T(8,128)(2,1)} %collective-permute-done.5.refs_1_, bf16[480,896]{1,0:T(8,128)(2,1)} %collective-permute-done.refs_2_, ...), custom_call_target="tpu_custom_call" | custom-call | tf_op jit(solution)/shard_map/combine/pallas_call | solution.py:234
  114.8 7.2 %all-to-all-start.4 = ((bf16[8,2,32,896]{3,2,1,0:T(8,128)(2,1)}), bf16[8,2,32,896]{3,2,1,0:T(8,128)(2,1)}, u32[]{:S(2)}, u32[]{:S(2)}) async-start(bf16[8,2,32,896]{3,2,1,0:T(8,128)(2,1)} %combine.1), calls=%async_computation.4 | async-start | bytes 1835008 | tf_op jit(solution)/shard_map/all_to_all | solution.py:29
  122.0 2.0 collective-permute-start.12
  124.0 14.0 %all-to-all-done.4 = bf16[8,2,32,896]{3,2,1,0:T(8,128)(2,1)} async-done(((bf16[8,2,32,896]{3,2,1,0:T(8,128)(2,1)}), bf16[8,2,32,896]{3,2,1,0:T(8,128)(2,1)}, u32[]{:S(2)}, u32[]{:S(2)}) %all-to-all-start.4) | async-done | bytes 917536 | tf_op jit(solution)/shard_map/all_to_all | solution.py:29
  138.0 1.3 convert_reduce_fusion.2
  140.2 1.5 broadcast_in_dim.29
  141.7 4.5 %all-to-all-start.5 = ((bf16[16,2,32,896]{3,2,1,0:T(8,128)(2,1)}), bf16[16,2,32,896]{3,2,1,0:T(8,128)(2,1)}, u32[]{:S(2)}, u32[]{:S(2)}) async-start(bf16[16,2,32,896]{3,2,1,0:T(8,128)(2,1)} %broadcast_in_dim.29), calls=%async_computation.5 | async-start | bytes 3670016 | tf_op jit(solution)/shard_map/all_to_all | solution.py:29
  147.3 3.9 %collective-permute-done.13.refs_4_ = bf16[384,1152]{1,0:T(8,128)(2,1)S(1)} collective-permute-done((bf16[384,1152]{1,0:T(8,128)(2,1)}, bf16[384,1152]{1,0:T(8,128)(2,1)S(1)}, u32[]{:S(2)}, u32[]{:S(2)}) %collective-permute-start.13) | collective-permute-done | bytes 884768 | tf_op jit(solution)/shard_map/ppermute | solution.py:37
  153.1 19.6 %all-to-all-done.5 = bf16[16,2,32,896]{3,2,1,0:T(8,128)(2,1)} async-done(((bf16[16,2,32,896]{3,2,1,0:T(8,128)(2,1)}), bf16[16,2,32,896]{3,2,1,0:T(8,128)(2,1)}, u32[]{:S(2)}, u32[]{:S(2)}) %all-to-all-start.5) | async-done | bytes 1835040 | tf_op jit(solution)/shard_map/all_to_all | solution.py:29
  172.7 1.3 copy-done.5
  173.9 1.2 copy-done.7
  175.1 9.5 %widen.1 = bf16[8,2,32,2432]{3,2,1,0:T(8,128)(2,1)} custom-call(s32[2]{0:T(128)S(1)} %copy-done.8, bf16[2,8,2,32,896]{4,3,2,1,0:T(8,128)(2,1)} %bitcast.22.rows_ref, bf16[896,1152]{1,0:T(8,128)(2,1)S(1)} %copy-done.3, bf16[384,1152]{1,0:T(8,128)(2,1)} %collective-permute-done.4.refs_1_, bf16[512,1152]{1,0:T(8,128)(2,1)S(1)} %collective-permute-done.10.refs_2_, ...), custom_call_target="tpu_custom_call" | custom-call | tf_op jit(solution)/shard_map/widen/pallas_call | solution.py:291
  184.6 4.8 %all-to-all-start.6 = ((bf16[8,64,2432]{2,1,0:T(8,128)(2,1)}), bf16[8,64,2432]{2,1,0:T(8,128)(2,1)S(1)}, u32[]{:S(2)}, u32[]{:S(2)}) async-start(bf16[8,64,2432]{2,1,0:T(8,128)(2,1)} %bitcast.23), calls=%async_computation.6 | async-start | bytes 4980736 | tf_op jit(solution)/shard_map/all_to_all | solution.py:29
  189.4 1.9 collective-permute-start.15
  191.2 33.1 %all-to-all-done.6 = bf16[8,64,2432]{2,1,0:T(8,128)(2,1)S(1)} async-done(((bf16[8,64,2432]{2,1,0:T(8,128)(2,1)}), bf16[8,64,2432]{2,1,0:T(8,128)(2,1)S(1)}, u32[]{:S(2)}, u32[]{:S(2)}) %all-to-all-start.6) | async-done | bytes 2490400 | tf_op jit(solution)/shard_map/all_to_all | solution.py:29
  225.2 1.6 broadcast_in_dim.31
  226.8 3.6 %all-to-all-start.7 = ((bf16[8,64,2304]{2,1,0:T(8,128)(2,1)}), bf16[8,64,2304]{2,1,0:T(8,128)(2,1)S(1)}, u32[]{:S(2)}, u32[]{:S(2)}) async-start(bf16[8,64,2304]{2,1,0:T(8,128)(2,1)} %broadcast_in_dim.31), calls=%async_computation.7 | async-start | bytes 4718592 | tf_op jit(solution)/shard_map/all_to_all | solution.py:29
  230.5 4.5 %pad_maximum_fusion.weight_ref = bf16[2304,896]{1,0:T(8,128)(2,1)} fusion(bf16[1152,896]{1,0:T(8,128)(2,1)} %collective-permute-done.15, bf16[1152,896]{1,0:T(8,128)(2,1)} %param.25), kind=kLoop, calls=%fused_computation.1 | loop fusion | flops 8257536 | bytes 8257536 | tf_op jit(solution)/shard_map/concatenate | solution.py:417
  235.0 28.2 %all-to-all-done.7.rows_ref = bf16[8,64,2304]{2,1,0:T(8,128)(2,1)S(1)} async-done(((bf16[8,64,2304]{2,1,0:T(8,128)(2,1)}), bf16[8,64,2304]{2,1,0:T(8,128)(2,1)S(1)}, u32[]{:S(2)}, u32[]{:S(2)}) %all-to-all-start.7) | async-done | bytes 2359328 | tf_op jit(solution)/shard_map/all_to_all | solution.py:29
  263.2 2.2 copy-done.2
  265.4 4.1 %project.1 = bf16[8,1,64,896]{3,2,1,0:T(8,128)(2,1)} custom-call(s32[2]{0:T(128)S(1)} %copy-done.8, bf16[8,64,2304]{2,1,0:T(8,128)(2,1)S(1)} %all-to-all-done.7.rows_ref, bf16[2304,896]{1,0:T(8,128)(2,1)S(1)} %copy-done.2), custom_call_target="tpu_custom_call" | custom-call | tf_op jit(solution)/shard_map/project/pallas_call | solution.py:182
  269.5 4.4 %all-to-all-start.8 = ((bf16[8,64,896]{2,1,0:T(8,128)(2,1)}), bf16[8,64,896]{2,1,0:T(8,128)(2,1)S(1)}, u32[]{:S(2)}, u32[]{:S(2)}) async-start(bf16[8,64,896]{2,1,0:T(8,128)(2,1)} %bitcast.26), calls=%async_computation.8 | async-start | bytes 1835008 | tf_op jit(solution)/shard_map/all_to_all | solution.py:29
  274.0 3.6 %collective-permute-done.11 = f32[32,896]{1,0:T(8,128)S(1)} collective-permute-done((f32[32,896]{1,0:T(8,128)S(1)}, f32[32,896]{1,0:T(8,128)S(1)}, u32[]{:S(2)}, u32[]{:S(2)}) %collective-permute-start.11) | collective-permute-done | bytes 114720 | tf_op jit(solution)/shard_map/ppermute | solution.py:37
  277.7 12.0 %all-to-all-done.8 = bf16[8,64,896]{2,1,0:T(8,128)(2,1)S(1)} async-done(((bf16[8,64,896]{2,1,0:T(8,128)(2,1)}), bf16[8,64,896]{2,1,0:T(8,128)(2,1)S(1)}, u32[]{:S(2)}, u32[]{:S(2)}) %all-to-all-start.8) | async-done | bytes 917536 | tf_op jit(solution)/shard_map/all_to_all | solution.py:29
  (94 shorter events, 16.4 us)
Async XLA Ops:
  0.0 91.6 %copy-start = (bf16[2,512,896]{2,1,0:T(8,128)(2,1)S(1)}, bf16[2,512,896]{2,1,0:T(8,128)(2,1)}, u32[]{:S(2)}) copy-start(bf16[2,512,896]{2,1,0:T(8,128)(2,1)} %param.21) | copy-start | bytes 5505028
  2.3 18.6 %copy-start.11 = (bf16[8,512,128]{2,1,0:T(8,128)(2,1)S(1)}, bf16[8,512,128]{2,1,0:T(8,128)(2,1)}, u32[]{:S(2)}) copy-start(bf16[8,512,128]{2,1,0:T(8,128)(2,1)} %param.19) | copy-start | bytes 3145732
  2.3 19.2 %copy-start.15 = (bf16[896]{0:T(1024)(128)(2,1)S(1)}, bf16[896]{0:T(1024)(128)(2,1)}, u32[]{:S(2)}) copy-start(bf16[896]{0:T(1024)(128)(2,1)} %param.22) | copy-start | bytes 5380
  2.3 28.6 %collective-permute-start = (bf16[480,896]{1,0:T(8,128)(2,1)}, bf16[480,896]{1,0:T(8,128)(2,1)}, u32[]{:S(2)}, u32[]{:S(2)}) collective-permute-start(bf16[480,896]{1,0:T(8,128)(2,1)} %slice.44), channel_id=1, source_target_pairs={{0,32},{32,0},{1,33},{33,1},{2,34},{34,2},{3,35},{35,3},{4,36},{36... | collective-permute-start | bytes 2580488 | tf_op jit(solution)/shard_map/ppermute | solution.py:37
  4.3 17.2 %copy-start.16 = (bf16[2,4,576]{2,1,0:T(4,128)(2,1)S(1)}, bf16[2,4,576]{2,1,0:T(4,128)(2,1)}, u32[]{:S(2)}) copy-start(bf16[2,4,576]{2,1,0:T(4,128)(2,1)} %param.18) | copy-start | bytes 27652
  4.3 18.4 %copy-start.17 = (s32[1,16]{1,0:T(1,128)S(1)}, s32[1,16]{1,0:T(1,128)}, u32[]{:S(2)}) copy-start(s32[1,16]{1,0:T(1,128)} %param.15) | copy-start | bytes 196
  6.9 24.0 %all-to-all-start = ((bf16[16,36,256]{2,1,0:T(8,128)(2,1)}), bf16[16,36,256]{2,1,0:T(8,128)(2,1)S(1)}, u32[]{:S(2)}, u32[]{:S(2)}) async-start(bf16[16,36,256]{2,1,0:T(8,128)(2,1)} %leave.1), calls=%async_computation | async-start | bytes 655360 | tf_op jit(solution)/shard_map/all_to_all | solution.py:29
  17.3 35.3 %collective-permute-start.3 = (bf16[160,896]{1,0:T(8,128)(2,1)}, bf16[160,896]{1,0:T(8,128)(2,1)S(1)}, u32[]{:S(2)}, u32[]{:S(2)}) collective-permute-start(bf16[160,896]{1,0:T(8,128)(2,1)} %slice.49), channel_id=1, source_target_pairs={{0,32},{32,0},{1,33},{33,1},{2,34},{34,2},{3,35},{35,3},{4,36},{36... | collective-permute-start | bytes 860168 | tf_op jit(solution)/shard_map/ppermute | solution.py:37
  19.6 28.8 %collective-permute-start.2 = (bf16[384,896]{1,0:T(8,128)(2,1)}, bf16[384,896]{1,0:T(8,128)(2,1)}, u32[]{:S(2)}, u32[]{:S(2)}) collective-permute-start(bf16[384,896]{1,0:T(8,128)(2,1)} %slice.48), channel_id=1, source_target_pairs={{0,32},{32,0},{1,33},{33,1},{2,34},{34,2},{3,35},{35,3},{4,36},{36... | collective-permute-start | bytes 2064392 | tf_op jit(solution)/shard_map/ppermute | solution.py:37
  20.9 24.8 %collective-permute-start.1 = (bf16[8,512,128]{2,1,0:T(8,128)(2,1)S(1)}, bf16[8,512,128]{2,1,0:T(8,128)(2,1)}, u32[]{:S(2)}, u32[]{:S(2)}) collective-permute-start(bf16[8,512,128]{2,1,0:T(8,128)(2,1)S(1)} %copy-done.11), channel_id=1, source_target_pairs={{0,1},{1,0},{2,3},{3,2},{4,5},{5,4},{6,7},{7,6},{8,9},{9,8},{10,11... | collective-permute-start | bytes 3145736 | tf_op jit(solution)/shard_map/ppermute | solution.py:37
  22.7 8.2 %copy-start.9 = (s32[1,16]{1,0:T(1,128)S(1)}, s32[1,16]{1,0:T(1,128)}, u32[]{:S(2)}) copy-start(s32[1,16]{1,0:T(1,128)} %param.16) | copy-start | bytes 196
  32.2 16.4 %all-to-all-start.1 = ((bf16[16,36,256]{2,1,0:T(8,128)(2,1)}), bf16[16,36,256]{2,1,0:T(8,128)(2,1)S(1)}, u32[]{:S(2)}, u32[]{:S(2)}) async-start(bf16[16,36,256]{2,1,0:T(8,128)(2,1)} %route.1), calls=%async_computation.1 | async-start | bytes 655360 | tf_op jit(solution)/shard_map/all_to_all | solution.py:29
  48.6 0.7 copy-start.10
  52.7 44.5 %copy-start.13 = (bf16[160,896]{1,0:T(8,128)(2,1)}, bf16[160,896]{1,0:T(8,128)(2,1)S(1)}, u32[]{:S(2)}) copy-start(bf16[160,896]{1,0:T(8,128)(2,1)S(1)} %collective-permute-done.3.refs_4_) | copy-start | bytes 860164
  52.7 28.4 %all-to-all-start.2 = ((bf16[16,2,32,512]{3,2,1,0:T(8,128)(2,1)}), bf16[16,2,32,512]{3,2,1,0:T(8,128)(2,1)S(1)}, u32[]{:S(2)}, u32[]{:S(2)}) async-start(bf16[16,2,32,512]{3,2,1,0:T(8,128)(2,1)} %bitcast.61), calls=%async_computation.2 | async-start | bytes 2097152 | tf_op jit(solution)/shard_map/all_to_all | solution.py:29
  59.7 21.4 %collective-permute-start.4 = (bf16[384,1152]{1,0:T(8,128)(2,1)}, bf16[384,1152]{1,0:T(8,128)(2,1)}, u32[]{:S(2)}, u32[]{:S(2)}) collective-permute-start(bf16[384,1152]{1,0:T(8,128)(2,1)} %multiply_convert_fusion.2), channel_id=1, source_target_pairs={{0,32},{32,0},{1,33},{33,1},{2,34},{34,2},{3,35},{35,3},{4,36},{36... | collective-permute-start | bytes 2654216 | tf_op jit(solution)/shard_map/ppermute | solution.py:37
  81.1 10.5 %collective-permute-start.5 = (bf16[1024,896]{1,0:T(8,128)(2,1)}, bf16[1024,896]{1,0:T(8,128)(2,1)}, u32[]{:S(2)}, u32[]{:S(2)}) collective-permute-start(bf16[1024,896]{1,0:T(8,128)(2,1)} %refs_0_), channel_id=1, source_target_pairs={{0,1},{1,0},{2,3},{3,2},{4,5},{5,4},{6,7},{7,6},{8,9},{9,8},{10,11... | collective-permute-start | bytes 5505032 | tf_op jit(solution)/shard_map/ppermute | solution.py:37
  85.4 20.5 %collective-permute-start.8 = (bf16[384,896]{1,0:T(8,128)(2,1)}, bf16[384,896]{1,0:T(8,128)(2,1)S(1)}, u32[]{:S(2)}, u32[]{:S(2)}) collective-permute-start(bf16[384,896]{1,0:T(8,128)(2,1)} %collective-permute-done.2.refs_3_), channel_id=1, source_target_pairs={{0,1},{1,0},{2,3},{3,2},{4,5},{5,4},{6,7},{7,6},{8,9},{9,8},{10,11... | collective-permute-start | bytes 2064392 | tf_op jit(solution)/shard_map/ppermute | solution.py:37
  86.6 20.2 %all-to-all-start.3 = ((bf16[8,32,2048]{2,1,0:T(8,128)(2,1)}), bf16[8,32,2048]{2,1,0:T(8,128)(2,1)}, u32[]{:S(2)}, u32[]{:S(2)}) async-start(bf16[8,32,2048]{2,1,0:T(8,128)(2,1)} %bitcast.12), calls=%async_computation.3 | async-start | bytes 2097152 | tf_op jit(solution)/shard_map/all_to_all | solution.py:29
  90.9 14.9 %collective-permute-start.7 = (bf16[480,896]{1,0:T(8,128)(2,1)}, bf16[480,896]{1,0:T(8,128)(2,1)}, u32[]{:S(2)}, u32[]{:S(2)}) collective-permute-start(bf16[480,896]{1,0:T(8,128)(2,1)} %collective-permute-done.refs_2_), channel_id=1, source_target_pairs={{0,1},{1,0},{2,3},{3,2},{4,5},{5,4},{6,7},{7,6},{8,9},{9,8},{10,11... | collective-permute-start | bytes 2580488 | tf_op jit(solution)/shard_map/ppermute | solution.py:37
  92.3 12.8 %collective-permute-start.6 = (bf16[32,896]{1,0:T(8,128)(2,1)S(1)}, bf16[32,896]{1,0:T(8,128)(2,1)S(1)}, u32[]{:S(2)}, u32[]{:S(2)}) collective-permute-start(bf16[32,896]{1,0:T(8,128)(2,1)S(1)} %bitcast.74), channel_id=1, source_target_pairs={{0,32},{32,0},{1,33},{33,1},{2,34},{34,2},{3,35},{35,3},{4,36},{36... | collective-permute-start | bytes 172040 | tf_op jit(solution)/shard_map/ppermute | solution.py:37
  97.2 8.6 %collective-permute-start.9 = (bf16[160,896]{1,0:T(8,128)(2,1)S(1)}, bf16[160,896]{1,0:T(8,128)(2,1)S(1)}, u32[]{:S(2)}, u32[]{:S(2)}) collective-permute-start(bf16[160,896]{1,0:T(8,128)(2,1)S(1)} %collective-permute-done.3.refs_4_), channel_id=1, source_target_pairs={{0,1},{1,0},{2,3},{3,2},{4,5},{5,4},{6,7},{7,6},{8,9},{9,8},{10,11... | collective-permute-start | bytes 860168 | tf_op jit(solution)/shard_map/ppermute | solution.py:37
  105.8 16.2 %copy-start.3 = (bf16[896,1152]{1,0:T(8,128)(2,1)S(1)}, bf16[896,1152]{1,0:T(8,128)(2,1)}, u32[]{:S(2)}) copy-start(bf16[896,1152]{1,0:T(8,128)(2,1)} %multiply_convert_fusion.refs_0_) | copy-start | bytes 6193156
  105.8 0.7 copy-start.14
  105.8 1.0 copy-start.12
  106.8 31.2 %collective-permute-start.10 = (bf16[512,1152]{1,0:T(8,128)(2,1)}, bf16[512,1152]{1,0:T(8,128)(2,1)S(1)}, u32[]{:S(2)}, u32[]{:S(2)}) collective-permute-start(bf16[512,1152]{1,0:T(8,128)(2,1)} %multiply_convert_fusion.1), channel_id=1, source_target_pairs={{0,32},{32,0},{1,33},{33,1},{2,34},{34,2},{3,35},{35,3},{4,36},{36... | collective-permute-start | bytes 3538952 | tf_op jit(solution)/shard_map/ppermute | solution.py:37
  114.8 23.2 %all-to-all-start.4 = ((bf16[8,2,32,896]{3,2,1,0:T(8,128)(2,1)}), bf16[8,2,32,896]{3,2,1,0:T(8,128)(2,1)}, u32[]{:S(2)}, u32[]{:S(2)}) async-start(bf16[8,2,32,896]{3,2,1,0:T(8,128)(2,1)} %combine.1), calls=%async_computation.4 | async-start | bytes 1835008 | tf_op jit(solution)/shard_map/all_to_all | solution.py:29
  122.0 30.1 %collective-permute-start.12 = (bf16[896,1152]{1,0:T(8,128)(2,1)S(1)}, bf16[896,1152]{1,0:T(8,128)(2,1)}, u32[]{:S(2)}, u32[]{:S(2)}) collective-permute-start(bf16[896,1152]{1,0:T(8,128)(2,1)S(1)} %copy-done.3), channel_id=1, source_target_pairs={{0,1},{1,0},{2,3},{3,2},{4,5},{5,4},{6,7},{7,6},{8,9},{9,8},{10,11... | collective-permute-start | bytes 6193160 | tf_op jit(solution)/shard_map/ppermute | solution.py:37
  141.7 31.0 %copy-start.8 = (s32[2]{0:T(128)S(1)}, s32[2]{0:T(128)}, u32[]{:S(2)}) copy-start(s32[2]{0:T(128)} %pad_add_fusion.ids_ref) | copy-start | bytes 28
  141.7 31.0 %all-to-all-start.5 = ((bf16[16,2,32,896]{3,2,1,0:T(8,128)(2,1)}), bf16[16,2,32,896]{3,2,1,0:T(8,128)(2,1)}, u32[]{:S(2)}, u32[]{:S(2)}) async-start(bf16[16,2,32,896]{3,2,1,0:T(8,128)(2,1)} %broadcast_in_dim.29), calls=%async_computation.5 | async-start | bytes 3670016 | tf_op jit(solution)/shard_map/all_to_all | solution.py:29
  146.3 5.8 %collective-permute-start.14 = (bf16[512,1152]{1,0:T(8,128)(2,1)S(1)}, bf16[512,1152]{1,0:T(8,128)(2,1)S(1)}, u32[]{:S(2)}, u32[]{:S(2)}) collective-permute-start(bf16[512,1152]{1,0:T(8,128)(2,1)S(1)} %collective-permute-done.10.refs_2_), channel_id=1, source_target_pairs={{0,1},{1,0},{2,3},{3,2},{4,5},{5,4},{6,7},{7,6},{8,9},{9,8},{10,11... | collective-permute-start | bytes 3538952 | tf_op jit(solution)/shard_map/ppermute | solution.py:37
  147.2 4.0 %collective-permute-start.13 = (bf16[384,1152]{1,0:T(8,128)(2,1)}, bf16[384,1152]{1,0:T(8,128)(2,1)S(1)}, u32[]{:S(2)}, u32[]{:S(2)}) collective-permute-start(bf16[384,1152]{1,0:T(8,128)(2,1)} %collective-permute-done.4.refs_1_), channel_id=1, source_target_pairs={{0,1},{1,0},{2,3},{3,2},{4,5},{5,4},{6,7},{7,6},{8,9},{9,8},{10,11... | collective-permute-start | bytes 2654216 | tf_op jit(solution)/shard_map/ppermute | solution.py:37
  151.2 0.9 copy-start.6
  152.1 1.0 copy-start.4
  172.7 1.3 copy-start.5
  173.9 1.2 copy-start.7
  184.6 39.8 %all-to-all-start.6 = ((bf16[8,64,2432]{2,1,0:T(8,128)(2,1)}), bf16[8,64,2432]{2,1,0:T(8,128)(2,1)S(1)}, u32[]{:S(2)}, u32[]{:S(2)}) async-start(bf16[8,64,2432]{2,1,0:T(8,128)(2,1)} %bitcast.23), calls=%async_computation.6 | async-start | bytes 4980736 | tf_op jit(solution)/shard_map/all_to_all | solution.py:29
  189.4 41.1 %collective-permute-start.15 = (bf16[1152,896]{1,0:T(8,128)(2,1)}, bf16[1152,896]{1,0:T(8,128)(2,1)}, u32[]{:S(2)}, u32[]{:S(2)}) collective-permute-start(bf16[1152,896]{1,0:T(8,128)(2,1)} %param.25), channel_id=1, source_target_pairs={{0,1},{1,0},{2,3},{3,2},{4,5},{5,4},{6,7},{7,6},{8,9},{9,8},{10,11... | collective-permute-start | bytes 6193160 | tf_op jit(solution)/shard_map/ppermute | solution.py:37
  226.8 36.4 %all-to-all-start.7 = ((bf16[8,64,2304]{2,1,0:T(8,128)(2,1)}), bf16[8,64,2304]{2,1,0:T(8,128)(2,1)S(1)}, u32[]{:S(2)}, u32[]{:S(2)}) async-start(bf16[8,64,2304]{2,1,0:T(8,128)(2,1)} %broadcast_in_dim.31), calls=%async_computation.7 | async-start | bytes 4718592 | tf_op jit(solution)/shard_map/all_to_all | solution.py:29
  263.2 2.2 copy-start.2
  269.5 20.3 %all-to-all-start.8 = ((bf16[8,64,896]{2,1,0:T(8,128)(2,1)}), bf16[8,64,896]{2,1,0:T(8,128)(2,1)S(1)}, u32[]{:S(2)}, u32[]{:S(2)}) async-start(bf16[8,64,896]{2,1,0:T(8,128)(2,1)} %bitcast.26), calls=%async_computation.8 | async-start | bytes 1835008 | tf_op jit(solution)/shard_map/all_to_all | solution.py:29
  273.9 3.7 %collective-permute-start.11 = (f32[32,896]{1,0:T(8,128)S(1)}, f32[32,896]{1,0:T(8,128)S(1)}, u32[]{:S(2)}, u32[]{:S(2)}) collective-permute-start(f32[32,896]{1,0:T(8,128)S(1)} %dynamic-slice_bitcast_fusion), channel_id=1, source_target_pairs={{0,32},{32,0},{1,33},{33,1},{2,34},{34,2},{3,35},{35,3},{4,36},{36... | collective-permute-start | bytes 344072 | tf_op jit(solution)/shard_map/ppermute | solution.py:37
  273.9 19.1 %copy-start.1 = (bf16[2,512,896]{2,1,0:T(8,128)(2,1)S(1)}, bf16[2,512,896]{2,1,0:T(8,128)(2,1)}, u32[]{:S(2)}) copy-start(bf16[2,512,896]{2,1,0:T(8,128)(2,1)} %param.21) | copy-start | bytes 5505028
  290.2 1.8 collective-permute-start.16

commit v11 on v7

--- a/solution.py
+++ b/solution.py
@@ -17,7 +17,7 @@
 N_TP = 16
 N_ZY = 8
 SWAP = [(0, 1), (1, 0)]
-CUTS = (0, 384, 896)
+CUT = 384
 TILE = 768
 bf16 = jnp.bfloat16
 f32 = jnp.float32
@@ -197,6 +197,57 @@
     )(ids, rows, weight)
 
 
+def fetches(refs, blocks, weight_ref, sems):
+    copies, n, left = [], 0, 0
+    for column in blocks:
+        top = 0
+        for w in column:
+            at = weight_ref.at[pl.ds(top, w.shape[0]), pl.ds(left, w.shape[1])]
+            copies.append(pltpu.make_async_copy(refs[n], at, sems.at[n]))
+            n, top = n + 1, top + w.shape[0]
+        left += column[0].shape[1]
+    return copies
+
+
+def combine(ids, rows, blocks):
+    groups, count, depth = rows.shape
+    width = blocks[0][0].shape[1]
+    flat = [w for column in blocks for w in column]
+    half = len(flat) // 2
+
+    def body(ids_ref, rows_ref, *refs):
+        out_ref, weight_ref, sems = refs[len(flat) :]
+        copies = fetches(refs, blocks, weight_ref, sems)
+        for copy in copies:
+            copy.start()
+        lhs = rows_ref[...].reshape(groups * count, depth)
+        for k in range(2):
+            for copy in copies[k * half : (k + 1) * half]:
+                copy.wait()
+            total = jnp.dot(
+                lhs, weight_ref[:, k * width : (k + 1) * width], preferred_element_type=f32
+            )
+            at = lax.rem(ids_ref[1] + k, 2)
+            out_ref[:, at] = total.astype(bf16).reshape(groups, count, width)
+
+    return pl.pallas_call(
+        body,
+        grid_spec=pltpu.PrefetchScalarGridSpec(
+            num_scalar_prefetch=1,
+            grid=(1,),
+            in_specs=[whole(rows.shape)] + [pl.BlockSpec(memory_space=pl.ANY) for _ in flat],
+            out_specs=whole((groups, 2, count, width)),
+            scratch_shapes=[
+                pltpu.VMEM((depth, 2 * width), bf16),
+                pltpu.SemaphoreType.DMA((len(flat),)),
+            ],
+        ),
+        out_shape=jax.ShapeDtypeStruct((groups, 2, count, width), bf16),
+        compiler_params=params(60),
+        name="combine",
+    )(ids, rows, *flat)
+
+
 def widen(ids, rows, weight):
     halves, chunks, blocks, count, features = rows.shape
     depth, columns = weight.shape
@@ -281,12 +332,6 @@
 
     out_came = swap(out_proj, "xl")
     value_ups = jnp.concatenate([value_up, swap(value_up, "c")], axis=0)
-    downs = jnp.concatenate([down_weight, swap(down_weight, "c")], axis=0)
-    residue = lax.dynamic_slice_in_dim(residual, lax.div(member, 2) * 2 * rows_out, 2 * rows_out, 1)
-    residue = residue.reshape(steps, 2, 2, rows_out // 8, 2, 2, features)
-    residue = lax.dynamic_index_in_dim(residue, core, 4, False)
-    residue = residue.transpose(2, 1, 3, 4, 0, 5).reshape(2, count, features)
-    residue_came = swap(at_other(residue), "xl")
     lanes = jnp.arange(N_TP, dtype=jnp.int32)
     own_slot = jnp.sum(jnp.where(lanes == member, move_slot[0], 0))
     ids = jnp.stack([own_slot, pair]).astype(jnp.int32)
@@ -300,27 +345,37 @@
         weight = jnp.where(pair == 0, first[low:high], second[low:high])
         return (weight.astype(f32) * gain[low:high]).astype(bf16)
 
-    sent = [
-        scaled(low, high, up_weight, gate_weight) for low, high in zip(CUTS[:-1], CUTS[1:])
-    ]
-    kept = scaled(0, CUTS[-1], gate_weight, up_weight)
+    kept = scaled(0, features, gate_weight, up_weight)
+    sent = scaled(0, CUT, up_weight, gate_weight)
     arrived = exchange(route(move_peer[0], pieces), TP)
+    arrived, kept, sent, value_ups = lax.optimization_barrier((arrived, kept, sent, value_ups))
     fresh_t = new_latent.transpose(1, 2, 0)
     queries_t = queries.transpose(0, 1, 3, 2)
     out = attend(ids, cache_length, cache_t, fresh_t, queries_t, heads, latent_width)
     out = attend(
         ids, cache_length, cache_t, fresh_t, queries_t, heads, latent_width, arrived, out
     )
-    out, out_came, sent[0] = lax.optimization_barrier((out, out_came, sent[0]))
-    came = [swap(sent[0], "xl")]
-    out_weights = jnp.concatenate(
-        [jnp.concatenate([w, swap(w, "c")], axis=0) for w in (out_proj, out_came)], axis=1
-    )
-    kept = [kept, swap(kept, "c")]
+    out, out_came, out_proj, down_weight = lax.optimization_barrier(
+        (out, out_came, out_proj, down_weight)
+    )
+    came = [swap(sent, "xl")]
+    out_near = swap(out_proj, "c")
+    out_weights = [[out_proj, out_near], [out_came, swap(out_came, "c")]]
     out = out.reshape((N_TP,) + out.shape[2:])
     by_head = exchange(out, TP).reshape(-1, 2 * heads, latent_width)
-    by_head, kept, came, out_weights, value_ups, residue_came, downs = lax.optimization_barrier(
-        (by_head, kept, came, out_weights, value_ups, residue_came, downs)
+
+    downs = jnp.concatenate([down_weight, swap(down_weight, "c")], axis=0)
+    out_weights[0][1], gate_weight, up_weight, residual = lax.optimization_barrier(
+        (out_near, gate_weight, up_weight, residual)
+    )
+    sent = scaled(CUT, features, up_weight, gate_weight)
+    residue = lax.dynamic_slice_in_dim(residual, lax.div(member, 2) * 2 * rows_out, 2 * rows_out, 1)
+    residue = residue.reshape(steps, 2, 2, rows_out // 8, 2, 2, features)
+    residue = lax.dynamic_index_in_dim(residue, core, 4, False)
+    residue = residue.transpose(2, 1, 3, 4, 0, 5).reshape(2, count, features)
+    residue = [at_pair(residue), at_other(residue)]
+    by_head, kept, came, sent, downs, residue, out_weights = lax.optimization_barrier(
+        (by_head, kept, came, sent, downs, residue, out_weights)
     )
     value_heads = jnp.einsum(
         "thl,hlv->thv", by_head, value_ups, preferred_element_type=f32
@@ -332,10 +387,12 @@
         value_heads[None, :, None], (2, 2, 2) + value_heads.shape[1:]
     ).reshape((N_DP,) + value_heads.shape[1:])
     gathered = exchange(value_heads, DP)
-    gathered, sent[1] = lax.optimization_barrier((gathered, sent[1]))
-    came.append(swap(sent[1], "xl"))
-    parts = exchange(project(ids, gathered, out_weights, 2), ZY)
-    parts, came[1] = lax.optimization_barrier((parts, came[1]))
+    gathered, sent, kept, residue = lax.optimization_barrier((gathered, sent, kept, residue))
+    came.append(swap(sent, "xl"))
+    residue[1] = swap(residue[1], "xl")
+    parts = exchange(combine(ids, gathered, out_weights), ZY)
+    parts, came, kept, residue = lax.optimization_barrier((parts, came, kept, residue))
+    kept = [kept, swap(kept, "c")]
     in_weight = jnp.concatenate(
         [
             jnp.concatenate([own, swap(own, "c") if k else kept[1]], axis=1)
@@ -343,11 +400,12 @@
         ],
         axis=0,
     )
-    residue = by_pair(at_pair(residue), residue_came)
-    hidden = residue.astype(f32) + jnp.sum(parts.astype(f32), axis=0)
+    hidden = by_pair(*residue).astype(f32) + jnp.sum(parts.astype(f32), axis=0)
 
     rows = spread(hidden.astype(bf16), PAIR, 2 * N_ZY).reshape((2, N_ZY) + hidden.shape)
-    rows, in_weight = lax.optimization_barrier((rows, in_weight))
+    near = swap(at_other(hidden), "xl")
+    near, in_weight = lax.optimization_barrier((near, in_weight))
+    rows, near = lax.optimization_barrier((rows, near))
     sums = exchange(widen(ids, rows, in_weight).reshape(N_DP, chunk, -1), DP)
     sums = jnp.sum(sums.reshape(2, 2, 2, chunk, -1).astype(f32), axis=(0, 2))
     squares = sums[0, :, 2 * units] + sums[0, :, 2 * units + 1]
@@ -355,7 +413,7 @@
     active = sums[:, :, : 2 * units] * inverse
     active = (jax.nn.silu(active[0]) * active[1]).astype(bf16)
     parts = exchange(project(ids, spread(active, DP, N_DP), downs, 1)[:, 0], ZY)
-    hidden = by_pair(at_pair(hidden), swap(at_other(hidden), "xl")).reshape(chunk, -1)
+    hidden = by_pair(at_pair(hidden), near).reshape(chunk, -1)
     result = (hidden + jnp.sum(parts.astype(f32), axis=0)).astype(bf16)
 
     result = result.reshape(2, 2, rows_out // 8, 2, steps, features)

time: 268 us -> 256 us (0.955)
  other arithmetic: 53.6 us -> 39.4 us
  waiting for transfers between devices: 40.8 us -> 45.8 us
  local copies, waits for them, and re-layouts: 13.1 us -> 9.06 us
  Pallas kernels: 27.6 us -> 31.2 us
    ppermute x13, waiting for transfers between devices: 5.46 us -> 21.6 us  [swap(): return lax.ppermute(block, axis, SWAP)]
    concatenate x1 -> x0, other arithmetic: 15.3 us -> none  [local(): jnp.concatenate([jnp.concatenate([w, swap(w, 'c')], axis=0) for w in (out...]
    all_to_all x6, waiting for transfers between devices: 35.3 us -> 24.2 us  [exchange(): return lax.all_to_all(blocks, axes, 0, 0, tiled=True)]
    pallas_call x0 -> x1, Pallas kernels: none -> 7.42 us  [combine(): pl.pallas_call(body, grid_spec=pltpu.PrefetchScalarGridSpec(num_scalar_pr...]
    pallas_call x2 -> x1, Pallas kernels: 7.88 us -> 4.07 us  [project(): pl.pallas_call(body, grid_spec=pltpu.PrefetchScalarGridSpec(num_scalar_pr...]
    unnamed x28, local copies, waits for them, and re-layouts: 8.34 us -> 5.25 us
  transfers between devices with their start and end apart: 19 -> 19, of which waited for: 7 -> 8; matrix products, arithmetic and copies ran while one was open for 21% -> 16% of each run, Pallas kernels for 6% -> 8%
where the time goes in v11:
time: 256 us; the launch traced here: 255 us
  blocking collectives  79.8 us (31%)
  starting transfers between devices  48.4 us (19%)
  waiting for transfers between devices  45.8 us (18%)
  other arithmetic  39.4 us (15%)
  Pallas kernels  31.2 us (12%)
  local copies, waits for them, and re-layouts  9.06 us (4%)
    all_to_all x3, blocking collectives, exchange(): return lax.all_to_all(blocks, axes, 0, 0, tiled=True)  79.8 us
    all_to_all x6, starting transfers between devices, exchange(): return lax.all_to_all(blocks, axes, 0, 0, tiled=True)  36.7 us
    all_to_all x6, waiting for transfers between devices, exchange(): return lax.all_to_all(blocks, axes, 0, 0, tiled=True)  24.2 us
    ppermute x13, waiting for transfers between devices, swap(): return lax.ppermute(block, axis, SWAP)  21.6 us
    concatenate x1, other arithmetic, local(): jnp.concatenate([jnp.concatenate([own, swap(own, 'c') if k else kept[1]],...  19.9 us
    ppermute x13, starting transfers between devices, swap(): return lax.ppermute(block, axis, SWAP)  11.7 us
    pallas_call x2, Pallas kernels, attend(): pl.pallas_call(body, grid_spec=pltpu.PrefetchScalarGridSpec(num_scalar_pr...  9.67 us
    convert_element_type x3, other arithmetic, scaled(): return (weight.astype(f32) * gain[low:high]).astype(bf16)  9.29 us
  transfers between devices with their start and end apart: 19, of which 8 were waited for; matrix products, arithmetic and copies ran while one was open for 16% of the time, Pallas kernels for 8%

profile of v11, /device:TPU:1, one launch (start us, length us, event | category | flops | bytes accessed | tf_op | source)
XLA Modules:
  0.0 255.4 jit_solution(6988633022384265313)
XLA Ops:
  0.0 2.1 collective-permute-start.1
  2.2 2.4 leave.1
  4.6 8.8 %all-to-all-start = ((bf16[16,36,256]{2,1,0:T(8,128)(2,1)}), bf16[16,36,256]{2,1,0:T(8,128)(2,1)S(1)}, u32[]{:S(2)}, u32[]{:S(2)}) async-start(bf16[16,36,256]{2,1,0:T(8,128)(2,1)} %leave.1), calls=%async_computation | async-start | bytes 655360 | tf_op jit(solution)/shard_map/all_to_all | solution.py:28
  13.5 1.1 copy.52
  14.6 0.7 fusion.11
  15.3 1.2 pad_add_fusion.ids_ref
  16.6 6.3 %attend.1.refs_1_ = bf16[8,2,2,32,512]{4,3,2,1,0:T(8,128)(2,1)} custom-call(s32[2]{0:T(128)} %pad_add_fusion.ids_ref, s32[4]{0:T(128)} %lengths_ref.3, bf16[4,576,2]{2,1,0:T(8,128)(2,1)} %bitcast.59, bf16[2,4,576,128]{3,2,1,0:T(8,128)(2,1)} %bitcast.61, bf16[4,576,256]{2,1,0:T(8,128)(2,1)} %bitcast.64), custom_call_target="tpu_custom_call" | custom-call | tf_op jit(solution)/shard_map/attend/pallas_call | solution.py:140
  22.9 1.3 route.1
  24.2 7.3 %all-to-all-start.1 = ((bf16[16,36,256]{2,1,0:T(8,128)(2,1)}), bf16[16,36,256]{2,1,0:T(8,128)(2,1)S(1)}, u32[]{:S(2)}, u32[]{:S(2)}) async-start(bf16[16,36,256]{2,1,0:T(8,128)(2,1)} %route.1), calls=%async_computation.1 | async-start | bytes 655360 | tf_op jit(solution)/shard_map/all_to_all | solution.py:28
  31.5 3.5 %multiply_convert_fusion = bf16[896,1152]{1,0:T(8,128)(2,1)} fusion(f32[896]{0:T(1024)S(1)} %convert_element_type.62, bf16[896,1152]{1,0:T(8,128)(2,1)} %param.23, bf16[896,1152]{1,0:T(8,128)(2,1)} %param.24, pred[]{:T(512)S(6)} %eq.17), kind=kLoop, calls=%fused_computation.3 | loop fusion | flops 4128768 | bytes 6196737 | tf_op jit(solution)/shard_map/convert_element_type | solution.py:346
  35.0 2.6 %multiply_convert_fusion.2 = bf16[384,1152]{1,0:T(8,128)(2,1)} fusion(f32[384]{0:T(512)S(1)} %slice.37, bf16[896,1152]{1,0:T(8,128)(2,1)} %param.23, bf16[896,1152]{1,0:T(8,128)(2,1)} %param.24, pred[]{:T(512)S(6)} %eq.17), kind=kLoop, calls=%fused_computation.8 | loop fusion | flops 1769472 | bytes 2655745 | tf_op jit(solution)/shard_map/convert_element_type | solution.py:346
  37.6 2.7 %pad_maximum_fusion.1 = bf16[16,512,128]{2,1,0:T(8,128)(2,1)} fusion(bf16[8,512,128]{2,1,0:T(8,128)(2,1)} %collective-permute-done, bf16[8,512,128]{2,1,0:T(8,128)(2,1)S(1)} %copy-done.9), kind=kLoop, calls=%fused_computation.5 | loop fusion | flops 1048576 | bytes 4194304 | tf_op jit(solution)/shard_map/concatenate | solution.py:334
  40.6 0.7 copy-done.8
  41.3 3.4 %again.1 = bf16[8,2,2,32,512]{4,3,2,1,0:T(8,128)(2,1)} custom-call(s32[2]{0:T(128)} %pad_add_fusion.ids_ref, s32[4]{0:T(128)} %lengths_ref.3, bf16[4,576,2]{2,1,0:T(8,128)(2,1)} %bitcast.60, bf16[2,4,576,128]{3,2,1,0:T(8,128)(2,1)} %bitcast.62, bf16[16,36,256]{2,1,0:T(8,128)(2,1)} %copy-done.8, ...), custom_call_target="tpu_custom_call", output_to_operand_aliasing={{}: (5, {})} | custom-call | tf_op jit(solution)/shard_map/again/pallas_call | solution.py:140
  44.7 1.0 collective-permute-start.3
  45.7 0.5 collective-permute-start.5
  46.2 0.4 collective-permute-start.2
  46.6 6.9 %all-to-all-start.2 = ((bf16[16,2,32,512]{3,2,1,0:T(8,128)(2,1)}), bf16[16,2,32,512]{3,2,1,0:T(8,128)(2,1)S(1)}, u32[]{:S(2)}, u32[]{:S(2)}) async-start(bf16[16,2,32,512]{3,2,1,0:T(8,128)(2,1)} %bitcast.58), calls=%async_computation.2 | async-start | bytes 2097152 | tf_op jit(solution)/shard_map/all_to_all | solution.py:28
  53.5 3.1 %multiply_convert_fusion.1 = bf16[512,1152]{1,0:T(8,128)(2,1)} fusion(f32[512]{0:T(512)S(1)} %slice.40, bf16[896,1152]{1,0:T(8,128)(2,1)} %param.23, bf16[896,1152]{1,0:T(8,128)(2,1)} %param.24, pred[]{:T(512)S(6)} %eq.17), kind=kLoop, calls=%fused_computation.4 | loop fusion | flops 2359296 | bytes 3540993 | tf_op jit(solution)/shard_map/convert_element_type | solution.py:346
  57.1 0.2 constant_dynamic-slice_fusion
  57.4 4.0 %pad_maximum_fusion.weight_ref = bf16[2304,896]{1,0:T(8,128)(2,1)} fusion(bf16[1152,896]{1,0:T(8,128)(2,1)} %collective-permute-done.4, bf16[1152,896]{1,0:T(8,128)(2,1)S(1)} %copy-done.7), kind=kLoop, calls=%fused_computation.2 | loop fusion | flops 8257536 | bytes 8257536 | tf_op jit(solution)/shard_map/concatenate | solution.py:367
  61.4 6.4 %collective-permute-done.2 = bf16[384,1152]{1,0:T(8,128)(2,1)} collective-permute-done((bf16[384,1152]{1,0:T(8,128)(2,1)}, bf16[384,1152]{1,0:T(8,128)(2,1)}, u32[]{:S(2)}, u32[]{:S(2)}) %collective-permute-start.2) | collective-permute-done | bytes 884768 | tf_op jit(solution)/shard_map/ppermute | solution.py:36
  67.8 3.0 %all-to-all-done.2 = bf16[16,2,32,512]{3,2,1,0:T(8,128)(2,1)S(1)} async-done(((bf16[16,2,32,512]{3,2,1,0:T(8,128)(2,1)}), bf16[16,2,32,512]{3,2,1,0:T(8,128)(2,1)S(1)}, u32[]{:S(2)}, u32[]{:S(2)}) %all-to-all-start.2) | async-done | bytes 1048608 | tf_op jit(solution)/shard_map/all_to_all | solution.py:28
  70.9 1.3 fusion
  72.6 18.3 %all_to_all.45.rows_ref = bf16[8,32,2048]{2,1,0:T(8,128)(2,1)} all-to-all(bf16[8,32,2048]{2,1,0:T(8,128)(2,1)S(1)} %bitcast.65), channel_id=1, replica_groups=mesh['xh'=2,'xl'=2,'zl'=2,'zh'=2,'y'=4,'c'=2] {'xh','xl','zl'}, dimensions={0} | all-to-all | bytes 2097152 | tf_op jit(solution)/shard_map/all_to_all | solution.py:28
  91.2 7.4 %combine.1 = bf16[8,2,32,896]{3,2,1,0:T(8,128)(2,1)} custom-call(s32[2]{0:T(128)} %pad_add_fusion.ids_ref, bf16[8,32,2048]{2,1,0:T(8,128)(2,1)} %all_to_all.45.rows_ref, bf16[1024,896]{1,0:T(8,128)(2,1)} %refs_0_, bf16[1024,896]{1,0:T(8,128)(2,1)} %collective-permute-done.3.refs_1_, bf16[1024,896]{1,0:T(8,128)(2,1)} %collective-permute-done.1.refs_2_, ...), custom_call_target="tpu_custom_call" | custom-call | tf_op jit(solution)/shard_map/combine/pallas_call | solution.py:233
  98.6 3.6 %all-to-all-start.4 = ((bf16[8,2,32,896]{3,2,1,0:T(8,128)(2,1)}), bf16[8,2,32,896]{3,2,1,0:T(8,128)(2,1)S(1)}, u32[]{:S(2)}, u32[]{:S(2)}) async-start(bf16[8,2,32,896]{3,2,1,0:T(8,128)(2,1)} %combine.1), calls=%async_computation.4 | async-start | bytes 1835008 | tf_op jit(solution)/shard_map/all_to_all | solution.py:28
  102.3 1.3 collective-permute-start.7
  103.5 14.3 %collective-permute-done.7 = bf16[32,896]{1,0:T(8,128)(2,1)S(1)} collective-permute-done((bf16[32,896]{1,0:T(8,128)(2,1)S(1)}, bf16[32,896]{1,0:T(8,128)(2,1)S(1)}, u32[]{:S(2)}, u32[]{:S(2)}) %collective-permute-start.7) | collective-permute-done | bytes 57376 | tf_op jit(solution)/shard_map/ppermute | solution.py:36
  117.8 0.3 all-to-all-done.4
  118.2 2.6 %collective-permute-start.9 = (bf16[896,1152]{1,0:T(8,128)(2,1)}, bf16[896,1152]{1,0:T(8,128)(2,1)}, u32[]{:S(2)}, u32[]{:S(2)}) collective-permute-start(bf16[896,1152]{1,0:T(8,128)(2,1)} %multiply_convert_fusion), channel_id=1, source_target_pairs={{0,1},{1,0},{2,3},{3,2},{4,5},{5,4},{6,7},{7,6},{8,9},{9,8},{10,11... | collective-permute-start | bytes 6193160 | tf_op jit(solution)/shard_map/ppermute | solution.py:36
  120.8 0.3 collective-permute-start.11
  121.5 0.3 collective-permute-start.8
  121.8 1.5 broadcast_in_dim.29
  123.3 4.7 %all-to-all-start.5 = ((bf16[16,2,32,896]{3,2,1,0:T(8,128)(2,1)}), bf16[16,2,32,896]{3,2,1,0:T(8,128)(2,1)S(1)}, u32[]{:S(2)}, u32[]{:S(2)}) async-start(bf16[16,2,32,896]{3,2,1,0:T(8,128)(2,1)} %broadcast_in_dim.29), calls=%async_computation.5 | async-start | bytes 3670016 | tf_op jit(solution)/shard_map/all_to_all | solution.py:28
  128.0 19.9 %maximum_maximum_fusion.weight_ref = bf16[1792,2304]{1,0:T(8,128)(2,1)} fusion(bf16[512,1152]{1,0:T(8,128)(2,1)} %collective-permute-done.11, bf16[512,1152]{1,0:T(8,128)(2,1)S(1)} %collective-permute-done.6, bf16[384,1152]{1,0:T(8,128)(2,1)} %collective-permute-done.10, bf16[384,1152]{1,0:T(8,128)(2,1)} %collective-permute-done.2, ...), kind=kLoop, calls=%fused_computation | loop fusion | flops 49545216 | bytes 16515072 | tf_op jit(solution)/shard_map/concatenate | solution.py:396
  147.9 6.5 %all-to-all-done.5 = bf16[16,2,32,896]{3,2,1,0:T(8,128)(2,1)S(1)} async-done(((bf16[16,2,32,896]{3,2,1,0:T(8,128)(2,1)}), bf16[16,2,32,896]{3,2,1,0:T(8,128)(2,1)S(1)}, u32[]{:S(2)}, u32[]{:S(2)}) %all-to-all-start.5) | async-done | bytes 1835040 | tf_op jit(solution)/shard_map/all_to_all | solution.py:28
  154.4 3.3 %copy-done.2 = bf16[1792,2304]{1,0:T(8,128)(2,1)S(1)} copy-done((bf16[1792,2304]{1,0:T(8,128)(2,1)S(1)}, bf16[1792,2304]{1,0:T(8,128)(2,1)}, u32[]{:S(2)}) %copy-start.2) | copy-done | bytes 8257560
  157.8 6.4 %widen.1 = bf16[8,2,32,2432]{3,2,1,0:T(8,128)(2,1)S(1)} custom-call(s32[2]{0:T(128)S(1)} %copy-done.4, bf16[2,8,2,32,896]{4,3,2,1,0:T(8,128)(2,1)S(1)} %bitcast.55, bf16[1792,2304]{1,0:T(8,128)(2,1)S(1)} %copy-done.2), custom_call_target="tpu_custom_call" | custom-call | tf_op jit(solution)/shard_map/widen/pallas_call | solution.py:280
  164.2 32.1 %all_to_all.46 = bf16[8,64,2432]{2,1,0:T(8,128)(2,1)S(1)} all-to-all(bf16[8,64,2432]{2,1,0:T(8,128)(2,1)S(1)} %bitcast.54), channel_id=1, replica_groups=mesh['xh'=2,'xl'=2,'zl'=2,'zh'=2,'y'=4,'c'=2] {'xh','xl','zl'}, dimensions={0} | all-to-all | bytes 4980736 | tf_op jit(solution)/shard_map/all_to_all | solution.py:28
  196.3 0.3 convert_reduce_fusion
  197.3 29.3 %all_to_all.47.rows_ref = bf16[8,64,2304]{2,1,0:T(8,128)(2,1)S(1)} all-to-all(bf16[8,64,2304]{2,1,0:T(8,128)(2,1)S(1)} %broadcast_in_dim.31), channel_id=1, replica_groups=mesh['xh'=2,'xl'=2,'zl'=2,'zh'=2,'y'=4,'c'=2] {'xh','xl','zl'}, dimensions={0} | all-to-all | bytes 4718592 | tf_op jit(solution)/shard_map/all_to_all | solution.py:28
  226.6 4.1 %project.1 = bf16[8,1,64,896]{3,2,1,0:T(8,128)(2,1)} custom-call(s32[2]{0:T(128)S(1)} %copy-done.4, bf16[8,64,2304]{2,1,0:T(8,128)(2,1)S(1)} %all_to_all.47.rows_ref, bf16[2304,896]{1,0:T(8,128)(2,1)S(1)} %copy-done.3), custom_call_target="tpu_custom_call" | custom-call | tf_op jit(solution)/shard_map/project/pallas_call | solution.py:181
  230.7 5.5 %all-to-all-start.8 = ((bf16[8,64,896]{2,1,0:T(8,128)(2,1)}), bf16[8,64,896]{2,1,0:T(8,128)(2,1)S(1)}, u32[]{:S(2)}, u32[]{:S(2)}) async-start(bf16[8,64,896]{2,1,0:T(8,128)(2,1)} %bitcast.26), calls=%async_computation.8 | async-start | bytes 1835008 | tf_op jit(solution)/shard_map/all_to_all | solution.py:28
  236.4 14.1 %all-to-all-done.8 = bf16[8,64,896]{2,1,0:T(8,128)(2,1)S(1)} async-done(((bf16[8,64,896]{2,1,0:T(8,128)(2,1)}), bf16[8,64,896]{2,1,0:T(8,128)(2,1)S(1)}, u32[]{:S(2)}, u32[]{:S(2)}) %all-to-all-start.8) | async-done | bytes 917536 | tf_op jit(solution)/shard_map/all_to_all | solution.py:28
  251.0 2.5 collective-permute-start.12
  253.5 0.9 collective-permute-done.12
  254.8 0.7 copy.60
  (70 shorter events, 3.6 us)
Async XLA Ops:
  0.0 56.6 %copy-start = (bf16[2,512,896]{2,1,0:T(8,128)(2,1)S(1)}, bf16[2,512,896]{2,1,0:T(8,128)(2,1)}, u32[]{:S(2)}) copy-start(bf16[2,512,896]{2,1,0:T(8,128)(2,1)} %param.21) | copy-start | bytes 5505028
  0.0 14.6 %copy-start.12 = (s32[1,16]{1,0:T(1,128)S(1)}, s32[1,16]{1,0:T(1,128)}, u32[]{:S(2)}) copy-start(s32[1,16]{1,0:T(1,128)} %param.15) | copy-start | bytes 196
  0.0 13.3 %copy-start.9 = (bf16[8,512,128]{2,1,0:T(8,128)(2,1)S(1)}, bf16[8,512,128]{2,1,0:T(8,128)(2,1)}, u32[]{:S(2)}) copy-start(bf16[8,512,128]{2,1,0:T(8,128)(2,1)} %param.19) | copy-start | bytes 3145732
  0.0 13.5 %copy-start.10 = (bf16[896]{0:T(1024)(128)(2,1)S(1)}, bf16[896]{0:T(1024)(128)(2,1)}, u32[]{:S(2)}) copy-start(bf16[896]{0:T(1024)(128)(2,1)} %param.22) | copy-start | bytes 5380
  0.0 13.5 %copy-start.11 = (bf16[2,4,576]{2,1,0:T(4,128)(2,1)S(1)}, bf16[2,4,576]{2,1,0:T(4,128)(2,1)}, u32[]{:S(2)}) copy-start(bf16[2,4,576]{2,1,0:T(4,128)(2,1)} %param.18) | copy-start | bytes 27652
  0.0 44.7 %collective-permute-start.1 = (bf16[1024,896]{1,0:T(8,128)(2,1)}, bf16[1024,896]{1,0:T(8,128)(2,1)}, u32[]{:S(2)}, u32[]{:S(2)}) collective-permute-start(bf16[1024,896]{1,0:T(8,128)(2,1)} %refs_0_), channel_id=1, source_target_pairs={{0,32},{32,0},{1,33},{33,1},{2,34},{34,2},{3,35},{35,3},{4,36},{36... | collective-permute-start | bytes 5505032 | tf_op jit(solution)/shard_map/ppermute | solution.py:36
  4.6 18.4 %all-to-all-start = ((bf16[16,36,256]{2,1,0:T(8,128)(2,1)}), bf16[16,36,256]{2,1,0:T(8,128)(2,1)S(1)}, u32[]{:S(2)}, u32[]{:S(2)}) async-start(bf16[16,36,256]{2,1,0:T(8,128)(2,1)} %leave.1), calls=%async_computation | async-start | bytes 655360 | tf_op jit(solution)/shard_map/all_to_all | solution.py:28
  13.3 24.3 %collective-permute-start = (bf16[8,512,128]{2,1,0:T(8,128)(2,1)S(1)}, bf16[8,512,128]{2,1,0:T(8,128)(2,1)}, u32[]{:S(2)}, u32[]{:S(2)}) collective-permute-start(bf16[8,512,128]{2,1,0:T(8,128)(2,1)S(1)} %copy-done.9), channel_id=1, source_target_pairs={{0,1},{1,0},{2,3},{3,2},{4,5},{5,4},{6,7},{7,6},{8,9},{9,8},{10,11... | collective-permute-start | bytes 3145736 | tf_op jit(solution)/shard_map/ppermute | solution.py:36
  14.6 8.3 %copy-start.5 = (s32[1,16]{1,0:T(1,128)S(1)}, s32[1,16]{1,0:T(1,128)}, u32[]{:S(2)}) copy-start(s32[1,16]{1,0:T(1,128)} %param.16) | copy-start | bytes 196
  24.2 16.4 %all-to-all-start.1 = ((bf16[16,36,256]{2,1,0:T(8,128)(2,1)}), bf16[16,36,256]{2,1,0:T(8,128)(2,1)S(1)}, u32[]{:S(2)}, u32[]{:S(2)}) async-start(bf16[16,36,256]{2,1,0:T(8,128)(2,1)} %route.1), calls=%async_computation.1 | async-start | bytes 655360 | tf_op jit(solution)/shard_map/all_to_all | solution.py:28
  40.6 0.7 copy-start.8
  44.7 8.8 %collective-permute-start.3 = (bf16[1024,896]{1,0:T(8,128)(2,1)}, bf16[1024,896]{1,0:T(8,128)(2,1)}, u32[]{:S(2)}, u32[]{:S(2)}) collective-permute-start(bf16[1024,896]{1,0:T(8,128)(2,1)} %refs_0_), channel_id=1, source_target_pairs={{0,1},{1,0},{2,3},{3,2},{4,5},{5,4},{6,7},{7,6},{8,9},{9,8},{10,11... | collective-permute-start | bytes 5505032 | tf_op jit(solution)/shard_map/ppermute | solution.py:36
  45.7 11.7 %collective-permute-start.4 = (bf16[1152,896]{1,0:T(8,128)(2,1)}, bf16[1152,896]{1,0:T(8,128)(2,1)}, u32[]{:S(2)}, u32[]{:S(2)}) collective-permute-start(bf16[1152,896]{1,0:T(8,128)(2,1)} %param.25), channel_id=1, source_target_pairs={{0,1},{1,0},{2,3},{3,2},{4,5},{5,4},{6,7},{7,6},{8,9},{9,8},{10,11... | collective-permute-start | bytes 6193160 | tf_op jit(solution)/shard_map/ppermute | solution.py:36
  45.7 25.1 %collective-permute-start.5 = (bf16[1024,896]{1,0:T(8,128)(2,1)}, bf16[1024,896]{1,0:T(8,128)(2,1)}, u32[]{:S(2)}, u32[]{:S(2)}) collective-permute-start(bf16[1024,896]{1,0:T(8,128)(2,1)} %collective-permute-done.1.refs_2_), channel_id=1, source_target_pairs={{0,1},{1,0},{2,3},{3,2},{4,5},{5,4},{6,7},{7,6},{8,9},{9,8},{10,11... | collective-permute-start | bytes 5505032 | tf_op jit(solution)/shard_map/ppermute | solution.py:36
  46.2 21.6 %collective-permute-start.2 = (bf16[384,1152]{1,0:T(8,128)(2,1)}, bf16[384,1152]{1,0:T(8,128)(2,1)}, u32[]{:S(2)}, u32[]{:S(2)}) collective-permute-start(bf16[384,1152]{1,0:T(8,128)(2,1)} %multiply_convert_fusion.2), channel_id=1, source_target_pairs={{0,32},{32,0},{1,33},{33,1},{2,34},{34,2},{3,35},{35,3},{4,36},{36... | collective-permute-start | bytes 2654216 | tf_op jit(solution)/shard_map/ppermute | solution.py:36
  46.6 24.3 %all-to-all-start.2 = ((bf16[16,2,32,512]{3,2,1,0:T(8,128)(2,1)}), bf16[16,2,32,512]{3,2,1,0:T(8,128)(2,1)S(1)}, u32[]{:S(2)}, u32[]{:S(2)}) async-start(bf16[16,2,32,512]{3,2,1,0:T(8,128)(2,1)} %bitcast.58), calls=%async_computation.2 | async-start | bytes 2097152 | tf_op jit(solution)/shard_map/all_to_all | solution.py:28
  53.5 3.9 %copy-start.7 = (bf16[1152,896]{1,0:T(8,128)(2,1)S(1)}, bf16[1152,896]{1,0:T(8,128)(2,1)}, u32[]{:S(2)}) copy-start(bf16[1152,896]{1,0:T(8,128)(2,1)} %param.25) | copy-start | bytes 6193156
  57.4 13.5 %copy-start.6 = (bf16[16,512,128]{2,1,0:T(8,128)(2,1)S(1)}, bf16[16,512,128]{2,1,0:T(8,128)(2,1)}, u32[]{:S(2)}) copy-start(bf16[16,512,128]{2,1,0:T(8,128)(2,1)} %pad_maximum_fusion.1) | copy-start | bytes 6291460
  91.0 27.2 %collective-permute-start.6 = (bf16[512,1152]{1,0:T(8,128)(2,1)}, bf16[512,1152]{1,0:T(8,128)(2,1)S(1)}, u32[]{:S(2)}, u32[]{:S(2)}) collective-permute-start(bf16[512,1152]{1,0:T(8,128)(2,1)} %multiply_convert_fusion.1), channel_id=1, source_target_pairs={{0,32},{32,0},{1,33},{33,1},{2,34},{34,2},{3,35},{35,3},{4,36},{36... | collective-permute-start | bytes 3538952 | tf_op jit(solution)/shard_map/ppermute | solution.py:36
  98.6 19.5 %all-to-all-start.4 = ((bf16[8,2,32,896]{3,2,1,0:T(8,128)(2,1)}), bf16[8,2,32,896]{3,2,1,0:T(8,128)(2,1)S(1)}, u32[]{:S(2)}, u32[]{:S(2)}) async-start(bf16[8,2,32,896]{3,2,1,0:T(8,128)(2,1)} %combine.1), calls=%async_computation.4 | async-start | bytes 1835008 | tf_op jit(solution)/shard_map/all_to_all | solution.py:28
  102.3 15.6 %collective-permute-start.7 = (bf16[32,896]{1,0:T(8,128)(2,1)S(1)}, bf16[32,896]{1,0:T(8,128)(2,1)S(1)}, u32[]{:S(2)}, u32[]{:S(2)}) collective-permute-start(bf16[32,896]{1,0:T(8,128)(2,1)S(1)} %get-tuple-element.75), channel_id=1, source_target_pairs={{0,32},{32,0},{1,33},{33,1},{2,34},{34,2},{3,35},{35,3},{4,36},{36... | collective-permute-start | bytes 172040 | tf_op jit(solution)/shard_map/ppermute | solution.py:36
  118.2 9.8 %collective-permute-start.9 = (bf16[896,1152]{1,0:T(8,128)(2,1)}, bf16[896,1152]{1,0:T(8,128)(2,1)}, u32[]{:S(2)}, u32[]{:S(2)}) collective-permute-start(bf16[896,1152]{1,0:T(8,128)(2,1)} %multiply_convert_fusion), channel_id=1, source_target_pairs={{0,1},{1,0},{2,3},{3,2},{4,5},{5,4},{6,7},{7,6},{8,9},{9,8},{10,11... | collective-permute-start | bytes 6193160 | tf_op jit(solution)/shard_map/ppermute | solution.py:36
  120.8 7.2 %collective-permute-start.11 = (bf16[512,1152]{1,0:T(8,128)(2,1)S(1)}, bf16[512,1152]{1,0:T(8,128)(2,1)}, u32[]{:S(2)}, u32[]{:S(2)}) collective-permute-start(bf16[512,1152]{1,0:T(8,128)(2,1)S(1)} %collective-permute-done.6), channel_id=1, source_target_pairs={{0,1},{1,0},{2,3},{3,2},{4,5},{5,4},{6,7},{7,6},{8,9},{9,8},{10,11... | collective-permute-start | bytes 3538952 | tf_op jit(solution)/shard_map/ppermute | solution.py:36
  121.1 6.9 %collective-permute-start.10 = (bf16[384,1152]{1,0:T(8,128)(2,1)}, bf16[384,1152]{1,0:T(8,128)(2,1)}, u32[]{:S(2)}, u32[]{:S(2)}) collective-permute-start(bf16[384,1152]{1,0:T(8,128)(2,1)} %collective-permute-done.2), channel_id=1, source_target_pairs={{0,1},{1,0},{2,3},{3,2},{4,5},{5,4},{6,7},{7,6},{8,9},{9,8},{10,11... | collective-permute-start | bytes 2654216 | tf_op jit(solution)/shard_map/ppermute | solution.py:36
  121.5 26.4 %collective-permute-start.8 = (f32[32,896]{1,0:T(8,128)S(1)}, f32[32,896]{1,0:T(8,128)S(1)}, u32[]{:S(2)}, u32[]{:S(2)}) collective-permute-start(f32[32,896]{1,0:T(8,128)S(1)} %dynamic-slice_bitcast_fusion), channel_id=1, source_target_pairs={{0,32},{32,0},{1,33},{33,1},{2,34},{34,2},{3,35},{35,3},{4,36},{36... | collective-permute-start | bytes 344072 | tf_op jit(solution)/shard_map/ppermute | solution.py:36
  123.3 31.1 %all-to-all-start.5 = ((bf16[16,2,32,896]{3,2,1,0:T(8,128)(2,1)}), bf16[16,2,32,896]{3,2,1,0:T(8,128)(2,1)S(1)}, u32[]{:S(2)}, u32[]{:S(2)}) async-start(bf16[16,2,32,896]{3,2,1,0:T(8,128)(2,1)} %broadcast_in_dim.29), calls=%async_computation.5 | async-start | bytes 3670016 | tf_op jit(solution)/shard_map/all_to_all | solution.py:28
  128.0 26.5 %copy-start.4 = (s32[2]{0:T(128)S(1)}, s32[2]{0:T(128)}, u32[]{:S(2)}) copy-start(s32[2]{0:T(128)} %pad_add_fusion.ids_ref) | copy-start | bytes 28
  154.4 3.3 %copy-start.2 = (bf16[1792,2304]{1,0:T(8,128)(2,1)S(1)}, bf16[1792,2304]{1,0:T(8,128)(2,1)}, u32[]{:S(2)}) copy-start(bf16[1792,2304]{1,0:T(8,128)(2,1)} %maximum_maximum_fusion.weight_ref) | copy-start | bytes 24772612
  197.3 29.3 %copy-start.3 = (bf16[2304,896]{1,0:T(8,128)(2,1)S(1)}, bf16[2304,896]{1,0:T(8,128)(2,1)}, u32[]{:S(2)}) copy-start(bf16[2304,896]{1,0:T(8,128)(2,1)} %pad_maximum_fusion.weight_ref) | copy-start | bytes 12386308
  230.7 19.8 %all-to-all-start.8 = ((bf16[8,64,896]{2,1,0:T(8,128)(2,1)}), bf16[8,64,896]{2,1,0:T(8,128)(2,1)S(1)}, u32[]{:S(2)}, u32[]{:S(2)}) async-start(bf16[8,64,896]{2,1,0:T(8,128)(2,1)} %bitcast.26), calls=%async_computation.8 | async-start | bytes 1835008 | tf_op jit(solution)/shard_map/all_to_all | solution.py:28
  236.2 19.2 %copy-start.1 = (bf16[2,512,896]{2,1,0:T(8,128)(2,1)S(1)}, bf16[2,512,896]{2,1,0:T(8,128)(2,1)}, u32[]{:S(2)}) copy-start(bf16[2,512,896]{2,1,0:T(8,128)(2,1)} %param.21) | copy-start | bytes 5505028
  251.0 3.4 %collective-permute-start.12 = (bf16[2,4,2,2,896]{4,3,2,1,0:T(2,128)(2,1)S(1)}, bf16[2,4,2,2,896]{4,3,2,1,0:T(2,128)(2,1)S(1)}, u32[]{:S(2)}, u32[]{:S(2)}) collective-permute-start(bf16[2,4,2,2,896]{4,3,2,1,0:T(2,128)(2,1)S(1)} %dynamic-slice_bitcast_fusion.2), channel_id=1, source_target_pairs={{0,1},{1,0},{2,3},{3,2},{4,5},{5,4},{6,7},{7,6},{8,9},{9,8},{10,11... | collective-permute-start | bytes 172040 | tf_op jit(solution)/shard_map/ppermute | solution.py:36

commit v12 on v11

--- a/solution.py
+++ b/solution.py
@@ -209,11 +209,34 @@
     return copies
 
 
+def join(blocks):
+    flat = [w for column in blocks for w in column]
+    depth = sum(w.shape[0] for w in blocks[0])
+    width = sum(column[0].shape[1] for column in blocks)
+
+    def body(*refs):
+        out_ref, sems = refs[len(flat) :]
+        copies = fetches(refs, blocks, out_ref, sems)
+        for copy in copies:
+            copy.start()
+        for copy in copies:
+            copy.wait()
+
+    return pl.pallas_call(
+        body,
+        in_specs=[pl.BlockSpec(memory_space=pl.ANY) for _ in flat],
+        out_specs=pl.BlockSpec(memory_space=pl.ANY),
+        scratch_shapes=[pltpu.SemaphoreType.DMA((len(flat),))],
+        out_shape=jax.ShapeDtypeStruct((depth, width), bf16),
+        compiler_params=params(8),
+        name="join",
+    )(*flat)
+
+
 def combine(ids, rows, blocks):
     groups, count, depth = rows.shape
     width = blocks[0][0].shape[1]
     flat = [w for column in blocks for w in column]
-    half = len(flat) // 2
 
     def body(ids_ref, rows_ref, *refs):
         out_ref, weight_ref, sems = refs[len(flat) :]
@@ -221,12 +244,18 @@
         for copy in copies:
             copy.start()
         lhs = rows_ref[...].reshape(groups * count, depth)
+        n = 0
         for k in range(2):
-            for copy in copies[k * half : (k + 1) * half]:
-                copy.wait()
-            total = jnp.dot(
-                lhs, weight_ref[:, k * width : (k + 1) * width], preferred_element_type=f32
-            )
+            total, top = 0.0, 0
+            for w in blocks[k]:
+                end = top + w.shape[0]
+                copies[n].wait()
+                total += jnp.dot(
+                    lhs[:, top:end],
+                    weight_ref[top:end, k * width : (k + 1) * width],
+                    preferred_element_type=f32,
+                )
+                n, top = n + 1, end
             at = lax.rem(ids_ref[1] + k, 2)
             out_ref[:, at] = total.astype(bf16).reshape(groups, count, width)
 
@@ -290,7 +319,7 @@
             scratch_shapes=[pltpu.VMEM((every, depth), bf16)],
         ),
         out_shape=jax.ShapeDtypeStruct((chunks, halves, count, columns + 128), bf16),
-        compiler_params=params(40),
+        compiler_params=params(51),
         name="widen",
     )(ids, rows, weight)
 
@@ -393,19 +422,14 @@
     parts = exchange(combine(ids, gathered, out_weights), ZY)
     parts, came, kept, residue = lax.optimization_barrier((parts, came, kept, residue))
     kept = [kept, swap(kept, "c")]
-    in_weight = jnp.concatenate(
-        [
-            jnp.concatenate([own, swap(own, "c") if k else kept[1]], axis=1)
-            for k, own in enumerate([kept[0]] + came)
-        ],
-        axis=0,
-    )
+    in_weight = join([[kept[0]] + came, [kept[1]] + [swap(w, "c") for w in came]])
     hidden = by_pair(*residue).astype(f32) + jnp.sum(parts.astype(f32), axis=0)
 
     rows = spread(hidden.astype(bf16), PAIR, 2 * N_ZY).reshape((2, N_ZY) + hidden.shape)
     near = swap(at_other(hidden), "xl")
-    near, in_weight = lax.optimization_barrier((near, in_weight))
-    rows, near = lax.optimization_barrier((rows, near))
+    hidden = by_pair(at_pair(hidden), near).reshape(chunk, -1)
+    hidden, in_weight = lax.optimization_barrier((hidden, in_weight))
+    rows, hidden = lax.optimization_barrier((rows, hidden))
     sums = exchange(widen(ids, rows, in_weight).reshape(N_DP, chunk, -1), DP)
     sums = jnp.sum(sums.reshape(2, 2, 2, chunk, -1).astype(f32), axis=(0, 2))
     squares = sums[0, :, 2 * units] + sums[0, :, 2 * units + 1]
@@ -413,7 +437,6 @@
     active = sums[:, :, : 2 * units] * inverse
     active = (jax.nn.silu(active[0]) * active[1]).astype(bf16)
     parts = exchange(project(ids, spread(active, DP, N_DP), downs, 1)[:, 0], ZY)
-    hidden = by_pair(at_pair(hidden), near).reshape(chunk, -1)
     result = (hidden + jnp.sum(parts.astype(f32), axis=0)).astype(bf16)
 
     result = result.reshape(2, 2, rows_out // 8, 2, steps, features)

time: 256 us -> 269 us (1.051)
  other arithmetic: 39.4 us -> 20.7 us
  waiting for transfers between devices: 45.8 us -> 64 us
  Pallas kernels: 31.2 us -> 37 us
    ppermute x13, waiting for transfers between devices: 21.6 us -> 44.8 us  [swap(): return lax.ppermute(block, axis, SWAP)]
    concatenate x1 -> x0, other arithmetic: 19.9 us -> none  [local(): jnp.concatenate([jnp.concatenate([own, swap(own, 'c') if k else kept[1]],...]
    all_to_all x6, waiting for transfers between devices: 24.2 us -> 19.2 us  [exchange(): return lax.all_to_all(blocks, axes, 0, 0, tiled=True)]
    pallas_call x1, Pallas kernels: 6.38 us -> 9.76 us  [widen(): pl.pallas_call(body, grid_spec=pltpu.PrefetchScalarGridSpec(num_scalar_pr...]
    all_to_all x6, starting transfers between devices: 36.7 us -> 39.5 us  [exchange(): return lax.all_to_all(blocks, axes, 0, 0, tiled=True)]
    unnamed x28 -> x32, local copies, waits for them, and re-layouts: 5.25 us -> 6.35 us
  transfers between devices with their start and end apart: 19 -> 19, of which waited for: 8 -> 8; matrix products, arithmetic and copies ran while one was open for 16% -> 8% of each run, Pallas kernels for 8% -> 9%
where the time goes in v12:
time: 269 us; the launch traced here: 268 us
  blocking collectives  82.1 us (31%)
  waiting for transfers between devices  64 us (24%)
  starting transfers between devices  51 us (19%)
  Pallas kernels  37 us (14%)
  other arithmetic  20.7 us (8%)
  local copies, waits for them, and re-layouts  9.92 us (4%)
  matrix products  3.23 us (1%)
    all_to_all x3, blocking collectives, exchange(): return lax.all_to_all(blocks, axes, 0, 0, tiled=True)  82.1 us
    ppermute x13, waiting for transfers between devices, swap(): return lax.ppermute(block, axis, SWAP)  44.8 us
    all_to_all x6, starting transfers between devices, exchange(): return lax.all_to_all(blocks, axes, 0, 0, tiled=True)  39.5 us
    all_to_all x6, waiting for transfers between devices, exchange(): return lax.all_to_all(blocks, axes, 0, 0, tiled=True)  19.2 us
    ppermute x13, starting transfers between devices, swap(): return lax.ppermute(block, axis, SWAP)  11.5 us
    pallas_call x1, Pallas kernels, widen(): pl.pallas_call(body, grid_spec=pltpu.PrefetchScalarGridSpec(num_scalar_pr...  9.76 us
    pallas_call x2, Pallas kernels, attend(): pl.pallas_call(body, grid_spec=pltpu.PrefetchScalarGridSpec(num_scalar_pr...  9.73 us
    convert_element_type x3, other arithmetic, scaled(): return (weight.astype(f32) * gain[low:high]).astype(bf16)  9.33 us
  transfers between devices with their start and end apart: 19, of which 8 were waited for; matrix products, arithmetic and copies ran while one was open for 8% of the time, Pallas kernels for 9%

profile of v12, /device:TPU:1, one launch (start us, length us, event | category | flops | bytes accessed | tf_op | source)
XLA Modules:
  0.0 268.3 jit_solution(2976510854749906107)
XLA Ops:
  0.0 2.1 collective-permute-start.1
  2.2 2.4 leave.1
  4.5 8.8 %all-to-all-start = ((bf16[16,36,256]{2,1,0:T(8,128)(2,1)}), bf16[16,36,256]{2,1,0:T(8,128)(2,1)S(1)}, u32[]{:S(2)}, u32[]{:S(2)}) async-start(bf16[16,36,256]{2,1,0:T(8,128)(2,1)} %leave.1), calls=%async_computation | async-start | bytes 655360 | tf_op jit(solution)/shard_map/all_to_all | solution.py:28
  13.5 1.1 copy.50
  14.6 0.7 fusion.12
  15.3 1.4 pad_add_fusion.ids_ref
  16.7 6.3 %attend.1.refs_1_ = bf16[8,2,2,32,512]{4,3,2,1,0:T(8,128)(2,1)} custom-call(s32[2]{0:T(128)} %pad_add_fusion.ids_ref, s32[4]{0:T(128)} %lengths_ref.3, bf16[4,576,2]{2,1,0:T(8,128)(2,1)} %bitcast.67, bf16[2,4,576,128]{3,2,1,0:T(8,128)(2,1)} %bitcast.69, bf16[4,576,256]{2,1,0:T(8,128)(2,1)} %bitcast.72), custom_call_target="tpu_custom_call" | custom-call | tf_op jit(solution)/shard_map/attend/pallas_call | solution.py:140
  23.0 1.3 route.1
  24.3 7.3 %all-to-all-start.1 = ((bf16[16,36,256]{2,1,0:T(8,128)(2,1)}), bf16[16,36,256]{2,1,0:T(8,128)(2,1)S(1)}, u32[]{:S(2)}, u32[]{:S(2)}) async-start(bf16[16,36,256]{2,1,0:T(8,128)(2,1)} %route.1), calls=%async_computation.1 | async-start | bytes 655360 | tf_op jit(solution)/shard_map/all_to_all | solution.py:28
  31.6 3.5 %multiply_convert_fusion.refs_0_ = bf16[896,1152]{1,0:T(8,128)(2,1)} fusion(f32[896]{0:T(1024)S(1)} %convert_element_type.61, bf16[896,1152]{1,0:T(8,128)(2,1)} %param.23, bf16[896,1152]{1,0:T(8,128)(2,1)} %param.24, pred[]{:T(512)S(6)} %eq.17), kind=kLoop, calls=%fused_computation.2 | loop fusion | flops 4128768 | bytes 6196737 | tf_op jit(solution)/shard_map/convert_element_type | solution.py:375
  35.1 2.6 multiply_convert_fusion.2
  37.8 2.7 %pad_maximum_fusion.1 = bf16[16,512,128]{2,1,0:T(8,128)(2,1)} fusion(bf16[8,512,128]{2,1,0:T(8,128)(2,1)} %collective-permute-done, bf16[8,512,128]{2,1,0:T(8,128)(2,1)S(1)} %copy-done.11), kind=kLoop, calls=%fused_computation.4 | loop fusion | flops 1048576 | bytes 4194304 | tf_op jit(solution)/shard_map/concatenate | solution.py:363
  40.8 0.7 copy-done.10
  41.5 3.4 %again.1 = bf16[8,2,2,32,512]{4,3,2,1,0:T(8,128)(2,1)} custom-call(s32[2]{0:T(128)} %pad_add_fusion.ids_ref, s32[4]{0:T(128)} %lengths_ref.3, bf16[4,576,2]{2,1,0:T(8,128)(2,1)} %bitcast.68, bf16[2,4,576,128]{3,2,1,0:T(8,128)(2,1)} %bitcast.70, bf16[16,36,256]{2,1,0:T(8,128)(2,1)} %copy-done.10, ...), custom_call_target="tpu_custom_call", output_to_operand_aliasing={{}: (5, {})} | custom-call | tf_op jit(solution)/shard_map/again/pallas_call | solution.py:140
  44.9 1.0 collective-permute-start.3
  45.9 0.5 collective-permute-start.5
  46.4 0.4 collective-permute-start.2
  46.8 6.7 %all-to-all-start.2 = ((bf16[16,2,32,512]{3,2,1,0:T(8,128)(2,1)}), bf16[16,2,32,512]{3,2,1,0:T(8,128)(2,1)}, u32[]{:S(2)}, u32[]{:S(2)}) async-start(bf16[16,2,32,512]{3,2,1,0:T(8,128)(2,1)} %bitcast.66), calls=%async_computation.2 | async-start | bytes 2097152 | tf_op jit(solution)/shard_map/all_to_all | solution.py:28
  53.5 3.2 %multiply_convert_fusion.1 = bf16[512,1152]{1,0:T(8,128)(2,1)} fusion(f32[512]{0:T(512)S(1)} %slice.40, bf16[896,1152]{1,0:T(8,128)(2,1)} %param.23, bf16[896,1152]{1,0:T(8,128)(2,1)} %param.24, pred[]{:T(512)S(6)} %eq.17), kind=kLoop, calls=%fused_computation.3 | loop fusion | flops 2359296 | bytes 3540993 | tf_op jit(solution)/shard_map/convert_element_type | solution.py:375
  57.5 3.9 %pad_maximum_fusion.weight_ref = bf16[2304,896]{1,0:T(8,128)(2,1)} fusion(bf16[1152,896]{1,0:T(8,128)(2,1)} %collective-permute-done.4, bf16[1152,896]{1,0:T(8,128)(2,1)S(1)} %copy-done.9), kind=kLoop, calls=%fused_computation.1 | loop fusion | flops 8257536 | bytes 8257536 | tf_op jit(solution)/shard_map/concatenate | solution.py:396
  61.3 6.5 %collective-permute-done.2.refs_1_ = bf16[384,1152]{1,0:T(8,128)(2,1)S(1)} collective-permute-done((bf16[384,1152]{1,0:T(8,128)(2,1)}, bf16[384,1152]{1,0:T(8,128)(2,1)S(1)}, u32[]{:S(2)}, u32[]{:S(2)}) %collective-permute-start.2) | collective-permute-done | bytes 884768 | tf_op jit(solution)/shard_map/ppermute | solution.py:36
  67.9 3.1 %all-to-all-done.2 = bf16[16,2,32,512]{3,2,1,0:T(8,128)(2,1)} async-done(((bf16[16,2,32,512]{3,2,1,0:T(8,128)(2,1)}), bf16[16,2,32,512]{3,2,1,0:T(8,128)(2,1)}, u32[]{:S(2)}, u32[]{:S(2)}) %all-to-all-start.2) | async-done | bytes 1048608 | tf_op jit(solution)/shard_map/all_to_all | solution.py:28
  71.0 3.2 %fusion = bf16[64,16,128]{2,0,1:T(8,128)(2,1)S(1)} fusion(bf16[16,512,128]{2,1,0:T(8,128)(2,1)} %pad_maximum_fusion.1, bf16[64,16,512]{2,1,0:T(8,128)(2,1)} %bitcast.8), kind=kOutput, calls=%fused_computation.10 | convolution fusion | flops 134348800 | bytes 3407872 | tf_op jit(solution)/shard_map/thl,hlv->thv/dot_general | solution.py:409
  74.7 18.3 %all_to_all.45.rows_ref = bf16[8,32,2048]{2,1,0:T(8,128)(2,1)} all-to-all(bf16[8,32,2048]{2,1,0:T(8,128)(2,1)S(1)} %bitcast.73), channel_id=1, replica_groups=mesh['xh'=2,'xl'=2,'zl'=2,'zh'=2,'y'=4,'c'=2] {'xh','xl','zl'}, dimensions={0} | all-to-all | bytes 2097152 | tf_op jit(solution)/shard_map/all_to_all | solution.py:28
  93.2 7.8 %combine.1 = bf16[8,2,32,896]{3,2,1,0:T(8,128)(2,1)} custom-call(s32[2]{0:T(128)} %pad_add_fusion.ids_ref, bf16[8,32,2048]{2,1,0:T(8,128)(2,1)} %all_to_all.45.rows_ref, bf16[1024,896]{1,0:T(8,128)(2,1)} %refs_0_, bf16[1024,896]{1,0:T(8,128)(2,1)} %collective-permute-done.3.refs_1_, bf16[1024,896]{1,0:T(8,128)(2,1)} %collective-permute-done.1.refs_2_, ...), custom_call_target="tpu_custom_call" | custom-call | tf_op jit(solution)/shard_map/combine/pallas_call | solution.py:262
  101.0 4.2 %all-to-all-start.4 = ((bf16[8,2,32,896]{3,2,1,0:T(8,128)(2,1)}), bf16[8,2,32,896]{3,2,1,0:T(8,128)(2,1)}, u32[]{:S(2)}, u32[]{:S(2)}) async-start(bf16[8,2,32,896]{3,2,1,0:T(8,128)(2,1)} %combine.1), calls=%async_computation.4 | async-start | bytes 1835008 | tf_op jit(solution)/shard_map/all_to_all | solution.py:28
  105.3 1.4 collective-permute-start.7
  106.7 13.3 %collective-permute-done.7 = bf16[32,896]{1,0:T(8,128)(2,1)S(1)} collective-permute-done((bf16[32,896]{1,0:T(8,128)(2,1)S(1)}, bf16[32,896]{1,0:T(8,128)(2,1)S(1)}, u32[]{:S(2)}, u32[]{:S(2)}) %collective-permute-start.7) | collective-permute-done | bytes 57376 | tf_op jit(solution)/shard_map/ppermute | solution.py:36
  120.0 1.3 all-to-all-done.4
  121.2 1.7 collective-permute-start.9
  122.9 1.3 convert_reduce_fusion.2
  124.3 1.5 broadcast_in_dim.29
  125.8 4.4 %all-to-all-start.5 = ((bf16[16,2,32,896]{3,2,1,0:T(8,128)(2,1)}), bf16[16,2,32,896]{3,2,1,0:T(8,128)(2,1)}, u32[]{:S(2)}, u32[]{:S(2)}) async-start(bf16[16,2,32,896]{3,2,1,0:T(8,128)(2,1)} %broadcast_in_dim.29), calls=%async_computation.5 | async-start | bytes 3670016 | tf_op jit(solution)/shard_map/all_to_all | solution.py:28
  130.3 0.5 collective-permute-start.10
  130.8 1.2 collective-permute-start.8
  132.0 24.0 %collective-permute-done.8 = f32[32,896]{1,0:T(8,128)S(1)} collective-permute-done((f32[32,896]{1,0:T(8,128)S(1)}, f32[32,896]{1,0:T(8,128)S(1)}, u32[]{:S(2)}, u32[]{:S(2)}) %collective-permute-start.8) | collective-permute-done | bytes 114720 | tf_op jit(solution)/shard_map/ppermute | solution.py:36
  156.2 1.2 copy-done.6
  157.3 2.0 join.1.weight_ref
  159.3 3.3 %copy-done.2 = bf16[1792,2304]{1,0:T(8,128)(2,1)} copy-done((bf16[1792,2304]{1,0:T(8,128)(2,1)}, bf16[1792,2304]{1,0:T(8,128)(2,1)S(1)}, u32[]{:S(2)}) %copy-start.2) | copy-done | bytes 8257560
  162.6 9.8 %widen.1 = bf16[8,2,32,2432]{3,2,1,0:T(8,128)(2,1)} custom-call(s32[2]{0:T(128)S(1)} %copy-done.7, bf16[2,8,2,32,896]{4,3,2,1,0:T(8,128)(2,1)} %bitcast.20.rows_ref, bf16[1792,2304]{1,0:T(8,128)(2,1)} %copy-done.2), custom_call_target="tpu_custom_call" | custom-call | tf_op jit(solution)/shard_map/widen/pallas_call | solution.py:309
  172.3 33.7 %all_to_all.46 = bf16[8,64,2432]{2,1,0:T(8,128)(2,1)S(1)} all-to-all(bf16[8,64,2432]{2,1,0:T(8,128)(2,1)} %bitcast.64), channel_id=1, replica_groups=mesh['xh'=2,'xl'=2,'zl'=2,'zh'=2,'y'=4,'c'=2] {'xh','xl','zl'}, dimensions={0} | all-to-all | bytes 4980736 | tf_op jit(solution)/shard_map/all_to_all | solution.py:28
  207.1 30.0 %all_to_all.47.rows_ref = bf16[8,64,2304]{2,1,0:T(8,128)(2,1)S(1)} all-to-all(bf16[8,64,2304]{2,1,0:T(8,128)(2,1)S(1)} %broadcast_in_dim.31), channel_id=1, replica_groups=mesh['xh'=2,'xl'=2,'zl'=2,'zh'=2,'y'=4,'c'=2] {'xh','xl','zl'}, dimensions={0} | all-to-all | bytes 4718592 | tf_op jit(solution)/shard_map/all_to_all | solution.py:28
  237.1 4.1 %project.1 = bf16[8,1,64,896]{3,2,1,0:T(8,128)(2,1)} custom-call(s32[2]{0:T(128)S(1)} %copy-done.7, bf16[8,64,2304]{2,1,0:T(8,128)(2,1)S(1)} %all_to_all.47.rows_ref, bf16[2304,896]{1,0:T(8,128)(2,1)S(1)} %copy-done.3), custom_call_target="tpu_custom_call" | custom-call | tf_op jit(solution)/shard_map/project/pallas_call | solution.py:181
  241.2 8.1 %all-to-all-start.8 = ((bf16[8,64,896]{2,1,0:T(8,128)(2,1)}), bf16[8,64,896]{2,1,0:T(8,128)(2,1)S(1)}, u32[]{:S(2)}, u32[]{:S(2)}) async-start(bf16[8,64,896]{2,1,0:T(8,128)(2,1)} %bitcast.29), calls=%async_computation.8 | async-start | bytes 1835008 | tf_op jit(solution)/shard_map/all_to_all | solution.py:28
  249.2 14.6 %all-to-all-done.8 = bf16[8,64,896]{2,1,0:T(8,128)(2,1)S(1)} async-done(((bf16[8,64,896]{2,1,0:T(8,128)(2,1)}), bf16[8,64,896]{2,1,0:T(8,128)(2,1)S(1)}, u32[]{:S(2)}, u32[]{:S(2)}) %all-to-all-start.8) | async-done | bytes 917536 | tf_op jit(solution)/shard_map/all_to_all | solution.py:28
  264.1 2.2 collective-permute-start.12
  266.3 0.9 collective-permute-done.12
  267.6 0.7 copy.58
  (73 shorter events, 3.7 us)
Async XLA Ops:
  0.0 56.7 %copy-start = (bf16[2,512,896]{2,1,0:T(8,128)(2,1)S(1)}, bf16[2,512,896]{2,1,0:T(8,128)(2,1)}, u32[]{:S(2)}) copy-start(bf16[2,512,896]{2,1,0:T(8,128)(2,1)} %param.21) | copy-start | bytes 5505028
  0.0 14.6 %copy-start.14 = (s32[1,16]{1,0:T(1,128)S(1)}, s32[1,16]{1,0:T(1,128)}, u32[]{:S(2)}) copy-start(s32[1,16]{1,0:T(1,128)} %param.15) | copy-start | bytes 196
  0.0 13.3 %copy-start.11 = (bf16[8,512,128]{2,1,0:T(8,128)(2,1)S(1)}, bf16[8,512,128]{2,1,0:T(8,128)(2,1)}, u32[]{:S(2)}) copy-start(bf16[8,512,128]{2,1,0:T(8,128)(2,1)} %param.19) | copy-start | bytes 3145732
  0.0 13.5 %copy-start.12 = (bf16[896]{0:T(1024)(128)(2,1)S(1)}, bf16[896]{0:T(1024)(128)(2,1)}, u32[]{:S(2)}) copy-start(bf16[896]{0:T(1024)(128)(2,1)} %param.22) | copy-start | bytes 5380
  0.0 13.5 %copy-start.13 = (bf16[2,4,576]{2,1,0:T(4,128)(2,1)S(1)}, bf16[2,4,576]{2,1,0:T(4,128)(2,1)}, u32[]{:S(2)}) copy-start(bf16[2,4,576]{2,1,0:T(4,128)(2,1)} %param.18) | copy-start | bytes 27652
  0.0 44.9 %collective-permute-start.1 = (bf16[1024,896]{1,0:T(8,128)(2,1)}, bf16[1024,896]{1,0:T(8,128)(2,1)}, u32[]{:S(2)}, u32[]{:S(2)}) collective-permute-start(bf16[1024,896]{1,0:T(8,128)(2,1)} %refs_0_), channel_id=1, source_target_pairs={{0,32},{32,0},{1,33},{33,1},{2,34},{34,2},{3,35},{35,3},{4,36},{36... | collective-permute-start | bytes 5505032 | tf_op jit(solution)/shard_map/ppermute | solution.py:36
  4.5 18.5 %all-to-all-start = ((bf16[16,36,256]{2,1,0:T(8,128)(2,1)}), bf16[16,36,256]{2,1,0:T(8,128)(2,1)S(1)}, u32[]{:S(2)}, u32[]{:S(2)}) async-start(bf16[16,36,256]{2,1,0:T(8,128)(2,1)} %leave.1), calls=%async_computation | async-start | bytes 655360 | tf_op jit(solution)/shard_map/all_to_all | solution.py:28
  13.3 24.5 %collective-permute-start = (bf16[8,512,128]{2,1,0:T(8,128)(2,1)S(1)}, bf16[8,512,128]{2,1,0:T(8,128)(2,1)}, u32[]{:S(2)}, u32[]{:S(2)}) collective-permute-start(bf16[8,512,128]{2,1,0:T(8,128)(2,1)S(1)} %copy-done.11), channel_id=1, source_target_pairs={{0,1},{1,0},{2,3},{3,2},{4,5},{5,4},{6,7},{7,6},{8,9},{9,8},{10,11... | collective-permute-start | bytes 3145736 | tf_op jit(solution)/shard_map/ppermute | solution.py:36
  14.6 8.4 %copy-start.8 = (s32[1,16]{1,0:T(1,128)S(1)}, s32[1,16]{1,0:T(1,128)}, u32[]{:S(2)}) copy-start(s32[1,16]{1,0:T(1,128)} %param.16) | copy-start | bytes 196
  24.3 16.4 %all-to-all-start.1 = ((bf16[16,36,256]{2,1,0:T(8,128)(2,1)}), bf16[16,36,256]{2,1,0:T(8,128)(2,1)S(1)}, u32[]{:S(2)}, u32[]{:S(2)}) async-start(bf16[16,36,256]{2,1,0:T(8,128)(2,1)} %route.1), calls=%async_computation.1 | async-start | bytes 655360 | tf_op jit(solution)/shard_map/all_to_all | solution.py:28
  40.7 0.7 copy-start.10
  44.9 8.6 %collective-permute-start.3 = (bf16[1024,896]{1,0:T(8,128)(2,1)}, bf16[1024,896]{1,0:T(8,128)(2,1)}, u32[]{:S(2)}, u32[]{:S(2)}) collective-permute-start(bf16[1024,896]{1,0:T(8,128)(2,1)} %refs_0_), channel_id=1, source_target_pairs={{0,1},{1,0},{2,3},{3,2},{4,5},{5,4},{6,7},{7,6},{8,9},{9,8},{10,11... | collective-permute-start | bytes 5505032 | tf_op jit(solution)/shard_map/ppermute | solution.py:36
  45.9 11.6 %collective-permute-start.4 = (bf16[1152,896]{1,0:T(8,128)(2,1)}, bf16[1152,896]{1,0:T(8,128)(2,1)}, u32[]{:S(2)}, u32[]{:S(2)}) collective-permute-start(bf16[1152,896]{1,0:T(8,128)(2,1)} %param.25), channel_id=1, source_target_pairs={{0,1},{1,0},{2,3},{3,2},{4,5},{5,4},{6,7},{7,6},{8,9},{9,8},{10,11... | collective-permute-start | bytes 6193160 | tf_op jit(solution)/shard_map/ppermute | solution.py:36
  45.9 25.1 %collective-permute-start.5 = (bf16[1024,896]{1,0:T(8,128)(2,1)}, bf16[1024,896]{1,0:T(8,128)(2,1)}, u32[]{:S(2)}, u32[]{:S(2)}) collective-permute-start(bf16[1024,896]{1,0:T(8,128)(2,1)} %collective-permute-done.1.refs_2_), channel_id=1, source_target_pairs={{0,1},{1,0},{2,3},{3,2},{4,5},{5,4},{6,7},{7,6},{8,9},{9,8},{10,11... | collective-permute-start | bytes 5505032 | tf_op jit(solution)/shard_map/ppermute | solution.py:36
  46.4 21.5 %collective-permute-start.2 = (bf16[384,1152]{1,0:T(8,128)(2,1)}, bf16[384,1152]{1,0:T(8,128)(2,1)S(1)}, u32[]{:S(2)}, u32[]{:S(2)}) collective-permute-start(bf16[384,1152]{1,0:T(8,128)(2,1)} %multiply_convert_fusion.2), channel_id=1, source_target_pairs={{0,32},{32,0},{1,33},{33,1},{2,34},{34,2},{3,35},{35,3},{4,36},{36... | collective-permute-start | bytes 2654216 | tf_op jit(solution)/shard_map/ppermute | solution.py:36
  46.8 24.2 %all-to-all-start.2 = ((bf16[16,2,32,512]{3,2,1,0:T(8,128)(2,1)}), bf16[16,2,32,512]{3,2,1,0:T(8,128)(2,1)}, u32[]{:S(2)}, u32[]{:S(2)}) async-start(bf16[16,2,32,512]{3,2,1,0:T(8,128)(2,1)} %bitcast.66), calls=%async_computation.2 | async-start | bytes 2097152 | tf_op jit(solution)/shard_map/all_to_all | solution.py:28
  53.5 4.0 %copy-start.9 = (bf16[1152,896]{1,0:T(8,128)(2,1)S(1)}, bf16[1152,896]{1,0:T(8,128)(2,1)}, u32[]{:S(2)}) copy-start(bf16[1152,896]{1,0:T(8,128)(2,1)} %param.25) | copy-start | bytes 6193156
  67.9 6.8 %copy-start.5 = (bf16[384,1152]{1,0:T(8,128)(2,1)}, bf16[384,1152]{1,0:T(8,128)(2,1)S(1)}, u32[]{:S(2)}) copy-start(bf16[384,1152]{1,0:T(8,128)(2,1)S(1)} %collective-permute-done.2.refs_1_) | copy-start | bytes 2654212
  93.0 28.2 %copy-start.4 = (bf16[896,1152]{1,0:T(8,128)(2,1)S(1)}, bf16[896,1152]{1,0:T(8,128)(2,1)}, u32[]{:S(2)}) copy-start(bf16[896,1152]{1,0:T(8,128)(2,1)} %multiply_convert_fusion.refs_0_) | copy-start | bytes 6193156
  93.0 28.2 %collective-permute-start.6 = (bf16[512,1152]{1,0:T(8,128)(2,1)}, bf16[512,1152]{1,0:T(8,128)(2,1)S(1)}, u32[]{:S(2)}, u32[]{:S(2)}) collective-permute-start(bf16[512,1152]{1,0:T(8,128)(2,1)} %multiply_convert_fusion.1), channel_id=1, source_target_pairs={{0,32},{32,0},{1,33},{33,1},{2,34},{34,2},{3,35},{35,3},{4,36},{36... | collective-permute-start | bytes 3538952 | tf_op jit(solution)/shard_map/ppermute | solution.py:36
  101.0 20.2 %all-to-all-start.4 = ((bf16[8,2,32,896]{3,2,1,0:T(8,128)(2,1)}), bf16[8,2,32,896]{3,2,1,0:T(8,128)(2,1)}, u32[]{:S(2)}, u32[]{:S(2)}) async-start(bf16[8,2,32,896]{3,2,1,0:T(8,128)(2,1)} %combine.1), calls=%async_computation.4 | async-start | bytes 1835008 | tf_op jit(solution)/shard_map/all_to_all | solution.py:28
  105.3 14.7 %collective-permute-start.7 = (bf16[32,896]{1,0:T(8,128)(2,1)S(1)}, bf16[32,896]{1,0:T(8,128)(2,1)S(1)}, u32[]{:S(2)}, u32[]{:S(2)}) collective-permute-start(bf16[32,896]{1,0:T(8,128)(2,1)S(1)} %get-tuple-element.75), channel_id=1, source_target_pairs={{0,32},{32,0},{1,33},{33,1},{2,34},{34,2},{3,35},{35,3},{4,36},{36... | collective-permute-start | bytes 172040 | tf_op jit(solution)/shard_map/ppermute | solution.py:36
  121.2 34.9 %collective-permute-start.9 = (bf16[896,1152]{1,0:T(8,128)(2,1)S(1)}, bf16[896,1152]{1,0:T(8,128)(2,1)}, u32[]{:S(2)}, u32[]{:S(2)}) collective-permute-start(bf16[896,1152]{1,0:T(8,128)(2,1)S(1)} %copy-done.4), channel_id=1, source_target_pairs={{0,1},{1,0},{2,3},{3,2},{4,5},{5,4},{6,7},{7,6},{8,9},{9,8},{10,11... | collective-permute-start | bytes 6193160 | tf_op jit(solution)/shard_map/ppermute | solution.py:36
  125.8 36.8 %all-to-all-start.5 = ((bf16[16,2,32,896]{3,2,1,0:T(8,128)(2,1)}), bf16[16,2,32,896]{3,2,1,0:T(8,128)(2,1)}, u32[]{:S(2)}, u32[]{:S(2)}) async-start(bf16[16,2,32,896]{3,2,1,0:T(8,128)(2,1)} %broadcast_in_dim.29), calls=%async_computation.5 | async-start | bytes 3670016 | tf_op jit(solution)/shard_map/all_to_all | solution.py:28
  130.2 25.9 %collective-permute-start.11 = (bf16[512,1152]{1,0:T(8,128)(2,1)S(1)}, bf16[512,1152]{1,0:T(8,128)(2,1)S(1)}, u32[]{:S(2)}, u32[]{:S(2)}) collective-permute-start(bf16[512,1152]{1,0:T(8,128)(2,1)S(1)} %collective-permute-done.6.refs_2_), channel_id=1, source_target_pairs={{0,1},{1,0},{2,3},{3,2},{4,5},{5,4},{6,7},{7,6},{8,9},{9,8},{10,11... | collective-permute-start | bytes 3538952 | tf_op jit(solution)/shard_map/ppermute | solution.py:36
  130.3 25.8 %collective-permute-start.10 = (bf16[384,1152]{1,0:T(8,128)(2,1)}, bf16[384,1152]{1,0:T(8,128)(2,1)S(1)}, u32[]{:S(2)}, u32[]{:S(2)}) collective-permute-start(bf16[384,1152]{1,0:T(8,128)(2,1)} %copy-done.5), channel_id=1, source_target_pairs={{0,1},{1,0},{2,3},{3,2},{4,5},{5,4},{6,7},{7,6},{8,9},{9,8},{10,11... | collective-permute-start | bytes 2654216 | tf_op jit(solution)/shard_map/ppermute | solution.py:36
  130.8 25.3 %collective-permute-start.8 = (f32[32,896]{1,0:T(8,128)S(1)}, f32[32,896]{1,0:T(8,128)S(1)}, u32[]{:S(2)}, u32[]{:S(2)}) collective-permute-start(f32[32,896]{1,0:T(8,128)S(1)} %dynamic-slice_bitcast_fusion), channel_id=1, source_target_pairs={{0,32},{32,0},{1,33},{33,1},{2,34},{34,2},{3,35},{35,3},{4,36},{36... | collective-permute-start | bytes 344072 | tf_op jit(solution)/shard_map/ppermute | solution.py:36
  156.1 6.5 %copy-start.7 = (s32[2]{0:T(128)S(1)}, s32[2]{0:T(128)}, u32[]{:S(2)}) copy-start(s32[2]{0:T(128)} %pad_add_fusion.ids_ref) | copy-start | bytes 28
  156.2 1.2 copy-start.6
  159.3 3.3 %copy-start.2 = (bf16[1792,2304]{1,0:T(8,128)(2,1)}, bf16[1792,2304]{1,0:T(8,128)(2,1)S(1)}, u32[]{:S(2)}) copy-start(bf16[1792,2304]{1,0:T(8,128)(2,1)S(1)} %join.1.weight_ref) | copy-start | bytes 24772612
  207.1 30.0 %copy-start.3 = (bf16[2304,896]{1,0:T(8,128)(2,1)S(1)}, bf16[2304,896]{1,0:T(8,128)(2,1)}, u32[]{:S(2)}) copy-start(bf16[2304,896]{1,0:T(8,128)(2,1)} %pad_maximum_fusion.weight_ref) | copy-start | bytes 12386308
  241.2 27.1 %copy-start.1 = (bf16[2,512,896]{2,1,0:T(8,128)(2,1)S(1)}, bf16[2,512,896]{2,1,0:T(8,128)(2,1)}, u32[]{:S(2)}) copy-start(bf16[2,512,896]{2,1,0:T(8,128)(2,1)} %param.21) | copy-start | bytes 5505028
  241.2 22.7 %all-to-all-start.8 = ((bf16[8,64,896]{2,1,0:T(8,128)(2,1)}), bf16[8,64,896]{2,1,0:T(8,128)(2,1)S(1)}, u32[]{:S(2)}, u32[]{:S(2)}) async-start(bf16[8,64,896]{2,1,0:T(8,128)(2,1)} %bitcast.29), calls=%async_computation.8 | async-start | bytes 1835008 | tf_op jit(solution)/shard_map/all_to_all | solution.py:28
  264.1 3.1 %collective-permute-start.12 = (bf16[2,4,2,2,896]{4,3,2,1,0:T(2,128)(2,1)S(1)}, bf16[2,4,2,2,896]{4,3,2,1,0:T(2,128)(2,1)S(1)}, u32[]{:S(2)}, u32[]{:S(2)}) collective-permute-start(bf16[2,4,2,2,896]{4,3,2,1,0:T(2,128)(2,1)S(1)} %dynamic-slice_bitcast_fusion.2), channel_id=1, source_target_pairs={{0,1},{1,0},{2,3},{3,2},{4,5},{5,4},{6,7},{7,6},{8,9},{9,8},{10,11... | collective-permute-start | bytes 172040 | tf_op jit(solution)/shard_map/ppermute | solution.py:36

commit v13 on v11

--- a/solution.py
+++ b/solution.py
@@ -46,7 +46,7 @@
 
 def leave(slots, cache_t):
     _, entries, length = cache_t.shape
-    piece = entries // N_TP
+    tall, wide = 2 * entries // N_TP, length // 2
 
     def body(slots_ref, cache_ref, out_ref, row_ref, sem):
         slot = slots_ref[lax.axis_index(TP)]
@@ -55,7 +55,8 @@
         copy.wait()
         row = row_ref[...].astype(f32)
         for j in range(N_TP):
-            out_ref[j] = row[j * piece : (j + 1) * piece].astype(bf16)
+            top, left = j // 2 * tall, j % 2 * wide
+            out_ref[j] = row[top : top + tall, left : left + wide].astype(bf16)
 
     return pl.pallas_call(
         body,
@@ -63,10 +64,10 @@
             num_scalar_prefetch=1,
             grid=(1,),
             in_specs=[pl.BlockSpec(memory_space=pl.ANY)],
-            out_specs=whole((N_TP, piece, length)),
+            out_specs=whole((N_TP, tall, wide)),
             scratch_shapes=[pltpu.VMEM((entries, length), bf16), pltpu.SemaphoreType.DMA],
         ),
-        out_shape=jax.ShapeDtypeStruct((N_TP, piece, length), bf16),
+        out_shape=jax.ShapeDtypeStruct((N_TP, tall, wide), bf16),
         compiler_params=params(60),
         name="leave",
     )(slots, cache_t)
@@ -105,7 +106,11 @@
         row = slot(pl.program_id(0), ids_ref)
         current = lengths_ref[row]
         if again:
-            latents = jnp.concatenate([refs[0][j].astype(f32) for j in range(N_TP)], axis=0)
+            latents = [
+                jnp.concatenate([refs[0][j + b].astype(f32) for b in range(2)], axis=1)
+                for j in range(0, N_TP, 2)
+            ]
+            latents = jnp.concatenate(latents, axis=0)
         else:
             latents = refs[0][0].astype(f32)
         position = lax.broadcasted_iota(jnp.int32, (entries, length), 1)
@@ -331,13 +336,18 @@
         return lax.dynamic_index_in_dim(blocks, 1 - pair, 0, False)
 
     out_came = swap(out_proj, "xl")
-    value_ups = jnp.concatenate([value_up, swap(value_up, "c")], axis=0)
+    value_near = swap(value_up, "c")
     lanes = jnp.arange(N_TP, dtype=jnp.int32)
-    own_slot = jnp.sum(jnp.where(lanes == member, move_slot[0], 0))
-    ids = jnp.stack([own_slot, pair]).astype(jnp.int32)
     cache_t = cache.transpose(0, 2, 1)
     pieces = exchange(leave(move_slot[0], cache_t), TP)
-    pieces, gate_weight, up_weight = lax.optimization_barrier((pieces, gate_weight, up_weight))
+    fresh_t = new_latent.transpose(1, 2, 0)
+    queries_t = queries.transpose(0, 1, 3, 2)
+    out = attend(cache_length, cache_length, cache_t, fresh_t, queries_t, heads, latent_width)
+    pieces, out, gate_weight, up_weight, slots = lax.optimization_barrier(
+        (pieces, out, gate_weight, up_weight, move_slot[0])
+    )
+    own_slot = jnp.sum(jnp.where(lanes == member, slots, 0))
+    ids = jnp.stack([own_slot, pair]).astype(jnp.int32)
 
     gain = norm_gain.astype(f32)[:, None]
 
@@ -348,10 +358,9 @@
     kept = scaled(0, features, gate_weight, up_weight)
     sent = scaled(0, CUT, up_weight, gate_weight)
     arrived = exchange(route(move_peer[0], pieces), TP)
-    arrived, kept, sent, value_ups = lax.optimization_barrier((arrived, kept, sent, value_ups))
-    fresh_t = new_latent.transpose(1, 2, 0)
-    queries_t = queries.transpose(0, 1, 3, 2)
-    out = attend(ids, cache_length, cache_t, fresh_t, queries_t, heads, latent_width)
+    arrived, kept, sent, ids, value_near = lax.optimization_barrier(
+        (arrived, kept, sent, ids, value_near)
+    )
     out = attend(
         ids, cache_length, cache_t, fresh_t, queries_t, heads, latent_width, arrived, out
     )
@@ -365,17 +374,18 @@
     by_head = exchange(out, TP).reshape(-1, 2 * heads, latent_width)
 
     downs = jnp.concatenate([down_weight, swap(down_weight, "c")], axis=0)
-    out_weights[0][1], gate_weight, up_weight, residual = lax.optimization_barrier(
-        (out_near, gate_weight, up_weight, residual)
-    )
+    out_weights[0][1], gate_weight, up_weight, residual, value_near = lax.optimization_barrier(
+        (out_near, gate_weight, up_weight, residual, value_near)
+    )
+    value_ups = jnp.concatenate([value_up, value_near], axis=0)
     sent = scaled(CUT, features, up_weight, gate_weight)
     residue = lax.dynamic_slice_in_dim(residual, lax.div(member, 2) * 2 * rows_out, 2 * rows_out, 1)
     residue = residue.reshape(steps, 2, 2, rows_out // 8, 2, 2, features)
     residue = lax.dynamic_index_in_dim(residue, core, 4, False)
     residue = residue.transpose(2, 1, 3, 4, 0, 5).reshape(2, count, features)
     residue = [at_pair(residue), at_other(residue)]
-    by_head, kept, came, sent, downs, residue, out_weights = lax.optimization_barrier(
-        (by_head, kept, came, sent, downs, residue, out_weights)
+    by_head, kept, came, sent, downs, residue, out_weights, value_ups = lax.optimization_barrier(
+        (by_head, kept, came, sent, downs, residue, out_weights, value_ups)
     )
     value_heads = jnp.einsum(
         "thl,hlv->thv", by_head, value_ups, preferred_element_type=f32

time: 256 us -> 256 us (level)
    all_to_all x6, waiting for transfers between devices: 24.2 us -> 28.2 us  [exchange(): return lax.all_to_all(blocks, axes, 0, 0, tiled=True)]
    ppermute x13, waiting for transfers between devices: 21.6 us -> 17.7 us  [swap(): return lax.ppermute(block, axis, SWAP)]
  transfers between devices with their start and end apart: 19 -> 19, of which waited for: 8 -> 9; matrix products, arithmetic and copies ran while one was open for 16% -> 16% of each run, Pallas kernels for 8% -> 8%
where the time goes in v13:
time: 256 us; the launch traced here: 255 us
  blocking collectives  79.8 us (31%)
  starting transfers between devices  49.3 us (19%)
  waiting for transfers between devices  46 us (18%)
  other arithmetic  38 us (15%)
  Pallas kernels  31.4 us (12%)
  local copies, waits for them, and re-layouts  9.35 us (4%)
    all_to_all x3, blocking collectives, exchange(): return lax.all_to_all(blocks, axes, 0, 0, tiled=True)  79.8 us
    all_to_all x6, starting transfers between devices, exchange(): return lax.all_to_all(blocks, axes, 0, 0, tiled=True)  36.7 us
    all_to_all x6, waiting for transfers between devices, exchange(): return lax.all_to_all(blocks, axes, 0, 0, tiled=True)  28.2 us
    concatenate x1, other arithmetic, local(): jnp.concatenate([jnp.concatenate([own, swap(own, 'c') if k else kept[1]],...  19.9 us
    ppermute x13, waiting for transfers between devices, swap(): return lax.ppermute(block, axis, SWAP)  17.7 us
    ppermute x13, starting transfers between devices, swap(): return lax.ppermute(block, axis, SWAP)  12.6 us
    pallas_call x2, Pallas kernels, attend(): pl.pallas_call(body, grid_spec=pltpu.PrefetchScalarGridSpec(num_scalar_pr...  9.78 us
    convert_element_type x3, other arithmetic, scaled(): return (weight.astype(f32) * gain[low:high]).astype(bf16)  9.25 us
  transfers between devices with their start and end apart: 19, of which 9 were waited for; matrix products, arithmetic and copies ran while one was open for 16% of the time, Pallas kernels for 8%

profile of v13, /device:TPU:1, one launch (start us, length us, event | category | flops | bytes accessed | tf_op | source)
XLA Modules:
  0.0 255.4 jit_solution(6660494017207626291)
XLA Ops:
  0.0 2.1 collective-permute-start.1
  2.1 2.4 leave.1
  4.6 8.8 %all-to-all-start = ((bf16[16,72,128]{2,1,0:T(8,128)(2,1)}), bf16[16,72,128]{2,1,0:T(8,128)(2,1)S(1)}, u32[]{:S(2)}, u32[]{:S(2)}) async-start(bf16[16,72,128]{2,1,0:T(8,128)(2,1)} %leave.1), calls=%async_computation | async-start | bytes 589824 | tf_op jit(solution)/shard_map/all_to_all | solution.py:28
  13.5 1.1 copy.52
  14.6 6.4 %attend.1.refs_1_ = bf16[8,2,2,32,512]{4,3,2,1,0:T(8,128)(2,1)} custom-call(s32[4]{0:T(128)} %lengths_ref.3, s32[4]{0:T(128)} %lengths_ref.3, bf16[4,576,2]{2,1,0:T(8,128)(2,1)} %bitcast.58, bf16[2,4,576,128]{3,2,1,0:T(8,128)(2,1)} %bitcast.60, bf16[4,576,256]{2,1,0:T(8,128)(2,1)} %bitcast.63), custom_call_target="tpu_custom_call" | custom-call | tf_op jit(solution)/shard_map/attend/pallas_call | solution.py:145
  21.1 1.2 all-to-all-done.in_ref
  22.2 1.3 route.1
  23.5 6.1 %all-to-all-start.1 = ((bf16[16,72,128]{2,1,0:T(8,128)(2,1)}), bf16[16,72,128]{2,1,0:T(8,128)(2,1)S(1)}, u32[]{:S(2)}, u32[]{:S(2)}) async-start(bf16[16,72,128]{2,1,0:T(8,128)(2,1)} %route.1), calls=%async_computation.1 | async-start | bytes 589824 | tf_op jit(solution)/shard_map/all_to_all | solution.py:28
  29.7 3.5 %multiply_convert_fusion = bf16[896,1152]{1,0:T(8,128)(2,1)} fusion(f32[896]{0:T(1024)S(1)} %convert_element_type.62, bf16[896,1152]{1,0:T(8,128)(2,1)} %param.23, bf16[896,1152]{1,0:T(8,128)(2,1)} %param.24, pred[]{:T(512)S(6)} %eq.17), kind=kLoop, calls=%fused_computation.3 | loop fusion | flops 4128768 | bytes 6196737 | tf_op jit(solution)/shard_map/convert_element_type | solution.py:356
  33.2 2.6 %multiply_convert_fusion.2 = bf16[384,1152]{1,0:T(8,128)(2,1)} fusion(f32[384]{0:T(512)S(1)} %slice.37, bf16[896,1152]{1,0:T(8,128)(2,1)} %param.23, bf16[896,1152]{1,0:T(8,128)(2,1)} %param.24, pred[]{:T(512)S(6)} %eq.17), kind=kLoop, calls=%fused_computation.8 | loop fusion | flops 1769472 | bytes 2655745 | tf_op jit(solution)/shard_map/convert_element_type | solution.py:356
  35.8 0.7 fusion.11
  36.5 1.2 pad_add_fusion.ids_ref
  37.7 0.9 all-to-all-done.1.refs_0_
  38.6 0.7 copy-done.7
  39.3 3.4 %again.1 = bf16[8,2,2,32,512]{4,3,2,1,0:T(8,128)(2,1)} custom-call(s32[2]{0:T(128)} %pad_add_fusion.ids_ref, s32[4]{0:T(128)} %lengths_ref.3, bf16[4,576,2]{2,1,0:T(8,128)(2,1)} %bitcast.59, bf16[2,4,576,128]{3,2,1,0:T(8,128)(2,1)} %bitcast.61, bf16[16,72,128]{2,1,0:T(8,128)(2,1)} %copy-done.7, ...), custom_call_target="tpu_custom_call", output_to_operand_aliasing={{}: (5, {})} | custom-call | tf_op jit(solution)/shard_map/again/pallas_call | solution.py:145
  42.6 0.9 collective-permute-start.3
  43.5 0.5 collective-permute-start.5
  44.0 1.4 collective-permute-start.2
  45.4 8.1 %all-to-all-start.2 = ((bf16[16,2,32,512]{3,2,1,0:T(8,128)(2,1)}), bf16[16,2,32,512]{3,2,1,0:T(8,128)(2,1)S(1)}, u32[]{:S(2)}, u32[]{:S(2)}) async-start(bf16[16,2,32,512]{3,2,1,0:T(8,128)(2,1)} %bitcast.57), calls=%async_computation.2 | async-start | bytes 2097152 | tf_op jit(solution)/shard_map/all_to_all | solution.py:28
  54.0 3.1 %multiply_convert_fusion.1 = bf16[512,1152]{1,0:T(8,128)(2,1)} fusion(f32[512]{0:T(512)S(1)} %slice.40, bf16[896,1152]{1,0:T(8,128)(2,1)} %param.23, bf16[896,1152]{1,0:T(8,128)(2,1)} %param.24, pred[]{:T(512)S(6)} %eq.17), kind=kLoop, calls=%fused_computation.4 | loop fusion | flops 2359296 | bytes 3540993 | tf_op jit(solution)/shard_map/convert_element_type | solution.py:356
  57.3 1.6 pad_maximum_fusion.1
  59.2 3.9 %pad_maximum_fusion.weight_ref = bf16[2304,896]{1,0:T(8,128)(2,1)} fusion(bf16[1152,896]{1,0:T(8,128)(2,1)} %collective-permute-done.4, bf16[1152,896]{1,0:T(8,128)(2,1)S(1)} %copy-done.6), kind=kLoop, calls=%fused_computation.2 | loop fusion | flops 8257536 | bytes 8257536 | tf_op jit(solution)/shard_map/concatenate | solution.py:376
  63.1 2.5 collective-permute-done.2
  65.6 5.2 %all-to-all-done.2 = bf16[16,2,32,512]{3,2,1,0:T(8,128)(2,1)S(1)} async-done(((bf16[16,2,32,512]{3,2,1,0:T(8,128)(2,1)}), bf16[16,2,32,512]{3,2,1,0:T(8,128)(2,1)S(1)}, u32[]{:S(2)}, u32[]{:S(2)}) %all-to-all-start.2) | async-done | bytes 1048608 | tf_op jit(solution)/shard_map/all_to_all | solution.py:28
  70.8 1.3 fusion
  72.6 18.3 %all_to_all.45.rows_ref = bf16[8,32,2048]{2,1,0:T(8,128)(2,1)} all-to-all(bf16[8,32,2048]{2,1,0:T(8,128)(2,1)S(1)} %bitcast.64), channel_id=1, replica_groups=mesh['xh'=2,'xl'=2,'zl'=2,'zh'=2,'y'=4,'c'=2] {'xh','xl','zl'}, dimensions={0} | all-to-all | bytes 2097152 | tf_op jit(solution)/shard_map/all_to_all | solution.py:28
  91.2 7.4 %combine.1 = bf16[8,2,32,896]{3,2,1,0:T(8,128)(2,1)} custom-call(s32[2]{0:T(128)} %pad_add_fusion.ids_ref, bf16[8,32,2048]{2,1,0:T(8,128)(2,1)} %all_to_all.45.rows_ref, bf16[1024,896]{1,0:T(8,128)(2,1)} %refs_0_, bf16[1024,896]{1,0:T(8,128)(2,1)} %collective-permute-done.3.refs_1_, bf16[1024,896]{1,0:T(8,128)(2,1)} %collective-permute-done.1.refs_2_, ...), custom_call_target="tpu_custom_call" | custom-call | tf_op jit(solution)/shard_map/combine/pallas_call | solution.py:238
  98.6 3.6 %all-to-all-start.4 = ((bf16[8,2,32,896]{3,2,1,0:T(8,128)(2,1)}), bf16[8,2,32,896]{3,2,1,0:T(8,128)(2,1)S(1)}, u32[]{:S(2)}, u32[]{:S(2)}) async-start(bf16[8,2,32,896]{3,2,1,0:T(8,128)(2,1)} %combine.1), calls=%async_computation.4 | async-start | bytes 1835008 | tf_op jit(solution)/shard_map/all_to_all | solution.py:28
  102.2 1.3 collective-permute-start.7
  103.5 14.3 %collective-permute-done.7 = bf16[32,896]{1,0:T(8,128)(2,1)S(1)} collective-permute-done((bf16[32,896]{1,0:T(8,128)(2,1)S(1)}, bf16[32,896]{1,0:T(8,128)(2,1)S(1)}, u32[]{:S(2)}, u32[]{:S(2)}) %collective-permute-start.7) | collective-permute-done | bytes 57376 | tf_op jit(solution)/shard_map/ppermute | solution.py:36
  117.8 0.3 all-to-all-done.4
  118.1 2.6 %collective-permute-start.9 = (bf16[896,1152]{1,0:T(8,128)(2,1)}, bf16[896,1152]{1,0:T(8,128)(2,1)}, u32[]{:S(2)}, u32[]{:S(2)}) collective-permute-start(bf16[896,1152]{1,0:T(8,128)(2,1)} %multiply_convert_fusion), channel_id=1, source_target_pairs={{0,1},{1,0},{2,3},{3,2},{4,5},{5,4},{6,7},{7,6},{8,9},{9,8},{10,11... | collective-permute-start | bytes 6193160 | tf_op jit(solution)/shard_map/ppermute | solution.py:36
  121.5 0.3 collective-permute-start.8
  121.8 1.5 broadcast_in_dim.29
  123.3 4.7 %all-to-all-start.5 = ((bf16[16,2,32,896]{3,2,1,0:T(8,128)(2,1)}), bf16[16,2,32,896]{3,2,1,0:T(8,128)(2,1)S(1)}, u32[]{:S(2)}, u32[]{:S(2)}) async-start(bf16[16,2,32,896]{3,2,1,0:T(8,128)(2,1)} %broadcast_in_dim.29), calls=%async_computation.5 | async-start | bytes 3670016 | tf_op jit(solution)/shard_map/all_to_all | solution.py:28
  128.0 19.9 %maximum_maximum_fusion.weight_ref = bf16[1792,2304]{1,0:T(8,128)(2,1)} fusion(bf16[512,1152]{1,0:T(8,128)(2,1)} %collective-permute-done.11, bf16[512,1152]{1,0:T(8,128)(2,1)S(1)} %collective-permute-done.6, bf16[384,1152]{1,0:T(8,128)(2,1)} %collective-permute-done.10, bf16[384,1152]{1,0:T(8,128)(2,1)} %collective-permute-done.2, ...), kind=kLoop, calls=%fused_computation | loop fusion | flops 49545216 | bytes 16515072 | tf_op jit(solution)/shard_map/concatenate | solution.py:406
  147.9 6.5 %all-to-all-done.5 = bf16[16,2,32,896]{3,2,1,0:T(8,128)(2,1)S(1)} async-done(((bf16[16,2,32,896]{3,2,1,0:T(8,128)(2,1)}), bf16[16,2,32,896]{3,2,1,0:T(8,128)(2,1)S(1)}, u32[]{:S(2)}, u32[]{:S(2)}) %all-to-all-start.5) | async-done | bytes 1835040 | tf_op jit(solution)/shard_map/all_to_all | solution.py:28
  154.4 3.3 %copy-done.2 = bf16[1792,2304]{1,0:T(8,128)(2,1)S(1)} copy-done((bf16[1792,2304]{1,0:T(8,128)(2,1)S(1)}, bf16[1792,2304]{1,0:T(8,128)(2,1)}, u32[]{:S(2)}) %copy-start.2) | copy-done | bytes 8257560
  157.8 6.4 %widen.1 = bf16[8,2,32,2432]{3,2,1,0:T(8,128)(2,1)S(1)} custom-call(s32[2]{0:T(128)S(1)} %copy-done.4, bf16[2,8,2,32,896]{4,3,2,1,0:T(8,128)(2,1)S(1)} %bitcast.54, bf16[1792,2304]{1,0:T(8,128)(2,1)S(1)} %copy-done.2), custom_call_target="tpu_custom_call" | custom-call | tf_op jit(solution)/shard_map/widen/pallas_call | solution.py:285
  164.2 32.1 %all_to_all.46 = bf16[8,64,2432]{2,1,0:T(8,128)(2,1)S(1)} all-to-all(bf16[8,64,2432]{2,1,0:T(8,128)(2,1)S(1)} %bitcast.53), channel_id=1, replica_groups=mesh['xh'=2,'xl'=2,'zl'=2,'zh'=2,'y'=4,'c'=2] {'xh','xl','zl'}, dimensions={0} | all-to-all | bytes 4980736 | tf_op jit(solution)/shard_map/all_to_all | solution.py:28
  196.3 0.3 convert_reduce_fusion
  197.3 29.3 %all_to_all.47.rows_ref = bf16[8,64,2304]{2,1,0:T(8,128)(2,1)S(1)} all-to-all(bf16[8,64,2304]{2,1,0:T(8,128)(2,1)S(1)} %broadcast_in_dim.31), channel_id=1, replica_groups=mesh['xh'=2,'xl'=2,'zl'=2,'zh'=2,'y'=4,'c'=2] {'xh','xl','zl'}, dimensions={0} | all-to-all | bytes 4718592 | tf_op jit(solution)/shard_map/all_to_all | solution.py:28
  226.6 4.1 %project.1 = bf16[8,1,64,896]{3,2,1,0:T(8,128)(2,1)} custom-call(s32[2]{0:T(128)S(1)} %copy-done.4, bf16[8,64,2304]{2,1,0:T(8,128)(2,1)S(1)} %all_to_all.47.rows_ref, bf16[2304,896]{1,0:T(8,128)(2,1)S(1)} %copy-done.3), custom_call_target="tpu_custom_call" | custom-call | tf_op jit(solution)/shard_map/project/pallas_call | solution.py:186
  230.7 5.5 %all-to-all-start.8 = ((bf16[8,64,896]{2,1,0:T(8,128)(2,1)}), bf16[8,64,896]{2,1,0:T(8,128)(2,1)S(1)}, u32[]{:S(2)}, u32[]{:S(2)}) async-start(bf16[8,64,896]{2,1,0:T(8,128)(2,1)} %bitcast.26), calls=%async_computation.8 | async-start | bytes 1835008 | tf_op jit(solution)/shard_map/all_to_all | solution.py:28
  236.4 14.1 %all-to-all-done.8 = bf16[8,64,896]{2,1,0:T(8,128)(2,1)S(1)} async-done(((bf16[8,64,896]{2,1,0:T(8,128)(2,1)}), bf16[8,64,896]{2,1,0:T(8,128)(2,1)S(1)}, u32[]{:S(2)}, u32[]{:S(2)}) %all-to-all-start.8) | async-done | bytes 917536 | tf_op jit(solution)/shard_map/all_to_all | solution.py:28
  251.0 2.5 collective-permute-start.12
  253.5 0.9 collective-permute-done.12
  254.8 0.7 copy.60
  (70 shorter events, 4.2 us)
Async XLA Ops:
  0.0 53.5 %copy-start = (bf16[2,512,896]{2,1,0:T(8,128)(2,1)S(1)}, bf16[2,512,896]{2,1,0:T(8,128)(2,1)}, u32[]{:S(2)}) copy-start(bf16[2,512,896]{2,1,0:T(8,128)(2,1)} %param.21) | copy-start | bytes 5505028
  0.0 13.3 %copy-start.8 = (bf16[8,512,128]{2,1,0:T(8,128)(2,1)S(1)}, bf16[8,512,128]{2,1,0:T(8,128)(2,1)}, u32[]{:S(2)}) copy-start(bf16[8,512,128]{2,1,0:T(8,128)(2,1)} %param.19) | copy-start | bytes 3145732
  0.0 13.5 %copy-start.10 = (bf16[896]{0:T(1024)(128)(2,1)S(1)}, bf16[896]{0:T(1024)(128)(2,1)}, u32[]{:S(2)}) copy-start(bf16[896]{0:T(1024)(128)(2,1)} %param.22) | copy-start | bytes 5380
  0.0 13.5 %copy-start.11 = (bf16[2,4,576]{2,1,0:T(4,128)(2,1)S(1)}, bf16[2,4,576]{2,1,0:T(4,128)(2,1)}, u32[]{:S(2)}) copy-start(bf16[2,4,576]{2,1,0:T(4,128)(2,1)} %param.18) | copy-start | bytes 27652
  0.0 42.6 %collective-permute-start.1 = (bf16[1024,896]{1,0:T(8,128)(2,1)}, bf16[1024,896]{1,0:T(8,128)(2,1)}, u32[]{:S(2)}, u32[]{:S(2)}) collective-permute-start(bf16[1024,896]{1,0:T(8,128)(2,1)} %refs_0_), channel_id=1, source_target_pairs={{0,32},{32,0},{1,33},{33,1},{2,34},{34,2},{3,35},{35,3},{4,36},{36... | collective-permute-start | bytes 5505032 | tf_op jit(solution)/shard_map/ppermute | solution.py:36
  4.6 17.7 %all-to-all-start = ((bf16[16,72,128]{2,1,0:T(8,128)(2,1)}), bf16[16,72,128]{2,1,0:T(8,128)(2,1)S(1)}, u32[]{:S(2)}, u32[]{:S(2)}) async-start(bf16[16,72,128]{2,1,0:T(8,128)(2,1)} %leave.1), calls=%async_computation | async-start | bytes 589824 | tf_op jit(solution)/shard_map/all_to_all | solution.py:28
  13.3 25.2 %collective-permute-start = (bf16[8,512,128]{2,1,0:T(8,128)(2,1)S(1)}, bf16[8,512,128]{2,1,0:T(8,128)(2,1)}, u32[]{:S(2)}, u32[]{:S(2)}) collective-permute-start(bf16[8,512,128]{2,1,0:T(8,128)(2,1)S(1)} %copy-done.8), channel_id=1, source_target_pairs={{0,1},{1,0},{2,3},{3,2},{4,5},{5,4},{6,7},{7,6},{8,9},{9,8},{10,11... | collective-permute-start | bytes 3145736 | tf_op jit(solution)/shard_map/ppermute | solution.py:36
  14.6 7.6 %copy-start.5 = (s32[1,16]{1,0:T(1,128)S(1)}, s32[1,16]{1,0:T(1,128)}, u32[]{:S(2)}) copy-start(s32[1,16]{1,0:T(1,128)} %param.16) | copy-start | bytes 196
  23.5 15.0 %all-to-all-start.1 = ((bf16[16,72,128]{2,1,0:T(8,128)(2,1)}), bf16[16,72,128]{2,1,0:T(8,128)(2,1)S(1)}, u32[]{:S(2)}, u32[]{:S(2)}) async-start(bf16[16,72,128]{2,1,0:T(8,128)(2,1)} %route.1), calls=%async_computation.1 | async-start | bytes 589824 | tf_op jit(solution)/shard_map/all_to_all | solution.py:28
  33.2 2.6 %copy-start.12 = (s32[1,16]{1,0:T(1,128)S(1)}, s32[1,16]{1,0:T(1,128)}, u32[]{:S(2)}) copy-start(s32[1,16]{1,0:T(1,128)} %param.15) | copy-start | bytes 196
  38.6 0.7 copy-start.7
  42.6 10.8 %collective-permute-start.3 = (bf16[1024,896]{1,0:T(8,128)(2,1)}, bf16[1024,896]{1,0:T(8,128)(2,1)}, u32[]{:S(2)}, u32[]{:S(2)}) collective-permute-start(bf16[1024,896]{1,0:T(8,128)(2,1)} %refs_0_), channel_id=1, source_target_pairs={{0,1},{1,0},{2,3},{3,2},{4,5},{5,4},{6,7},{7,6},{8,9},{9,8},{10,11... | collective-permute-start | bytes 5505032 | tf_op jit(solution)/shard_map/ppermute | solution.py:36
  43.5 15.4 %collective-permute-start.4 = (bf16[1152,896]{1,0:T(8,128)(2,1)}, bf16[1152,896]{1,0:T(8,128)(2,1)}, u32[]{:S(2)}, u32[]{:S(2)}) collective-permute-start(bf16[1152,896]{1,0:T(8,128)(2,1)} %param.25), channel_id=1, source_target_pairs={{0,1},{1,0},{2,3},{3,2},{4,5},{5,4},{6,7},{7,6},{8,9},{9,8},{10,11... | collective-permute-start | bytes 6193160 | tf_op jit(solution)/shard_map/ppermute | solution.py:36
  43.5 27.3 %collective-permute-start.5 = (bf16[1024,896]{1,0:T(8,128)(2,1)}, bf16[1024,896]{1,0:T(8,128)(2,1)}, u32[]{:S(2)}, u32[]{:S(2)}) collective-permute-start(bf16[1024,896]{1,0:T(8,128)(2,1)} %collective-permute-done.1.refs_2_), channel_id=1, source_target_pairs={{0,1},{1,0},{2,3},{3,2},{4,5},{5,4},{6,7},{7,6},{8,9},{9,8},{10,11... | collective-permute-start | bytes 5505032 | tf_op jit(solution)/shard_map/ppermute | solution.py:36
  44.0 21.6 %collective-permute-start.2 = (bf16[384,1152]{1,0:T(8,128)(2,1)}, bf16[384,1152]{1,0:T(8,128)(2,1)}, u32[]{:S(2)}, u32[]{:S(2)}) collective-permute-start(bf16[384,1152]{1,0:T(8,128)(2,1)} %multiply_convert_fusion.2), channel_id=1, source_target_pairs={{0,32},{32,0},{1,33},{33,1},{2,34},{34,2},{3,35},{35,3},{4,36},{36... | collective-permute-start | bytes 2654216 | tf_op jit(solution)/shard_map/ppermute | solution.py:36
  45.4 25.4 %all-to-all-start.2 = ((bf16[16,2,32,512]{3,2,1,0:T(8,128)(2,1)}), bf16[16,2,32,512]{3,2,1,0:T(8,128)(2,1)S(1)}, u32[]{:S(2)}, u32[]{:S(2)}) async-start(bf16[16,2,32,512]{3,2,1,0:T(8,128)(2,1)} %bitcast.57), calls=%async_computation.2 | async-start | bytes 2097152 | tf_op jit(solution)/shard_map/all_to_all | solution.py:28
  53.9 3.4 %copy-start.9 = (bf16[8,512,128]{2,1,0:T(8,128)(2,1)S(1)}, bf16[8,512,128]{2,1,0:T(8,128)(2,1)}, u32[]{:S(2)}) copy-start(bf16[8,512,128]{2,1,0:T(8,128)(2,1)} %param.19) | copy-start | bytes 3145732
  57.3 1.9 copy-start.6
  91.0 27.2 %collective-permute-start.6 = (bf16[512,1152]{1,0:T(8,128)(2,1)}, bf16[512,1152]{1,0:T(8,128)(2,1)S(1)}, u32[]{:S(2)}, u32[]{:S(2)}) collective-permute-start(bf16[512,1152]{1,0:T(8,128)(2,1)} %multiply_convert_fusion.1), channel_id=1, source_target_pairs={{0,32},{32,0},{1,33},{33,1},{2,34},{34,2},{3,35},{35,3},{4,36},{36... | collective-permute-start | bytes 3538952 | tf_op jit(solution)/shard_map/ppermute | solution.py:36
  98.6 19.5 %all-to-all-start.4 = ((bf16[8,2,32,896]{3,2,1,0:T(8,128)(2,1)}), bf16[8,2,32,896]{3,2,1,0:T(8,128)(2,1)S(1)}, u32[]{:S(2)}, u32[]{:S(2)}) async-start(bf16[8,2,32,896]{3,2,1,0:T(8,128)(2,1)} %combine.1), calls=%async_computation.4 | async-start | bytes 1835008 | tf_op jit(solution)/shard_map/all_to_all | solution.py:28
  102.2 15.6 %collective-permute-start.7 = (bf16[32,896]{1,0:T(8,128)(2,1)S(1)}, bf16[32,896]{1,0:T(8,128)(2,1)S(1)}, u32[]{:S(2)}, u32[]{:S(2)}) collective-permute-start(bf16[32,896]{1,0:T(8,128)(2,1)S(1)} %get-tuple-element.85), channel_id=1, source_target_pairs={{0,32},{32,0},{1,33},{33,1},{2,34},{34,2},{3,35},{35,3},{4,36},{36... | collective-permute-start | bytes 172040 | tf_op jit(solution)/shard_map/ppermute | solution.py:36
  118.1 9.8 %collective-permute-start.9 = (bf16[896,1152]{1,0:T(8,128)(2,1)}, bf16[896,1152]{1,0:T(8,128)(2,1)}, u32[]{:S(2)}, u32[]{:S(2)}) collective-permute-start(bf16[896,1152]{1,0:T(8,128)(2,1)} %multiply_convert_fusion), channel_id=1, source_target_pairs={{0,1},{1,0},{2,3},{3,2},{4,5},{5,4},{6,7},{7,6},{8,9},{9,8},{10,11... | collective-permute-start | bytes 6193160 | tf_op jit(solution)/shard_map/ppermute | solution.py:36
  120.8 7.2 %collective-permute-start.11 = (bf16[512,1152]{1,0:T(8,128)(2,1)S(1)}, bf16[512,1152]{1,0:T(8,128)(2,1)}, u32[]{:S(2)}, u32[]{:S(2)}) collective-permute-start(bf16[512,1152]{1,0:T(8,128)(2,1)S(1)} %collective-permute-done.6), channel_id=1, source_target_pairs={{0,1},{1,0},{2,3},{3,2},{4,5},{5,4},{6,7},{7,6},{8,9},{9,8},{10,11... | collective-permute-start | bytes 3538952 | tf_op jit(solution)/shard_map/ppermute | solution.py:36
  121.1 6.9 %collective-permute-start.10 = (bf16[384,1152]{1,0:T(8,128)(2,1)}, bf16[384,1152]{1,0:T(8,128)(2,1)}, u32[]{:S(2)}, u32[]{:S(2)}) collective-permute-start(bf16[384,1152]{1,0:T(8,128)(2,1)} %collective-permute-done.2), channel_id=1, source_target_pairs={{0,1},{1,0},{2,3},{3,2},{4,5},{5,4},{6,7},{7,6},{8,9},{9,8},{10,11... | collective-permute-start | bytes 2654216 | tf_op jit(solution)/shard_map/ppermute | solution.py:36
  121.5 26.4 %collective-permute-start.8 = (f32[32,896]{1,0:T(8,128)S(1)}, f32[32,896]{1,0:T(8,128)S(1)}, u32[]{:S(2)}, u32[]{:S(2)}) collective-permute-start(f32[32,896]{1,0:T(8,128)S(1)} %dynamic-slice_bitcast_fusion), channel_id=1, source_target_pairs={{0,32},{32,0},{1,33},{33,1},{2,34},{34,2},{3,35},{35,3},{4,36},{36... | collective-permute-start | bytes 344072 | tf_op jit(solution)/shard_map/ppermute | solution.py:36
  123.3 31.1 %all-to-all-start.5 = ((bf16[16,2,32,896]{3,2,1,0:T(8,128)(2,1)}), bf16[16,2,32,896]{3,2,1,0:T(8,128)(2,1)S(1)}, u32[]{:S(2)}, u32[]{:S(2)}) async-start(bf16[16,2,32,896]{3,2,1,0:T(8,128)(2,1)} %broadcast_in_dim.29), calls=%async_computation.5 | async-start | bytes 3670016 | tf_op jit(solution)/shard_map/all_to_all | solution.py:28
  128.0 26.5 %copy-start.4 = (s32[2]{0:T(128)S(1)}, s32[2]{0:T(128)}, u32[]{:S(2)}) copy-start(s32[2]{0:T(128)} %pad_add_fusion.ids_ref) | copy-start | bytes 28
  154.4 3.3 %copy-start.2 = (bf16[1792,2304]{1,0:T(8,128)(2,1)S(1)}, bf16[1792,2304]{1,0:T(8,128)(2,1)}, u32[]{:S(2)}) copy-start(bf16[1792,2304]{1,0:T(8,128)(2,1)} %maximum_maximum_fusion.weight_ref) | copy-start | bytes 24772612
  197.3 29.3 %copy-start.3 = (bf16[2304,896]{1,0:T(8,128)(2,1)S(1)}, bf16[2304,896]{1,0:T(8,128)(2,1)}, u32[]{:S(2)}) copy-start(bf16[2304,896]{1,0:T(8,128)(2,1)} %pad_maximum_fusion.weight_ref) | copy-start | bytes 12386308
  230.7 19.8 %all-to-all-start.8 = ((bf16[8,64,896]{2,1,0:T(8,128)(2,1)}), bf16[8,64,896]{2,1,0:T(8,128)(2,1)S(1)}, u32[]{:S(2)}, u32[]{:S(2)}) async-start(bf16[8,64,896]{2,1,0:T(8,128)(2,1)} %bitcast.26), calls=%async_computation.8 | async-start | bytes 1835008 | tf_op jit(solution)/shard_map/all_to_all | solution.py:28
  236.2 19.2 %copy-start.1 = (bf16[2,512,896]{2,1,0:T(8,128)(2,1)S(1)}, bf16[2,512,896]{2,1,0:T(8,128)(2,1)}, u32[]{:S(2)}) copy-start(bf16[2,512,896]{2,1,0:T(8,128)(2,1)} %param.21) | copy-start | bytes 5505028
  251.0 3.4 %collective-permute-start.12 = (bf16[2,4,2,2,896]{4,3,2,1,0:T(2,128)(2,1)S(1)}, bf16[2,4,2,2,896]{4,3,2,1,0:T(2,128)(2,1)S(1)}, u32[]{:S(2)}, u32[]{:S(2)}) collective-permute-start(bf16[2,4,2,2,896]{4,3,2,1,0:T(2,128)(2,1)S(1)} %dynamic-slice_bitcast_fusion.2), channel_id=1, source_target_pairs={{0,1},{1,0},{2,3},{3,2},{4,5},{5,4},{6,7},{7,6},{8,9},{9,8},{10,11... | collective-permute-start | bytes 172040 | tf_op jit(solution)/shard_map/ppermute | solution.py:36

commit v14 on v13

--- a/solution.py
+++ b/solution.py
@@ -17,7 +17,7 @@
 N_TP = 16
 N_ZY = 8
 SWAP = [(0, 1), (1, 0)]
-CUT = 384
+CUT = 448
 TILE = 768
 bf16 = jnp.bfloat16
 f32 = jnp.float32

time: 256 us -> 258 us (level)
    all_to_all x6, waiting for transfers between devices: 28.2 us -> 32.2 us  [exchange(): return lax.all_to_all(blocks, axes, 0, 0, tiled=True)]
    convert_element_type x3, other arithmetic: 9.25 us -> 6.26 us  [scaled(): return (weight.astype(f32) * gain[low:high]).astype(bf16)]
    unnamed x28 -> x36, local copies, waits for them, and re-layouts: 5.53 us -> 6.63 us
  transfers between devices with their start and end apart: 19 -> 19, of which waited for: 9 -> 9; matrix products, arithmetic and copies ran while one was open for 16% -> 15% of each run, Pallas kernels for 8% -> 8%
where the time goes in v14:
time: 258 us; the launch traced here: 257 us
  blocking collectives  80.7 us (31%)
  starting transfers between devices  48.5 us (19%)
  waiting for transfers between devices  48.1 us (19%)
  other arithmetic  36 us (14%)
  Pallas kernels  31.4 us (12%)
  local copies, waits for them, and re-layouts  10.5 us (4%)
    all_to_all x3, blocking collectives, exchange(): return lax.all_to_all(blocks, axes, 0, 0, tiled=True)  80.7 us
    all_to_all x6, starting transfers between devices, exchange(): return lax.all_to_all(blocks, axes, 0, 0, tiled=True)  37 us
    all_to_all x6, waiting for transfers between devices, exchange(): return lax.all_to_all(blocks, axes, 0, 0, tiled=True)  32.2 us
    concatenate x1, other arithmetic, local(): jnp.concatenate([jnp.concatenate([own, swap(own, 'c') if k else kept[1]],...  20.8 us
    ppermute x13, waiting for transfers between devices, swap(): return lax.ppermute(block, axis, SWAP)  15.9 us
    ppermute x13, starting transfers between devices, swap(): return lax.ppermute(block, axis, SWAP)  11.6 us
    pallas_call x2, Pallas kernels, attend(): pl.pallas_call(body, grid_spec=pltpu.PrefetchScalarGridSpec(num_scalar_pr...  9.82 us
    pallas_call x1, Pallas kernels, combine(): pl.pallas_call(body, grid_spec=pltpu.PrefetchScalarGridSpec(num_scalar_pr...  7.4 us
  transfers between devices with their start and end apart: 19, of which 9 were waited for; matrix products, arithmetic and copies ran while one was open for 15% of the time, Pallas kernels for 8%

profile of v14, /device:TPU:1, one launch (start us, length us, event | category | flops | bytes accessed | tf_op | source)
XLA Modules:
  0.0 256.9 jit_solution(4415943299458232810)
XLA Ops:
  0.0 2.1 collective-permute-start.1
  2.1 2.4 leave.1
  4.6 8.8 %all-to-all-start = ((bf16[16,72,128]{2,1,0:T(8,128)(2,1)}), bf16[16,72,128]{2,1,0:T(8,128)(2,1)S(1)}, u32[]{:S(2)}, u32[]{:S(2)}) async-start(bf16[16,72,128]{2,1,0:T(8,128)(2,1)} %leave.1), calls=%async_computation | async-start | bytes 589824 | tf_op jit(solution)/shard_map/all_to_all | solution.py:28
  13.5 1.1 copy.52
  14.6 6.5 %attend.1.refs_1_ = bf16[8,2,2,32,512]{4,3,2,1,0:T(8,128)(2,1)} custom-call(s32[4]{0:T(128)} %lengths_ref.3, s32[4]{0:T(128)} %lengths_ref.3, bf16[4,576,2]{2,1,0:T(8,128)(2,1)} %bitcast.58, bf16[2,4,576,128]{3,2,1,0:T(8,128)(2,1)} %bitcast.60, bf16[4,576,256]{2,1,0:T(8,128)(2,1)} %bitcast.63), custom_call_target="tpu_custom_call" | custom-call | tf_op jit(solution)/shard_map/attend/pallas_call | solution.py:145
  21.2 1.0 all-to-all-done.in_ref
  22.2 1.3 route.1
  23.5 6.3 %all-to-all-start.1 = ((bf16[16,72,128]{2,1,0:T(8,128)(2,1)}), bf16[16,72,128]{2,1,0:T(8,128)(2,1)S(1)}, u32[]{:S(2)}, u32[]{:S(2)}) async-start(bf16[16,72,128]{2,1,0:T(8,128)(2,1)} %route.1), calls=%async_computation.1 | async-start | bytes 589824 | tf_op jit(solution)/shard_map/all_to_all | solution.py:28
  29.8 3.7 %multiply_convert_fusion = bf16[896,1152]{1,0:T(8,128)(2,1)} fusion(f32[896]{0:T(1024)S(1)} %convert_element_type.62, bf16[896,1152]{1,0:T(8,128)(2,1)} %param.23, bf16[896,1152]{1,0:T(8,128)(2,1)} %param.24, pred[]{:T(512)S(6)} %eq.17), kind=kLoop, calls=%fused_computation.3 | loop fusion | flops 4128768 | bytes 6196737 | tf_op jit(solution)/shard_map/convert_element_type | solution.py:356
  33.5 1.3 multiply_convert_fusion.2
  34.8 0.7 fusion.11
  35.5 1.3 pad_add_fusion.ids_ref
  36.8 1.9 all-to-all-done.1.refs_0_
  38.7 0.7 copy-done.11
  39.4 3.3 %again.1 = bf16[8,2,2,32,512]{4,3,2,1,0:T(8,128)(2,1)} custom-call(s32[2]{0:T(128)} %pad_add_fusion.ids_ref, s32[4]{0:T(128)} %lengths_ref.3, bf16[4,576,2]{2,1,0:T(8,128)(2,1)} %bitcast.59, bf16[2,4,576,128]{3,2,1,0:T(8,128)(2,1)} %bitcast.61, bf16[16,72,128]{2,1,0:T(8,128)(2,1)} %copy-done.11, ...), custom_call_target="tpu_custom_call", output_to_operand_aliasing={{}: (5, {})} | custom-call | tf_op jit(solution)/shard_map/again/pallas_call | solution.py:145
  42.8 0.9 collective-permute-start.3
  43.7 0.5 collective-permute-start.5
  44.2 1.2 collective-permute-start.2
  45.4 8.1 %all-to-all-start.2 = ((bf16[16,2,32,512]{3,2,1,0:T(8,128)(2,1)}), bf16[16,2,32,512]{3,2,1,0:T(8,128)(2,1)S(1)}, u32[]{:S(2)}, u32[]{:S(2)}) async-start(bf16[16,2,32,512]{3,2,1,0:T(8,128)(2,1)} %bitcast.57), calls=%async_computation.2 | async-start | bytes 2097152 | tf_op jit(solution)/shard_map/all_to_all | solution.py:28
  54.7 1.6 pad_maximum_fusion.1
  56.6 0.6 copy-done.9
  57.2 1.3 multiply_convert_fusion.1
  58.5 3.9 %pad_maximum_fusion.weight_ref = bf16[2304,896]{1,0:T(8,128)(2,1)} fusion(bf16[1152,896]{1,0:T(8,128)(2,1)} %collective-permute-done.4, bf16[1152,896]{1,0:T(8,128)(2,1)S(1)} %copy-done.10), kind=kLoop, calls=%fused_computation.2 | loop fusion | flops 8257536 | bytes 8257536 | tf_op jit(solution)/shard_map/concatenate | solution.py:376
  62.4 6.6 %collective-permute-done.2 = bf16[448,1152]{1,0:T(8,128)(2,1)} collective-permute-done((bf16[448,1152]{1,0:T(8,128)(2,1)}, bf16[448,1152]{1,0:T(8,128)(2,1)}, u32[]{:S(2)}, u32[]{:S(2)}) %collective-permute-start.2) | collective-permute-done | bytes 1032224 | tf_op jit(solution)/shard_map/ppermute | solution.py:36
  68.9 1.9 all-to-all-done.2
  70.8 1.3 fusion
  72.6 18.3 %all_to_all.45.rows_ref = bf16[8,32,2048]{2,1,0:T(8,128)(2,1)} all-to-all(bf16[8,32,2048]{2,1,0:T(8,128)(2,1)S(1)} %bitcast.64), channel_id=1, replica_groups=mesh['xh'=2,'xl'=2,'zl'=2,'zh'=2,'y'=4,'c'=2] {'xh','xl','zl'}, dimensions={0} | all-to-all | bytes 2097152 | tf_op jit(solution)/shard_map/all_to_all | solution.py:28
  91.2 7.4 %combine.1 = bf16[8,2,32,896]{3,2,1,0:T(8,128)(2,1)} custom-call(s32[2]{0:T(128)} %pad_add_fusion.ids_ref, bf16[8,32,2048]{2,1,0:T(8,128)(2,1)} %all_to_all.45.rows_ref, bf16[1024,896]{1,0:T(8,128)(2,1)} %refs_0_, bf16[1024,896]{1,0:T(8,128)(2,1)} %collective-permute-done.3.refs_1_, bf16[1024,896]{1,0:T(8,128)(2,1)} %collective-permute-done.1.refs_2_, ...), custom_call_target="tpu_custom_call" | custom-call | tf_op jit(solution)/shard_map/combine/pallas_call | solution.py:238
  98.6 6.5 %all-to-all-start.4 = ((bf16[8,2,32,896]{3,2,1,0:T(8,128)(2,1)}), bf16[8,2,32,896]{3,2,1,0:T(8,128)(2,1)S(1)}, u32[]{:S(2)}, u32[]{:S(2)}) async-start(bf16[8,2,32,896]{3,2,1,0:T(8,128)(2,1)} %combine.1), calls=%async_computation.4 | async-start | bytes 1835008 | tf_op jit(solution)/shard_map/all_to_all | solution.py:28
  105.1 1.1 collective-permute-start.7
  106.2 8.4 %collective-permute-done.7 = bf16[32,896]{1,0:T(8,128)(2,1)S(1)} collective-permute-done((bf16[32,896]{1,0:T(8,128)(2,1)S(1)}, bf16[32,896]{1,0:T(8,128)(2,1)S(1)}, u32[]{:S(2)}, u32[]{:S(2)}) %collective-permute-start.7) | collective-permute-done | bytes 57376 | tf_op jit(solution)/shard_map/ppermute | solution.py:36
  114.6 6.2 %all-to-all-done.4 = bf16[8,2,32,896]{3,2,1,0:T(8,128)(2,1)S(1)} async-done(((bf16[8,2,32,896]{3,2,1,0:T(8,128)(2,1)}), bf16[8,2,32,896]{3,2,1,0:T(8,128)(2,1)S(1)}, u32[]{:S(2)}, u32[]{:S(2)}) %all-to-all-start.4) | async-done | bytes 917536 | tf_op jit(solution)/shard_map/all_to_all | solution.py:28
  120.8 1.0 collective-permute-start.9
  122.5 1.2 collective-permute-start.8
  123.8 1.5 broadcast_in_dim.29
  125.2 3.7 %all-to-all-start.5 = ((bf16[16,2,32,896]{3,2,1,0:T(8,128)(2,1)}), bf16[16,2,32,896]{3,2,1,0:T(8,128)(2,1)S(1)}, u32[]{:S(2)}, u32[]{:S(2)}) async-start(bf16[16,2,32,896]{3,2,1,0:T(8,128)(2,1)} %broadcast_in_dim.29), calls=%async_computation.5 | async-start | bytes 3670016 | tf_op jit(solution)/shard_map/all_to_all | solution.py:28
  129.0 20.8 %maximum_maximum_fusion.weight_ref = bf16[1792,2304]{1,0:T(8,128)(2,1)} fusion(bf16[448,1152]{1,0:T(8,128)(2,1)} %collective-permute-done.11, bf16[448,1152]{1,0:T(8,128)(2,1)S(1)} %collective-permute-done.6, bf16[448,1152]{1,0:T(8,128)(2,1)} %collective-permute-done.10, bf16[448,1152]{1,0:T(8,128)(2,1)} %collective-permute-done.2, ...), kind=kLoop, calls=%fused_computation | loop fusion | flops 49545216 | bytes 16515072 | tf_op jit(solution)/shard_map/concatenate | solution.py:406
  149.7 7.0 %all-to-all-done.5 = bf16[16,2,32,896]{3,2,1,0:T(8,128)(2,1)S(1)} async-done(((bf16[16,2,32,896]{3,2,1,0:T(8,128)(2,1)}), bf16[16,2,32,896]{3,2,1,0:T(8,128)(2,1)S(1)}, u32[]{:S(2)}, u32[]{:S(2)}) %all-to-all-start.5) | async-done | bytes 1835040 | tf_op jit(solution)/shard_map/all_to_all | solution.py:28
  156.8 3.3 %copy-done.2 = bf16[1792,2304]{1,0:T(8,128)(2,1)S(1)} copy-done((bf16[1792,2304]{1,0:T(8,128)(2,1)S(1)}, bf16[1792,2304]{1,0:T(8,128)(2,1)}, u32[]{:S(2)}) %copy-start.2) | copy-done | bytes 8257560
  160.1 6.4 %widen.1 = bf16[8,2,32,2432]{3,2,1,0:T(8,128)(2,1)S(1)} custom-call(s32[2]{0:T(128)S(1)} %copy-done.4, bf16[2,8,2,32,896]{4,3,2,1,0:T(8,128)(2,1)S(1)} %bitcast.54, bf16[1792,2304]{1,0:T(8,128)(2,1)S(1)} %copy-done.2), custom_call_target="tpu_custom_call" | custom-call | tf_op jit(solution)/shard_map/widen/pallas_call | solution.py:285
  166.5 31.8 %all_to_all.46 = bf16[8,64,2432]{2,1,0:T(8,128)(2,1)S(1)} all-to-all(bf16[8,64,2432]{2,1,0:T(8,128)(2,1)S(1)} %bitcast.53), channel_id=1, replica_groups=mesh['xh'=2,'xl'=2,'zl'=2,'zh'=2,'y'=4,'c'=2] {'xh','xl','zl'}, dimensions={0} | all-to-all | bytes 4980736 | tf_op jit(solution)/shard_map/all_to_all | solution.py:28
  199.4 30.5 %all_to_all.47.rows_ref = bf16[8,64,2304]{2,1,0:T(8,128)(2,1)S(1)} all-to-all(bf16[8,64,2304]{2,1,0:T(8,128)(2,1)S(1)} %broadcast_in_dim.31), channel_id=1, replica_groups=mesh['xh'=2,'xl'=2,'zl'=2,'zh'=2,'y'=4,'c'=2] {'xh','xl','zl'}, dimensions={0} | all-to-all | bytes 4718592 | tf_op jit(solution)/shard_map/all_to_all | solution.py:28
  229.9 4.1 %project.1 = bf16[8,1,64,896]{3,2,1,0:T(8,128)(2,1)} custom-call(s32[2]{0:T(128)S(1)} %copy-done.4, bf16[8,64,2304]{2,1,0:T(8,128)(2,1)S(1)} %all_to_all.47.rows_ref, bf16[2304,896]{1,0:T(8,128)(2,1)S(1)} %copy-done.3), custom_call_target="tpu_custom_call" | custom-call | tf_op jit(solution)/shard_map/project/pallas_call | solution.py:186
  234.0 3.7 %all-to-all-start.8 = ((bf16[8,64,896]{2,1,0:T(8,128)(2,1)}), bf16[8,64,896]{2,1,0:T(8,128)(2,1)S(1)}, u32[]{:S(2)}, u32[]{:S(2)}) async-start(bf16[8,64,896]{2,1,0:T(8,128)(2,1)} %bitcast.26), calls=%async_computation.8 | async-start | bytes 1835008 | tf_op jit(solution)/shard_map/all_to_all | solution.py:28
  237.9 14.2 %all-to-all-done.8 = bf16[8,64,896]{2,1,0:T(8,128)(2,1)S(1)} async-done(((bf16[8,64,896]{2,1,0:T(8,128)(2,1)}), bf16[8,64,896]{2,1,0:T(8,128)(2,1)S(1)}, u32[]{:S(2)}, u32[]{:S(2)}) %all-to-all-start.8) | async-done | bytes 917536 | tf_op jit(solution)/shard_map/all_to_all | solution.py:28
  252.5 2.5 collective-permute-start.12
  255.0 0.9 collective-permute-done.12
  256.2 0.7 copy.60
  (77 shorter events, 5.1 us)
Async XLA Ops:
  0.0 53.5 %copy-start = (bf16[2,512,896]{2,1,0:T(8,128)(2,1)S(1)}, bf16[2,512,896]{2,1,0:T(8,128)(2,1)}, u32[]{:S(2)}) copy-start(bf16[2,512,896]{2,1,0:T(8,128)(2,1)} %param.21) | copy-start | bytes 5505028
  0.0 13.3 %copy-start.12 = (bf16[8,512,128]{2,1,0:T(8,128)(2,1)S(1)}, bf16[8,512,128]{2,1,0:T(8,128)(2,1)}, u32[]{:S(2)}) copy-start(bf16[8,512,128]{2,1,0:T(8,128)(2,1)} %param.19) | copy-start | bytes 3145732
  0.0 13.5 %copy-start.15 = (bf16[2,4,576]{2,1,0:T(4,128)(2,1)S(1)}, bf16[2,4,576]{2,1,0:T(4,128)(2,1)}, u32[]{:S(2)}) copy-start(bf16[2,4,576]{2,1,0:T(4,128)(2,1)} %param.18) | copy-start | bytes 27652
  0.0 14.6 %copy-start.14 = (bf16[896]{0:T(1024)(128)(2,1)S(1)}, bf16[896]{0:T(1024)(128)(2,1)}, u32[]{:S(2)}) copy-start(bf16[896]{0:T(1024)(128)(2,1)} %param.22) | copy-start | bytes 5380
  0.0 42.7 %collective-permute-start.1 = (bf16[1024,896]{1,0:T(8,128)(2,1)}, bf16[1024,896]{1,0:T(8,128)(2,1)}, u32[]{:S(2)}, u32[]{:S(2)}) collective-permute-start(bf16[1024,896]{1,0:T(8,128)(2,1)} %refs_0_), channel_id=1, source_target_pairs={{0,32},{32,0},{1,33},{33,1},{2,34},{34,2},{3,35},{35,3},{4,36},{36... | collective-permute-start | bytes 5505032 | tf_op jit(solution)/shard_map/ppermute | solution.py:36
  4.6 17.7 %all-to-all-start = ((bf16[16,72,128]{2,1,0:T(8,128)(2,1)}), bf16[16,72,128]{2,1,0:T(8,128)(2,1)S(1)}, u32[]{:S(2)}, u32[]{:S(2)}) async-start(bf16[16,72,128]{2,1,0:T(8,128)(2,1)} %leave.1), calls=%async_computation | async-start | bytes 589824 | tf_op jit(solution)/shard_map/all_to_all | solution.py:28
  13.3 25.4 %collective-permute-start = (bf16[8,512,128]{2,1,0:T(8,128)(2,1)S(1)}, bf16[8,512,128]{2,1,0:T(8,128)(2,1)}, u32[]{:S(2)}, u32[]{:S(2)}) collective-permute-start(bf16[8,512,128]{2,1,0:T(8,128)(2,1)S(1)} %copy-done.12), channel_id=1, source_target_pairs={{0,1},{1,0},{2,3},{3,2},{4,5},{5,4},{6,7},{7,6},{8,9},{9,8},{10,11... | collective-permute-start | bytes 3145736 | tf_op jit(solution)/shard_map/ppermute | solution.py:36
  14.6 7.6 %copy-start.5 = (s32[1,16]{1,0:T(1,128)S(1)}, s32[1,16]{1,0:T(1,128)}, u32[]{:S(2)}) copy-start(s32[1,16]{1,0:T(1,128)} %param.16) | copy-start | bytes 196
  23.5 15.2 %all-to-all-start.1 = ((bf16[16,72,128]{2,1,0:T(8,128)(2,1)}), bf16[16,72,128]{2,1,0:T(8,128)(2,1)S(1)}, u32[]{:S(2)}, u32[]{:S(2)}) async-start(bf16[16,72,128]{2,1,0:T(8,128)(2,1)} %route.1), calls=%async_computation.1 | async-start | bytes 589824 | tf_op jit(solution)/shard_map/all_to_all | solution.py:28
  29.8 3.7 %copy-start.6 = (bf16[896,1152]{1,0:T(8,128)(2,1)S(1)}, bf16[896,1152]{1,0:T(8,128)(2,1)}, u32[]{:S(2)}) copy-start(bf16[896,1152]{1,0:T(8,128)(2,1)} %param.23) | copy-start | bytes 6193156
  29.8 3.7 %copy-start.8 = (bf16[896,1152]{1,0:T(8,128)(2,1)S(1)}, bf16[896,1152]{1,0:T(8,128)(2,1)}, u32[]{:S(2)}) copy-start(bf16[896,1152]{1,0:T(8,128)(2,1)} %param.24) | copy-start | bytes 6193156
  33.5 1.3 copy-start.16
  38.7 0.7 copy-start.11
  42.8 10.7 %collective-permute-start.3 = (bf16[1024,896]{1,0:T(8,128)(2,1)}, bf16[1024,896]{1,0:T(8,128)(2,1)}, u32[]{:S(2)}, u32[]{:S(2)}) collective-permute-start(bf16[1024,896]{1,0:T(8,128)(2,1)} %refs_0_), channel_id=1, source_target_pairs={{0,1},{1,0},{2,3},{3,2},{4,5},{5,4},{6,7},{7,6},{8,9},{9,8},{10,11... | collective-permute-start | bytes 5505032 | tf_op jit(solution)/shard_map/ppermute | solution.py:36
  43.7 14.8 %collective-permute-start.4 = (bf16[1152,896]{1,0:T(8,128)(2,1)}, bf16[1152,896]{1,0:T(8,128)(2,1)}, u32[]{:S(2)}, u32[]{:S(2)}) collective-permute-start(bf16[1152,896]{1,0:T(8,128)(2,1)} %param.25), channel_id=1, source_target_pairs={{0,1},{1,0},{2,3},{3,2},{4,5},{5,4},{6,7},{7,6},{8,9},{9,8},{10,11... | collective-permute-start | bytes 6193160 | tf_op jit(solution)/shard_map/ppermute | solution.py:36
  43.7 27.2 %collective-permute-start.5 = (bf16[1024,896]{1,0:T(8,128)(2,1)}, bf16[1024,896]{1,0:T(8,128)(2,1)}, u32[]{:S(2)}, u32[]{:S(2)}) collective-permute-start(bf16[1024,896]{1,0:T(8,128)(2,1)} %collective-permute-done.1.refs_2_), channel_id=1, source_target_pairs={{0,1},{1,0},{2,3},{3,2},{4,5},{5,4},{6,7},{7,6},{8,9},{9,8},{10,11... | collective-permute-start | bytes 5505032 | tf_op jit(solution)/shard_map/ppermute | solution.py:36
  44.2 24.8 %collective-permute-start.2 = (bf16[448,1152]{1,0:T(8,128)(2,1)}, bf16[448,1152]{1,0:T(8,128)(2,1)}, u32[]{:S(2)}, u32[]{:S(2)}) collective-permute-start(bf16[448,1152]{1,0:T(8,128)(2,1)} %multiply_convert_fusion.2), channel_id=1, source_target_pairs={{0,32},{32,0},{1,33},{33,1},{2,34},{34,2},{3,35},{35,3},{4,36},{36... | collective-permute-start | bytes 3096584 | tf_op jit(solution)/shard_map/ppermute | solution.py:36
  45.4 25.4 %all-to-all-start.2 = ((bf16[16,2,32,512]{3,2,1,0:T(8,128)(2,1)}), bf16[16,2,32,512]{3,2,1,0:T(8,128)(2,1)S(1)}, u32[]{:S(2)}, u32[]{:S(2)}) async-start(bf16[16,2,32,512]{3,2,1,0:T(8,128)(2,1)} %bitcast.57), calls=%async_computation.2 | async-start | bytes 2097152 | tf_op jit(solution)/shard_map/all_to_all | solution.py:28
  53.5 1.2 copy-start.13
  54.7 1.9 copy-start.7
  54.7 2.5 copy-start.9
  56.3 2.2 copy-start.10
  91.0 29.9 %collective-permute-start.6 = (bf16[448,1152]{1,0:T(8,128)(2,1)}, bf16[448,1152]{1,0:T(8,128)(2,1)S(1)}, u32[]{:S(2)}, u32[]{:S(2)}) collective-permute-start(bf16[448,1152]{1,0:T(8,128)(2,1)} %multiply_convert_fusion.1), channel_id=1, source_target_pairs={{0,32},{32,0},{1,33},{33,1},{2,34},{34,2},{3,35},{35,3},{4,36},{36... | collective-permute-start | bytes 3096584 | tf_op jit(solution)/shard_map/ppermute | solution.py:36
  98.6 22.2 %all-to-all-start.4 = ((bf16[8,2,32,896]{3,2,1,0:T(8,128)(2,1)}), bf16[8,2,32,896]{3,2,1,0:T(8,128)(2,1)S(1)}, u32[]{:S(2)}, u32[]{:S(2)}) async-start(bf16[8,2,32,896]{3,2,1,0:T(8,128)(2,1)} %combine.1), calls=%async_computation.4 | async-start | bytes 1835008 | tf_op jit(solution)/shard_map/all_to_all | solution.py:28
  105.1 9.6 %collective-permute-start.7 = (bf16[32,896]{1,0:T(8,128)(2,1)S(1)}, bf16[32,896]{1,0:T(8,128)(2,1)S(1)}, u32[]{:S(2)}, u32[]{:S(2)}) collective-permute-start(bf16[32,896]{1,0:T(8,128)(2,1)S(1)} %get-tuple-element.85), channel_id=1, source_target_pairs={{0,32},{32,0},{1,33},{33,1},{2,34},{34,2},{3,35},{35,3},{4,36},{36... | collective-permute-start | bytes 172040 | tf_op jit(solution)/shard_map/ppermute | solution.py:36
  120.8 8.2 %collective-permute-start.9 = (bf16[896,1152]{1,0:T(8,128)(2,1)}, bf16[896,1152]{1,0:T(8,128)(2,1)}, u32[]{:S(2)}, u32[]{:S(2)}) collective-permute-start(bf16[896,1152]{1,0:T(8,128)(2,1)} %multiply_convert_fusion), channel_id=1, source_target_pairs={{0,1},{1,0},{2,3},{3,2},{4,5},{5,4},{6,7},{7,6},{8,9},{9,8},{10,11... | collective-permute-start | bytes 6193160 | tf_op jit(solution)/shard_map/ppermute | solution.py:36
  121.8 7.1 %collective-permute-start.10 = (bf16[448,1152]{1,0:T(8,128)(2,1)}, bf16[448,1152]{1,0:T(8,128)(2,1)}, u32[]{:S(2)}, u32[]{:S(2)}) collective-permute-start(bf16[448,1152]{1,0:T(8,128)(2,1)} %collective-permute-done.2), channel_id=1, source_target_pairs={{0,1},{1,0},{2,3},{3,2},{4,5},{5,4},{6,7},{7,6},{8,9},{9,8},{10,11... | collective-permute-start | bytes 3096584 | tf_op jit(solution)/shard_map/ppermute | solution.py:36
  121.8 7.1 %collective-permute-start.11 = (bf16[448,1152]{1,0:T(8,128)(2,1)S(1)}, bf16[448,1152]{1,0:T(8,128)(2,1)}, u32[]{:S(2)}, u32[]{:S(2)}) collective-permute-start(bf16[448,1152]{1,0:T(8,128)(2,1)S(1)} %collective-permute-done.6), channel_id=1, source_target_pairs={{0,1},{1,0},{2,3},{3,2},{4,5},{5,4},{6,7},{7,6},{8,9},{9,8},{10,11... | collective-permute-start | bytes 3096584 | tf_op jit(solution)/shard_map/ppermute | solution.py:36
  122.5 27.2 %collective-permute-start.8 = (f32[32,896]{1,0:T(8,128)S(1)}, f32[32,896]{1,0:T(8,128)S(1)}, u32[]{:S(2)}, u32[]{:S(2)}) collective-permute-start(f32[32,896]{1,0:T(8,128)S(1)} %dynamic-slice_bitcast_fusion), channel_id=1, source_target_pairs={{0,32},{32,0},{1,33},{33,1},{2,34},{34,2},{3,35},{35,3},{4,36},{36... | collective-permute-start | bytes 344072 | tf_op jit(solution)/shard_map/ppermute | solution.py:36
  125.2 31.6 %all-to-all-start.5 = ((bf16[16,2,32,896]{3,2,1,0:T(8,128)(2,1)}), bf16[16,2,32,896]{3,2,1,0:T(8,128)(2,1)S(1)}, u32[]{:S(2)}, u32[]{:S(2)}) async-start(bf16[16,2,32,896]{3,2,1,0:T(8,128)(2,1)} %broadcast_in_dim.29), calls=%async_computation.5 | async-start | bytes 3670016 | tf_op jit(solution)/shard_map/all_to_all | solution.py:28
  128.9 27.8 %copy-start.4 = (s32[2]{0:T(128)S(1)}, s32[2]{0:T(128)}, u32[]{:S(2)}) copy-start(s32[2]{0:T(128)} %pad_add_fusion.ids_ref) | copy-start | bytes 28
  156.8 3.3 %copy-start.2 = (bf16[1792,2304]{1,0:T(8,128)(2,1)S(1)}, bf16[1792,2304]{1,0:T(8,128)(2,1)}, u32[]{:S(2)}) copy-start(bf16[1792,2304]{1,0:T(8,128)(2,1)} %maximum_maximum_fusion.weight_ref) | copy-start | bytes 24772612
  199.4 30.5 %copy-start.3 = (bf16[2304,896]{1,0:T(8,128)(2,1)S(1)}, bf16[2304,896]{1,0:T(8,128)(2,1)}, u32[]{:S(2)}) copy-start(bf16[2304,896]{1,0:T(8,128)(2,1)} %pad_maximum_fusion.weight_ref) | copy-start | bytes 12386308
  234.0 18.1 %all-to-all-start.8 = ((bf16[8,64,896]{2,1,0:T(8,128)(2,1)}), bf16[8,64,896]{2,1,0:T(8,128)(2,1)S(1)}, u32[]{:S(2)}, u32[]{:S(2)}) async-start(bf16[8,64,896]{2,1,0:T(8,128)(2,1)} %bitcast.26), calls=%async_computation.8 | async-start | bytes 1835008 | tf_op jit(solution)/shard_map/all_to_all | solution.py:28
  237.7 19.2 %copy-start.1 = (bf16[2,512,896]{2,1,0:T(8,128)(2,1)S(1)}, bf16[2,512,896]{2,1,0:T(8,128)(2,1)}, u32[]{:S(2)}) copy-start(bf16[2,512,896]{2,1,0:T(8,128)(2,1)} %param.21) | copy-start | bytes 5505028
  252.5 3.4 %collective-permute-start.12 = (bf16[2,4,2,2,896]{4,3,2,1,0:T(2,128)(2,1)S(1)}, bf16[2,4,2,2,896]{4,3,2,1,0:T(2,128)(2,1)S(1)}, u32[]{:S(2)}, u32[]{:S(2)}) collective-permute-start(bf16[2,4,2,2,896]{4,3,2,1,0:T(2,128)(2,1)S(1)} %dynamic-slice_bitcast_fusion.2), channel_id=1, source_target_pairs={{0,1},{1,0},{2,3},{3,2},{4,5},{5,4},{6,7},{7,6},{8,9},{9,8},{10,11... | collective-permute-start | bytes 172040 | tf_op jit(solution)/shard_map/ppermute | solution.py:36

commit v15 on v14

--- a/solution.py
+++ b/solution.py
@@ -34,6 +34,10 @@
 
 def swap(block, axis):
     return lax.ppermute(block, axis, SWAP)
+
+
+def cross(block):
+    return lax.ppermute(block, ("xh", "xl"), [(i, 3 - i) for i in range(4)])
 
 
 def params(mib):
@@ -232,8 +236,7 @@
             total = jnp.dot(
                 lhs, weight_ref[:, k * width : (k + 1) * width], preferred_element_type=f32
             )
-            at = lax.rem(ids_ref[1] + k, 2)
-            out_ref[:, at] = total.astype(bf16).reshape(groups, count, width)
+            out_ref[:, k] = total.astype(bf16).reshape(groups, count, width)
 
     return pl.pallas_call(
         body,
@@ -254,23 +257,21 @@
 
 
 def widen(ids, rows, weight):
-    halves, chunks, blocks, count, features = rows.shape
+    blocks, chunks, count, features = rows.shape
     depth, columns = weight.shape
-    every = halves * chunks * count
+    every = chunks * count
 
     def body(ids_ref, rows_ref, weight_ref, out_ref, lhs_ref):
         tile = pl.program_id(0)
 
         def put(at, value):
-            value = value.astype(bf16).reshape(halves, chunks, count, value.shape[1])
-            for h in range(halves):
-                out_ref[:, h, :, at] = value[h]
+            out_ref[:, :, at] = value.astype(bf16).reshape(chunks, count, value.shape[1])
 
         @pl.when(tile == 0)
         def _():
             squares = jnp.zeros((every, 1), f32)
             for k in range(blocks):
-                block = rows_ref[:, :, lax.rem(ids_ref[1] + k, blocks)].reshape(every, features)
+                block = rows_ref[lax.rem(ids_ref[1] + k, blocks)].reshape(every, features)
                 lhs_ref[:, k * features : (k + 1) * features] = block
                 wide = block.astype(f32)
                 squares += jnp.sum(wide * wide, axis=1, keepdims=True)
@@ -291,10 +292,10 @@
                 whole(rows.shape),
                 pl.BlockSpec((depth, TILE), lambda k, ids: (0, k)),
             ],
-            out_specs=whole((chunks, halves, count, columns + 128)),
+            out_specs=whole((chunks, count, columns + 128)),
             scratch_shapes=[pltpu.VMEM((every, depth), bf16)],
         ),
-        out_shape=jax.ShapeDtypeStruct((chunks, halves, count, columns + 128), bf16),
+        out_shape=jax.ShapeDtypeStruct((chunks, count, columns + 128), bf16),
         compiler_params=params(40),
         name="widen",
     )(ids, rows, weight)
@@ -325,17 +326,7 @@
     count = chunk // 2
     features, units = gate_weight.shape
 
-    def by_pair(mine, other):
-        first = pair == 0
-        return jnp.stack([jnp.where(first, mine, other), jnp.where(first, other, mine)])
-
-    def at_pair(blocks):
-        return lax.dynamic_index_in_dim(blocks, pair, 0, False)
-
-    def at_other(blocks):
-        return lax.dynamic_index_in_dim(blocks, 1 - pair, 0, False)
-
-    out_came = swap(out_proj, "xl")
+    out_came = cross(out_proj)
     value_near = swap(value_up, "c")
     lanes = jnp.arange(N_TP, dtype=jnp.int32)
     cache_t = cache.transpose(0, 2, 1)
@@ -369,12 +360,11 @@
     )
     came = [swap(sent, "xl")]
     out_near = swap(out_proj, "c")
-    out_weights = [[out_proj, out_near], [out_came, swap(out_came, "c")]]
     out = out.reshape((N_TP,) + out.shape[2:])
     by_head = exchange(out, TP).reshape(-1, 2 * heads, latent_width)
 
     downs = jnp.concatenate([down_weight, swap(down_weight, "c")], axis=0)
-    out_weights[0][1], gate_weight, up_weight, residual, value_near = lax.optimization_barrier(
+    out_near, gate_weight, up_weight, residual, value_near = lax.optimization_barrier(
         (out_near, gate_weight, up_weight, residual, value_near)
     )
     value_ups = jnp.concatenate([value_up, value_near], axis=0)
@@ -383,10 +373,13 @@
     residue = residue.reshape(steps, 2, 2, rows_out // 8, 2, 2, features)
     residue = lax.dynamic_index_in_dim(residue, core, 4, False)
     residue = residue.transpose(2, 1, 3, 4, 0, 5).reshape(2, count, features)
-    residue = [at_pair(residue), at_other(residue)]
-    by_head, kept, came, sent, downs, residue, out_weights, value_ups = lax.optimization_barrier(
-        (by_head, kept, came, sent, downs, residue, out_weights, value_ups)
-    )
+    residue = residue.reshape(chunk, features)
+    by_head, kept, came, sent, downs, residue, out_near, out_came, value_ups = (
+        lax.optimization_barrier(
+            (by_head, kept, came, sent, downs, residue, out_near, out_came, value_ups)
+        )
+    )
+    out_weights = [[out_proj, out_near], [out_came, swap(out_came, "c")]]
     value_heads = jnp.einsum(
         "thl,hlv->thv", by_head, value_ups, preferred_element_type=f32
     ).astype(bf16)
@@ -394,14 +387,13 @@
     value_heads = value_heads.reshape(2, 2, count // 2, 2 * heads * value_width)
     value_heads = value_heads.transpose(1, 0, 2, 3).reshape(2, count, -1)
     value_heads = jnp.broadcast_to(
-        value_heads[None, :, None], (2, 2, 2) + value_heads.shape[1:]
+        value_heads[:, None, None], (2, 2, 2) + value_heads.shape[1:]
     ).reshape((N_DP,) + value_heads.shape[1:])
     gathered = exchange(value_heads, DP)
-    gathered, sent, kept, residue = lax.optimization_barrier((gathered, sent, kept, residue))
+    gathered, sent, kept = lax.optimization_barrier((gathered, sent, kept))
     came.append(swap(sent, "xl"))
-    residue[1] = swap(residue[1], "xl")
     parts = exchange(combine(ids, gathered, out_weights), ZY)
-    parts, came, kept, residue = lax.optimization_barrier((parts, came, kept, residue))
+    parts, came, kept = lax.optimization_barrier((parts, came, kept))
     kept = [kept, swap(kept, "c")]
     in_weight = jnp.concatenate(
         [
@@ -410,20 +402,21 @@
         ],
         axis=0,
     )
-    hidden = by_pair(*residue).astype(f32) + jnp.sum(parts.astype(f32), axis=0)
-
-    rows = spread(hidden.astype(bf16), PAIR, 2 * N_ZY).reshape((2, N_ZY) + hidden.shape)
-    near = swap(at_other(hidden), "xl")
-    near, in_weight = lax.optimization_barrier((near, in_weight))
-    rows, near = lax.optimization_barrier((rows, near))
-    sums = exchange(widen(ids, rows, in_weight).reshape(N_DP, chunk, -1), DP)
+    attended = jnp.sum(parts.astype(f32), axis=0)
+    mine, near = attended[0], cross(attended[1])
+    low = lax.axis_index("xh") == 0
+    attended = jnp.concatenate([jnp.where(low, mine, near), jnp.where(low, near, mine)], axis=0)
+    hidden = residue.astype(f32) + attended
+
+    rows = spread(hidden.astype(bf16), PAIR, 2 * N_ZY).reshape(2, N_ZY, chunk, features)
+    rows, in_weight = lax.optimization_barrier((rows, in_weight))
+    sums = exchange(widen(ids, rows, in_weight), DP)
     sums = jnp.sum(sums.reshape(2, 2, 2, chunk, -1).astype(f32), axis=(0, 2))
     squares = sums[0, :, 2 * units] + sums[0, :, 2 * units + 1]
     inverse = lax.rsqrt(squares / D + norm_eps)[:, None]
     active = sums[:, :, : 2 * units] * inverse
     active = (jax.nn.silu(active[0]) * active[1]).astype(bf16)
     parts = exchange(project(ids, spread(active, DP, N_DP), downs, 1)[:, 0], ZY)
-    hidden = by_pair(at_pair(hidden), near).reshape(chunk, -1)
     result = (hidden + jnp.sum(parts.astype(f32), axis=0)).astype(bf16)
 
     result = result.reshape(2, 2, rows_out // 8, 2, steps, features)

time: 258 us -> 264 us (1.023)
  waiting for transfers between devices: 48.1 us -> 53.7 us
    ppermute x13 -> x10, starting transfers between devices: 11.6 us -> 5.8 us  [swap(): return lax.ppermute(block, axis, SWAP)]
    ppermute x0 -> x2, waiting for transfers between devices: none -> 5.11 us  [cross(): return lax.ppermute(block, ('xh', 'xl'), [(i, 3 - i) for i in range(4)])]
    ppermute x0 -> x2, starting transfers between devices: none -> 4.35 us  [cross(): return lax.ppermute(block, ('xh', 'xl'), [(i, 3 - i) for i in range(4)])]
    ppermute x13 -> x10, waiting for transfers between devices: 15.9 us -> 18 us  [swap(): return lax.ppermute(block, axis, SWAP)]
    unnamed x36 -> x33, local copies, waits for them, and re-layouts: 6.63 us -> 6.17 us
  transfers between devices with their start and end apart: 19 -> 18, of which waited for: 9 -> 10; matrix products, arithmetic and copies ran while one was open for 15% -> 15% of each run, Pallas kernels for 8% -> 8%
where the time goes in v15:
time: 264 us; the launch traced here: 263 us
  blocking collectives  81.2 us (31%)
  waiting for transfers between devices  53.7 us (20%)
  starting transfers between devices  48.9 us (19%)
  other arithmetic  36.1 us (14%)
  Pallas kernels  31.4 us (12%)
  local copies, waits for them, and re-layouts  9.66 us (4%)
    all_to_all x3, blocking collectives, exchange(): return lax.all_to_all(blocks, axes, 0, 0, tiled=True)  81.2 us
    all_to_all x6, starting transfers between devices, exchange(): return lax.all_to_all(blocks, axes, 0, 0, tiled=True)  38.7 us
    all_to_all x6, waiting for transfers between devices, exchange(): return lax.all_to_all(blocks, axes, 0, 0, tiled=True)  30.6 us
    concatenate x1, other arithmetic, local(): jnp.concatenate([jnp.concatenate([own, swap(own, 'c') if k else kept[1]],...  20.7 us
    ppermute x10, waiting for transfers between devices, swap(): return lax.ppermute(block, axis, SWAP)  18 us
    pallas_call x2, Pallas kernels, attend(): pl.pallas_call(body, grid_spec=pltpu.PrefetchScalarGridSpec(num_scalar_pr...  9.82 us
    pallas_call x1, Pallas kernels, combine(): pl.pallas_call(body, grid_spec=pltpu.PrefetchScalarGridSpec(num_scalar_pr...  7.45 us
    pallas_call x1, Pallas kernels, widen(): pl.pallas_call(body, grid_spec=pltpu.PrefetchScalarGridSpec(num_scalar_pr...  6.36 us
  transfers between devices with their start and end apart: 18, of which 10 were waited for; matrix products, arithmetic and copies ran while one was open for 15% of the time, Pallas kernels for 8%

profile of v15, /device:TPU:1, one launch (start us, length us, event | category | flops | bytes accessed | tf_op | source)
XLA Modules:
  0.0 262.6 jit_solution(5239715702264195565)
XLA Ops:
  0.0 3.4 %collective-permute-start.1 = (bf16[1024,896]{1,0:T(8,128)(2,1)}, bf16[1024,896]{1,0:T(8,128)(2,1)}, u32[]{:S(2)}, u32[]{:S(2)}) collective-permute-start(bf16[1024,896]{1,0:T(8,128)(2,1)} %refs_0_), channel_id=1, source_target_pairs={{0,96},{32,64},{64,32},{96,0},{1,97},{33,65},{65,33},{97,1},{2,98}... | collective-permute-start | bytes 5505032 | tf_op jit(solution)/shard_map/ppermute | solution.py:40
  3.4 2.4 leave.1
  5.8 8.8 %all-to-all-start = ((bf16[16,72,128]{2,1,0:T(8,128)(2,1)}), bf16[16,72,128]{2,1,0:T(8,128)(2,1)S(1)}, u32[]{:S(2)}, u32[]{:S(2)}) async-start(bf16[16,72,128]{2,1,0:T(8,128)(2,1)} %leave.1), calls=%async_computation | async-start | bytes 589824 | tf_op jit(solution)/shard_map/all_to_all | solution.py:28
  14.8 1.1 copy.69
  15.9 6.5 %attend.1.refs_1_ = bf16[8,2,2,32,512]{4,3,2,1,0:T(8,128)(2,1)} custom-call(s32[4]{0:T(128)} %lengths_ref.3, s32[4]{0:T(128)} %lengths_ref.3, bf16[4,576,2]{2,1,0:T(8,128)(2,1)} %bitcast.54, bf16[2,4,576,128]{3,2,1,0:T(8,128)(2,1)} %bitcast.56, bf16[4,576,256]{2,1,0:T(8,128)(2,1)} %bitcast.59), custom_call_target="tpu_custom_call" | custom-call | tf_op jit(solution)/shard_map/attend/pallas_call | solution.py:149
  22.4 1.0 all-to-all-done.in_ref
  23.5 1.3 route.1
  24.8 6.2 %all-to-all-start.1 = ((bf16[16,72,128]{2,1,0:T(8,128)(2,1)}), bf16[16,72,128]{2,1,0:T(8,128)(2,1)S(1)}, u32[]{:S(2)}, u32[]{:S(2)}) async-start(bf16[16,72,128]{2,1,0:T(8,128)(2,1)} %route.1), calls=%async_computation.1 | async-start | bytes 589824 | tf_op jit(solution)/shard_map/all_to_all | solution.py:28
  31.1 3.7 %multiply_convert_fusion = bf16[896,1152]{1,0:T(8,128)(2,1)} fusion(f32[896]{0:T(1024)S(1)} %convert_element_type.53, bf16[896,1152]{1,0:T(8,128)(2,1)} %param.23, bf16[896,1152]{1,0:T(8,128)(2,1)} %param.24, pred[]{:T(512)S(6)} %eq.18), kind=kLoop, calls=%fused_computation.3 | loop fusion | flops 4128768 | bytes 6196737 | tf_op jit(solution)/shard_map/convert_element_type | solution.py:347
  34.7 1.3 multiply_convert_fusion.2
  36.0 0.7 fusion.13
  36.7 1.2 pad_add_fusion.ids_ref
  38.0 2.0 all-to-all-done.1.refs_0_
  39.9 0.7 copy-done.11
  40.7 3.4 %again.1 = bf16[8,2,2,32,512]{4,3,2,1,0:T(8,128)(2,1)} custom-call(s32[2]{0:T(128)} %pad_add_fusion.ids_ref, s32[4]{0:T(128)} %lengths_ref.3, bf16[4,576,2]{2,1,0:T(8,128)(2,1)} %bitcast.55, bf16[2,4,576,128]{3,2,1,0:T(8,128)(2,1)} %bitcast.57, bf16[16,72,128]{2,1,0:T(8,128)(2,1)} %copy-done.11, ...), custom_call_target="tpu_custom_call", output_to_operand_aliasing={{}: (5, {})} | custom-call | tf_op jit(solution)/shard_map/again/pallas_call | solution.py:149
  44.0 0.9 collective-permute-start.3
  44.9 8.5 %all-to-all-start.2 = ((bf16[16,2,32,512]{3,2,1,0:T(8,128)(2,1)}), bf16[16,2,32,512]{3,2,1,0:T(8,128)(2,1)S(1)}, u32[]{:S(2)}, u32[]{:S(2)}) async-start(bf16[16,2,32,512]{3,2,1,0:T(8,128)(2,1)} %bitcast.53), calls=%async_computation.2 | async-start | bytes 2097152 | tf_op jit(solution)/shard_map/all_to_all | solution.py:28
  54.0 1.9 pad_maximum_fusion.1
  56.2 0.6 copy-done.9
  56.8 1.3 multiply_convert_fusion.1
  58.1 3.9 %pad_maximum_fusion.weight_ref = bf16[2304,896]{1,0:T(8,128)(2,1)} fusion(bf16[1152,896]{1,0:T(8,128)(2,1)} %collective-permute-done.4, bf16[1152,896]{1,0:T(8,128)(2,1)S(1)} %copy-done.10), kind=kLoop, calls=%fused_computation.2 | loop fusion | flops 8257536 | bytes 8257536 | tf_op jit(solution)/shard_map/concatenate | solution.py:366
  62.0 7.1 %collective-permute-done.2 = bf16[448,1152]{1,0:T(8,128)(2,1)} collective-permute-done((bf16[448,1152]{1,0:T(8,128)(2,1)}, bf16[448,1152]{1,0:T(8,128)(2,1)}, u32[]{:S(2)}, u32[]{:S(2)}) %collective-permute-start.2) | collective-permute-done | bytes 1032224 | tf_op jit(solution)/shard_map/ppermute | solution.py:36
  69.1 1.7 all-to-all-done.2
  70.8 0.7 collective-permute-start.5
  71.6 1.3 fusion
  73.3 20.4 %all_to_all.45.rows_ref = bf16[8,32,2048]{2,1,0:T(8,128)(2,1)} all-to-all(bf16[8,32,2048]{2,1,0:T(8,128)(2,1)S(1)} %bitcast.60), channel_id=1, replica_groups=mesh['xh'=2,'xl'=2,'zl'=2,'zh'=2,'y'=4,'c'=2] {'xh','xl','zl'}, dimensions={0} | all-to-all | bytes 2097152 | tf_op jit(solution)/shard_map/all_to_all | solution.py:28
  93.8 7.5 %combine.1 = bf16[8,2,32,896]{3,2,1,0:T(8,128)(2,1)} custom-call(s32[2]{0:T(128)} %pad_add_fusion.ids_ref, bf16[8,32,2048]{2,1,0:T(8,128)(2,1)} %all_to_all.45.rows_ref, bf16[1024,896]{1,0:T(8,128)(2,1)} %refs_0_, bf16[1024,896]{1,0:T(8,128)(2,1)} %collective-permute-done.3.refs_1_, bf16[1024,896]{1,0:T(8,128)(2,1)} %collective-permute-done.1.refs_2_, ...), custom_call_target="tpu_custom_call" | custom-call | tf_op jit(solution)/shard_map/combine/pallas_call | solution.py:241
  101.3 5.8 %all-to-all-start.4 = ((bf16[8,2,32,896]{3,2,1,0:T(8,128)(2,1)}), bf16[8,2,32,896]{3,2,1,0:T(8,128)(2,1)S(1)}, u32[]{:S(2)}, u32[]{:S(2)}) async-start(bf16[8,2,32,896]{3,2,1,0:T(8,128)(2,1)} %combine.1), calls=%async_computation.4 | async-start | bytes 1835008 | tf_op jit(solution)/shard_map/all_to_all | solution.py:28
  107.1 10.0 %collective-permute-done.6 = bf16[448,1152]{1,0:T(8,128)(2,1)S(1)} collective-permute-done((bf16[448,1152]{1,0:T(8,128)(2,1)}, bf16[448,1152]{1,0:T(8,128)(2,1)S(1)}, u32[]{:S(2)}, u32[]{:S(2)}) %collective-permute-start.6) | collective-permute-done | bytes 1032224 | tf_op jit(solution)/shard_map/ppermute | solution.py:36
  117.1 5.9 %all-to-all-done.4 = bf16[8,2,32,896]{3,2,1,0:T(8,128)(2,1)S(1)} async-done(((bf16[8,2,32,896]{3,2,1,0:T(8,128)(2,1)}), bf16[8,2,32,896]{3,2,1,0:T(8,128)(2,1)S(1)}, u32[]{:S(2)}, u32[]{:S(2)}) %all-to-all-start.4) | async-done | bytes 917536 | tf_op jit(solution)/shard_map/all_to_all | solution.py:28
  123.0 0.9 collective-permute-start.8
  123.9 0.5 collective-permute-start.9
  124.5 1.0 collective-permute-start.7
  125.5 5.1 %collective-permute-done.7 = f32[32,896]{1,0:T(8,128)S(1)} collective-permute-done((f32[32,896]{1,0:T(8,128)S(1)}, f32[32,896]{1,0:T(8,128)S(1)}, u32[]{:S(2)}, u32[]{:S(2)}) %collective-permute-start.7) | collective-permute-done | bytes 114720 | tf_op jit(solution)/shard_map/ppermute | solution.py:40
  130.6 1.5 broadcast_in_dim.29
  132.2 3.7 %all-to-all-start.5 = ((bf16[16,64,896]{2,1,0:T(8,128)(2,1)}), bf16[16,64,896]{2,1,0:T(8,128)(2,1)S(1)}, u32[]{:S(2)}, u32[]{:S(2)}) async-start(bf16[16,64,896]{2,1,0:T(8,128)(2,1)} %broadcast_in_dim.29), calls=%async_computation.5 | async-start | bytes 3670016 | tf_op jit(solution)/shard_map/all_to_all | solution.py:28
  135.9 20.7 %maximum_maximum_fusion.weight_ref = bf16[1792,2304]{1,0:T(8,128)(2,1)} fusion(bf16[448,1152]{1,0:T(8,128)(2,1)} %collective-permute-done.10, bf16[448,1152]{1,0:T(8,128)(2,1)S(1)} %collective-permute-done.6, bf16[448,1152]{1,0:T(8,128)(2,1)} %collective-permute-done.9, bf16[448,1152]{1,0:T(8,128)(2,1)} %collective-permute-done.2, ...), kind=kLoop, calls=%fused_computation | loop fusion | flops 49545216 | bytes 16515072 | tf_op jit(solution)/shard_map/concatenate | solution.py:398
  156.6 5.7 %all-to-all-done.5 = bf16[16,64,896]{2,1,0:T(8,128)(2,1)S(1)} async-done(((bf16[16,64,896]{2,1,0:T(8,128)(2,1)}), bf16[16,64,896]{2,1,0:T(8,128)(2,1)S(1)}, u32[]{:S(2)}, u32[]{:S(2)}) %all-to-all-start.5) | async-done | bytes 1835040 | tf_op jit(solution)/shard_map/all_to_all | solution.py:28
  162.3 3.3 %copy-done.2 = bf16[1792,2304]{1,0:T(8,128)(2,1)S(1)} copy-done((bf16[1792,2304]{1,0:T(8,128)(2,1)S(1)}, bf16[1792,2304]{1,0:T(8,128)(2,1)}, u32[]{:S(2)}) %copy-start.2) | copy-done | bytes 8257560
  165.7 6.4 %widen.1 = bf16[8,64,2432]{2,1,0:T(8,128)(2,1)S(1)} custom-call(s32[2]{0:T(128)S(1)} %copy-done.4, bf16[2,8,64,896]{3,2,1,0:T(8,128)(2,1)S(1)} %bitcast.50, bf16[1792,2304]{1,0:T(8,128)(2,1)S(1)} %copy-done.2), custom_call_target="tpu_custom_call" | custom-call | tf_op jit(solution)/shard_map/widen/pallas_call | solution.py:286
  172.0 31.5 %all_to_all.46 = bf16[8,64,2432]{2,1,0:T(8,128)(2,1)S(1)} all-to-all(bf16[8,64,2432]{2,1,0:T(8,128)(2,1)S(1)} %widen.1), channel_id=1, replica_groups=mesh['xh'=2,'xl'=2,'zl'=2,'zh'=2,'y'=4,'c'=2] {'xh','xl','zl'}, dimensions={0} | all-to-all | bytes 4980736 | tf_op jit(solution)/shard_map/all_to_all | solution.py:28
  204.6 29.2 %all_to_all.47.rows_ref = bf16[8,64,2304]{2,1,0:T(8,128)(2,1)S(1)} all-to-all(bf16[8,64,2304]{2,1,0:T(8,128)(2,1)S(1)} %broadcast_in_dim.31), channel_id=1, replica_groups=mesh['xh'=2,'xl'=2,'zl'=2,'zh'=2,'y'=4,'c'=2] {'xh','xl','zl'}, dimensions={0} | all-to-all | bytes 4718592 | tf_op jit(solution)/shard_map/all_to_all | solution.py:28
  233.8 4.1 %project.1 = bf16[8,1,64,896]{3,2,1,0:T(8,128)(2,1)} custom-call(s32[2]{0:T(128)S(1)} %copy-done.4, bf16[8,64,2304]{2,1,0:T(8,128)(2,1)S(1)} %all_to_all.47.rows_ref, bf16[2304,896]{1,0:T(8,128)(2,1)S(1)} %copy-done.3), custom_call_target="tpu_custom_call" | custom-call | tf_op jit(solution)/shard_map/project/pallas_call | solution.py:190
  237.9 5.6 %all-to-all-start.8 = ((bf16[8,64,896]{2,1,0:T(8,128)(2,1)}), bf16[8,64,896]{2,1,0:T(8,128)(2,1)S(1)}, u32[]{:S(2)}, u32[]{:S(2)}) async-start(bf16[8,64,896]{2,1,0:T(8,128)(2,1)} %bitcast.22), calls=%async_computation.8 | async-start | bytes 1835008 | tf_op jit(solution)/shard_map/all_to_all | solution.py:28
  243.5 14.3 %all-to-all-done.8 = bf16[8,64,896]{2,1,0:T(8,128)(2,1)S(1)} async-done(((bf16[8,64,896]{2,1,0:T(8,128)(2,1)}), bf16[8,64,896]{2,1,0:T(8,128)(2,1)S(1)}, u32[]{:S(2)}, u32[]{:S(2)}) %all-to-all-start.8) | async-done | bytes 917536 | tf_op jit(solution)/shard_map/all_to_all | solution.py:28
  258.1 2.5 collective-permute-start.11
  260.7 0.9 collective-permute-done.11
  261.9 0.7 copy.79
  (69 shorter events, 3.4 us)
Async XLA Ops:
  0.0 53.5 %copy-start = (bf16[2,512,896]{2,1,0:T(8,128)(2,1)S(1)}, bf16[2,512,896]{2,1,0:T(8,128)(2,1)}, u32[]{:S(2)}) copy-start(bf16[2,512,896]{2,1,0:T(8,128)(2,1)} %param.21) | copy-start | bytes 5505028
  0.0 14.6 %copy-start.12 = (bf16[8,512,128]{2,1,0:T(8,128)(2,1)S(1)}, bf16[8,512,128]{2,1,0:T(8,128)(2,1)}, u32[]{:S(2)}) copy-start(bf16[8,512,128]{2,1,0:T(8,128)(2,1)} %param.19) | copy-start | bytes 3145732
  0.0 14.8 %copy-start.14 = (bf16[2,4,576]{2,1,0:T(4,128)(2,1)S(1)}, bf16[2,4,576]{2,1,0:T(4,128)(2,1)}, u32[]{:S(2)}) copy-start(bf16[2,4,576]{2,1,0:T(4,128)(2,1)} %param.18) | copy-start | bytes 27652
  0.0 15.9 %copy-start.13 = (bf16[896]{0:T(1024)(128)(2,1)S(1)}, bf16[896]{0:T(1024)(128)(2,1)}, u32[]{:S(2)}) copy-start(bf16[896]{0:T(1024)(128)(2,1)} %param.22) | copy-start | bytes 5380
  0.0 44.0 %collective-permute-start.1 = (bf16[1024,896]{1,0:T(8,128)(2,1)}, bf16[1024,896]{1,0:T(8,128)(2,1)}, u32[]{:S(2)}, u32[]{:S(2)}) collective-permute-start(bf16[1024,896]{1,0:T(8,128)(2,1)} %refs_0_), channel_id=1, source_target_pairs={{0,96},{32,64},{64,32},{96,0},{1,97},{33,65},{65,33},{97,1},{2,98}... | collective-permute-start | bytes 5505032 | tf_op jit(solution)/shard_map/ppermute | solution.py:40
  5.8 17.7 %all-to-all-start = ((bf16[16,72,128]{2,1,0:T(8,128)(2,1)}), bf16[16,72,128]{2,1,0:T(8,128)(2,1)S(1)}, u32[]{:S(2)}, u32[]{:S(2)}) async-start(bf16[16,72,128]{2,1,0:T(8,128)(2,1)} %leave.1), calls=%async_computation | async-start | bytes 589824 | tf_op jit(solution)/shard_map/all_to_all | solution.py:28
  14.6 25.3 %collective-permute-start = (bf16[8,512,128]{2,1,0:T(8,128)(2,1)S(1)}, bf16[8,512,128]{2,1,0:T(8,128)(2,1)}, u32[]{:S(2)}, u32[]{:S(2)}) collective-permute-start(bf16[8,512,128]{2,1,0:T(8,128)(2,1)S(1)} %copy-done.12), channel_id=1, source_target_pairs={{0,1},{1,0},{2,3},{3,2},{4,5},{5,4},{6,7},{7,6},{8,9},{9,8},{10,11... | collective-permute-start | bytes 3145736 | tf_op jit(solution)/shard_map/ppermute | solution.py:36
  15.9 7.6 %copy-start.5 = (s32[1,16]{1,0:T(1,128)S(1)}, s32[1,16]{1,0:T(1,128)}, u32[]{:S(2)}) copy-start(s32[1,16]{1,0:T(1,128)} %param.16) | copy-start | bytes 196
  24.8 15.1 %all-to-all-start.1 = ((bf16[16,72,128]{2,1,0:T(8,128)(2,1)}), bf16[16,72,128]{2,1,0:T(8,128)(2,1)S(1)}, u32[]{:S(2)}, u32[]{:S(2)}) async-start(bf16[16,72,128]{2,1,0:T(8,128)(2,1)} %route.1), calls=%async_computation.1 | async-start | bytes 589824 | tf_op jit(solution)/shard_map/all_to_all | solution.py:28
  31.0 3.7 %copy-start.6 = (bf16[896,1152]{1,0:T(8,128)(2,1)S(1)}, bf16[896,1152]{1,0:T(8,128)(2,1)}, u32[]{:S(2)}) copy-start(bf16[896,1152]{1,0:T(8,128)(2,1)} %param.23) | copy-start | bytes 6193156
  31.0 3.7 %copy-start.8 = (bf16[896,1152]{1,0:T(8,128)(2,1)S(1)}, bf16[896,1152]{1,0:T(8,128)(2,1)}, u32[]{:S(2)}) copy-start(bf16[896,1152]{1,0:T(8,128)(2,1)} %param.24) | copy-start | bytes 6193156
  34.7 1.3 copy-start.15
  39.9 0.7 copy-start.11
  44.0 9.5 %collective-permute-start.3 = (bf16[1024,896]{1,0:T(8,128)(2,1)}, bf16[1024,896]{1,0:T(8,128)(2,1)}, u32[]{:S(2)}, u32[]{:S(2)}) collective-permute-start(bf16[1024,896]{1,0:T(8,128)(2,1)} %refs_0_), channel_id=1, source_target_pairs={{0,1},{1,0},{2,3},{3,2},{4,5},{5,4},{6,7},{7,6},{8,9},{9,8},{10,11... | collective-permute-start | bytes 5505032 | tf_op jit(solution)/shard_map/ppermute | solution.py:36
  44.9 13.2 %collective-permute-start.4 = (bf16[1152,896]{1,0:T(8,128)(2,1)}, bf16[1152,896]{1,0:T(8,128)(2,1)}, u32[]{:S(2)}, u32[]{:S(2)}) collective-permute-start(bf16[1152,896]{1,0:T(8,128)(2,1)} %param.25), channel_id=1, source_target_pairs={{0,1},{1,0},{2,3},{3,2},{4,5},{5,4},{6,7},{7,6},{8,9},{9,8},{10,11... | collective-permute-start | bytes 6193160 | tf_op jit(solution)/shard_map/ppermute | solution.py:36
  44.9 24.2 %collective-permute-start.2 = (bf16[448,1152]{1,0:T(8,128)(2,1)}, bf16[448,1152]{1,0:T(8,128)(2,1)}, u32[]{:S(2)}, u32[]{:S(2)}) collective-permute-start(bf16[448,1152]{1,0:T(8,128)(2,1)} %multiply_convert_fusion.2), channel_id=1, source_target_pairs={{0,32},{32,0},{1,33},{33,1},{2,34},{34,2},{3,35},{35,3},{4,36},{36... | collective-permute-start | bytes 3096584 | tf_op jit(solution)/shard_map/ppermute | solution.py:36
  44.9 25.9 %all-to-all-start.2 = ((bf16[16,2,32,512]{3,2,1,0:T(8,128)(2,1)}), bf16[16,2,32,512]{3,2,1,0:T(8,128)(2,1)S(1)}, u32[]{:S(2)}, u32[]{:S(2)}) async-start(bf16[16,2,32,512]{3,2,1,0:T(8,128)(2,1)} %bitcast.53), calls=%async_computation.2 | async-start | bytes 2097152 | tf_op jit(solution)/shard_map/all_to_all | solution.py:28
  54.0 2.2 copy-start.7
  54.0 2.8 %copy-start.9 = (bf16[896,1152]{1,0:T(8,128)(2,1)S(1)}, bf16[896,1152]{1,0:T(8,128)(2,1)}, u32[]{:S(2)}) copy-start(bf16[896,1152]{1,0:T(8,128)(2,1)} %param.24) | copy-start | bytes 6193156
  55.9 2.2 copy-start.10
  70.8 23.0 %collective-permute-start.5 = (bf16[1024,896]{1,0:T(8,128)(2,1)}, bf16[1024,896]{1,0:T(8,128)(2,1)}, u32[]{:S(2)}, u32[]{:S(2)}) collective-permute-start(bf16[1024,896]{1,0:T(8,128)(2,1)} %collective-permute-done.1.refs_2_), channel_id=1, source_target_pairs={{0,1},{1,0},{2,3},{3,2},{4,5},{5,4},{6,7},{7,6},{8,9},{9,8},{10,11... | collective-permute-start | bytes 5505032 | tf_op jit(solution)/shard_map/ppermute | solution.py:36
  93.8 23.4 %collective-permute-start.6 = (bf16[448,1152]{1,0:T(8,128)(2,1)}, bf16[448,1152]{1,0:T(8,128)(2,1)S(1)}, u32[]{:S(2)}, u32[]{:S(2)}) collective-permute-start(bf16[448,1152]{1,0:T(8,128)(2,1)} %multiply_convert_fusion.1), channel_id=1, source_target_pairs={{0,32},{32,0},{1,33},{33,1},{2,34},{34,2},{3,35},{35,3},{4,36},{36... | collective-permute-start | bytes 3096584 | tf_op jit(solution)/shard_map/ppermute | solution.py:36
  101.3 21.7 %all-to-all-start.4 = ((bf16[8,2,32,896]{3,2,1,0:T(8,128)(2,1)}), bf16[8,2,32,896]{3,2,1,0:T(8,128)(2,1)S(1)}, u32[]{:S(2)}, u32[]{:S(2)}) async-start(bf16[8,2,32,896]{3,2,1,0:T(8,128)(2,1)} %combine.1), calls=%async_computation.4 | async-start | bytes 1835008 | tf_op jit(solution)/shard_map/all_to_all | solution.py:28
  123.0 12.9 %collective-permute-start.8 = (bf16[896,1152]{1,0:T(8,128)(2,1)}, bf16[896,1152]{1,0:T(8,128)(2,1)}, u32[]{:S(2)}, u32[]{:S(2)}) collective-permute-start(bf16[896,1152]{1,0:T(8,128)(2,1)} %multiply_convert_fusion), channel_id=1, source_target_pairs={{0,1},{1,0},{2,3},{3,2},{4,5},{5,4},{6,7},{7,6},{8,9},{9,8},{10,11... | collective-permute-start | bytes 6193160 | tf_op jit(solution)/shard_map/ppermute | solution.py:36
  123.9 12.0 %collective-permute-start.10 = (bf16[448,1152]{1,0:T(8,128)(2,1)S(1)}, bf16[448,1152]{1,0:T(8,128)(2,1)}, u32[]{:S(2)}, u32[]{:S(2)}) collective-permute-start(bf16[448,1152]{1,0:T(8,128)(2,1)S(1)} %collective-permute-done.6), channel_id=1, source_target_pairs={{0,1},{1,0},{2,3},{3,2},{4,5},{5,4},{6,7},{7,6},{8,9},{9,8},{10,11... | collective-permute-start | bytes 3096584 | tf_op jit(solution)/shard_map/ppermute | solution.py:36
  123.9 12.0 %collective-permute-start.9 = (bf16[448,1152]{1,0:T(8,128)(2,1)}, bf16[448,1152]{1,0:T(8,128)(2,1)}, u32[]{:S(2)}, u32[]{:S(2)}) collective-permute-start(bf16[448,1152]{1,0:T(8,128)(2,1)} %collective-permute-done.2), channel_id=1, source_target_pairs={{0,1},{1,0},{2,3},{3,2},{4,5},{5,4},{6,7},{7,6},{8,9},{9,8},{10,11... | collective-permute-start | bytes 3096584 | tf_op jit(solution)/shard_map/ppermute | solution.py:36
  124.5 6.1 %collective-permute-start.7 = (f32[32,896]{1,0:T(8,128)S(1)}, f32[32,896]{1,0:T(8,128)S(1)}, u32[]{:S(2)}, u32[]{:S(2)}) collective-permute-start(f32[32,896]{1,0:T(8,128)S(1)} %slice_bitcast_fusion), channel_id=1, source_target_pairs={{0,96},{32,64},{64,32},{96,0},{1,97},{33,65},{65,33},{97,1},{2,98}... | collective-permute-start | bytes 344072 | tf_op jit(solution)/shard_map/ppermute | solution.py:40
  132.2 30.2 %all-to-all-start.5 = ((bf16[16,64,896]{2,1,0:T(8,128)(2,1)}), bf16[16,64,896]{2,1,0:T(8,128)(2,1)S(1)}, u32[]{:S(2)}, u32[]{:S(2)}) async-start(bf16[16,64,896]{2,1,0:T(8,128)(2,1)} %broadcast_in_dim.29), calls=%async_computation.5 | async-start | bytes 3670016 | tf_op jit(solution)/shard_map/all_to_all | solution.py:28
  135.9 26.4 %copy-start.4 = (s32[2]{0:T(128)S(1)}, s32[2]{0:T(128)}, u32[]{:S(2)}) copy-start(s32[2]{0:T(128)} %pad_add_fusion.ids_ref) | copy-start | bytes 28
  162.3 3.3 %copy-start.2 = (bf16[1792,2304]{1,0:T(8,128)(2,1)S(1)}, bf16[1792,2304]{1,0:T(8,128)(2,1)}, u32[]{:S(2)}) copy-start(bf16[1792,2304]{1,0:T(8,128)(2,1)} %maximum_maximum_fusion.weight_ref) | copy-start | bytes 24772612
  204.5 29.3 %copy-start.3 = (bf16[2304,896]{1,0:T(8,128)(2,1)S(1)}, bf16[2304,896]{1,0:T(8,128)(2,1)}, u32[]{:S(2)}) copy-start(bf16[2304,896]{1,0:T(8,128)(2,1)} %pad_maximum_fusion.weight_ref) | copy-start | bytes 12386308
  237.9 24.7 %copy-start.1 = (bf16[2,512,896]{2,1,0:T(8,128)(2,1)S(1)}, bf16[2,512,896]{2,1,0:T(8,128)(2,1)}, u32[]{:S(2)}) copy-start(bf16[2,512,896]{2,1,0:T(8,128)(2,1)} %param.21) | copy-start | bytes 5505028
  237.9 20.0 %all-to-all-start.8 = ((bf16[8,64,896]{2,1,0:T(8,128)(2,1)}), bf16[8,64,896]{2,1,0:T(8,128)(2,1)S(1)}, u32[]{:S(2)}, u32[]{:S(2)}) async-start(bf16[8,64,896]{2,1,0:T(8,128)(2,1)} %bitcast.22), calls=%async_computation.8 | async-start | bytes 1835008 | tf_op jit(solution)/shard_map/all_to_all | solution.py:28
  258.1 3.4 %collective-permute-start.11 = (bf16[2,4,2,2,896]{4,3,2,1,0:T(2,128)(2,1)S(1)}, bf16[2,4,2,2,896]{4,3,2,1,0:T(2,128)(2,1)S(1)}, u32[]{:S(2)}, u32[]{:S(2)}) collective-permute-start(bf16[2,4,2,2,896]{4,3,2,1,0:T(2,128)(2,1)S(1)} %dynamic-slice_bitcast_fusion.1), channel_id=1, source_target_pairs={{0,1},{1,0},{2,3},{3,2},{4,5},{5,4},{6,7},{7,6},{8,9},{9,8},{10,11... | collective-permute-start | bytes 172040 | tf_op jit(solution)/shard_map/ppermute | solution.py:36

commit v16 on v13

--- a/solution.py
+++ b/solution.py
@@ -174,32 +174,27 @@
     )(ids, lengths, fresh_t, queries_t, *extra)
 
 
-def project(ids, rows, weight, blocks):
+def project(rows, weight):
     groups, count, depth = rows.shape
-    width = weight.shape[1] // blocks
-
-    def body(ids_ref, rows_ref, weight_ref, out_ref):
+    width = weight.shape[1]
+    part = count // 4
+
+    def body(rows_ref, weight_ref, out_ref):
         lhs = rows_ref[...].reshape(groups * count, depth)
         total = jnp.dot(lhs, weight_ref[...], preferred_element_type=f32)
-        out_ref[:, 0] = total.astype(bf16).reshape(groups, count, width)
-
-    return pl.pallas_call(
-        body,
-        grid_spec=pltpu.PrefetchScalarGridSpec(
-            num_scalar_prefetch=1,
-            grid=(blocks,),
-            in_specs=[
-                whole(rows.shape),
-                pl.BlockSpec((depth, width), lambda k, ids: (0, k)),
-            ],
-            out_specs=pl.BlockSpec(
-                (groups, 1, count, width), lambda k, ids: (0, lax.rem(ids[1] + k, blocks), 0, 0)
-            ),
-        ),
-        out_shape=jax.ShapeDtypeStruct((groups, blocks, count, width), bf16),
+        total = total.astype(bf16).reshape(groups, count, width)
+        for k in range(4):
+            out_ref[:, k % 2, k // 2] = total[:, k * part : (k + 1) * part]
+
+    return pl.pallas_call(
+        body,
+        grid=(1,),
+        in_specs=[whole(rows.shape), whole(weight.shape)],
+        out_specs=whole((groups, 2, 2, part, width)),
+        out_shape=jax.ShapeDtypeStruct((groups, 2, 2, part, width), bf16),
         compiler_params=params(40),
         name="project",
-    )(ids, rows, weight)
+    )(rows, weight)
 
 
 def fetches(refs, blocks, weight_ref, sems):
@@ -415,22 +410,21 @@
     rows = spread(hidden.astype(bf16), PAIR, 2 * N_ZY).reshape((2, N_ZY) + hidden.shape)
     near = swap(at_other(hidden), "xl")
     near, in_weight = lax.optimization_barrier((near, in_weight))
-    rows, near = lax.optimization_barrier((rows, near))
+    hidden = by_pair(at_pair(hidden), near).reshape(2, 2, count // 2, features)
+    mine = lax.dynamic_index_in_dim(hidden, core, 1, False)
+    near = swap(lax.dynamic_index_in_dim(hidden, 1 - core, 1, False), "c")
+    first = core == 0
+    hidden = jnp.stack([jnp.where(first, mine, near), jnp.where(first, near, mine)])
     sums = exchange(widen(ids, rows, in_weight).reshape(N_DP, chunk, -1), DP)
     sums = jnp.sum(sums.reshape(2, 2, 2, chunk, -1).astype(f32), axis=(0, 2))
     squares = sums[0, :, 2 * units] + sums[0, :, 2 * units + 1]
     inverse = lax.rsqrt(squares / D + norm_eps)[:, None]
     active = sums[:, :, : 2 * units] * inverse
     active = (jax.nn.silu(active[0]) * active[1]).astype(bf16)
-    parts = exchange(project(ids, spread(active, DP, N_DP), downs, 1)[:, 0], ZY)
-    hidden = by_pair(at_pair(hidden), near).reshape(chunk, -1)
+    parts = project(spread(active, DP, N_DP), downs).reshape(N_TP, count, features)
+    parts = exchange(parts, TP).reshape((N_ZY,) + hidden.shape)
     result = (hidden + jnp.sum(parts.astype(f32), axis=0)).astype(bf16)
-
     result = result.reshape(2, 2, rows_out // 8, 2, steps, features)
-    mine = lax.dynamic_index_in_dim(result, core, 1, False)
-    near = swap(lax.dynamic_index_in_dim(result, 1 - core, 1, False), "c")
-    first = core == 0
-    result = jnp.stack([jnp.where(first, mine, near), jnp.where(first, near, mine)])
     return result.transpose(4, 1, 2, 0, 3, 5).reshape(steps, rows_out, features)
 
 

time: 256 us -> 259 us (1.012)
    all_to_all x6, starting transfers between devices: 36.7 us -> 40.5 us  [exchange(): return lax.all_to_all(blocks, axes, 0, 0, tiled=True)]
    unnamed x28 -> x26, local copies, waits for them, and re-layouts: 5.53 us -> 5.26 us
where the time goes in v16:
time: 259 us; the launch traced here: 258 us
  blocking collectives  79.8 us (31%)
  starting transfers between devices  50.6 us (20%)
  waiting for transfers between devices  45 us (17%)
  other arithmetic  39.6 us (15%)
  Pallas kernels  30.8 us (12%)
  local copies, waits for them, and re-layouts  8.95 us (3%)
  matrix products  2.91 us (1%)
    all_to_all x3, blocking collectives, exchange(): return lax.all_to_all(blocks, axes, 0, 0, tiled=True)  79.8 us
    all_to_all x6, starting transfers between devices, exchange(): return lax.all_to_all(blocks, axes, 0, 0, tiled=True)  40.5 us
    all_to_all x6, waiting for transfers between devices, exchange(): return lax.all_to_all(blocks, axes, 0, 0, tiled=True)  28.3 us
    concatenate x1, other arithmetic, local(): jnp.concatenate([jnp.concatenate([own, swap(own, 'c') if k else kept[1]],...  19.9 us
    ppermute x13, waiting for transfers between devices, swap(): return lax.ppermute(block, axis, SWAP)  16.7 us
    ppermute x13, starting transfers between devices, swap(): return lax.ppermute(block, axis, SWAP)  10.2 us
    pallas_call x2, Pallas kernels, attend(): pl.pallas_call(body, grid_spec=pltpu.PrefetchScalarGridSpec(num_scalar_pr...  9.79 us
    convert_element_type x3, other arithmetic, scaled(): return (weight.astype(f32) * gain[low:high]).astype(bf16)  9.23 us
  transfers between devices with their start and end apart: 19, of which 9 were waited for; matrix products, arithmetic and copies ran while one was open for 16% of the time, Pallas kernels for 8%

profile of v16, /device:TPU:1, one launch (start us, length us, event | category | flops | bytes accessed | tf_op | source)
XLA Modules:
  0.0 258.1 jit_solution(4971722808789182758)
XLA Ops:
  0.0 2.1 collective-permute-start.1
  2.1 2.4 leave.1
  4.6 8.8 %all-to-all-start = ((bf16[16,72,128]{2,1,0:T(8,128)(2,1)}), bf16[16,72,128]{2,1,0:T(8,128)(2,1)S(1)}, u32[]{:S(2)}, u32[]{:S(2)}) async-start(bf16[16,72,128]{2,1,0:T(8,128)(2,1)} %leave.1), calls=%async_computation | async-start | bytes 589824 | tf_op jit(solution)/shard_map/all_to_all | solution.py:28
  13.5 1.1 copy.57
  14.7 6.4 %attend.1.refs_1_ = bf16[8,2,2,32,512]{4,3,2,1,0:T(8,128)(2,1)} custom-call(s32[4]{0:T(128)} %lengths_ref.3, s32[4]{0:T(128)} %lengths_ref.3, bf16[4,576,2]{2,1,0:T(8,128)(2,1)} %bitcast.62, bf16[2,4,576,128]{3,2,1,0:T(8,128)(2,1)} %bitcast.64, bf16[4,576,256]{2,1,0:T(8,128)(2,1)} %bitcast.67), custom_call_target="tpu_custom_call" | custom-call | tf_op jit(solution)/shard_map/attend/pallas_call | solution.py:145
  21.1 1.1 all-to-all-done.in_ref
  22.2 1.3 route.1
  23.5 6.2 %all-to-all-start.1 = ((bf16[16,72,128]{2,1,0:T(8,128)(2,1)}), bf16[16,72,128]{2,1,0:T(8,128)(2,1)S(1)}, u32[]{:S(2)}, u32[]{:S(2)}) async-start(bf16[16,72,128]{2,1,0:T(8,128)(2,1)} %route.1), calls=%async_computation.1 | async-start | bytes 589824 | tf_op jit(solution)/shard_map/all_to_all | solution.py:28
  29.7 3.5 %multiply_convert_fusion = bf16[896,1152]{1,0:T(8,128)(2,1)} fusion(f32[896]{0:T(1024)S(1)} %convert_element_type.65, bf16[896,1152]{1,0:T(8,128)(2,1)} %param.23, bf16[896,1152]{1,0:T(8,128)(2,1)} %param.24, pred[]{:T(512)S(6)} %eq.17), kind=kLoop, calls=%fused_computation.3 | loop fusion | flops 4128768 | bytes 6196737 | tf_op jit(solution)/shard_map/convert_element_type | solution.py:351
  33.2 2.6 %multiply_convert_fusion.2 = bf16[384,1152]{1,0:T(8,128)(2,1)} fusion(f32[384]{0:T(512)S(1)} %slice.37, bf16[896,1152]{1,0:T(8,128)(2,1)} %param.23, bf16[896,1152]{1,0:T(8,128)(2,1)} %param.24, pred[]{:T(512)S(6)} %eq.17), kind=kLoop, calls=%fused_computation.8 | loop fusion | flops 1769472 | bytes 2655745 | tf_op jit(solution)/shard_map/convert_element_type | solution.py:351
  35.9 0.7 fusion.12
  36.5 1.2 pad_add_fusion.ids_ref
  37.7 0.9 all-to-all-done.1.refs_0_
  38.6 0.7 copy-done.6
  39.3 3.3 %again.1 = bf16[8,2,2,32,512]{4,3,2,1,0:T(8,128)(2,1)} custom-call(s32[2]{0:T(128)} %pad_add_fusion.ids_ref, s32[4]{0:T(128)} %lengths_ref.3, bf16[4,576,2]{2,1,0:T(8,128)(2,1)} %bitcast.63, bf16[2,4,576,128]{3,2,1,0:T(8,128)(2,1)} %bitcast.65, bf16[16,72,128]{2,1,0:T(8,128)(2,1)} %copy-done.6, ...), custom_call_target="tpu_custom_call", output_to_operand_aliasing={{}: (5, {})} | custom-call | tf_op jit(solution)/shard_map/again/pallas_call | solution.py:145
  42.7 0.9 collective-permute-start.3
  43.6 0.5 collective-permute-start.5
  44.1 1.3 collective-permute-start.2
  45.4 8.1 %all-to-all-start.2 = ((bf16[16,2,32,512]{3,2,1,0:T(8,128)(2,1)}), bf16[16,2,32,512]{3,2,1,0:T(8,128)(2,1)S(1)}, u32[]{:S(2)}, u32[]{:S(2)}) async-start(bf16[16,2,32,512]{3,2,1,0:T(8,128)(2,1)} %bitcast.61), calls=%async_computation.2 | async-start | bytes 2097152 | tf_op jit(solution)/shard_map/all_to_all | solution.py:28
  54.0 3.1 %multiply_convert_fusion.1 = bf16[512,1152]{1,0:T(8,128)(2,1)} fusion(f32[512]{0:T(512)S(1)} %slice.40, bf16[896,1152]{1,0:T(8,128)(2,1)} %param.23, bf16[896,1152]{1,0:T(8,128)(2,1)} %param.24, pred[]{:T(512)S(6)} %eq.17), kind=kLoop, calls=%fused_computation.4 | loop fusion | flops 2359296 | bytes 3540993 | tf_op jit(solution)/shard_map/convert_element_type | solution.py:351
  57.3 2.7 %pad_maximum_fusion.1 = bf16[16,512,128]{2,1,0:T(8,128)(2,1)} fusion(bf16[8,512,128]{2,1,0:T(8,128)(2,1)} %collective-permute-done, bf16[8,512,128]{2,1,0:T(8,128)(2,1)S(1)} %copy-done.8), kind=kLoop, calls=%fused_computation.5 | loop fusion | flops 1048576 | bytes 4194304 | tf_op jit(solution)/shard_map/concatenate | solution.py:375
  60.1 4.5 %pad_maximum_fusion.weight_ref = bf16[2304,896]{1,0:T(8,128)(2,1)} fusion(bf16[1152,896]{1,0:T(8,128)(2,1)} %collective-permute-done.4, bf16[1152,896]{1,0:T(8,128)(2,1)} %param.25), kind=kLoop, calls=%fused_computation.2 | loop fusion | flops 8257536 | bytes 8257536 | tf_op jit(solution)/shard_map/concatenate | solution.py:371
  64.6 1.1 collective-permute-done.2
  65.7 5.1 %all-to-all-done.2 = bf16[16,2,32,512]{3,2,1,0:T(8,128)(2,1)S(1)} async-done(((bf16[16,2,32,512]{3,2,1,0:T(8,128)(2,1)}), bf16[16,2,32,512]{3,2,1,0:T(8,128)(2,1)S(1)}, u32[]{:S(2)}, u32[]{:S(2)}) %all-to-all-start.2) | async-done | bytes 1048608 | tf_op jit(solution)/shard_map/all_to_all | solution.py:28
  70.8 2.9 %fusion = bf16[64,16,128]{2,0,1:T(8,128)(2,1)S(1)} fusion(bf16[16,512,128]{2,1,0:T(8,128)(2,1)} %pad_maximum_fusion.1, bf16[64,16,512]{2,1,0:T(8,128)(2,1)S(1)} %bitcast.69), kind=kOutput, calls=%fused_computation.11 | convolution fusion | flops 134348800 | bytes 3407872 | tf_op jit(solution)/shard_map/thl,hlv->thv/dot_general | solution.py:385
  74.2 18.3 %all_to_all.45.rows_ref = bf16[8,32,2048]{2,1,0:T(8,128)(2,1)} all-to-all(bf16[8,32,2048]{2,1,0:T(8,128)(2,1)S(1)} %bitcast.68), channel_id=1, replica_groups=mesh['xh'=2,'xl'=2,'zl'=2,'zh'=2,'y'=4,'c'=2] {'xh','xl','zl'}, dimensions={0} | all-to-all | bytes 2097152 | tf_op jit(solution)/shard_map/all_to_all | solution.py:28
  92.8 7.4 %combine.1 = bf16[8,2,32,896]{3,2,1,0:T(8,128)(2,1)} custom-call(s32[2]{0:T(128)} %pad_add_fusion.ids_ref, bf16[8,32,2048]{2,1,0:T(8,128)(2,1)} %all_to_all.45.rows_ref, bf16[1024,896]{1,0:T(8,128)(2,1)} %refs_0_, bf16[1024,896]{1,0:T(8,128)(2,1)} %collective-permute-done.3.refs_1_, bf16[1024,896]{1,0:T(8,128)(2,1)} %collective-permute-done.1.refs_2_, ...), custom_call_target="tpu_custom_call" | custom-call | tf_op jit(solution)/shard_map/combine/pallas_call | solution.py:233
  100.2 3.6 %all-to-all-start.4 = ((bf16[8,2,32,896]{3,2,1,0:T(8,128)(2,1)}), bf16[8,2,32,896]{3,2,1,0:T(8,128)(2,1)S(1)}, u32[]{:S(2)}, u32[]{:S(2)}) async-start(bf16[8,2,32,896]{3,2,1,0:T(8,128)(2,1)} %combine.1), calls=%async_computation.4 | async-start | bytes 1835008 | tf_op jit(solution)/shard_map/all_to_all | solution.py:28
  103.8 1.3 collective-permute-start.7
  105.1 14.3 %collective-permute-done.7 = bf16[32,896]{1,0:T(8,128)(2,1)S(1)} collective-permute-done((bf16[32,896]{1,0:T(8,128)(2,1)S(1)}, bf16[32,896]{1,0:T(8,128)(2,1)S(1)}, u32[]{:S(2)}, u32[]{:S(2)}) %collective-permute-start.7) | collective-permute-done | bytes 57376 | tf_op jit(solution)/shard_map/ppermute | solution.py:36
  119.4 0.3 all-to-all-done.4
  119.7 2.6 %collective-permute-start.9 = (bf16[896,1152]{1,0:T(8,128)(2,1)}, bf16[896,1152]{1,0:T(8,128)(2,1)}, u32[]{:S(2)}, u32[]{:S(2)}) collective-permute-start(bf16[896,1152]{1,0:T(8,128)(2,1)} %multiply_convert_fusion), channel_id=1, source_target_pairs={{0,1},{1,0},{2,3},{3,2},{4,5},{5,4},{6,7},{7,6},{8,9},{9,8},{10,11... | collective-permute-start | bytes 6193160 | tf_op jit(solution)/shard_map/ppermute | solution.py:36
  122.4 0.3 collective-permute-start.11
  123.1 0.3 collective-permute-start.8
  123.4 1.5 broadcast_in_dim.29
  124.9 4.7 %all-to-all-start.5 = ((bf16[16,2,32,896]{3,2,1,0:T(8,128)(2,1)}), bf16[16,2,32,896]{3,2,1,0:T(8,128)(2,1)S(1)}, u32[]{:S(2)}, u32[]{:S(2)}) async-start(bf16[16,2,32,896]{3,2,1,0:T(8,128)(2,1)} %broadcast_in_dim.29), calls=%async_computation.5 | async-start | bytes 3670016 | tf_op jit(solution)/shard_map/all_to_all | solution.py:28
  129.6 19.9 %maximum_maximum_fusion.weight_ref = bf16[1792,2304]{1,0:T(8,128)(2,1)} fusion(bf16[512,1152]{1,0:T(8,128)(2,1)} %collective-permute-done.11, bf16[512,1152]{1,0:T(8,128)(2,1)S(1)} %collective-permute-done.6, bf16[384,1152]{1,0:T(8,128)(2,1)} %collective-permute-done.10, bf16[384,1152]{1,0:T(8,128)(2,1)} %collective-permute-done.2, ...), kind=kLoop, calls=%fused_computation | loop fusion | flops 49545216 | bytes 16515072 | tf_op jit(solution)/shard_map/concatenate | solution.py:401
  149.5 6.5 %all-to-all-done.5 = bf16[16,2,32,896]{3,2,1,0:T(8,128)(2,1)S(1)} async-done(((bf16[16,2,32,896]{3,2,1,0:T(8,128)(2,1)}), bf16[16,2,32,896]{3,2,1,0:T(8,128)(2,1)S(1)}, u32[]{:S(2)}, u32[]{:S(2)}) %all-to-all-start.5) | async-done | bytes 1835040 | tf_op jit(solution)/shard_map/all_to_all | solution.py:28
  156.0 3.3 %copy-done.2 = bf16[1792,2304]{1,0:T(8,128)(2,1)S(1)} copy-done((bf16[1792,2304]{1,0:T(8,128)(2,1)S(1)}, bf16[1792,2304]{1,0:T(8,128)(2,1)}, u32[]{:S(2)}) %copy-start.2) | copy-done | bytes 8257560
  159.4 6.4 %widen.1 = bf16[8,2,32,2432]{3,2,1,0:T(8,128)(2,1)S(1)} custom-call(s32[2]{0:T(128)S(1)} %copy-done.4, bf16[2,8,2,32,896]{4,3,2,1,0:T(8,128)(2,1)S(1)} %bitcast.58, bf16[1792,2304]{1,0:T(8,128)(2,1)S(1)} %copy-done.2), custom_call_target="tpu_custom_call" | custom-call | tf_op jit(solution)/shard_map/widen/pallas_call | solution.py:280
  165.7 32.1 %all_to_all.46 = bf16[8,64,2432]{2,1,0:T(8,128)(2,1)S(1)} all-to-all(bf16[8,64,2432]{2,1,0:T(8,128)(2,1)S(1)} %bitcast.57), channel_id=1, replica_groups=mesh['xh'=2,'xl'=2,'zl'=2,'zh'=2,'y'=4,'c'=2] {'xh','xl','zl'}, dimensions={0} | all-to-all | bytes 4980736 | tf_op jit(solution)/shard_map/all_to_all | solution.py:28
  197.9 0.4 convert_reduce_fusion
  198.9 29.3 %all_to_all.47.rows_ref = bf16[8,64,2304]{2,1,0:T(8,128)(2,1)S(1)} all-to-all(bf16[8,64,2304]{2,1,0:T(8,128)(2,1)S(1)} %broadcast_in_dim.31), channel_id=1, replica_groups=mesh['xh'=2,'xl'=2,'zl'=2,'zh'=2,'y'=4,'c'=2] {'xh','xl','zl'}, dimensions={0} | all-to-all | bytes 4718592 | tf_op jit(solution)/shard_map/all_to_all | solution.py:28
  228.2 3.5 %project.1 = bf16[8,2,2,16,896]{4,3,2,1,0:T(8,128)(2,1)} custom-call(bf16[8,64,2304]{2,1,0:T(8,128)(2,1)S(1)} %all_to_all.47.rows_ref, bf16[2304,896]{1,0:T(8,128)(2,1)S(1)} %copy-done.3), custom_call_target="tpu_custom_call" | custom-call | tf_op jit(solution)/shard_map/project/pallas_call | solution.py:189
  231.8 9.2 %all-to-all-start.8 = ((bf16[16,32,896]{2,1,0:T(8,128)(2,1)}), bf16[16,32,896]{2,1,0:T(8,128)(2,1)S(1)}, u32[]{:S(2)}, u32[]{:S(2)}) async-start(bf16[16,32,896]{2,1,0:T(8,128)(2,1)} %bitcast.32), calls=%async_computation.8 | async-start | bytes 1835008 | tf_op jit(solution)/shard_map/all_to_all | solution.py:28
  241.3 1.2 collective-permute-done.12
  242.6 14.3 %all-to-all-done.8 = bf16[16,32,896]{2,1,0:T(8,128)(2,1)S(1)} async-done(((bf16[16,32,896]{2,1,0:T(8,128)(2,1)}), bf16[16,32,896]{2,1,0:T(8,128)(2,1)S(1)}, u32[]{:S(2)}, u32[]{:S(2)}) %all-to-all-start.8) | async-done | bytes 917536 | tf_op jit(solution)/shard_map/all_to_all | solution.py:28
  257.4 0.7 copy.68
  (66 shorter events, 3.6 us)
Async XLA Ops:
  0.0 53.5 %copy-start = (bf16[2,512,896]{2,1,0:T(8,128)(2,1)S(1)}, bf16[2,512,896]{2,1,0:T(8,128)(2,1)}, u32[]{:S(2)}) copy-start(bf16[2,512,896]{2,1,0:T(8,128)(2,1)} %param.21) | copy-start | bytes 5505028
  0.0 13.3 %copy-start.7 = (bf16[8,512,128]{2,1,0:T(8,128)(2,1)S(1)}, bf16[8,512,128]{2,1,0:T(8,128)(2,1)}, u32[]{:S(2)}) copy-start(bf16[8,512,128]{2,1,0:T(8,128)(2,1)} %param.19) | copy-start | bytes 3145732
  0.0 13.5 %copy-start.9 = (bf16[896]{0:T(1024)(128)(2,1)S(1)}, bf16[896]{0:T(1024)(128)(2,1)}, u32[]{:S(2)}) copy-start(bf16[896]{0:T(1024)(128)(2,1)} %param.22) | copy-start | bytes 5380
  0.0 13.5 %copy-start.10 = (bf16[2,4,576]{2,1,0:T(4,128)(2,1)S(1)}, bf16[2,4,576]{2,1,0:T(4,128)(2,1)}, u32[]{:S(2)}) copy-start(bf16[2,4,576]{2,1,0:T(4,128)(2,1)} %param.18) | copy-start | bytes 27652
  0.0 42.7 %collective-permute-start.1 = (bf16[1024,896]{1,0:T(8,128)(2,1)}, bf16[1024,896]{1,0:T(8,128)(2,1)}, u32[]{:S(2)}, u32[]{:S(2)}) collective-permute-start(bf16[1024,896]{1,0:T(8,128)(2,1)} %refs_0_), channel_id=1, source_target_pairs={{0,32},{32,0},{1,33},{33,1},{2,34},{34,2},{3,35},{35,3},{4,36},{36... | collective-permute-start | bytes 5505032 | tf_op jit(solution)/shard_map/ppermute | solution.py:36
  4.6 17.7 %all-to-all-start = ((bf16[16,72,128]{2,1,0:T(8,128)(2,1)}), bf16[16,72,128]{2,1,0:T(8,128)(2,1)S(1)}, u32[]{:S(2)}, u32[]{:S(2)}) async-start(bf16[16,72,128]{2,1,0:T(8,128)(2,1)} %leave.1), calls=%async_computation | async-start | bytes 589824 | tf_op jit(solution)/shard_map/all_to_all | solution.py:28
  13.3 25.3 %collective-permute-start = (bf16[8,512,128]{2,1,0:T(8,128)(2,1)S(1)}, bf16[8,512,128]{2,1,0:T(8,128)(2,1)}, u32[]{:S(2)}, u32[]{:S(2)}) collective-permute-start(bf16[8,512,128]{2,1,0:T(8,128)(2,1)S(1)} %copy-done.7), channel_id=1, source_target_pairs={{0,1},{1,0},{2,3},{3,2},{4,5},{5,4},{6,7},{7,6},{8,9},{9,8},{10,11... | collective-permute-start | bytes 3145736 | tf_op jit(solution)/shard_map/ppermute | solution.py:36
  14.7 7.6 %copy-start.5 = (s32[1,16]{1,0:T(1,128)S(1)}, s32[1,16]{1,0:T(1,128)}, u32[]{:S(2)}) copy-start(s32[1,16]{1,0:T(1,128)} %param.16) | copy-start | bytes 196
  23.5 15.1 %all-to-all-start.1 = ((bf16[16,72,128]{2,1,0:T(8,128)(2,1)}), bf16[16,72,128]{2,1,0:T(8,128)(2,1)S(1)}, u32[]{:S(2)}, u32[]{:S(2)}) async-start(bf16[16,72,128]{2,1,0:T(8,128)(2,1)} %route.1), calls=%async_computation.1 | async-start | bytes 589824 | tf_op jit(solution)/shard_map/all_to_all | solution.py:28
  33.2 2.6 %copy-start.11 = (s32[1,16]{1,0:T(1,128)S(1)}, s32[1,16]{1,0:T(1,128)}, u32[]{:S(2)}) copy-start(s32[1,16]{1,0:T(1,128)} %param.15) | copy-start | bytes 196
  38.6 0.7 copy-start.6
  42.7 10.8 %collective-permute-start.3 = (bf16[1024,896]{1,0:T(8,128)(2,1)}, bf16[1024,896]{1,0:T(8,128)(2,1)}, u32[]{:S(2)}, u32[]{:S(2)}) collective-permute-start(bf16[1024,896]{1,0:T(8,128)(2,1)} %refs_0_), channel_id=1, source_target_pairs={{0,1},{1,0},{2,3},{3,2},{4,5},{5,4},{6,7},{7,6},{8,9},{9,8},{10,11... | collective-permute-start | bytes 5505032 | tf_op jit(solution)/shard_map/ppermute | solution.py:36
  43.6 16.5 %collective-permute-start.4 = (bf16[1152,896]{1,0:T(8,128)(2,1)}, bf16[1152,896]{1,0:T(8,128)(2,1)}, u32[]{:S(2)}, u32[]{:S(2)}) collective-permute-start(bf16[1152,896]{1,0:T(8,128)(2,1)} %param.25), channel_id=1, source_target_pairs={{0,1},{1,0},{2,3},{3,2},{4,5},{5,4},{6,7},{7,6},{8,9},{9,8},{10,11... | collective-permute-start | bytes 6193160 | tf_op jit(solution)/shard_map/ppermute | solution.py:36
  43.6 27.2 %collective-permute-start.5 = (bf16[1024,896]{1,0:T(8,128)(2,1)}, bf16[1024,896]{1,0:T(8,128)(2,1)}, u32[]{:S(2)}, u32[]{:S(2)}) collective-permute-start(bf16[1024,896]{1,0:T(8,128)(2,1)} %collective-permute-done.1.refs_2_), channel_id=1, source_target_pairs={{0,1},{1,0},{2,3},{3,2},{4,5},{5,4},{6,7},{7,6},{8,9},{9,8},{10,11... | collective-permute-start | bytes 5505032 | tf_op jit(solution)/shard_map/ppermute | solution.py:36
  44.1 21.6 %collective-permute-start.2 = (bf16[384,1152]{1,0:T(8,128)(2,1)}, bf16[384,1152]{1,0:T(8,128)(2,1)}, u32[]{:S(2)}, u32[]{:S(2)}) collective-permute-start(bf16[384,1152]{1,0:T(8,128)(2,1)} %multiply_convert_fusion.2), channel_id=1, source_target_pairs={{0,32},{32,0},{1,33},{33,1},{2,34},{34,2},{3,35},{35,3},{4,36},{36... | collective-permute-start | bytes 2654216 | tf_op jit(solution)/shard_map/ppermute | solution.py:36
  45.4 25.4 %all-to-all-start.2 = ((bf16[16,2,32,512]{3,2,1,0:T(8,128)(2,1)}), bf16[16,2,32,512]{3,2,1,0:T(8,128)(2,1)S(1)}, u32[]{:S(2)}, u32[]{:S(2)}) async-start(bf16[16,2,32,512]{3,2,1,0:T(8,128)(2,1)} %bitcast.61), calls=%async_computation.2 | async-start | bytes 2097152 | tf_op jit(solution)/shard_map/all_to_all | solution.py:28
  53.9 3.4 %copy-start.8 = (bf16[8,512,128]{2,1,0:T(8,128)(2,1)S(1)}, bf16[8,512,128]{2,1,0:T(8,128)(2,1)}, u32[]{:S(2)}) copy-start(bf16[8,512,128]{2,1,0:T(8,128)(2,1)} %param.19) | copy-start | bytes 3145732
  92.5 27.2 %collective-permute-start.6 = (bf16[512,1152]{1,0:T(8,128)(2,1)}, bf16[512,1152]{1,0:T(8,128)(2,1)S(1)}, u32[]{:S(2)}, u32[]{:S(2)}) collective-permute-start(bf16[512,1152]{1,0:T(8,128)(2,1)} %multiply_convert_fusion.1), channel_id=1, source_target_pairs={{0,32},{32,0},{1,33},{33,1},{2,34},{34,2},{3,35},{35,3},{4,36},{36... | collective-permute-start | bytes 3538952 | tf_op jit(solution)/shard_map/ppermute | solution.py:36
  100.2 19.5 %all-to-all-start.4 = ((bf16[8,2,32,896]{3,2,1,0:T(8,128)(2,1)}), bf16[8,2,32,896]{3,2,1,0:T(8,128)(2,1)S(1)}, u32[]{:S(2)}, u32[]{:S(2)}) async-start(bf16[8,2,32,896]{3,2,1,0:T(8,128)(2,1)} %combine.1), calls=%async_computation.4 | async-start | bytes 1835008 | tf_op jit(solution)/shard_map/all_to_all | solution.py:28
  103.8 15.6 %collective-permute-start.7 = (bf16[32,896]{1,0:T(8,128)(2,1)S(1)}, bf16[32,896]{1,0:T(8,128)(2,1)S(1)}, u32[]{:S(2)}, u32[]{:S(2)}) collective-permute-start(bf16[32,896]{1,0:T(8,128)(2,1)S(1)} %get-tuple-element.83), channel_id=1, source_target_pairs={{0,32},{32,0},{1,33},{33,1},{2,34},{34,2},{3,35},{35,3},{4,36},{36... | collective-permute-start | bytes 172040 | tf_op jit(solution)/shard_map/ppermute | solution.py:36
  119.7 9.8 %collective-permute-start.9 = (bf16[896,1152]{1,0:T(8,128)(2,1)}, bf16[896,1152]{1,0:T(8,128)(2,1)}, u32[]{:S(2)}, u32[]{:S(2)}) collective-permute-start(bf16[896,1152]{1,0:T(8,128)(2,1)} %multiply_convert_fusion), channel_id=1, source_target_pairs={{0,1},{1,0},{2,3},{3,2},{4,5},{5,4},{6,7},{7,6},{8,9},{9,8},{10,11... | collective-permute-start | bytes 6193160 | tf_op jit(solution)/shard_map/ppermute | solution.py:36
  122.4 7.2 %collective-permute-start.11 = (bf16[512,1152]{1,0:T(8,128)(2,1)S(1)}, bf16[512,1152]{1,0:T(8,128)(2,1)}, u32[]{:S(2)}, u32[]{:S(2)}) collective-permute-start(bf16[512,1152]{1,0:T(8,128)(2,1)S(1)} %collective-permute-done.6), channel_id=1, source_target_pairs={{0,1},{1,0},{2,3},{3,2},{4,5},{5,4},{6,7},{7,6},{8,9},{9,8},{10,11... | collective-permute-start | bytes 3538952 | tf_op jit(solution)/shard_map/ppermute | solution.py:36
  122.6 6.9 %collective-permute-start.10 = (bf16[384,1152]{1,0:T(8,128)(2,1)}, bf16[384,1152]{1,0:T(8,128)(2,1)}, u32[]{:S(2)}, u32[]{:S(2)}) collective-permute-start(bf16[384,1152]{1,0:T(8,128)(2,1)} %collective-permute-done.2), channel_id=1, source_target_pairs={{0,1},{1,0},{2,3},{3,2},{4,5},{5,4},{6,7},{7,6},{8,9},{9,8},{10,11... | collective-permute-start | bytes 2654216 | tf_op jit(solution)/shard_map/ppermute | solution.py:36
  123.1 26.4 %collective-permute-start.8 = (f32[32,896]{1,0:T(8,128)S(1)}, f32[32,896]{1,0:T(8,128)S(1)}, u32[]{:S(2)}, u32[]{:S(2)}) collective-permute-start(f32[32,896]{1,0:T(8,128)S(1)} %dynamic-slice_bitcast_fusion), channel_id=1, source_target_pairs={{0,32},{32,0},{1,33},{33,1},{2,34},{34,2},{3,35},{35,3},{4,36},{36... | collective-permute-start | bytes 344072 | tf_op jit(solution)/shard_map/ppermute | solution.py:36
  124.9 31.1 %all-to-all-start.5 = ((bf16[16,2,32,896]{3,2,1,0:T(8,128)(2,1)}), bf16[16,2,32,896]{3,2,1,0:T(8,128)(2,1)S(1)}, u32[]{:S(2)}, u32[]{:S(2)}) async-start(bf16[16,2,32,896]{3,2,1,0:T(8,128)(2,1)} %broadcast_in_dim.29), calls=%async_computation.5 | async-start | bytes 3670016 | tf_op jit(solution)/shard_map/all_to_all | solution.py:28
  129.6 26.5 %copy-start.4 = (s32[2]{0:T(128)S(1)}, s32[2]{0:T(128)}, u32[]{:S(2)}) copy-start(s32[2]{0:T(128)} %pad_add_fusion.ids_ref) | copy-start | bytes 28
  156.0 3.3 %copy-start.2 = (bf16[1792,2304]{1,0:T(8,128)(2,1)S(1)}, bf16[1792,2304]{1,0:T(8,128)(2,1)}, u32[]{:S(2)}) copy-start(bf16[1792,2304]{1,0:T(8,128)(2,1)} %maximum_maximum_fusion.weight_ref) | copy-start | bytes 24772612
  198.9 29.3 %copy-start.3 = (bf16[2304,896]{1,0:T(8,128)(2,1)S(1)}, bf16[2304,896]{1,0:T(8,128)(2,1)}, u32[]{:S(2)}) copy-start(bf16[2304,896]{1,0:T(8,128)(2,1)} %pad_maximum_fusion.weight_ref) | copy-start | bytes 12386308
  231.8 25.1 %all-to-all-start.8 = ((bf16[16,32,896]{2,1,0:T(8,128)(2,1)}), bf16[16,32,896]{2,1,0:T(8,128)(2,1)S(1)}, u32[]{:S(2)}, u32[]{:S(2)}) async-start(bf16[16,32,896]{2,1,0:T(8,128)(2,1)} %bitcast.32), calls=%async_computation.8 | async-start | bytes 1835008 | tf_op jit(solution)/shard_map/all_to_all | solution.py:28
  240.9 17.1 %copy-start.1 = (bf16[2,512,896]{2,1,0:T(8,128)(2,1)S(1)}, bf16[2,512,896]{2,1,0:T(8,128)(2,1)}, u32[]{:S(2)}) copy-start(bf16[2,512,896]{2,1,0:T(8,128)(2,1)} %param.21) | copy-start | bytes 5505028
  241.1 1.4 collective-permute-start.12

commit v17 on v13

--- a/solution.py
+++ b/solution.py
@@ -387,6 +387,7 @@
     by_head, kept, came, sent, downs, residue, out_weights, value_ups = lax.optimization_barrier(
         (by_head, kept, came, sent, downs, residue, out_weights, value_ups)
     )
+    residue[1] = swap(residue[1], "xl")
     value_heads = jnp.einsum(
         "thl,hlv->thv", by_head, value_ups, preferred_element_type=f32
     ).astype(bf16)
@@ -399,7 +400,6 @@
     gathered = exchange(value_heads, DP)
     gathered, sent, kept, residue = lax.optimization_barrier((gathered, sent, kept, residue))
     came.append(swap(sent, "xl"))
-    residue[1] = swap(residue[1], "xl")
     parts = exchange(combine(ids, gathered, out_weights), ZY)
     parts, came, kept, residue = lax.optimization_barrier((parts, came, kept, residue))
     kept = [kept, swap(kept, "c")]

time: 256 us -> 258 us (level)
    unnamed x28 -> x30, local copies, waits for them, and re-layouts: 5.53 us -> 6.29 us
where the time goes in v17:
time: 258 us; the launch traced here: 257 us
  blocking collectives  79.8 us (31%)
  starting transfers between devices  50 us (19%)
  waiting for transfers between devices  45.2 us (18%)
  other arithmetic  38.1 us (15%)
  Pallas kernels  31.4 us (12%)
  local copies, waits for them, and re-layouts  11.1 us (4%)
    all_to_all x3, blocking collectives, exchange(): return lax.all_to_all(blocks, axes, 0, 0, tiled=True)  79.8 us
    all_to_all x6, starting transfers between devices, exchange(): return lax.all_to_all(blocks, axes, 0, 0, tiled=True)  37 us
    all_to_all x6, waiting for transfers between devices, exchange(): return lax.all_to_all(blocks, axes, 0, 0, tiled=True)  29.1 us
    concatenate x1, other arithmetic, local(): jnp.concatenate([jnp.concatenate([own, swap(own, 'c') if k else kept[1]],...  19.9 us
    ppermute x13, waiting for transfers between devices, swap(): return lax.ppermute(block, axis, SWAP)  16.1 us
    ppermute x13, starting transfers between devices, swap(): return lax.ppermute(block, axis, SWAP)  13 us
    pallas_call x2, Pallas kernels, attend(): pl.pallas_call(body, grid_spec=pltpu.PrefetchScalarGridSpec(num_scalar_pr...  9.84 us
    convert_element_type x3, other arithmetic, scaled(): return (weight.astype(f32) * gain[low:high]).astype(bf16)  9.27 us
  transfers between devices with their start and end apart: 19, of which 9 were waited for; matrix products, arithmetic and copies ran while one was open for 16% of the time, Pallas kernels for 8%

profile of v17, /device:TPU:1, one launch (start us, length us, event | category | flops | bytes accessed | tf_op | source)
XLA Modules:
  0.0 257.3 jit_solution(5547779151480700949)
XLA Ops:
  0.0 2.1 collective-permute-start.1
  2.1 2.4 leave.1
  4.6 8.8 %all-to-all-start = ((bf16[16,72,128]{2,1,0:T(8,128)(2,1)}), bf16[16,72,128]{2,1,0:T(8,128)(2,1)S(1)}, u32[]{:S(2)}, u32[]{:S(2)}) async-start(bf16[16,72,128]{2,1,0:T(8,128)(2,1)} %leave.1), calls=%async_computation | async-start | bytes 589824 | tf_op jit(solution)/shard_map/all_to_all | solution.py:28
  13.5 1.1 copy.52
  14.6 6.5 %attend.1.refs_1_ = bf16[8,2,2,32,512]{4,3,2,1,0:T(8,128)(2,1)} custom-call(s32[4]{0:T(128)} %lengths_ref.3, s32[4]{0:T(128)} %lengths_ref.3, bf16[4,576,2]{2,1,0:T(8,128)(2,1)} %bitcast.58, bf16[2,4,576,128]{3,2,1,0:T(8,128)(2,1)} %bitcast.60, bf16[4,576,256]{2,1,0:T(8,128)(2,1)} %bitcast.63), custom_call_target="tpu_custom_call" | custom-call | tf_op jit(solution)/shard_map/attend/pallas_call | solution.py:145
  21.1 1.1 all-to-all-done.in_ref
  22.2 1.3 route.1
  23.5 6.2 %all-to-all-start.1 = ((bf16[16,72,128]{2,1,0:T(8,128)(2,1)}), bf16[16,72,128]{2,1,0:T(8,128)(2,1)S(1)}, u32[]{:S(2)}, u32[]{:S(2)}) async-start(bf16[16,72,128]{2,1,0:T(8,128)(2,1)} %route.1), calls=%async_computation.1 | async-start | bytes 589824 | tf_op jit(solution)/shard_map/all_to_all | solution.py:28
  29.7 3.5 %multiply_convert_fusion = bf16[896,1152]{1,0:T(8,128)(2,1)} fusion(f32[896]{0:T(1024)S(1)} %convert_element_type.62, bf16[896,1152]{1,0:T(8,128)(2,1)} %param.23, bf16[896,1152]{1,0:T(8,128)(2,1)} %param.24, pred[]{:T(512)S(6)} %eq.17), kind=kLoop, calls=%fused_computation.3 | loop fusion | flops 4128768 | bytes 6196737 | tf_op jit(solution)/shard_map/convert_element_type | solution.py:356
  33.3 2.6 %multiply_convert_fusion.2 = bf16[384,1152]{1,0:T(8,128)(2,1)} fusion(f32[384]{0:T(512)S(1)} %slice.37, bf16[896,1152]{1,0:T(8,128)(2,1)} %param.23, bf16[896,1152]{1,0:T(8,128)(2,1)} %param.24, pred[]{:T(512)S(6)} %eq.17), kind=kLoop, calls=%fused_computation.8 | loop fusion | flops 1769472 | bytes 2655745 | tf_op jit(solution)/shard_map/convert_element_type | solution.py:356
  35.9 0.7 fusion.11
  36.6 1.3 pad_add_fusion.ids_ref
  37.9 0.7 all-to-all-done.1.refs_0_
  38.6 0.7 copy-done.8
  39.3 3.3 %again.1 = bf16[8,2,2,32,512]{4,3,2,1,0:T(8,128)(2,1)} custom-call(s32[2]{0:T(128)} %pad_add_fusion.ids_ref, s32[4]{0:T(128)} %lengths_ref.3, bf16[4,576,2]{2,1,0:T(8,128)(2,1)} %bitcast.59, bf16[2,4,576,128]{3,2,1,0:T(8,128)(2,1)} %bitcast.61, bf16[16,72,128]{2,1,0:T(8,128)(2,1)} %copy-done.8, ...), custom_call_target="tpu_custom_call", output_to_operand_aliasing={{}: (5, {})} | custom-call | tf_op jit(solution)/shard_map/again/pallas_call | solution.py:145
  42.7 0.9 collective-permute-start.3
  44.1 1.3 collective-permute-start.2
  45.4 8.1 %all-to-all-start.2 = ((bf16[16,2,32,512]{3,2,1,0:T(8,128)(2,1)}), bf16[16,2,32,512]{3,2,1,0:T(8,128)(2,1)S(1)}, u32[]{:S(2)}, u32[]{:S(2)}) async-start(bf16[16,2,32,512]{3,2,1,0:T(8,128)(2,1)} %bitcast.57), calls=%async_computation.2 | async-start | bytes 2097152 | tf_op jit(solution)/shard_map/all_to_all | solution.py:28
  54.0 3.1 %multiply_convert_fusion.1 = bf16[512,1152]{1,0:T(8,128)(2,1)} fusion(f32[512]{0:T(512)S(1)} %slice.40, bf16[896,1152]{1,0:T(8,128)(2,1)} %param.23, bf16[896,1152]{1,0:T(8,128)(2,1)} %param.24, pred[]{:T(512)S(6)} %eq.17), kind=kLoop, calls=%fused_computation.4 | loop fusion | flops 2359296 | bytes 3540993 | tf_op jit(solution)/shard_map/convert_element_type | solution.py:356
  57.3 1.6 pad_maximum_fusion.1
  59.2 3.9 %pad_maximum_fusion.weight_ref = bf16[2304,896]{1,0:T(8,128)(2,1)} fusion(bf16[1152,896]{1,0:T(8,128)(2,1)} %collective-permute-done.4, bf16[1152,896]{1,0:T(8,128)(2,1)S(1)} %copy-done.7), kind=kLoop, calls=%fused_computation.2 | loop fusion | flops 8257536 | bytes 8257536 | tf_op jit(solution)/shard_map/concatenate | solution.py:376
  63.1 2.6 %collective-permute-done.2 = bf16[384,1152]{1,0:T(8,128)(2,1)} collective-permute-done((bf16[384,1152]{1,0:T(8,128)(2,1)}, bf16[384,1152]{1,0:T(8,128)(2,1)}, u32[]{:S(2)}, u32[]{:S(2)}) %collective-permute-start.2) | collective-permute-done | bytes 884768 | tf_op jit(solution)/shard_map/ppermute | solution.py:36
  65.7 5.1 %all-to-all-done.2 = bf16[16,2,32,512]{3,2,1,0:T(8,128)(2,1)S(1)} async-done(((bf16[16,2,32,512]{3,2,1,0:T(8,128)(2,1)}), bf16[16,2,32,512]{3,2,1,0:T(8,128)(2,1)S(1)}, u32[]{:S(2)}, u32[]{:S(2)}) %all-to-all-start.2) | async-done | bytes 1048608 | tf_op jit(solution)/shard_map/all_to_all | solution.py:28
  70.8 1.3 fusion
  72.5 1.1 broadcast_in_dim.28
  73.6 4.2 %all-to-all-start.3 = ((bf16[8,32,2048]{2,1,0:T(8,128)(2,1)}), bf16[8,32,2048]{2,1,0:T(8,128)(2,1)S(1)}, u32[]{:S(2)}, u32[]{:S(2)}) async-start(bf16[8,32,2048]{2,1,0:T(8,128)(2,1)} %bitcast.17), calls=%async_computation.3 | async-start | bytes 2097152 | tf_op jit(solution)/shard_map/all_to_all | solution.py:28
  77.8 1.5 collective-permute-start.6
  79.2 12.5 %collective-permute-done.6 = bf16[32,896]{1,0:T(8,128)(2,1)S(1)} collective-permute-done((bf16[32,896]{1,0:T(8,128)(2,1)S(1)}, bf16[32,896]{1,0:T(8,128)(2,1)S(1)}, u32[]{:S(2)}, u32[]{:S(2)}) %collective-permute-start.6) | collective-permute-done | bytes 57376 | tf_op jit(solution)/shard_map/ppermute | solution.py:36
  91.7 1.2 all-to-all-done.3.rows_ref
  93.1 0.8 copy-done.6
  93.9 7.4 %combine.1 = bf16[8,2,32,896]{3,2,1,0:T(8,128)(2,1)} custom-call(s32[2]{0:T(128)} %pad_add_fusion.ids_ref, bf16[8,32,2048]{2,1,0:T(8,128)(2,1)} %copy-done.6, bf16[1024,896]{1,0:T(8,128)(2,1)} %refs_0_, bf16[1024,896]{1,0:T(8,128)(2,1)} %collective-permute-done.3.refs_1_, bf16[1024,896]{1,0:T(8,128)(2,1)} %collective-permute-done.1.refs_2_, ...), custom_call_target="tpu_custom_call" | custom-call | tf_op jit(solution)/shard_map/combine/pallas_call | solution.py:238
  101.3 18.0 %all_to_all.45 = bf16[8,2,32,896]{3,2,1,0:T(8,128)(2,1)S(1)} all-to-all(bf16[8,2,32,896]{3,2,1,0:T(8,128)(2,1)} %combine.1), channel_id=1, replica_groups=mesh['xh'=2,'xl'=2,'zl'=2,'zh'=2,'y'=4,'c'=2] {'zh','y'}, dimensions={0} | all-to-all | bytes 1835008 | tf_op jit(solution)/shard_map/all_to_all | solution.py:28
  119.3 2.7 %collective-permute-start.9 = (bf16[896,1152]{1,0:T(8,128)(2,1)}, bf16[896,1152]{1,0:T(8,128)(2,1)}, u32[]{:S(2)}, u32[]{:S(2)}) collective-permute-start(bf16[896,1152]{1,0:T(8,128)(2,1)} %multiply_convert_fusion), channel_id=1, source_target_pairs={{0,1},{1,0},{2,3},{3,2},{4,5},{5,4},{6,7},{7,6},{8,9},{9,8},{10,11... | collective-permute-start | bytes 6193160 | tf_op jit(solution)/shard_map/ppermute | solution.py:36
  122.8 0.6 collective-permute-start.8
  123.3 1.5 broadcast_in_dim.29
  124.8 4.2 %all-to-all-start.5 = ((bf16[16,2,32,896]{3,2,1,0:T(8,128)(2,1)}), bf16[16,2,32,896]{3,2,1,0:T(8,128)(2,1)S(1)}, u32[]{:S(2)}, u32[]{:S(2)}) async-start(bf16[16,2,32,896]{3,2,1,0:T(8,128)(2,1)} %broadcast_in_dim.29), calls=%async_computation.5 | async-start | bytes 3670016 | tf_op jit(solution)/shard_map/all_to_all | solution.py:28
  129.1 19.9 %maximum_maximum_fusion.weight_ref = bf16[1792,2304]{1,0:T(8,128)(2,1)} fusion(bf16[512,1152]{1,0:T(8,128)(2,1)} %collective-permute-done.11, bf16[512,1152]{1,0:T(8,128)(2,1)S(1)} %collective-permute-done.7, bf16[384,1152]{1,0:T(8,128)(2,1)} %collective-permute-done.10, bf16[384,1152]{1,0:T(8,128)(2,1)} %collective-permute-done.2, ...), kind=kLoop, calls=%fused_computation | loop fusion | flops 49545216 | bytes 16515072 | tf_op jit(solution)/shard_map/concatenate | solution.py:406
  149.0 6.9 %all-to-all-done.5 = bf16[16,2,32,896]{3,2,1,0:T(8,128)(2,1)S(1)} async-done(((bf16[16,2,32,896]{3,2,1,0:T(8,128)(2,1)}), bf16[16,2,32,896]{3,2,1,0:T(8,128)(2,1)S(1)}, u32[]{:S(2)}, u32[]{:S(2)}) %all-to-all-start.5) | async-done | bytes 1835040 | tf_op jit(solution)/shard_map/all_to_all | solution.py:28
  155.8 3.3 %copy-done.2 = bf16[1792,2304]{1,0:T(8,128)(2,1)S(1)} copy-done((bf16[1792,2304]{1,0:T(8,128)(2,1)S(1)}, bf16[1792,2304]{1,0:T(8,128)(2,1)}, u32[]{:S(2)}) %copy-start.2) | copy-done | bytes 8257560
  159.2 6.4 %widen.1 = bf16[8,2,32,2432]{3,2,1,0:T(8,128)(2,1)S(1)} custom-call(s32[2]{0:T(128)S(1)} %copy-done.4, bf16[2,8,2,32,896]{4,3,2,1,0:T(8,128)(2,1)S(1)} %bitcast.54, bf16[1792,2304]{1,0:T(8,128)(2,1)S(1)} %copy-done.2), custom_call_target="tpu_custom_call" | custom-call | tf_op jit(solution)/shard_map/widen/pallas_call | solution.py:285
  165.6 32.5 %all_to_all.46 = bf16[8,64,2432]{2,1,0:T(8,128)(2,1)S(1)} all-to-all(bf16[8,64,2432]{2,1,0:T(8,128)(2,1)S(1)} %bitcast.53), channel_id=1, replica_groups=mesh['xh'=2,'xl'=2,'zl'=2,'zh'=2,'y'=4,'c'=2] {'xh','xl','zl'}, dimensions={0} | all-to-all | bytes 4980736 | tf_op jit(solution)/shard_map/all_to_all | solution.py:28
  199.1 29.3 %all_to_all.47.rows_ref = bf16[8,64,2304]{2,1,0:T(8,128)(2,1)S(1)} all-to-all(bf16[8,64,2304]{2,1,0:T(8,128)(2,1)S(1)} %broadcast_in_dim.31), channel_id=1, replica_groups=mesh['xh'=2,'xl'=2,'zl'=2,'zh'=2,'y'=4,'c'=2] {'xh','xl','zl'}, dimensions={0} | all-to-all | bytes 4718592 | tf_op jit(solution)/shard_map/all_to_all | solution.py:28
  228.4 4.1 %project.1 = bf16[8,1,64,896]{3,2,1,0:T(8,128)(2,1)} custom-call(s32[2]{0:T(128)S(1)} %copy-done.4, bf16[8,64,2304]{2,1,0:T(8,128)(2,1)S(1)} %all_to_all.47.rows_ref, bf16[2304,896]{1,0:T(8,128)(2,1)S(1)} %copy-done.3), custom_call_target="tpu_custom_call" | custom-call | tf_op jit(solution)/shard_map/project/pallas_call | solution.py:186
  232.5 5.6 %all-to-all-start.8 = ((bf16[8,64,896]{2,1,0:T(8,128)(2,1)}), bf16[8,64,896]{2,1,0:T(8,128)(2,1)S(1)}, u32[]{:S(2)}, u32[]{:S(2)}) async-start(bf16[8,64,896]{2,1,0:T(8,128)(2,1)} %bitcast.26), calls=%async_computation.8 | async-start | bytes 1835008 | tf_op jit(solution)/shard_map/all_to_all | solution.py:28
  238.2 14.1 %all-to-all-done.8 = bf16[8,64,896]{2,1,0:T(8,128)(2,1)S(1)} async-done(((bf16[8,64,896]{2,1,0:T(8,128)(2,1)}), bf16[8,64,896]{2,1,0:T(8,128)(2,1)S(1)}, u32[]{:S(2)}, u32[]{:S(2)}) %all-to-all-start.8) | async-done | bytes 917536 | tf_op jit(solution)/shard_map/all_to_all | solution.py:28
  252.8 2.5 collective-permute-start.12
  255.4 0.9 collective-permute-done.12
  256.6 0.7 copy.60
  (72 shorter events, 5.0 us)
Async XLA Ops:
  0.0 53.5 %copy-start = (bf16[2,512,896]{2,1,0:T(8,128)(2,1)S(1)}, bf16[2,512,896]{2,1,0:T(8,128)(2,1)}, u32[]{:S(2)}) copy-start(bf16[2,512,896]{2,1,0:T(8,128)(2,1)} %param.21) | copy-start | bytes 5505028
  0.0 13.3 %copy-start.9 = (bf16[8,512,128]{2,1,0:T(8,128)(2,1)S(1)}, bf16[8,512,128]{2,1,0:T(8,128)(2,1)}, u32[]{:S(2)}) copy-start(bf16[8,512,128]{2,1,0:T(8,128)(2,1)} %param.19) | copy-start | bytes 3145732
  0.0 13.5 %copy-start.11 = (bf16[896]{0:T(1024)(128)(2,1)S(1)}, bf16[896]{0:T(1024)(128)(2,1)}, u32[]{:S(2)}) copy-start(bf16[896]{0:T(1024)(128)(2,1)} %param.22) | copy-start | bytes 5380
  0.0 13.5 %copy-start.12 = (bf16[2,4,576]{2,1,0:T(4,128)(2,1)S(1)}, bf16[2,4,576]{2,1,0:T(4,128)(2,1)}, u32[]{:S(2)}) copy-start(bf16[2,4,576]{2,1,0:T(4,128)(2,1)} %param.18) | copy-start | bytes 27652
  0.0 42.7 %collective-permute-start.1 = (bf16[1024,896]{1,0:T(8,128)(2,1)}, bf16[1024,896]{1,0:T(8,128)(2,1)}, u32[]{:S(2)}, u32[]{:S(2)}) collective-permute-start(bf16[1024,896]{1,0:T(8,128)(2,1)} %refs_0_), channel_id=1, source_target_pairs={{0,32},{32,0},{1,33},{33,1},{2,34},{34,2},{3,35},{35,3},{4,36},{36... | collective-permute-start | bytes 5505032 | tf_op jit(solution)/shard_map/ppermute | solution.py:36
  4.6 17.7 %all-to-all-start = ((bf16[16,72,128]{2,1,0:T(8,128)(2,1)}), bf16[16,72,128]{2,1,0:T(8,128)(2,1)S(1)}, u32[]{:S(2)}, u32[]{:S(2)}) async-start(bf16[16,72,128]{2,1,0:T(8,128)(2,1)} %leave.1), calls=%async_computation | async-start | bytes 589824 | tf_op jit(solution)/shard_map/all_to_all | solution.py:28
  13.3 25.3 %collective-permute-start = (bf16[8,512,128]{2,1,0:T(8,128)(2,1)S(1)}, bf16[8,512,128]{2,1,0:T(8,128)(2,1)}, u32[]{:S(2)}, u32[]{:S(2)}) collective-permute-start(bf16[8,512,128]{2,1,0:T(8,128)(2,1)S(1)} %copy-done.9), channel_id=1, source_target_pairs={{0,1},{1,0},{2,3},{3,2},{4,5},{5,4},{6,7},{7,6},{8,9},{9,8},{10,11... | collective-permute-start | bytes 3145736 | tf_op jit(solution)/shard_map/ppermute | solution.py:36
  14.6 7.6 %copy-start.5 = (s32[1,16]{1,0:T(1,128)S(1)}, s32[1,16]{1,0:T(1,128)}, u32[]{:S(2)}) copy-start(s32[1,16]{1,0:T(1,128)} %param.16) | copy-start | bytes 196
  23.5 15.1 %all-to-all-start.1 = ((bf16[16,72,128]{2,1,0:T(8,128)(2,1)}), bf16[16,72,128]{2,1,0:T(8,128)(2,1)S(1)}, u32[]{:S(2)}, u32[]{:S(2)}) async-start(bf16[16,72,128]{2,1,0:T(8,128)(2,1)} %route.1), calls=%async_computation.1 | async-start | bytes 589824 | tf_op jit(solution)/shard_map/all_to_all | solution.py:28
  33.3 2.7 %copy-start.13 = (s32[1,16]{1,0:T(1,128)S(1)}, s32[1,16]{1,0:T(1,128)}, u32[]{:S(2)}) copy-start(s32[1,16]{1,0:T(1,128)} %param.15) | copy-start | bytes 196
  38.6 0.7 copy-start.8
  42.7 10.8 %collective-permute-start.3 = (bf16[1024,896]{1,0:T(8,128)(2,1)}, bf16[1024,896]{1,0:T(8,128)(2,1)}, u32[]{:S(2)}, u32[]{:S(2)}) collective-permute-start(bf16[1024,896]{1,0:T(8,128)(2,1)} %refs_0_), channel_id=1, source_target_pairs={{0,1},{1,0},{2,3},{3,2},{4,5},{5,4},{6,7},{7,6},{8,9},{9,8},{10,11... | collective-permute-start | bytes 5505032 | tf_op jit(solution)/shard_map/ppermute | solution.py:36
  43.6 15.3 %collective-permute-start.4 = (bf16[1152,896]{1,0:T(8,128)(2,1)}, bf16[1152,896]{1,0:T(8,128)(2,1)}, u32[]{:S(2)}, u32[]{:S(2)}) collective-permute-start(bf16[1152,896]{1,0:T(8,128)(2,1)} %param.25), channel_id=1, source_target_pairs={{0,1},{1,0},{2,3},{3,2},{4,5},{5,4},{6,7},{7,6},{8,9},{9,8},{10,11... | collective-permute-start | bytes 6193160 | tf_op jit(solution)/shard_map/ppermute | solution.py:36
  43.6 27.2 %collective-permute-start.5 = (bf16[1024,896]{1,0:T(8,128)(2,1)}, bf16[1024,896]{1,0:T(8,128)(2,1)}, u32[]{:S(2)}, u32[]{:S(2)}) collective-permute-start(bf16[1024,896]{1,0:T(8,128)(2,1)} %collective-permute-done.1.refs_2_), channel_id=1, source_target_pairs={{0,1},{1,0},{2,3},{3,2},{4,5},{5,4},{6,7},{7,6},{8,9},{9,8},{10,11... | collective-permute-start | bytes 5505032 | tf_op jit(solution)/shard_map/ppermute | solution.py:36
  44.1 21.6 %collective-permute-start.2 = (bf16[384,1152]{1,0:T(8,128)(2,1)}, bf16[384,1152]{1,0:T(8,128)(2,1)}, u32[]{:S(2)}, u32[]{:S(2)}) collective-permute-start(bf16[384,1152]{1,0:T(8,128)(2,1)} %multiply_convert_fusion.2), channel_id=1, source_target_pairs={{0,32},{32,0},{1,33},{33,1},{2,34},{34,2},{3,35},{35,3},{4,36},{36... | collective-permute-start | bytes 2654216 | tf_op jit(solution)/shard_map/ppermute | solution.py:36
  45.4 25.4 %all-to-all-start.2 = ((bf16[16,2,32,512]{3,2,1,0:T(8,128)(2,1)}), bf16[16,2,32,512]{3,2,1,0:T(8,128)(2,1)S(1)}, u32[]{:S(2)}, u32[]{:S(2)}) async-start(bf16[16,2,32,512]{3,2,1,0:T(8,128)(2,1)} %bitcast.57), calls=%async_computation.2 | async-start | bytes 2097152 | tf_op jit(solution)/shard_map/all_to_all | solution.py:28
  53.9 3.4 %copy-start.10 = (bf16[8,512,128]{2,1,0:T(8,128)(2,1)S(1)}, bf16[8,512,128]{2,1,0:T(8,128)(2,1)}, u32[]{:S(2)}) copy-start(bf16[8,512,128]{2,1,0:T(8,128)(2,1)} %param.19) | copy-start | bytes 3145732
  57.3 1.9 copy-start.7
  73.6 19.3 %all-to-all-start.3 = ((bf16[8,32,2048]{2,1,0:T(8,128)(2,1)}), bf16[8,32,2048]{2,1,0:T(8,128)(2,1)S(1)}, u32[]{:S(2)}, u32[]{:S(2)}) async-start(bf16[8,32,2048]{2,1,0:T(8,128)(2,1)} %bitcast.17), calls=%async_computation.3 | async-start | bytes 2097152 | tf_op jit(solution)/shard_map/all_to_all | solution.py:28
  77.8 13.9 %collective-permute-start.6 = (bf16[32,896]{1,0:T(8,128)(2,1)S(1)}, bf16[32,896]{1,0:T(8,128)(2,1)S(1)}, u32[]{:S(2)}, u32[]{:S(2)}) collective-permute-start(bf16[32,896]{1,0:T(8,128)(2,1)S(1)} %get-tuple-element.75), channel_id=1, source_target_pairs={{0,32},{32,0},{1,33},{33,1},{2,34},{34,2},{3,35},{35,3},{4,36},{36... | collective-permute-start | bytes 172040 | tf_op jit(solution)/shard_map/ppermute | solution.py:36
  92.9 1.0 copy-start.6
  92.9 26.4 %collective-permute-start.7 = (bf16[512,1152]{1,0:T(8,128)(2,1)}, bf16[512,1152]{1,0:T(8,128)(2,1)S(1)}, u32[]{:S(2)}, u32[]{:S(2)}) collective-permute-start(bf16[512,1152]{1,0:T(8,128)(2,1)} %multiply_convert_fusion.1), channel_id=1, source_target_pairs={{0,32},{32,0},{1,33},{33,1},{2,34},{34,2},{3,35},{35,3},{4,36},{36... | collective-permute-start | bytes 3538952 | tf_op jit(solution)/shard_map/ppermute | solution.py:36
  119.3 9.8 %collective-permute-start.9 = (bf16[896,1152]{1,0:T(8,128)(2,1)}, bf16[896,1152]{1,0:T(8,128)(2,1)}, u32[]{:S(2)}, u32[]{:S(2)}) collective-permute-start(bf16[896,1152]{1,0:T(8,128)(2,1)} %multiply_convert_fusion), channel_id=1, source_target_pairs={{0,1},{1,0},{2,3},{3,2},{4,5},{5,4},{6,7},{7,6},{8,9},{9,8},{10,11... | collective-permute-start | bytes 6193160 | tf_op jit(solution)/shard_map/ppermute | solution.py:36
  122.0 7.0 %collective-permute-start.11 = (bf16[512,1152]{1,0:T(8,128)(2,1)S(1)}, bf16[512,1152]{1,0:T(8,128)(2,1)}, u32[]{:S(2)}, u32[]{:S(2)}) collective-permute-start(bf16[512,1152]{1,0:T(8,128)(2,1)S(1)} %collective-permute-done.7), channel_id=1, source_target_pairs={{0,1},{1,0},{2,3},{3,2},{4,5},{5,4},{6,7},{7,6},{8,9},{9,8},{10,11... | collective-permute-start | bytes 3538952 | tf_op jit(solution)/shard_map/ppermute | solution.py:36
  122.0 7.0 %collective-permute-start.10 = (bf16[384,1152]{1,0:T(8,128)(2,1)}, bf16[384,1152]{1,0:T(8,128)(2,1)}, u32[]{:S(2)}, u32[]{:S(2)}) collective-permute-start(bf16[384,1152]{1,0:T(8,128)(2,1)} %collective-permute-done.2), channel_id=1, source_target_pairs={{0,1},{1,0},{2,3},{3,2},{4,5},{5,4},{6,7},{7,6},{8,9},{9,8},{10,11... | collective-permute-start | bytes 2654216 | tf_op jit(solution)/shard_map/ppermute | solution.py:36
  122.8 26.2 %collective-permute-start.8 = (f32[32,896]{1,0:T(8,128)S(1)}, f32[32,896]{1,0:T(8,128)S(1)}, u32[]{:S(2)}, u32[]{:S(2)}) collective-permute-start(f32[32,896]{1,0:T(8,128)S(1)} %dynamic-slice_bitcast_fusion), channel_id=1, source_target_pairs={{0,32},{32,0},{1,33},{33,1},{2,34},{34,2},{3,35},{35,3},{4,36},{36... | collective-permute-start | bytes 344072 | tf_op jit(solution)/shard_map/ppermute | solution.py:36
  124.8 31.0 %all-to-all-start.5 = ((bf16[16,2,32,896]{3,2,1,0:T(8,128)(2,1)}), bf16[16,2,32,896]{3,2,1,0:T(8,128)(2,1)S(1)}, u32[]{:S(2)}, u32[]{:S(2)}) async-start(bf16[16,2,32,896]{3,2,1,0:T(8,128)(2,1)} %broadcast_in_dim.29), calls=%async_computation.5 | async-start | bytes 3670016 | tf_op jit(solution)/shard_map/all_to_all | solution.py:28
  129.0 26.8 %copy-start.4 = (s32[2]{0:T(128)S(1)}, s32[2]{0:T(128)}, u32[]{:S(2)}) copy-start(s32[2]{0:T(128)} %pad_add_fusion.ids_ref) | copy-start | bytes 28
  155.8 3.3 %copy-start.2 = (bf16[1792,2304]{1,0:T(8,128)(2,1)S(1)}, bf16[1792,2304]{1,0:T(8,128)(2,1)}, u32[]{:S(2)}) copy-start(bf16[1792,2304]{1,0:T(8,128)(2,1)} %maximum_maximum_fusion.weight_ref) | copy-start | bytes 24772612
  199.1 29.3 %copy-start.3 = (bf16[2304,896]{1,0:T(8,128)(2,1)S(1)}, bf16[2304,896]{1,0:T(8,128)(2,1)}, u32[]{:S(2)}) copy-start(bf16[2304,896]{1,0:T(8,128)(2,1)} %pad_maximum_fusion.weight_ref) | copy-start | bytes 12386308
  232.5 19.9 %all-to-all-start.8 = ((bf16[8,64,896]{2,1,0:T(8,128)(2,1)}), bf16[8,64,896]{2,1,0:T(8,128)(2,1)S(1)}, u32[]{:S(2)}, u32[]{:S(2)}) async-start(bf16[8,64,896]{2,1,0:T(8,128)(2,1)} %bitcast.26), calls=%async_computation.8 | async-start | bytes 1835008 | tf_op jit(solution)/shard_map/all_to_all | solution.py:28
  238.1 19.2 %copy-start.1 = (bf16[2,512,896]{2,1,0:T(8,128)(2,1)S(1)}, bf16[2,512,896]{2,1,0:T(8,128)(2,1)}, u32[]{:S(2)}) copy-start(bf16[2,512,896]{2,1,0:T(8,128)(2,1)} %param.21) | copy-start | bytes 5505028
  252.8 3.4 %collective-permute-start.12 = (bf16[2,4,2,2,896]{4,3,2,1,0:T(2,128)(2,1)S(1)}, bf16[2,4,2,2,896]{4,3,2,1,0:T(2,128)(2,1)S(1)}, u32[]{:S(2)}, u32[]{:S(2)}) collective-permute-start(bf16[2,4,2,2,896]{4,3,2,1,0:T(2,128)(2,1)S(1)} %dynamic-slice_bitcast_fusion.2), channel_id=1, source_target_pairs={{0,1},{1,0},{2,3},{3,2},{4,5},{5,4},{6,7},{7,6},{8,9},{9,8},{10,11... | collective-permute-start | bytes 172040 | tf_op jit(solution)/shard_map/ppermute | solution.py:36
